TPU v7x, 32 devices: a whole 2x2x4 slice. The times are simulated.
32 devices in a mesh: xi: 4 (over x, core), eta: 4 (over z), zeta: 2 (over y).
Axes of the slice: x: 2, y: 2, z: 4, core: 2. Of those that a mesh axis runs over, the one named last changes fastest.
Arguments:
- conserved_solution: float32 [5, 64, 64, 256], P(None, 'xi', 'eta', 'zeta'), may hold values from -1.2 to 6, as said below
- metrics: float32 [3, 3, 64, 64, 256], P(None, None, 'xi', 'eta', 'zeta'), may hold values from -0.4 to 1.4, as said below
- jacobian: float32 [64, 64, 256], P('xi', 'eta', 'zeta'), may hold values from 0.7 to 1.4
Outputs:
- filtered: float32 [5, 64, 64, 256], P(None, 'xi', 'eta', 'zeta')
Inputs may be any that keep to these rules, and one draw needn't show every extreme that they name: conserved_solution[0] (density) lies between 0.5 and 2, and the pressure 0.4 (conserved_solution[4] - (conserved_solution[1]^2 + conserved_solution[2]^2 + conserved_solution[3]^2) / (2 conserved_solution[0])) lies between 0.5 and 1.5. The entries metrics[k, k] lie between 0.7 and 1.4, the others between -0.4 and 0.4.
All inputs are finite; a program needn't handle non-finite values.
Results may differ from a plain program's by a relative error of at most 0.00005.
Values sent between devices are 32-bit elements; how exact they have to be, the bound alone decides.
No kernel may reach another device: no remote copies, remote signals or barrier semaphores. Data moves between devices by JAX's collectives and lax.ppermute only.
A program may use at most 64 MiB of HBM per device.

v0:
```python
import jax
import jax.numpy as jnp
import numpy as np
from jax import lax
from jax.sharding import PartitionSpec as P

WIDTH = 5


viscosity = 0.15
conduction = 0.15 * 1.4 / (0.4 * 0.72)
step_duration = 0.08
line_forms = ("", "al,flyz->fayz", "al,fxlz->fxaz", "al,fxyl->fxya")


def with_halo(value, sides, width):
    for axis, dim in sides:
        count, length = (lax.axis_size(axis), value.shape[dim])
        up = [(i, (i + 1) % count) for i in range(count)]
        down = [(j, i) for i, j in up]
        last = lax.slice_in_dim(value, length - width, length, axis=dim)
        initial = lax.slice_in_dim(value, 0, width, axis=dim)
        before = lax.ppermute(last, axis, up)
        after = lax.ppermute(initial, axis, down)
        value = jnp.concatenate([before, value, after], axis=dim)
    return value


def banded_solve(system, source):
    extent = system.shape[0]
    lower = np.zeros(extent)
    upper = np.zeros(extent)
    middle = np.array([float(system[index, index]) for index in range(extent)])
    for index in range(1, extent):
        lower[index] = system[index, index - 1]
        upper[index - 1] = system[index - 1, index]
    rights = np.array(source)
    for index in range(1, extent):
        factor = lower[index] / middle[index - 1]
        middle[index] = middle[index] - factor * upper[index - 1]
        rights[index] = rights[index] - factor * rights[index - 1]
    answer = np.zeros(rights.shape)
    answer[extent - 1] = rights[extent - 1] / middle[extent - 1]
    for index in range(extent - 2, -1, -1):
        answer[index] = (rights[index] - upper[index] * answer[index + 1]) / middle[index]
    return answer


def derivative_table(length):
    extent = length + 2 * WIDTH
    system = np.eye(extent)
    source = np.zeros((extent, extent))
    for position in range(2, extent - 2):
        system[position, position - 1] = 1.0 / 3.0
        system[position, position + 1] = 1.0 / 3.0
        source[position, position + 1] = 7.0 / 9.0
        source[position, position - 1] = -7.0 / 9.0
        source[position, position + 2] = 1.0 / 36.0
        source[position, position - 2] = -1.0 / 36.0
    source[1, 2] = 0.5
    source[1, 0] = -0.5
    source[extent - 2, extent - 1] = 0.5
    source[extent - 2, extent - 3] = -0.5
    source[0, 1] = 1.0
    source[0, 0] = -1.0
    source[extent - 1, extent - 1] = 1.0
    source[extent - 1, extent - 2] = -1.0
    return banded_solve(system, source)[WIDTH : WIDTH + length]


def filter_table(length):
    strength = 0.4
    coeffs = [
        (193.0 + 126.0 * strength) / 256.0,
        (105.0 + 302.0 * strength) / 256.0,
        15.0 * (2.0 * strength - 1.0) / 64.0,
        45.0 * (1.0 - 2.0 * strength) / 512.0,
        5.0 * (2.0 * strength - 1.0) / 256.0,
        (1.0 - 2.0 * strength) / 512.0,
    ]
    extent = length + 2 * WIDTH
    system = np.eye(extent)
    source = np.eye(extent)
    for position in range(5, extent - 5):
        system[position, position - 1] = strength
        system[position, position + 1] = strength
        source[position, position] = coeffs[0]
        for offset in range(1, 6):
            source[position, position + offset] = coeffs[offset] / 2.0
            source[position, position - offset] = coeffs[offset] / 2.0
    return banded_solve(system, source)[WIDTH : WIDTH + length]


def sweep_lines(padded, matrix, dim):
    return jnp.einsum(line_forms[dim], matrix, padded, precision=lax.Precision.HIGHEST)


def faces_xi(values):
    return with_halo(values, (("xi", 1),), WIDTH)


def faces_eta(values):
    return with_halo(values, (("eta", 2),), WIDTH)


def faces_zeta(values):
    return with_halo(values, (("zeta", 3),), WIDTH)


def basic_quantities(conserved_solution):
    density = conserved_solution[0]
    fluid_speed_vector = conserved_solution[1:4] / density
    thermodynamic_stress_scalar = 0.4 * (
        conserved_solution[4] - 0.5 * jnp.sum(conserved_solution[1:4] * fluid_speed_vector, axis=0)
    )
    return (fluid_speed_vector, thermodynamic_stress_scalar, thermodynamic_stress_scalar / density)


def fluxes(
    conserved_solution, fluid_speed_vector, thermodynamic_stress_scalar, slopes, metrics, jacobian
):
    physical = [
        [
            jacobian
            * (
                metrics[0, column] * slopes[0][member]
                + metrics[1, column] * slopes[1][member]
                + metrics[2, column] * slopes[2][member]
            )
            for column in range(3)
        ]
        for member in range(4)
    ]
    spread = physical[0][0] + physical[1][1] + physical[2][2]
    totals = []
    for column in range(3):
        stress = [
            viscosity * (physical[member][column] + physical[column][member]) for member in range(3)
        ]
        stress[column] = stress[column] - 2.0 / 3.0 * viscosity * spread
        subdomain_parts = [conserved_solution[1 + column]]
        for member in range(3):
            carried = conserved_solution[1 + member] * fluid_speed_vector[column] - stress[member]
            if member == column:
                carried = carried + thermodynamic_stress_scalar
            subdomain_parts.append(carried)
        worked = (
            fluid_speed_vector[0] * stress[0]
            + fluid_speed_vector[1] * stress[1]
            + fluid_speed_vector[2] * stress[2]
        )
        subdomain_parts.append(
            (conserved_solution[4] + thermodynamic_stress_scalar) * fluid_speed_vector[column]
            - worked
            - conduction * physical[3][column]
        )
        totals.append(jnp.stack(subdomain_parts))
    return [
        metrics[direction, 0] * totals[0]
        + metrics[direction, 1] * totals[1]
        + metrics[direction, 2] * totals[2]
        for direction in range(3)
    ]


def local(conserved_solution, metrics, jacobian):
    lengths = conserved_solution.shape[1:]
    derive = [jnp.asarray(derivative_table(length), dtype=jnp.float32) for length in lengths]
    smooth = [jnp.asarray(filter_table(length), dtype=jnp.float32) for length in lengths]
    fluid_speed_vector, thermodynamic_stress_scalar, thermal_level = basic_quantities(
        conserved_solution
    )
    basic_quantity = jnp.concatenate([fluid_speed_vector, thermal_level[None]], axis=0)
    padded = with_halo(basic_quantity, (("xi", 1), ("eta", 2), ("zeta", 3)), WIDTH)
    slopes = [
        sweep_lines(padded[:, :, WIDTH:-WIDTH, WIDTH:-WIDTH], derive[0], 1),
        sweep_lines(padded[:, WIDTH:-WIDTH, :, WIDTH:-WIDTH], derive[1], 2),
        sweep_lines(padded[:, WIDTH:-WIDTH, WIDTH:-WIDTH, :], derive[2], 3),
    ]
    contra = fluxes(
        conserved_solution,
        fluid_speed_vector,
        thermodynamic_stress_scalar,
        slopes,
        metrics,
        jacobian,
    )
    divergence = sweep_lines(faces_xi(contra[0]), derive[0], 1)
    divergence = divergence + sweep_lines(faces_eta(contra[1]), derive[1], 2)
    divergence = divergence + sweep_lines(faces_zeta(contra[2]), derive[2], 3)
    sectioned = conserved_solution - step_duration * jacobian * divergence
    padded = with_halo(sectioned, (("xi", 1), ("eta", 2), ("zeta", 3)), WIDTH)
    result = sweep_lines(padded, smooth[0], 1)
    result = sweep_lines(result, smooth[1], 2)
    result = sweep_lines(result, smooth[2], 3)
    return result


def solution(mesh):
    in_specs = (
        P(None, "xi", "eta", "zeta"),
        P(None, None, "xi", "eta", "zeta"),
        P("xi", "eta", "zeta"),
    )
    out_specs = P(None, "xi", "eta", "zeta")
    return jax.shard_map(local, mesh=mesh, in_specs=in_specs, out_specs=out_specs, check_vma=False)
```

profile of v0, /device:TPU:0, one launch (start us, length us, event | category | flops | bytes accessed | tf_op | source)
XLA Modules:
  0.0 157.6 jit_solution(5553356456078909301)
XLA Ops:
  0.0 1.3 copy.140
  2.1 2.4 %collective-permute-start.1 = (f32[4,5,16,128]{3,1,2,0:T(8,128)S(1)}, f32[4,5,16,128]{3,1,2,0:T(8,128)S(1)}, u32[]{:S(2)}, u32[]{:S(2)}) collective-permute-start(f32[4,5,16,128]{3,1,2,0:T(8,128)S(1)} %get-tuple-element.55), channel_id=1, source_target_pairs={{8,0},{16,8},{24,16},{0,24},{9,1},{17,9},{25,17},{1,25},{10,2},{18... | collective-permute-start | bytes 491528 | tf_op jit(solution)/shard_map/ppermute | solution.py:24
  6.1 0.8 copy_bitcast_fusion.5
  8.4 2.8 %collective-permute-done.1 = f32[4,5,16,128]{3,1,2,0:T(8,128)S(1)} collective-permute-done((f32[4,5,16,128]{3,1,2,0:T(8,128)S(1)}, f32[4,5,16,128]{3,1,2,0:T(8,128)S(1)}, u32[]{:S(2)}, u32[]{:S(2)}) %collective-permute-start.1) | collective-permute-done | bytes 163872 | tf_op jit(solution)/shard_map/ppermute | solution.py:24
  11.2 1.1 collective-permute-done
  12.4 3.7 %collective-permute-start.3 = (f32[4,26,5,128]{3,1,2,0:T(8,128)S(1)}, f32[4,26,5,128]{3,1,2,0:T(8,128)S(1)}, u32[]{:S(2)}, u32[]{:S(2)}) collective-permute-start(f32[4,26,5,128]{3,1,2,0:T(8,128)S(1)} %get-tuple-element.40), channel_id=1, source_target_pairs={{2,0},{4,2},{6,4},{0,6},{3,1},{5,3},{7,5},{1,7},{10,8},{12,10},{14... | collective-permute-start | bytes 798728 | tf_op jit(solution)/shard_map/ppermute | solution.py:24
  17.5 1.7 %convolution_bitcast_fusion = f32[4,16,16,128]{3,1,2,0:T(8,128)} fusion(f32[16,26,1,1]{1,0,3,2:T(8,128)S(1)} %copy-done.41, f32[4,5,16,128]{3,1,2,0:T(8,128)S(1)} %collective-permute-done.1, f32[1,16,16,128]{3,1,2,0:T(8,128)S(1)} %get-tuple-element.52, f32[3,16,16,128]{3,1,2,0:T(8,128)S(1)} %get-tuple-element.18, f32[4,5,16,128]{3,1,2,0:T(8,128)S(1)} %collective-permute-done), kind=kOutput, calls=%fused_computation.41 | convolution fusion | flops 41533440 | bytes 1377920 | tf_op jit(solution)/shard_map/al,flyz->fayz/dot_general | solution.py:95
  19.2 5.0 %collective-permute-done.3 = f32[4,26,5,128]{3,1,2,0:T(8,128)S(1)} collective-permute-done((f32[4,26,5,128]{3,1,2,0:T(8,128)S(1)}, f32[4,26,5,128]{3,1,2,0:T(8,128)S(1)}, u32[]{:S(2)}, u32[]{:S(2)}) %collective-permute-start.3) | collective-permute-done | bytes 266272 | tf_op jit(solution)/shard_map/ppermute | solution.py:24
  24.3 6.1 %collective-permute-done.2 = f32[4,26,5,128]{3,1,2,0:T(8,128)S(1)} collective-permute-done((f32[4,26,5,128]{3,1,2,0:T(8,128)S(1)}, f32[4,26,5,128]{3,1,2,0:T(8,128)S(1)}, u32[]{:S(2)}, u32[]{:S(2)}) %collective-permute-start.2) | collective-permute-done | bytes 266272 | tf_op jit(solution)/shard_map/ppermute | solution.py:23
  31.4 1.8 %fusion.92 = (f32[4,26,26,5]{3,1,2,0:T(8,128)S(1)}, f32[4,26,26,5]{3,1,2,0:T(8,128)}) fusion(f32[4,26,26,128]{3,1,2,0:T(8,128)S(1)} %pad_maximum_fusion.1), kind=kLoop, calls=%fused_computation.159 | loop fusion | bytes 216320 | tf_op jit(solution)/shard_map/slice | solution.py:21
  33.2 1.0 slice.299
  34.3 2.7 %copy.107 = f32[4,26,26,5]{2,0,3,1:T(4,128)S(1)} copy(f32[4,26,26,5]{3,1,2,0:T(8,128)} %get-tuple-element.25) | data formatting | bytes 108160 | tf_op jit(solution)/shard_map/slice | solution.py:22
  37.0 1.6 collective-permute-start.5
  38.5 2.1 %copy.106 = f32[4,26,26,5]{2,0,3,1:T(4,128)} copy(f32[4,26,26,5]{3,1,2,0:T(8,128)S(1)} %get-tuple-element.24) | data formatting | bytes 108160 | tf_op jit(solution)/shard_map/slice | solution.py:21
  41.2 2.1 %fusion.65 = f32[4,16,128,16]{2,3,1,0:T(8,128)S(1)} fusion(f32[16,26,1,1]{1,0,3,2:T(8,128)S(1)} %copy-done.41, f32[4,16,26,128]{3,1,2,0:T(8,128)} %slice.299), kind=kOutput, calls=%fused_computation.57 | convolution fusion | flops 40894464 | bytes 1377920 | tf_op jit(solution)/shard_map/al,fxlz->fxaz/dot_general | solution.py:95
  43.5 2.4 %collective-permute-done.5 = f32[4,26,26,5]{2,0,3,1:T(4,128)} collective-permute-done((f32[4,26,26,5]{2,0,3,1:T(4,128)S(1)}, f32[4,26,26,5]{2,0,3,1:T(4,128)}, u32[]{:S(2)}, u32[]{:S(2)}) %collective-permute-start.5) | collective-permute-done | bytes 54112 | tf_op jit(solution)/shard_map/ppermute | solution.py:24
  45.9 2.5 %copy.109 = f32[4,26,26,5]{3,1,2,0:T(8,128)S(1)} copy(f32[4,26,26,5]{2,0,3,1:T(4,128)} %collective-permute-done.5) | data formatting | bytes 108160 | tf_op jit(solution)/shard_map/ppermute | solution.py:24
  48.4 1.1 collective-permute-done.4
  49.4 3.6 %copy.108 = f32[4,26,26,5]{3,1,2,0:T(8,128)} copy(f32[4,26,26,5]{2,0,3,1:T(4,128)} %collective-permute-done.4) | data formatting | bytes 108160 | tf_op jit(solution)/shard_map/ppermute | solution.py:23
  53.1 2.7 %fusion.67 = f32[4,16,16,128]{3,1,2,0:T(8,128)S(1)} fusion(f32[128,138,1,1]{0,1,3,2:T(8,128)} %constant.27, f32[3,16,16,128]{3,1,2,0:T(8,128)S(1)} %get-tuple-element.18, f32[1,16,16,128]{3,1,2,0:T(8,128)} %copy-done.18, f32[4,26,26,5]{3,1,2,0:T(8,128)S(1)} %copy.109, f32[4,26,26,5]{3,1,2,0:T(8,128)} %copy.108, f32[4,26,5,128]{3,1,2,0:T(8,128)} %copy-done.22, ...), kind=kOutput, calls=%fused_computation.59 | convolution fusion | flops 218044416 | bytes 2087552 | tf_op jit(solution)/shard_map/al,fxyl->fxya/dot_general | solution.py:95
  60.2 1.3 copy.135
  61.5 1.5 collective-permute-start.11
  64.2 0.9 fusion.96
  65.6 0.8 fusion.95
  66.4 1.7 %collective-permute-start.9 = (f32[5,16,5,128]{3,1,2,0:T(8,128)}, f32[5,16,5,128]{3,1,2,0:T(8,128)S(1)}, u32[]{:S(2)}, u32[]{:S(2)}) collective-permute-start(f32[5,16,5,128]{3,1,2,0:T(8,128)} %get-tuple-element.44), channel_id=1, source_target_pairs={{2,0},{4,2},{6,4},{0,6},{3,1},{5,3},{7,5},{1,7},{10,8},{12,10},{14... | collective-permute-start | bytes 614408 | tf_op jit(solution)/shard_map/ppermute | solution.py:24
  68.9 1.7 %collective-permute-start.8 = (f32[5,16,5,128]{3,1,2,0:T(8,128)}, f32[5,16,5,128]{3,1,2,0:T(8,128)}, u32[]{:S(2)}, u32[]{:S(2)}) collective-permute-start(f32[5,16,5,128]{3,1,2,0:T(8,128)} %get-tuple-element.43), channel_id=1, source_target_pairs={{0,2},{2,4},{4,6},{6,0},{1,3},{3,5},{5,7},{7,1},{8,10},{10,12},{12... | collective-permute-start | bytes 614408 | tf_op jit(solution)/shard_map/ppermute | solution.py:23
  71.2 1.5 copy.136
  72.6 1.4 fusion.28
  74.1 4.8 %collective-permute-done.8 = f32[5,16,5,128]{3,1,2,0:T(8,128)} collective-permute-done((f32[5,16,5,128]{3,1,2,0:T(8,128)}, f32[5,16,5,128]{3,1,2,0:T(8,128)}, u32[]{:S(2)}, u32[]{:S(2)}) %collective-permute-start.8) | collective-permute-done | bytes 204832 | tf_op jit(solution)/shard_map/ppermute | solution.py:23
  78.9 1.0 pad_maximum_fusion.2
  79.9 1.2 fusion.34
  81.1 2.6 %fusion.48 = f32[5,16,16,128]{3,1,2,0:T(8,128)S(1)} fusion(f32[5,16,16,128]{3,1,2,0:T(8,128)S(1)} %fusion.28, f32[16,26,1,1]{1,0,3,2:T(8,128)S(1)} %copy-done.42, f32[5,5,16,128]{3,1,2,0:T(8,128)} %collective-permute-done.7, f32[5,16,16,128]{3,1,2,0:T(8,128)S(1)} %get-tuple-element.23, f32[5,5,16,128]{3,1,2,0:T(8,128)} %collective-permute-done.6, ...), kind=kOutput, calls=%fused_computation.40 | convolution fusion | flops 52305920 | bytes 3819136 | tf_op jit(solution)/shard_map/al,flyz->fayz/dot_general | solution.py:95
  84.4 6.8 %collective-permute-done.13 = f32[5,5,16,128]{3,1,2,0:T(8,128)S(1)} collective-permute-done((f32[5,5,16,128]{3,1,2,0:T(8,128)S(1)}, f32[5,5,16,128]{3,1,2,0:T(8,128)S(1)}, u32[]{:S(2)}, u32[]{:S(2)}) %collective-permute-start.13) | collective-permute-done | bytes 204832 | tf_op jit(solution)/shard_map/ppermute | solution.py:24
  91.2 3.2 %collective-permute-done.12 = f32[5,5,16,128]{3,1,2,0:T(8,128)S(1)} collective-permute-done((f32[5,5,16,128]{3,1,2,0:T(8,128)S(1)}, f32[5,5,16,128]{3,1,2,0:T(8,128)S(1)}, u32[]{:S(2)}, u32[]{:S(2)}) %collective-permute-start.12) | collective-permute-done | bytes 204832 | tf_op jit(solution)/shard_map/ppermute | solution.py:23
  94.5 3.0 %collective-permute-start.15 = (f32[5,26,5,128]{3,1,2,0:T(8,128)S(1)}, f32[5,26,5,128]{3,1,2,0:T(8,128)S(1)}, u32[]{:S(2)}, u32[]{:S(2)}) collective-permute-start(f32[5,26,5,128]{3,1,2,0:T(8,128)S(1)} %get-tuple-element.27), channel_id=1, source_target_pairs={{2,0},{4,2},{6,4},{0,6},{3,1},{5,3},{7,5},{1,7},{10,8},{12,10},{14... | collective-permute-start | bytes 998408 | tf_op jit(solution)/shard_map/ppermute | solution.py:24
  97.5 9.9 %collective-permute-done.15 = f32[5,26,5,128]{3,1,2,0:T(8,128)S(1)} collective-permute-done((f32[5,26,5,128]{3,1,2,0:T(8,128)S(1)}, f32[5,26,5,128]{3,1,2,0:T(8,128)S(1)}, u32[]{:S(2)}, u32[]{:S(2)}) %collective-permute-start.15) | collective-permute-done | bytes 332832 | tf_op jit(solution)/shard_map/ppermute | solution.py:24
  107.4 8.6 %collective-permute-done.14 = f32[5,26,5,128]{3,1,2,0:T(8,128)S(1)} collective-permute-done((f32[5,26,5,128]{3,1,2,0:T(8,128)S(1)}, f32[5,26,5,128]{3,1,2,0:T(8,128)S(1)}, u32[]{:S(2)}, u32[]{:S(2)}) %collective-permute-start.14) | collective-permute-done | bytes 332832 | tf_op jit(solution)/shard_map/ppermute | solution.py:23
  117.1 2.1 %fusion.91 = (f32[5,26,26,5]{3,1,2,0:T(8,128)S(1)}, f32[5,26,26,5]{3,1,2,0:T(8,128)}) fusion(f32[5,26,26,128]{3,1,2,0:T(8,128)S(1)} %pad_maximum_fusion), kind=kLoop, calls=%fused_computation.158 | loop fusion | bytes 270400 | tf_op jit(solution)/shard_map/slice | solution.py:21
  119.2 3.7 %copy.142 = f32[5,26,26,5]{2,1,3,0:T(8,128)} copy(f32[5,26,26,5]{3,1,2,0:T(8,128)} %get-tuple-element.20) | data formatting | bytes 135200 | tf_op jit(solution)/shard_map/slice | solution.py:22
  123.0 1.5 collective-permute-start.17
  124.5 2.3 %copy.141 = f32[5,26,26,5]{2,1,3,0:T(8,128)} copy(f32[5,26,26,5]{3,1,2,0:T(8,128)S(1)} %get-tuple-element.19) | data formatting | bytes 135200 | tf_op jit(solution)/shard_map/slice | solution.py:21
  127.3 8.4 %collective-permute-done.17 = f32[5,26,26,5]{2,1,3,0:T(8,128)} collective-permute-done((f32[5,26,26,5]{2,1,3,0:T(8,128)}, f32[5,26,26,5]{2,1,3,0:T(8,128)}, u32[]{:S(2)}, u32[]{:S(2)}) %collective-permute-start.17) | collective-permute-done | bytes 67632 | tf_op jit(solution)/shard_map/ppermute | solution.py:24
  135.7 3.0 %copy.144 = f32[5,26,26,5]{3,1,2,0:T(8,128)S(1)} copy(f32[5,26,26,5]{2,1,3,0:T(8,128)} %collective-permute-done.17) | data formatting | bytes 135200 | tf_op jit(solution)/shard_map/ppermute | solution.py:24
  138.7 3.3 %collective-permute-done.16 = f32[5,26,26,5]{2,1,3,0:T(8,128)} collective-permute-done((f32[5,26,26,5]{2,1,3,0:T(8,128)}, f32[5,26,26,5]{2,1,3,0:T(8,128)}, u32[]{:S(2)}, u32[]{:S(2)}) %collective-permute-start.16) | collective-permute-done | bytes 67632 | tf_op jit(solution)/shard_map/ppermute | solution.py:23
  142.0 4.0 %copy.143 = f32[5,26,26,5]{3,1,2,0:T(8,128)} copy(f32[5,26,26,5]{2,1,3,0:T(8,128)} %collective-permute-done.16) | data formatting | bytes 135200 | tf_op jit(solution)/shard_map/ppermute | solution.py:23
  146.1 6.1 %fusion.16 = f32[5,16,26,138]{3,1,2,0:T(8,128)S(1)} fusion(f32[16,26,1,1]{1,0,3,2:T(8,128)S(1)} %copy-done.44, f32[5,26,26,5]{3,1,2,0:T(8,128)S(1)} %copy.144, f32[5,26,5,128]{3,1,2,0:T(8,128)} %copy-done.38, f32[5,5,16,128]{3,1,2,0:T(8,128)S(1)} %collective-permute-done.13, f32[5,16,16,128]{3,1,2,0:T(8,128)S(1)} %fusion.48, ...), kind=kOutput, calls=%fused_computation.20 | convolution fusion | flops 92355120 | bytes 3015584 | tf_op jit(solution)/shard_map/al,flyz->fayz/dot_general | solution.py:95
  152.2 3.3 %fusion.19 = f32[5,16,16,138]{3,2,1,0:T(8,128)S(1)} fusion(f32[16,26,1,1]{1,0,3,2:T(8,128)S(1)} %copy-done.44, f32[5,16,26,138]{3,1,2,0:T(8,128)S(1)} %fusion.16), kind=kOutput, calls=%fused_computation.21 | convolution fusion | flops 55111680 | bytes 1856384 | tf_op jit(solution)/shard_map/al,fxlz->fxaz/dot_general | solution.py:95
  155.6 2.0 %fusion.98 = f32[5,16,16,128]{3,2,1,0:T(8,128)} fusion(f32[5,16,16,138]{3,2,1,0:T(8,128)S(1)} %fusion.19, f32[128,138,1,1]{0,1,3,2:T(8,128)S(1)} %copy-done.43), kind=kOutput, calls=%fused_computation.165 | convolution fusion | flops 271319040 | bytes 1432576 | tf_op jit(solution)/shard_map/al,fxyl->fxya/dot_general | solution.py:95
  (137 shorter events, 16.7 us)
Async XLA Ops:
  1.3 3.3 %copy-start.24 = (f32[3,3,16,16,128]{4,3,2,1,0:T(8,128)S(1)}, f32[3,3,16,16,128]{4,3,2,1,0:T(8,128)}, u32[]{:S(2)}) copy-start(f32[3,3,16,16,128]{4,3,2,1,0:T(8,128)} %param.10) | copy-start | bytes 3538948
  1.4 3.2 %copy-start.25 = (f32[16,16,128]{2,0,1:T(8,128)}, f32[16,16,128]{2,0,1:T(8,128)S(1)}, u32[]{:S(2)}) copy-start(f32[16,16,128]{2,0,1:T(8,128)S(1)} %get-tuple-element.17) | copy-start | bytes 393220
  2.1 28.3 %copy-start.18 = (f32[1,16,16,128]{3,1,2,0:T(8,128)}, f32[1,16,16,128]{3,1,2,0:T(8,128)S(1)}, u32[]{:S(2)}) copy-start(f32[1,16,16,128]{3,1,2,0:T(8,128)S(1)} %get-tuple-element.52) | copy-start | bytes 393220
  2.1 9.1 %collective-permute-start.1 = (f32[4,5,16,128]{3,1,2,0:T(8,128)S(1)}, f32[4,5,16,128]{3,1,2,0:T(8,128)S(1)}, u32[]{:S(2)}, u32[]{:S(2)}) collective-permute-start(f32[4,5,16,128]{3,1,2,0:T(8,128)S(1)} %get-tuple-element.55), channel_id=1, source_target_pairs={{8,0},{16,8},{24,16},{0,24},{9,1},{17,9},{25,17},{1,25},{10,2},{18... | collective-permute-start | bytes 491528 | tf_op jit(solution)/shard_map/ppermute | solution.py:24
  4.6 7.7 %collective-permute-start = (f32[4,5,16,128]{3,1,2,0:T(8,128)S(1)}, f32[4,5,16,128]{3,1,2,0:T(8,128)S(1)}, u32[]{:S(2)}, u32[]{:S(2)}) collective-permute-start(f32[4,5,16,128]{3,1,2,0:T(8,128)S(1)} %get-tuple-element.54), channel_id=1, source_target_pairs={{0,8},{8,16},{16,24},{24,0},{1,9},{9,17},{17,25},{25,1},{2,10},{10... | collective-permute-start | bytes 491528 | tf_op jit(solution)/shard_map/ppermute | solution.py:23
  4.7 7.7 %copy-start.2 = (f32[1,1,16,16,128]{4,3,2,1,0:T(8,128)}, f32[1,1,16,16,128]{4,3,2,1,0:T(8,128)S(1)}, u32[]{:S(2)}) copy-start(f32[1,1,16,16,128]{4,3,2,1,0:T(8,128)S(1)} %get-tuple-element.31) | copy-start | bytes 393220
  4.7 7.7 %copy-start.4 = (f32[1,1,16,16,128]{4,3,2,1,0:T(8,128)}, f32[1,1,16,16,128]{4,3,2,1,0:T(8,128)S(1)}, u32[]{:S(2)}) copy-start(f32[1,1,16,16,128]{4,3,2,1,0:T(8,128)S(1)} %get-tuple-element.32) | copy-start | bytes 393220
  4.7 7.7 %copy-start.6 = (f32[1,1,16,16,128]{4,3,2,1,0:T(8,128)}, f32[1,1,16,16,128]{4,3,2,1,0:T(8,128)S(1)}, u32[]{:S(2)}) copy-start(f32[1,1,16,16,128]{4,3,2,1,0:T(8,128)S(1)} %get-tuple-element.28) | copy-start | bytes 393220
  4.7 7.7 %copy-start.10 = (f32[1,1,16,16,128]{4,3,2,1,0:T(8,128)}, f32[1,1,16,16,128]{4,3,2,1,0:T(8,128)S(1)}, u32[]{:S(2)}) copy-start(f32[1,1,16,16,128]{4,3,2,1,0:T(8,128)S(1)} %get-tuple-element.36) | copy-start | bytes 393220
  4.7 7.7 %copy-start.14 = (f32[1,1,16,16,128]{4,3,2,1,0:T(8,128)}, f32[1,1,16,16,128]{4,3,2,1,0:T(8,128)S(1)}, u32[]{:S(2)}) copy-start(f32[1,1,16,16,128]{4,3,2,1,0:T(8,128)S(1)} %get-tuple-element.33) | copy-start | bytes 393220
  4.7 7.7 %copy-start.16 = (f32[1,1,16,16,128]{4,3,2,1,0:T(8,128)}, f32[1,1,16,16,128]{4,3,2,1,0:T(8,128)S(1)}, u32[]{:S(2)}) copy-start(f32[1,1,16,16,128]{4,3,2,1,0:T(8,128)S(1)} %get-tuple-element.34) | copy-start | bytes 393220
  4.7 11.4 %copy-start.12 = (f32[1,1,16,16,128]{4,3,2,1,0:T(8,128)}, f32[1,1,16,16,128]{4,3,2,1,0:T(8,128)S(1)}, u32[]{:S(2)}) copy-start(f32[1,1,16,16,128]{4,3,2,1,0:T(8,128)S(1)} %get-tuple-element.35) | copy-start | bytes 393220
  6.1 10.0 %copy-start = (f32[16,16,128]{2,1,0:T(8,128)S(1)}, f32[16,16,128]{2,1,0:T(8,128)}, u32[]{:S(2)}) copy-start(f32[16,16,128]{2,1,0:T(8,128)} %param.11) | copy-start | bytes 393220
  6.9 10.6 %copy-start.41 = (f32[16,26,1,1]{1,0,3,2:T(8,128)S(1)}, f32[16,26,1,1]{1,0,3,2:T(8,128)}, u32[]{:S(2)}) copy-start(f32[16,26,1,1]{1,0,3,2:T(8,128)} %constant.26) | copy-start | bytes 4996
  11.2 19.2 %copy-start.20 = (f32[4,5,16,128]{3,1,2,0:T(8,128)}, f32[4,5,16,128]{3,1,2,0:T(8,128)S(1)}, u32[]{:S(2)}) copy-start(f32[4,5,16,128]{3,1,2,0:T(8,128)S(1)} %collective-permute-done.1) | copy-start | bytes 491524
  12.3 18.1 %copy-start.21 = (f32[4,5,16,128]{3,1,2,0:T(8,128)}, f32[4,5,16,128]{3,1,2,0:T(8,128)S(1)}, u32[]{:S(2)}) copy-start(f32[4,5,16,128]{3,1,2,0:T(8,128)S(1)} %collective-permute-done) | copy-start | bytes 491524
  12.4 11.8 %collective-permute-start.3 = (f32[4,26,5,128]{3,1,2,0:T(8,128)S(1)}, f32[4,26,5,128]{3,1,2,0:T(8,128)S(1)}, u32[]{:S(2)}, u32[]{:S(2)}) collective-permute-start(f32[4,26,5,128]{3,1,2,0:T(8,128)S(1)} %get-tuple-element.40), channel_id=1, source_target_pairs={{2,0},{4,2},{6,4},{0,6},{3,1},{5,3},{7,5},{1,7},{10,8},{12,10},{14... | collective-permute-start | bytes 798728 | tf_op jit(solution)/shard_map/ppermute | solution.py:24
  16.1 14.3 %collective-permute-start.2 = (f32[4,26,5,128]{3,1,2,0:T(8,128)S(1)}, f32[4,26,5,128]{3,1,2,0:T(8,128)S(1)}, u32[]{:S(2)}, u32[]{:S(2)}) collective-permute-start(f32[4,26,5,128]{3,1,2,0:T(8,128)S(1)} %get-tuple-element.39), channel_id=1, source_target_pairs={{0,2},{2,4},{4,6},{6,0},{1,3},{3,5},{5,7},{7,1},{8,10},{10,12},{12... | collective-permute-start | bytes 798728 | tf_op jit(solution)/shard_map/ppermute | solution.py:23
  24.3 6.2 %copy-start.22 = (f32[4,26,5,128]{3,1,2,0:T(8,128)}, f32[4,26,5,128]{3,1,2,0:T(8,128)S(1)}, u32[]{:S(2)}) copy-start(f32[4,26,5,128]{3,1,2,0:T(8,128)S(1)} %collective-permute-done.3) | copy-start | bytes 798724
  37.0 8.9 %collective-permute-start.5 = (f32[4,26,26,5]{2,0,3,1:T(4,128)S(1)}, f32[4,26,26,5]{2,0,3,1:T(4,128)}, u32[]{:S(2)}, u32[]{:S(2)}) collective-permute-start(f32[4,26,26,5]{2,0,3,1:T(4,128)S(1)} %copy.107), channel_id=1, source_target_pairs={{1,0},{0,1},{3,2},{2,3},{5,4},{4,5},{7,6},{6,7},{9,8},{8,9},{11,10... | collective-permute-start | bytes 162248 | tf_op jit(solution)/shard_map/ppermute | solution.py:24
  40.7 8.8 %collective-permute-start.4 = (f32[4,26,26,5]{2,0,3,1:T(4,128)}, f32[4,26,26,5]{2,0,3,1:T(4,128)}, u32[]{:S(2)}, u32[]{:S(2)}) collective-permute-start(f32[4,26,26,5]{2,0,3,1:T(4,128)} %copy.106), channel_id=1, source_target_pairs={{0,1},{1,0},{2,3},{3,2},{4,5},{5,4},{6,7},{7,6},{8,9},{9,8},{10,11... | collective-permute-start | bytes 162248 | tf_op jit(solution)/shard_map/ppermute | solution.py:23
  53.0 2.8 %copy-start.7 = (f32[1,1,16,16,128]{4,3,2,1,0:T(8,128)S(1)}, f32[1,1,16,16,128]{4,3,2,1,0:T(8,128)}, u32[]{:S(2)}) copy-start(f32[1,1,16,16,128]{4,3,2,1,0:T(8,128)} %copy-done.6) | copy-start | bytes 393220
  53.0 2.8 %copy-start.9 = (f32[1,1,16,16,128]{4,3,2,1,0:T(8,128)S(1)}, f32[1,1,16,16,128]{4,3,2,1,0:T(8,128)}, u32[]{:S(2)}) copy-start(f32[1,1,16,16,128]{4,3,2,1,0:T(8,128)} %copy-done.8) | copy-start | bytes 393220
  53.0 2.8 %copy-start.11 = (f32[1,1,16,16,128]{4,3,2,1,0:T(8,128)S(1)}, f32[1,1,16,16,128]{4,3,2,1,0:T(8,128)}, u32[]{:S(2)}) copy-start(f32[1,1,16,16,128]{4,3,2,1,0:T(8,128)} %copy-done.10) | copy-start | bytes 393220
  53.0 2.8 %copy-start.13 = (f32[1,1,16,16,128]{4,3,2,1,0:T(8,128)S(1)}, f32[1,1,16,16,128]{4,3,2,1,0:T(8,128)}, u32[]{:S(2)}) copy-start(f32[1,1,16,16,128]{4,3,2,1,0:T(8,128)} %copy-done.12) | copy-start | bytes 393220
  53.1 2.8 %copy-start.15 = (f32[1,1,16,16,128]{4,3,2,1,0:T(8,128)S(1)}, f32[1,1,16,16,128]{4,3,2,1,0:T(8,128)}, u32[]{:S(2)}) copy-start(f32[1,1,16,16,128]{4,3,2,1,0:T(8,128)} %copy-done.14) | copy-start | bytes 393220
  53.1 2.8 %copy-start.17 = (f32[1,1,16,16,128]{4,3,2,1,0:T(8,128)S(1)}, f32[1,1,16,16,128]{4,3,2,1,0:T(8,128)}, u32[]{:S(2)}) copy-start(f32[1,1,16,16,128]{4,3,2,1,0:T(8,128)} %copy-done.16) | copy-start | bytes 393220
  53.1 2.8 %copy-start.26 = (f32[16,16,128]{2,0,1:T(8,128)S(1)}, f32[16,16,128]{2,0,1:T(8,128)}, u32[]{:S(2)}) copy-start(f32[16,16,128]{2,0,1:T(8,128)} %copy-done.25) | copy-start | bytes 393220
  53.1 2.8 %copy-start.27 = (f32[5,16,16,128]{3,1,2,0:T(8,128)S(1)}, f32[5,16,16,128]{3,1,2,0:T(8,128)}, u32[]{:S(2)}) copy-start(f32[5,16,16,128]{3,1,2,0:T(8,128)} %get-tuple-element.53) | copy-start | bytes 1966084
  61.5 7.4 %collective-permute-start.11 = (f32[5,16,16,5]{2,1,3,0:T(8,128)}, f32[5,16,16,5]{2,1,3,0:T(8,128)S(1)}, u32[]{:S(2)}, u32[]{:S(2)}) collective-permute-start(f32[5,16,16,5]{2,1,3,0:T(8,128)} %copy.135), channel_id=1, source_target_pairs={{1,0},{0,1},{3,2},{2,3},{5,4},{4,5},{7,6},{6,7},{9,8},{8,9},{11,10... | collective-permute-start | bytes 76808 | tf_op jit(solution)/shard_map/ppermute | solution.py:24
  63.6 7.5 %collective-permute-start.10 = (f32[5,16,16,5]{2,1,3,0:T(8,128)S(1)}, f32[5,16,16,5]{2,1,3,0:T(8,128)}, u32[]{:S(2)}, u32[]{:S(2)}) collective-permute-start(f32[5,16,16,5]{2,1,3,0:T(8,128)S(1)} %copy.134), channel_id=1, source_target_pairs={{0,1},{1,0},{2,3},{3,2},{4,5},{5,4},{6,7},{7,6},{8,9},{9,8},{10,11... | collective-permute-start | bytes 76808 | tf_op jit(solution)/shard_map/ppermute | solution.py:23
  64.2 8.5 %copy-start.40 = (f32[128,138,1,1]{0,1,3,2:T(8,128)S(1)}, f32[128,138,1,1]{0,1,3,2:T(8,128)}, u32[]{:S(2)}) copy-start(f32[128,138,1,1]{0,1,3,2:T(8,128)} %constant.27) | copy-start | bytes 211972
  65.1 16.0 %collective-permute-start.7 = (f32[5,5,16,128]{3,1,2,0:T(8,128)}, f32[5,5,16,128]{3,1,2,0:T(8,128)}, u32[]{:S(2)}, u32[]{:S(2)}) collective-permute-start(f32[5,5,16,128]{3,1,2,0:T(8,128)} %get-tuple-element.46), channel_id=1, source_target_pairs={{8,0},{16,8},{24,16},{0,24},{9,1},{17,9},{25,17},{1,25},{10,2},{18... | collective-permute-start | bytes 614408 | tf_op jit(solution)/shard_map/ppermute | solution.py:24
  65.6 15.6 %collective-permute-start.6 = (f32[5,5,16,128]{3,1,2,0:T(8,128)}, f32[5,5,16,128]{3,1,2,0:T(8,128)}, u32[]{:S(2)}, u32[]{:S(2)}) collective-permute-start(f32[5,5,16,128]{3,1,2,0:T(8,128)} %get-tuple-element.45), channel_id=1, source_target_pairs={{0,8},{8,16},{16,24},{24,0},{1,9},{9,17},{17,25},{25,1},{2,10},{10... | collective-permute-start | bytes 614408 | tf_op jit(solution)/shard_map/ppermute | solution.py:23
  66.4 7.7 %collective-permute-start.9 = (f32[5,16,5,128]{3,1,2,0:T(8,128)}, f32[5,16,5,128]{3,1,2,0:T(8,128)S(1)}, u32[]{:S(2)}, u32[]{:S(2)}) collective-permute-start(f32[5,16,5,128]{3,1,2,0:T(8,128)} %get-tuple-element.44), channel_id=1, source_target_pairs={{2,0},{4,2},{6,4},{0,6},{3,1},{5,3},{7,5},{1,7},{10,8},{12,10},{14... | collective-permute-start | bytes 614408 | tf_op jit(solution)/shard_map/ppermute | solution.py:24
  68.9 10.0 %collective-permute-start.8 = (f32[5,16,5,128]{3,1,2,0:T(8,128)}, f32[5,16,5,128]{3,1,2,0:T(8,128)}, u32[]{:S(2)}, u32[]{:S(2)}) collective-permute-start(f32[5,16,5,128]{3,1,2,0:T(8,128)} %get-tuple-element.43), channel_id=1, source_target_pairs={{0,2},{2,4},{4,6},{6,0},{1,3},{3,5},{5,7},{7,1},{8,10},{10,12},{12... | collective-permute-start | bytes 614408 | tf_op jit(solution)/shard_map/ppermute | solution.py:23
  74.0 5.9 %copy-start.42 = (f32[16,26,1,1]{1,0,3,2:T(8,128)S(1)}, f32[16,26,1,1]{1,0,3,2:T(8,128)}, u32[]{:S(2)}) copy-start(f32[16,26,1,1]{1,0,3,2:T(8,128)} %constant.26) | copy-start | bytes 4996
  74.0 7.1 %copy-start.19 = (f32[5,16,16,128]{3,2,1,0:T(8,128)S(1)}, f32[5,16,16,128]{3,2,1,0:T(8,128)}, u32[]{:S(2)}) copy-start(f32[5,16,16,128]{3,2,1,0:T(8,128)} %param.9) | copy-start | bytes 1966084
  74.1 7.1 %copy-start.28 = (f32[16,16,128]{2,0,1:T(8,128)S(1)}, f32[16,16,128]{2,0,1:T(8,128)}, u32[]{:S(2)}) copy-start(f32[16,16,128]{2,0,1:T(8,128)} %copy.96) | copy-start | bytes 393220
  83.8 7.4 %collective-permute-start.13 = (f32[5,5,16,128]{3,1,2,0:T(8,128)S(1)}, f32[5,5,16,128]{3,1,2,0:T(8,128)S(1)}, u32[]{:S(2)}, u32[]{:S(2)}) collective-permute-start(f32[5,5,16,128]{3,1,2,0:T(8,128)S(1)} %get-tuple-element.42), channel_id=1, source_target_pairs={{8,0},{16,8},{24,16},{0,24},{9,1},{17,9},{25,17},{1,25},{10,2},{18... | collective-permute-start | bytes 614408 | tf_op jit(solution)/shard_map/ppermute | solution.py:24
  84.4 10.0 %collective-permute-start.12 = (f32[5,5,16,128]{3,1,2,0:T(8,128)S(1)}, f32[5,5,16,128]{3,1,2,0:T(8,128)S(1)}, u32[]{:S(2)}, u32[]{:S(2)}) collective-permute-start(f32[5,5,16,128]{3,1,2,0:T(8,128)S(1)} %get-tuple-element.41), channel_id=1, source_target_pairs={{0,8},{8,16},{16,24},{24,0},{1,9},{9,17},{17,25},{25,1},{2,10},{10... | collective-permute-start | bytes 614408 | tf_op jit(solution)/shard_map/ppermute | solution.py:23
  94.5 12.9 %collective-permute-start.15 = (f32[5,26,5,128]{3,1,2,0:T(8,128)S(1)}, f32[5,26,5,128]{3,1,2,0:T(8,128)S(1)}, u32[]{:S(2)}, u32[]{:S(2)}) collective-permute-start(f32[5,26,5,128]{3,1,2,0:T(8,128)S(1)} %get-tuple-element.27), channel_id=1, source_target_pairs={{2,0},{4,2},{6,4},{0,6},{3,1},{5,3},{7,5},{1,7},{10,8},{12,10},{14... | collective-permute-start | bytes 998408 | tf_op jit(solution)/shard_map/ppermute | solution.py:24
  97.5 18.5 %collective-permute-start.14 = (f32[5,26,5,128]{3,1,2,0:T(8,128)S(1)}, f32[5,26,5,128]{3,1,2,0:T(8,128)S(1)}, u32[]{:S(2)}, u32[]{:S(2)}) collective-permute-start(f32[5,26,5,128]{3,1,2,0:T(8,128)S(1)} %get-tuple-element.26), channel_id=1, source_target_pairs={{0,2},{2,4},{4,6},{6,0},{1,3},{3,5},{5,7},{7,1},{8,10},{10,12},{12... | collective-permute-start | bytes 998408 | tf_op jit(solution)/shard_map/ppermute | solution.py:23
  107.4 8.6 %copy-start.38 = (f32[5,26,5,128]{3,1,2,0:T(8,128)}, f32[5,26,5,128]{3,1,2,0:T(8,128)S(1)}, u32[]{:S(2)}) copy-start(f32[5,26,5,128]{3,1,2,0:T(8,128)S(1)} %collective-permute-done.15) | copy-start | bytes 998404
  123.0 12.7 %collective-permute-start.17 = (f32[5,26,26,5]{2,1,3,0:T(8,128)}, f32[5,26,26,5]{2,1,3,0:T(8,128)}, u32[]{:S(2)}, u32[]{:S(2)}) collective-permute-start(f32[5,26,26,5]{2,1,3,0:T(8,128)} %copy.142), channel_id=1, source_target_pairs={{1,0},{0,1},{3,2},{2,3},{5,4},{4,5},{7,6},{6,7},{9,8},{8,9},{11,10... | collective-permute-start | bytes 202808 | tf_op jit(solution)/shard_map/ppermute | solution.py:24
  126.7 15.3 %collective-permute-start.16 = (f32[5,26,26,5]{2,1,3,0:T(8,128)}, f32[5,26,26,5]{2,1,3,0:T(8,128)}, u32[]{:S(2)}, u32[]{:S(2)}) collective-permute-start(f32[5,26,26,5]{2,1,3,0:T(8,128)} %copy.141), channel_id=1, source_target_pairs={{0,1},{1,0},{2,3},{3,2},{4,5},{5,4},{6,7},{7,6},{8,9},{9,8},{10,11... | collective-permute-start | bytes 202808 | tf_op jit(solution)/shard_map/ppermute | solution.py:23
  138.7 7.4 %copy-start.44 = (f32[16,26,1,1]{1,0,3,2:T(8,128)S(1)}, f32[16,26,1,1]{1,0,3,2:T(8,128)}, u32[]{:S(2)}) copy-start(f32[16,26,1,1]{1,0,3,2:T(8,128)} %constant.28) | copy-start | bytes 4996
  152.2 3.3 %copy-start.43 = (f32[128,138,1,1]{0,1,3,2:T(8,128)S(1)}, f32[128,138,1,1]{0,1,3,2:T(8,128)}, u32[]{:S(2)}) copy-start(f32[128,138,1,1]{0,1,3,2:T(8,128)} %constant.29) | copy-start | bytes 211972
  (15 other events, 20.5 us)
where the time goes:
time: 158 us
  waiting for transfers between devices  64.4 us (41%)
  local copies, waits for them, and re-layouts  43.7 us (28%)
  matrix products  23.1 us (15%)
  starting transfers between devices  19.8 us (13%)
  other arithmetic  5.78 us (4%)
    ppermute x9, waiting for transfers between devices, with_halo(): after = lax.ppermute(initial, axis, down)  36.1 us
    ppermute x9, waiting for transfers between devices, with_halo(): before = lax.ppermute(last, axis, up)  28.3 us
    dot_general x9, matrix products, sweep_lines(): jnp.einsum(line_forms[dim], matrix, padded, precision=lax.Precision.HIGHEST)  23.1 us
    ppermute x9, starting transfers between devices, with_halo(): after = lax.ppermute(initial, axis, down)  16.5 us
    slice x9, local copies, waits for them, and re-layouts, with_halo(): last = lax.slice_in_dim(value, length - width, length, axis=dim)  10.9 us
    ppermute x3, local copies, waits for them, and re-layouts, with_halo(): before = lax.ppermute(last, axis, up)  9.09 us
    slice x3, local copies, waits for them, and re-layouts, with_halo(): initial = lax.slice_in_dim(value, 0, width, axis=dim)  7.72 us
    ppermute x3, local copies, waits for them, and re-layouts, with_halo(): after = lax.ppermute(initial, axis, down)  6.02 us
  transfers between devices with their start and end apart: 18, of which 15 were waited for; matrix products, arithmetic and copies ran while one was open for 17% of the time, Pallas kernels for 0%

commit v1 on v0

v1 whole, which is shorter than its diff:
```python
import functools

import jax
import jax.numpy as jnp
import numpy as np
from jax import lax
from jax.experimental import pallas as pl
from jax.experimental.pallas import tpu as pltpu
from jax.sharding import PartitionSpec as P

WIDTH = 5
LANES = 128
TILE = 8

viscosity = 0.15
conduction = 0.15 * 1.4 / (0.4 * 0.72)
step_duration = 0.08


def derivative_system(length):
    extent = length + 2 * WIDTH
    system = np.eye(extent)
    source = np.zeros((extent, extent))
    for position in range(2, extent - 2):
        system[position, position - 1] = 1.0 / 3.0
        system[position, position + 1] = 1.0 / 3.0
        source[position, position + 1] = 7.0 / 9.0
        source[position, position - 1] = -7.0 / 9.0
        source[position, position + 2] = 1.0 / 36.0
        source[position, position - 2] = -1.0 / 36.0
    source[1, 2] = 0.5
    source[1, 0] = -0.5
    source[extent - 2, extent - 1] = 0.5
    source[extent - 2, extent - 3] = -0.5
    source[0, 1] = 1.0
    source[0, 0] = -1.0
    source[extent - 1, extent - 1] = 1.0
    source[extent - 1, extent - 2] = -1.0
    return system, source


def filter_coefficients():
    strength = 0.4
    return [
        (193.0 + 126.0 * strength) / 256.0,
        (105.0 + 302.0 * strength) / 256.0,
        15.0 * (2.0 * strength - 1.0) / 64.0,
        45.0 * (1.0 - 2.0 * strength) / 512.0,
        5.0 * (2.0 * strength - 1.0) / 256.0,
        (1.0 - 2.0 * strength) / 512.0,
    ]


def filter_system(length):
    strength = 0.4
    coeffs = filter_coefficients()
    extent = length + 2 * WIDTH
    system = np.eye(extent)
    source = np.eye(extent)
    for position in range(5, extent - 5):
        system[position, position - 1] = strength
        system[position, position + 1] = strength
        source[position, position] = coeffs[0]
        for offset in range(1, 6):
            source[position, position + offset] = coeffs[offset] / 2.0
            source[position, position - offset] = coeffs[offset] / 2.0
    return system, source


def own_rows(system, source, length):
    return np.linalg.solve(system, source)[WIDTH : WIDTH + length]


def derivative_parts(length):
    system, source = derivative_system(length)
    halo = np.linalg.solve(system[:WIDTH, :WIDTH], source[:WIDTH])
    row = source[WIDTH] - system[WIDTH, WIDTH - 1] * halo[WIDTH - 1]
    pivots = [1.0]
    for position in range(3, WIDTH + length):
        pivots.append(1.0 - 1.0 / 9.0 / pivots[-1])
    return pivots[WIDTH - 2 :], row[:WIDTH], row[WIDTH : WIDTH + 3]


def split_weights(table):
    table = np.asarray(table, np.float32)
    high = table.astype(jnp.bfloat16)
    low = (table - high.astype(np.float32)).astype(jnp.bfloat16)
    return np.block([[high, low], [high, np.zeros_like(low)]]).astype(jnp.bfloat16)


def pad_rows(table):
    return np.concatenate([table, np.zeros((LANES - table.shape[0], table.shape[1]))], axis=0)


def pad_columns(table):
    return np.concatenate([table, np.zeros((table.shape[0], LANES - table.shape[1]))], axis=1)


def zeta_tables(length):
    system, source = derivative_system(length)
    table = own_rows(system, source, length)
    _, edge, _ = derivative_parts(length)
    inverse = np.linalg.inv(system)
    extent = length + 2 * WIDTH
    sums = np.zeros((length, 4))
    sums[length - WIDTH :, 0] = edge
    sums[length - 1, 1] = 1.0
    sums[:WIDTH, 2] = -edge[::-1]
    sums[0, 3] = 1.0
    own = slice(WIDTH, WIDTH + length)
    back = np.stack(
        [
            inverse[own, WIDTH],
            -1.0 / 36.0 * inverse[own, WIDTH + 1],
            inverse[own, extent - WIDTH - 1],
            1.0 / 36.0 * inverse[own, extent - WIDTH - 2],
        ]
    )
    smooth = own_rows(*filter_system(length), length)
    ends = np.concatenate([smooth[:, :WIDTH], smooth[:, WIDTH + length :]], axis=1)
    return {
        "derive": split_weights(table[:, own].T),
        "sums": split_weights(pad_columns(sums)),
        "back": split_weights(pad_rows(back)),
        "smooth": split_weights(smooth[:, own].T),
        "ends": split_weights(pad_rows(ends.T)),
    }


def twisted_solve(rights, pivots, off):
    count = len(rights)
    half = count // 2
    low = [rights[0]]
    high = [rights[count - 1]]
    for step in range(1, half):
        factor = off / pivots[step - 1]
        low.append(rights[step] - factor * low[-1])
        high.append(rights[count - 1 - step] - factor * high[-1])
    middle = pivots[half - 1]
    det = middle * middle - off * off
    first, second = low[-1], high[-1]
    answer = [None] * count
    answer[half - 1] = (middle / det) * first - (off / det) * second
    answer[half] = (middle / det) * second - (off / det) * first
    for step in range(half - 2, -1, -1):
        scale = 1.0 / pivots[step]
        factor = off / pivots[step]
        answer[step] = scale * low[step] - factor * answer[step + 1]
        answer[count - 1 - step] = scale * high[step] - factor * answer[count - 2 - step]
    return answer


def derive_line(cells, below, above):
    count = len(cells)
    pivots, _, edge = derivative_parts(count)
    near, far = 7.0 / 9.0, 1.0 / 36.0
    rights = [None] * count
    rights[0] = below[0] + edge[0] * cells[0] + edge[1] * cells[1] + edge[2] * cells[2]
    rights[1] = near * (cells[2] - cells[0]) + far * (cells[3] - below[1])
    for step in range(2, count - 2):
        rights[step] = near * (cells[step + 1] - cells[step - 1]) + far * (
            cells[step + 2] - cells[step - 2]
        )
    rights[count - 2] = near * (cells[count - 1] - cells[count - 3]) + far * (
        above[1] - cells[count - 4]
    )
    rights[count - 1] = above[0] - (
        edge[0] * cells[count - 1] + edge[1] * cells[count - 2] + edge[2] * cells[count - 3]
    )
    return twisted_solve(rights, pivots, 1.0 / 3.0)


def end_sums(cells):
    _, edge, _ = derivative_parts(16)
    total = edge[WIDTH - 1] * cells[0]
    for step in range(1, WIDTH):
        total = total + edge[WIDTH - 1 - step] * cells[step]
    return total, cells[0]


def smooth_line(cells):
    count = len(cells) - 2 * WIDTH
    coeffs = filter_coefficients()
    pivots = [1.0]
    for _ in range(count):
        pivots.append(1.0 - 0.16 / pivots[-1])
    rights = []
    for step in range(WIDTH, WIDTH + count):
        total = coeffs[0] * cells[step]
        for offset in range(1, WIDTH + 1):
            total = total + (0.5 * coeffs[offset]) * (cells[step + offset] + cells[step - offset])
        rights.append(total)
    rights[0] = rights[0] - 0.4 * cells[WIDTH - 1]
    rights[-1] = rights[-1] - 0.4 * cells[WIDTH + count]
    return twisted_solve(rights, pivots, 0.4)


def split_values(values):
    high = values.astype(jnp.bfloat16)
    low = (values - high.astype(jnp.float32)).astype(jnp.bfloat16)
    return jnp.concatenate([high, low], axis=1)


def lane_product(values, weights):
    both = jnp.dot(split_values(values), weights, preferred_element_type=jnp.float32)
    return both[:, :LANES] + both[:, LANES:]


class Grid:
    def __init__(self, nx, ny):
        self.nx, self.ny, self.rows = nx, ny, nx * ny
        self.eta_groups = ny // TILE
        self.xi_groups = nx // TILE

    def xi_tile(self, position, group):
        return pl.ds(position * self.ny + group * TILE, TILE)

    def eta_tile(self, position, group):
        return pl.ds(position + group * TILE * self.ny, TILE, stride=self.ny)


def group_rows(group):
    return pl.ds(group * TILE, TILE)


def odd(axis):
    return lax.rem(lax.axis_index(axis), 2) == 1


def send_sums(read, groups, count, flag, first_ref, second_ref, field):
    for group in range(groups):
        top = end_sums([read(count - 1 - step, group) for step in range(WIDTH)])
        low = end_sums([read(step, group) for step in range(WIDTH)])
        low = (-low[0], low[1])
        for part in range(2):
            first_ref[2 * field + part, group_rows(group), :] = jnp.where(flag, low[part], top[part])
            second_ref[2 * field + part, group_rows(group), :] = jnp.where(flag, top[part], low[part])


def take_sums(first_ref, second_ref, flag, field, group):
    below, above = [], []
    for part in range(2):
        first = first_ref[2 * field + part, group_rows(group), :]
        second = second_ref[2 * field + part, group_rows(group), :]
        below.append(jnp.where(flag, first, second))
        above.append(jnp.where(flag, second, first))
    return below, above


def pack_sums(values, weights, grid):
    sums = lane_product(values, weights)
    packed = None
    for group in range(grid.rows // TILE):
        part = sums[group * TILE : (group + 1) * TILE]
        if group:
            part = pltpu.roll(part, 4 * group, axis=1)
        packed = part if packed is None else packed + part
    return packed


def unpack_sums(below, above, grid):
    lane = lax.broadcasted_iota(jnp.int32, below.shape, 1)
    packed = jnp.where(lax.rem(lane, 4) < 2, below, above)
    parts = [packed]
    for group in range(1, grid.rows // TILE):
        parts.append(pltpu.roll(packed, LANES - 4 * group, axis=1))
    return jnp.concatenate(parts, axis=0)


def primitive_kernel(
    grid, u_ref, sums_ref, prim_ref, eta_first, eta_second, xi_first, xi_second, zeta_ref
):
    step = 4 * TILE

    def body(index, carry):
        rows = pl.ds(pl.multiple_of(index * step, step), step)
        inverse = 1.0 / u_ref[0, rows, :]
        work = None
        for c in range(3):
            momentum = u_ref[1 + c, rows, :]
            speed = momentum * inverse
            prim_ref[c, rows, :] = speed
            work = momentum * speed if work is None else work + momentum * speed
        pressure = 0.4 * (u_ref[4, rows, :] - 0.5 * work)
        prim_ref[3, rows, :] = pressure * inverse
        return carry

    lax.fori_loop(0, grid.rows // step, body, 0)
    for field in range(4):
        send_sums(
            lambda position, group: prim_ref[field, grid.eta_tile(position, group), :],
            grid.xi_groups, grid.ny, odd("eta"), eta_first, eta_second, field,
        )
        send_sums(
            lambda position, group: prim_ref[field, grid.xi_tile(position, group), :],
            grid.eta_groups, grid.nx, odd("xi"), xi_first, xi_second, field,
        )
        zeta_ref[field] = pack_sums(prim_ref[field], sums_ref[...], grid)


def flux_kernel(
    grid,
    u_ref, prim_ref, metrics_ref, jacobian_ref,
    eta_a, eta_b, xi_a, xi_b, zeta_below, zeta_above,
    derive_ref, back_ref, sums_ref,
    contra_ref, eta_first, eta_second, xi_first, xi_second, zeta_ref,
    slope_ref,
):
    for field in range(4):
        for group in range(grid.eta_groups):
            below, above = take_sums(xi_a, xi_b, odd("xi"), field, group)
            cells = [prim_ref[field, grid.xi_tile(i, group), :] for i in range(grid.nx)]
            for i, value in enumerate(derive_line(cells, below, above)):
                slope_ref[0, field, grid.xi_tile(i, group), :] = value
        for group in range(grid.xi_groups):
            below, above = take_sums(eta_a, eta_b, odd("eta"), field, group)
            cells = [prim_ref[field, grid.eta_tile(i, group), :] for i in range(grid.ny)]
            for i, value in enumerate(derive_line(cells, below, above)):
                slope_ref[1, field, grid.eta_tile(i, group), :] = value
        halo = unpack_sums(zeta_below[field], zeta_above[field], grid)
        slope_ref[2, field] = lane_product(prim_ref[field], derive_ref[...]) + lane_product(
            halo, back_ref[...]
        )

    step = TILE

    def body(index, carry):
        rows = pl.ds(pl.multiple_of(index * step, step), step)
        u = [u_ref[c, rows, :] for c in range(5)]
        speed = [prim_ref[c, rows, :] for c in range(3)]
        pressure = prim_ref[3, rows, :] * u[0]
        jacobian = jacobian_ref[rows, :]
        metrics = [[metrics_ref[3 * k + j, rows, :] for j in range(3)] for k in range(3)]
        physical = []
        for c in range(4):
            slopes = [slope_ref[k, c, rows, :] for k in range(3)]
            physical.append(
                [
                    jacobian
                    * (
                        metrics[0][j] * slopes[0] + metrics[1][j] * slopes[1] + metrics[2][j] * slopes[2]
                    )
                    for j in range(3)
                ]
            )
        spread = (2.0 / 3.0 * viscosity) * (physical[0][0] + physical[1][1] + physical[2][2])
        stress = [[None] * 3 for _ in range(3)]
        for c in range(3):
            stress[c][c] = (2.0 * viscosity) * physical[c][c] - spread
            for j in range(c):
                stress[c][j] = stress[j][c] = viscosity * (physical[c][j] + physical[j][c])
        total = u[4] + pressure
        fluxes = []
        for j in range(3):
            parts = [u[1 + j]]
            for c in range(3):
                carried = u[1 + c] * speed[j] - stress[c][j]
                if c == j:
                    carried = carried + pressure
                parts.append(carried)
            worked = speed[0] * stress[0][j] + speed[1] * stress[1][j] + speed[2] * stress[2][j]
            parts.append(total * speed[j] - worked - conduction * physical[3][j])
            fluxes.append(parts)
        for k in range(3):
            for f in range(5):
                contra_ref[k, f, rows, :] = (
                    metrics[k][0] * fluxes[0][f]
                    + metrics[k][1] * fluxes[1][f]
                    + metrics[k][2] * fluxes[2][f]
                )
        return carry

    lax.fori_loop(0, grid.rows // step, body, 0)
    for field in range(5):
        send_sums(
            lambda position, group: contra_ref[1, field, grid.eta_tile(position, group), :],
            grid.xi_groups, grid.ny, odd("eta"), eta_first, eta_second, field,
        )
        send_sums(
            lambda position, group: contra_ref[0, field, grid.xi_tile(position, group), :],
            grid.eta_groups, grid.nx, odd("xi"), xi_first, xi_second, field,
        )
        zeta_ref[field] = pack_sums(contra_ref[2, field], sums_ref[...], grid)


def step_kernel(
    grid,
    u_ref, jacobian_ref, contra_ref,
    eta_a, eta_b, xi_a, xi_b, zeta_below, zeta_above,
    derive_ref, back_ref,
    state_ref, eta_first, eta_second,
):
    flag = odd("eta")
    for field in range(5):
        halo = unpack_sums(zeta_below[field], zeta_above[field], grid)
        state_ref[field] = lane_product(contra_ref[2, field], derive_ref[...]) + lane_product(
            halo, back_ref[...]
        )
        for group in range(grid.xi_groups):
            below, above = take_sums(eta_a, eta_b, flag, field, group)
            cells = [contra_ref[1, field, grid.eta_tile(i, group), :] for i in range(grid.ny)]
            for i, value in enumerate(derive_line(cells, below, above)):
                rows = grid.eta_tile(i, group)
                state_ref[field, rows, :] = state_ref[field, rows, :] + value
        for group in range(grid.eta_groups):
            below, above = take_sums(xi_a, xi_b, odd("xi"), field, group)
            cells = [contra_ref[0, field, grid.xi_tile(i, group), :] for i in range(grid.nx)]
            for i, value in enumerate(derive_line(cells, below, above)):
                rows = grid.xi_tile(i, group)
                total = state_ref[field, rows, :] + value
                state_ref[field, rows, :] = u_ref[field, rows, :] - (
                    step_duration * jacobian_ref[rows, :]
                ) * total
        send_cells(
            lambda position, group: state_ref[field, grid.eta_tile(position, group), :],
            grid.xi_groups, grid.ny, flag, eta_first, eta_second, field,
        )


def send_cells(read, groups, count, flag, first_ref, second_ref, field):
    for group in range(groups):
        for step in range(WIDTH):
            low = read(step, group)
            top = read(count - 1 - step, group)
            index = WIDTH * field + step
            first_ref[index, group_rows(group), :] = jnp.where(flag, low, top)
            second_ref[index, group_rows(group), :] = jnp.where(flag, top, low)


def take_cells(first_ref, second_ref, flag, field, group):
    below, above = [], []
    for step in range(WIDTH):
        first = first_ref[WIDTH * field + step, group_rows(group), :]
        second = second_ref[WIDTH * field + step, group_rows(group), :]
        below.insert(0, jnp.where(flag, first, second))
        above.append(jnp.where(flag, second, first))
    return below, above


def eta_filter_kernel(grid, state_ref, eta_a, eta_b, result_ref, xi_first, xi_second):
    flag = odd("eta")
    for field in range(5):
        for group in range(grid.xi_groups):
            below, above = take_cells(eta_a, eta_b, flag, field, group)
            cells = [state_ref[field, grid.eta_tile(i, group), :] for i in range(grid.ny)]
            for i, value in enumerate(smooth_line(below + cells + above)):
                result_ref[field, grid.eta_tile(i, group), :] = value
        send_cells(
            lambda position, group: result_ref[field, grid.xi_tile(position, group), :],
            grid.eta_groups, grid.nx, odd("xi"), xi_first, xi_second, field,
        )


PACKED = 12


def xi_filter_kernel(grid, state_ref, xi_a, xi_b, result_ref, zeta_ref):
    flag = odd("xi")
    tiles = grid.rows // TILE
    for field in range(5):
        for group in range(grid.eta_groups):
            below, above = take_cells(xi_a, xi_b, flag, field, group)
            cells = [state_ref[field, grid.xi_tile(i, group), :] for i in range(grid.nx)]
            for i, value in enumerate(smooth_line(below + cells + above)):
                result_ref[field, grid.xi_tile(i, group), :] = value
        lane = lax.broadcasted_iota(jnp.int32, (TILE, LANES), 1)
        for start in range(0, tiles, PACKED):
            packed = None
            for slot in range(min(PACKED, tiles - start)):
                part = result_ref[field, group_rows(start + slot), :]
                part = pltpu.roll(part, WIDTH + 2 * WIDTH * slot, axis=1)
                packed = part if packed is None else jnp.where(lane >= 2 * WIDTH * slot, part, packed)
            zeta_ref[field, group_rows(start // PACKED), :] = packed


def zeta_filter_kernel(grid, state_ref, below_ref, above_ref, smooth_ref, ends_ref, result_ref):
    tiles = grid.rows // TILE
    lane = lax.broadcasted_iota(jnp.int32, (TILE, LANES), 1)
    for field in range(5):
        parts = []
        for start in range(0, tiles, PACKED):
            rows = group_rows(start // PACKED)
            packed = jnp.where(
                lax.rem(lane, 2 * WIDTH) < WIDTH, below_ref[field, rows, :], above_ref[field, rows, :]
            )
            for slot in range(min(PACKED, tiles - start)):
                parts.append(pltpu.roll(packed, LANES - 2 * WIDTH * slot, axis=1) if slot else packed)
        halo = jnp.concatenate(parts, axis=0)
        result_ref[field] = lane_product(state_ref[field], smooth_ref[...]) + lane_product(
            halo, ends_ref[...]
        )


def pair_swap(value, axis, parity):
    count = lax.axis_size(axis)
    pairs = []
    for index in range(count):
        step = 1 if index % 2 == parity else -1
        pairs.append((index, (index + step) % count))
    return lax.ppermute(value, axis, pairs)


def ring_swap(value, axis):
    count = lax.axis_size(axis)
    if count == 2:
        other = lax.ppermute(value, axis, [(0, 1), (1, 0)])
        return other, other
    up = [(index, (index + 1) % count) for index in range(count)]
    down = [(index, (index - 1) % count) for index in range(count)]
    return lax.ppermute(value, axis, up), lax.ppermute(value, axis, down)


def call(kernel, outs, *operands, scratch=()):
    shapes = [jax.ShapeDtypeStruct(shape, jnp.float32) for shape in outs]
    return pl.pallas_call(
        kernel,
        out_shape=shapes,
        scratch_shapes=[pltpu.VMEM(shape, jnp.float32) for shape in scratch],
        compiler_params=pltpu.CompilerParams(vmem_limit_bytes=20 * 2**20),
    )(*operands)


def local(conserved_solution, metrics, jacobian):
    _, nx, ny, nz = conserved_solution.shape
    grid = Grid(nx, ny)
    rows = grid.rows
    u = conserved_solution.reshape(5, rows, nz)
    metrics = metrics.reshape(9, rows, nz)
    jacobian = jacobian.reshape(rows, nz)
    tables = {name: jnp.asarray(table) for name, table in zeta_tables(nz).items()}
    packs = -(-(rows // TILE) // PACKED)

    def exchange(eta_first, eta_second, xi_first, xi_second, zeta):
        eta_b = pair_swap(eta_second, "eta", 1)
        eta_a = pair_swap(eta_first, "eta", 0)
        xi_b = pair_swap(xi_second, "xi", 1)
        below, above = ring_swap(zeta, "zeta")
        xi_a = pair_swap(xi_first, "xi", 0)
        return eta_a, eta_b, xi_a, xi_b, below, above

    def sums_shapes(fields):
        return [(2 * fields, nx, nz)] * 2 + [(2 * fields, ny, nz)] * 2 + [(fields, TILE, LANES)]

    prim, *sends = call(
        functools.partial(primitive_kernel, grid),
        [(4, rows, nz)] + sums_shapes(4),
        u, tables["sums"],
    )
    got = exchange(*sends)
    contra, *sends = call(
        functools.partial(flux_kernel, grid),
        [(3, 5, rows, nz)] + sums_shapes(5),
        u, prim, metrics, jacobian, *got, tables["derive"], tables["back"], tables["sums"],
        scratch=[(3, 4, rows, nz)],
    )
    got = exchange(*sends)
    state, eta_first, eta_second = call(
        functools.partial(step_kernel, grid),
        [(5, rows, nz)] + [(5 * WIDTH, nx, nz)] * 2,
        u, jacobian, contra, *got, tables["derive"], tables["back"],
    )
    eta_b = pair_swap(eta_second, "eta", 1)
    eta_a = pair_swap(eta_first, "eta", 0)
    state, xi_first, xi_second = call(
        functools.partial(eta_filter_kernel, grid),
        [(5, rows, nz)] + [(5 * WIDTH, ny, nz)] * 2,
        state, eta_a, eta_b,
    )
    xi_b = pair_swap(xi_second, "xi", 1)
    xi_a = pair_swap(xi_first, "xi", 0)
    state, zeta = call(
        functools.partial(xi_filter_kernel, grid),
        [(5, rows, nz), (5, packs * TILE, LANES)],
        state, xi_a, xi_b,
    )
    below, above = ring_swap(zeta, "zeta")
    (result,) = call(
        functools.partial(zeta_filter_kernel, grid),
        [(5, rows, nz)],
        state, below, above, tables["smooth"], tables["ends"],
    )
    return result.reshape(5, nx, ny, nz)


def solution(mesh):
    in_specs = (
        P(None, "xi", "eta", "zeta"),
        P(None, None, "xi", "eta", "zeta"),
        P("xi", "eta", "zeta"),
    )
    out_specs = P(None, "xi", "eta", "zeta")
    return jax.shard_map(local, mesh=mesh, in_specs=in_specs, out_specs=out_specs, check_vma=False)
```

time: 158 us -> 55.4 us (0.35)
  waiting for transfers between devices: 64.4 us -> 23.6 us
  local copies, waits for them, and re-layouts: 43.7 us -> 5.99 us
  matrix products: 23.1 us -> 0 us
  Pallas kernels: 0 us -> 7.8 us
  other arithmetic: 5.78 us -> 0 us
  starting transfers between devices: 19.8 us -> 17.7 us
    ppermute x18 -> x15, waiting for transfers between devices: 64.4 us -> 23.6 us  [the longest x12 16.4 us: pair_swap(): return lax.ppermute(value, axis, pairs)]
    dot_general x9 -> x0, matrix products: 23.1 us -> none  [sweep_lines(): jnp.einsum(line_forms[dim], matrix, padded, precision=lax.Precision.HIGHEST)]
    slice x14 -> x0, local copies, waits for them, and re-layouts: 19.7 us -> none  [the longest x9 10.9 us: with_halo(): last = lax.slice_in_dim(value, length - width, length, axis=dim)]
    ppermute x6 -> x0, local copies, waits for them, and re-layouts: 15.1 us -> none  [the longest x3 9.09 us: with_halo(): before = lax.ppermute(last, axis, up)]
    pallas_call x0 -> x6, Pallas kernels: none -> 7.8 us  [call(): pl.pallas_call(kernel, out_shape=shapes, scratch_shapes=[pltpu.VMEM(shape...]
    squeeze x4 -> x0, local copies, waits for them, and re-layouts: 3.13 us -> none  [the longest x2 1.56 us: fluxes(): metrics[2, column] * slopes[2][member]]
    ppermute x18 -> x15, starting transfers between devices: 19.8 us -> 17.7 us  [the longest x12 13 us: pair_swap(): return lax.ppermute(value, axis, pairs)]
    unnamed x8 -> x0, other arithmetic: 1.82 us -> none
  transfers between devices with their start and end apart: 18 -> 15, of which waited for: 15 -> 8; matrix products, arithmetic and copies ran while one was open for 17% -> 0% of each run, Pallas kernels for 0% -> 0%
where the time goes in v1:
time: 55.4 us; the launch traced here: 55.2 us
  waiting for transfers between devices  23.6 us (43%)
  starting transfers between devices  17.7 us (32%)
  Pallas kernels  7.8 us (14%)
  local copies, waits for them, and re-layouts  5.99 us (11%)
    ppermute x12, waiting for transfers between devices, pair_swap(): return lax.ppermute(value, axis, pairs)  16.4 us
    ppermute x12, starting transfers between devices, pair_swap(): return lax.ppermute(value, axis, pairs)  13 us
    pallas_call x6, Pallas kernels, call(): pl.pallas_call(kernel, out_shape=shapes, scratch_shapes=[pltpu.VMEM(shape...  7.8 us
    ppermute x3, waiting for transfers between devices, ring_swap(): other = lax.ppermute(value, axis, [(0, 1), (1, 0)])  7.25 us
    unnamed x20, local copies, waits for them, and re-layouts  5.99 us
    ppermute x3, starting transfers between devices, ring_swap(): other = lax.ppermute(value, axis, [(0, 1), (1, 0)])  4.63 us
  transfers between devices with their start and end apart: 15, of which 8 were waited for; matrix products, arithmetic and copies ran while one was open for 0% of the time, Pallas kernels for 0%

profile of v1, /device:TPU:0, one launch (start us, length us, event | category | flops | bytes accessed | tf_op | source)
XLA Modules:
  0.0 55.2 jit_solution(5847382829019733429)
XLA Ops:
  0.0 1.1 %copy-done = f32[5,16,16,128]{3,2,1,0:T(8,128)S(1)} copy-done((f32[5,16,16,128]{3,2,1,0:T(8,128)S(1)}, f32[5,16,16,128]{3,2,1,0:T(8,128)}, u32[]{:S(2)}) %copy-start) | copy-done | bytes 655384
  1.1 0.9 %copy-done.7 = bf16[256,256]{1,0:T(8,128)(2,1)S(1)} copy-done((bf16[256,256]{1,0:T(8,128)(2,1)S(1)}, bf16[256,256]{1,0:T(8,128)(2,1)}, u32[]{:S(2)}) %copy-start.7) | copy-done | bytes 131096
  2.0 0.6 %shard_map.82 = (f32[4,256,128]{2,1,0:T(8,128)S(1)}, f32[8,16,128]{2,1,0:T(8,128)S(1)}, f32[8,16,128]{2,1,0:T(8,128)S(1)}, f32[8,16,128]{2,1,0:T(8,128)S(1)}, f3...) custom-call(f32[5,256,128]{2,1,0:T(8,128)S(1)} %bitcast.4, bf16[256,256]{1,0:T(8,128)(2,1)S(1)} %copy-done.7), custom_call_target="tpu_custom_call" | custom-call | tf_op jit(solution)/shard_map/pallas_call | solution.py:515
  2.6 3.1 %collective-permute-start = (f32[8,16,128]{2,1,0:T(8,128)S(1)}, f32[8,16,128]{2,1,0:T(8,128)S(1)}, u32[]{:S(2)}, u32[]{:S(2)}) collective-permute-start(f32[8,16,128]{2,1,0:T(8,128)S(1)} %get-tuple-element.26), channel_id=1, source_target_pairs={{0,2},{2,0},{4,6},{6,4},{1,3},{3,1},{5,7},{7,5},{8,10},{10,8},{12,... | collective-permute-start | bytes 196616 | tf_op jit(solution)/shard_map/ppermute | solution.py:500
  5.7 2.5 %collective-permute-start.1 = (f32[8,16,128]{2,1,0:T(8,128)S(1)}, f32[8,16,128]{2,1,0:T(8,128)S(1)}, u32[]{:S(2)}, u32[]{:S(2)}) collective-permute-start(f32[8,16,128]{2,1,0:T(8,128)S(1)} %get-tuple-element.27), channel_id=1, source_target_pairs={{0,6},{2,4},{4,2},{6,0},{1,7},{3,5},{5,3},{7,1},{8,14},{10,12},{12... | collective-permute-start | bytes 196616 | tf_op jit(solution)/shard_map/ppermute | solution.py:500
  8.2 0.0 collective-permute-start.2
  8.2 1.6 %collective-permute-start.3 = (f32[8,16,128]{2,1,0:T(8,128)S(1)}, f32[8,16,128]{2,1,0:T(8,128)S(1)}, u32[]{:S(2)}, u32[]{:S(2)}) collective-permute-start(f32[8,16,128]{2,1,0:T(8,128)S(1)} %get-tuple-element.29), channel_id=1, source_target_pairs={{0,24},{8,16},{16,8},{24,0},{1,25},{9,17},{17,9},{25,1},{2,26},{10... | collective-permute-start | bytes 196616 | tf_op jit(solution)/shard_map/ppermute | solution.py:500
  9.8 1.5 %collective-permute-start.4 = (f32[4,8,128]{2,1,0:T(8,128)S(1)}, f32[4,8,128]{2,1,0:T(8,128)S(1)}, u32[]{:S(2)}, u32[]{:S(2)}) collective-permute-start(f32[4,8,128]{2,1,0:T(8,128)S(1)} %get-tuple-element.30), channel_id=1, source_target_pairs={{0,1},{1,0},{2,3},{3,2},{4,5},{5,4},{6,7},{7,6},{8,9},{9,8},{10,11... | collective-permute-start | bytes 49160 | tf_op jit(solution)/shard_map/ppermute | solution.py:506
  11.3 2.2 %collective-permute-done.4.zeta_below.zeta_above = f32[4,8,128]{2,1,0:T(8,128)S(1)} collective-permute-done((f32[4,8,128]{2,1,0:T(8,128)S(1)}, f32[4,8,128]{2,1,0:T(8,128)S(1)}, u32[]{:S(2)}, u32[]{:S(2)}) %collective-permute-start.4) | collective-permute-done | bytes 16416 | tf_op jit(solution)/shard_map/ppermute | solution.py:506
  13.5 0.0 collective-permute-done.eta_a
  13.5 0.0 collective-permute-done.1.eta_b
  13.5 0.0 collective-permute-done.2.xi_a
  13.6 0.0 collective-permute-done.3.xi_b
  13.6 0.0 copy-start.1
  13.6 1.3 %copy-done.1 = f32[3,3,16,16,128]{4,3,2,1,0:T(8,128)S(1)} copy-done((f32[3,3,16,16,128]{4,3,2,1,0:T(8,128)S(1)}, f32[3,3,16,16,128]{4,3,2,1,0:T(8,128)}, u32[]{:S(2)}) %copy-start.1) | copy-done | bytes 1179672
  14.8 0.9 %copy-done.2 = f32[16,16,128]{2,1,0:T(8,128)S(1)} copy-done((f32[16,16,128]{2,1,0:T(8,128)S(1)}, f32[16,16,128]{2,1,0:T(8,128)}, u32[]{:S(2)}) %copy-start.2) | copy-done | bytes 131096
  15.7 0.9 %copy-done.3 = bf16[256,256]{1,0:T(8,128)(2,1)S(1)} copy-done((bf16[256,256]{1,0:T(8,128)(2,1)S(1)}, bf16[256,256]{1,0:T(8,128)(2,1)}, u32[]{:S(2)}) %copy-start.3) | copy-done | bytes 131096
  16.7 0.9 %copy-done.5 = bf16[256,256]{1,0:T(8,128)(2,1)S(1)} copy-done((bf16[256,256]{1,0:T(8,128)(2,1)S(1)}, bf16[256,256]{1,0:T(8,128)(2,1)}, u32[]{:S(2)}) %copy-start.5) | copy-done | bytes 131096
  17.6 2.8 %shard_map.83 = (f32[3,5,256,128]{3,2,1,0:T(8,128)S(1)}, f32[10,16,128]{2,1,0:T(8,128)S(1)}, f32[10,16,128]{2,1,0:T(8,128)S(1)}, f32[10,16,128]{2,1,0:T(8,128)S(...) custom-call(f32[5,256,128]{2,1,0:T(8,128)S(1)} %bitcast.5, f32[4,256,128]{2,1,0:T(8,128)S(1)} %get-tuple-element.25.prim_ref, ...), custom_call_target="tpu_custom_call" | custom-call | tf_op jit(solution)/shard_map/pallas_call | solution.py:515
  20.3 0.7 %collective-permute-start.5 = (f32[10,16,128]{2,1,0:T(8,128)S(1)}, f32[10,16,128]{2,1,0:T(8,128)S(1)}, u32[]{:S(2)}, u32[]{:S(2)}) collective-permute-start(f32[10,16,128]{2,1,0:T(8,128)S(1)} %get-tuple-element.32), channel_id=1, source_target_pairs={{0,2},{2,0},{4,6},{6,4},{1,3},{3,1},{5,7},{7,5},{8,10},{10,8},{12,... | collective-permute-start | bytes 245768 | tf_op jit(solution)/shard_map/ppermute | solution.py:500
  21.0 0.9 %collective-permute-start.6 = (f32[10,16,128]{2,1,0:T(8,128)S(1)}, f32[10,16,128]{2,1,0:T(8,128)S(1)}, u32[]{:S(2)}, u32[]{:S(2)}) collective-permute-start(f32[10,16,128]{2,1,0:T(8,128)S(1)} %get-tuple-element.33), channel_id=1, source_target_pairs={{0,6},{2,4},{4,2},{6,0},{1,7},{3,5},{5,3},{7,1},{8,14},{10,12},{12... | collective-permute-start | bytes 245768 | tf_op jit(solution)/shard_map/ppermute | solution.py:500
  21.9 0.0 collective-permute-start.7
  21.9 0.8 %collective-permute-start.8 = (f32[10,16,128]{2,1,0:T(8,128)S(1)}, f32[10,16,128]{2,1,0:T(8,128)S(1)}, u32[]{:S(2)}, u32[]{:S(2)}) collective-permute-start(f32[10,16,128]{2,1,0:T(8,128)S(1)} %get-tuple-element.35), channel_id=1, source_target_pairs={{0,24},{8,16},{16,8},{24,0},{1,25},{9,17},{17,9},{25,1},{2,26},{10... | collective-permute-start | bytes 245768 | tf_op jit(solution)/shard_map/ppermute | solution.py:500
  22.8 1.5 %collective-permute-start.9 = (f32[5,8,128]{2,1,0:T(8,128)S(1)}, f32[5,8,128]{2,1,0:T(8,128)S(1)}, u32[]{:S(2)}, u32[]{:S(2)}) collective-permute-start(f32[5,8,128]{2,1,0:T(8,128)S(1)} %get-tuple-element.36), channel_id=1, source_target_pairs={{0,1},{1,0},{2,3},{3,2},{4,5},{5,4},{6,7},{7,6},{8,9},{9,8},{10,11... | collective-permute-start | bytes 61448 | tf_op jit(solution)/shard_map/ppermute | solution.py:506
  24.3 2.3 %collective-permute-done.9.zeta_below.zeta_above = f32[5,8,128]{2,1,0:T(8,128)S(1)} collective-permute-done((f32[5,8,128]{2,1,0:T(8,128)S(1)}, f32[5,8,128]{2,1,0:T(8,128)S(1)}, u32[]{:S(2)}, u32[]{:S(2)}) %collective-permute-start.9) | collective-permute-done | bytes 20512 | tf_op jit(solution)/shard_map/ppermute | solution.py:506
  26.5 0.0 collective-permute-done.5.eta_a
  26.5 0.7 %collective-permute-done.6.eta_b = f32[10,16,128]{2,1,0:T(8,128)S(1)} collective-permute-done((f32[10,16,128]{2,1,0:T(8,128)S(1)}, f32[10,16,128]{2,1,0:T(8,128)S(1)}, u32[]{:S(2)}, u32[]{:S(2)}) %collective-permute-start.6) | collective-permute-done | bytes 81952 | tf_op jit(solution)/shard_map/ppermute | solution.py:500
  27.3 0.0 collective-permute-done.7.xi_a
  27.3 0.0 collective-permute-done.8.xi_b
  27.3 0.0 copy-done.4
  27.3 0.0 copy-done.6
  27.3 0.0 copy-start.8
  27.3 0.0 copy-start.9
  27.3 1.7 %shard_map.84 = (f32[5,256,128]{2,1,0:T(8,128)S(1)}, f32[25,16,128]{2,1,0:T(8,128)S(1)}, f32[25,16,128]{2,1,0:T(8,128)S(1)}) custom-call(f32[5,256,128]{2,1,0:T(8,128)S(1)} %bitcast.6, f32[256,128]{1,0:T(8,128)S(1)} %bitcast.9, f32[3,5,256,128]{3,2,1,0:T(8,128)S(1)} %get-tuple-element.31.contra_ref, f32[10,16,128]{2,1,0:T(8,128)S(1)} %collective-permute-done.5.eta_a, ...), custom_call_target="tpu_custom_call" | custom-call | tf_op jit(solution)/shard_map/pallas_call | solution.py:515
  29.0 0.4 collective-permute-start.10
  29.4 2.2 %collective-permute-start.11 = (f32[25,16,128]{2,1,0:T(8,128)S(1)}, f32[25,16,128]{2,1,0:T(8,128)S(1)}, u32[]{:S(2)}, u32[]{:S(2)}) collective-permute-start(f32[25,16,128]{2,1,0:T(8,128)S(1)} %get-tuple-element.39), channel_id=1, source_target_pairs={{0,6},{2,4},{4,2},{6,0},{1,7},{3,5},{5,3},{7,1},{8,14},{10,12},{12... | collective-permute-start | bytes 614408 | tf_op jit(solution)/shard_map/ppermute | solution.py:500
  31.6 4.0 %collective-permute-done.10.eta_a = f32[25,16,128]{2,1,0:T(8,128)S(1)} collective-permute-done((f32[25,16,128]{2,1,0:T(8,128)S(1)}, f32[25,16,128]{2,1,0:T(8,128)S(1)}, u32[]{:S(2)}, u32[]{:S(2)}) %collective-permute-start.10) | collective-permute-done | bytes 204832 | tf_op jit(solution)/shard_map/ppermute | solution.py:500
  35.6 5.6 %collective-permute-done.11.eta_b = f32[25,16,128]{2,1,0:T(8,128)S(1)} collective-permute-done((f32[25,16,128]{2,1,0:T(8,128)S(1)}, f32[25,16,128]{2,1,0:T(8,128)S(1)}, u32[]{:S(2)}, u32[]{:S(2)}) %collective-permute-start.11) | collective-permute-done | bytes 204832 | tf_op jit(solution)/shard_map/ppermute | solution.py:500
  41.1 0.7 %shard_map.85 = (f32[5,256,128]{2,1,0:T(8,128)S(1)}, f32[25,16,128]{2,1,0:T(8,128)S(1)}, f32[25,16,128]{2,1,0:T(8,128)S(1)}) custom-call(f32[5,256,128]{2,1,0:T(8,128)S(1)} %get-tuple-element.37.state_ref, f32[25,16,128]{2,1,0:T(8,128)S(1)} %collective-permute-done.10.eta_a, f32[25,16,128]{2,1,0:T(8,128)S(1)} %collective-permute-done.11.eta_b), custom_call_target="tpu_custom_call" | custom-call | tf_op jit(solution)/shard_map/pallas_call | solution.py:515
  41.9 0.1 collective-permute-start.12
  42.0 0.8 %collective-permute-start.13 = (f32[25,16,128]{2,1,0:T(8,128)S(1)}, f32[25,16,128]{2,1,0:T(8,128)S(1)}, u32[]{:S(2)}, u32[]{:S(2)}) collective-permute-start(f32[25,16,128]{2,1,0:T(8,128)S(1)} %get-tuple-element.42), channel_id=1, source_target_pairs={{0,24},{8,16},{16,8},{24,0},{1,25},{9,17},{17,9},{25,1},{2,26},{10... | collective-permute-start | bytes 614408 | tf_op jit(solution)/shard_map/ppermute | solution.py:500
  42.8 0.6 %collective-permute-done.12.xi_a = f32[25,16,128]{2,1,0:T(8,128)S(1)} collective-permute-done((f32[25,16,128]{2,1,0:T(8,128)S(1)}, f32[25,16,128]{2,1,0:T(8,128)S(1)}, u32[]{:S(2)}, u32[]{:S(2)}) %collective-permute-start.12) | collective-permute-done | bytes 204832 | tf_op jit(solution)/shard_map/ppermute | solution.py:500
  43.4 5.4 %collective-permute-done.13.xi_b = f32[25,16,128]{2,1,0:T(8,128)S(1)} collective-permute-done((f32[25,16,128]{2,1,0:T(8,128)S(1)}, f32[25,16,128]{2,1,0:T(8,128)S(1)}, u32[]{:S(2)}, u32[]{:S(2)}) %collective-permute-start.13) | collective-permute-done | bytes 204832 | tf_op jit(solution)/shard_map/ppermute | solution.py:500
  48.8 0.6 %shard_map.86 = (f32[5,256,128]{2,1,0:T(8,128)S(1)}, f32[5,24,128]{2,1,0:T(8,128)S(1)}) custom-call(f32[5,256,128]{2,1,0:T(8,128)S(1)} %get-tuple-element.40.state_ref, f32[25,16,128]{2,1,0:T(8,128)S(1)} %collective-permute-done.12.xi_a, f32[25,16,128]{2,1,0:T(8,128)S(1)} %collective-permute-done.13.xi_b), custom_call_target="tpu_custom_call" | custom-call | tf_op jit(solution)/shard_map/pallas_call | solution.py:515
  49.4 1.6 %collective-permute-start.14 = (f32[5,24,128]{2,1,0:T(8,128)S(1)}, f32[5,24,128]{2,1,0:T(8,128)S(1)}, u32[]{:S(2)}, u32[]{:S(2)}) collective-permute-start(f32[5,24,128]{2,1,0:T(8,128)S(1)} %get-tuple-element.44), channel_id=1, source_target_pairs={{0,1},{1,0},{2,3},{3,2},{4,5},{5,4},{6,7},{7,6},{8,9},{9,8},{10,11... | collective-permute-start | bytes 184328 | tf_op jit(solution)/shard_map/ppermute | solution.py:506
  51.0 2.8 %collective-permute-done.14.below_ref.above_ref = f32[5,24,128]{2,1,0:T(8,128)S(1)} collective-permute-done((f32[5,24,128]{2,1,0:T(8,128)S(1)}, f32[5,24,128]{2,1,0:T(8,128)S(1)}, u32[]{:S(2)}, u32[]{:S(2)}) %collective-permute-start.14) | collective-permute-done | bytes 61472 | tf_op jit(solution)/shard_map/ppermute | solution.py:506
  53.8 0.0 copy-done.8
  53.8 1.4 %shard_map.87 = f32[5,256,128]{2,1,0:T(8,128)} custom-call(f32[5,256,128]{2,1,0:T(8,128)S(1)} %get-tuple-element.43.state_ref, f32[5,24,128]{2,1,0:T(8,128)S(1)} %collective-permute-done.14.below_ref.above_ref, f32[5,24,128]{2,1,0:T(8,128)S(1)} %collective-permute-done.14.below_ref.above_ref, bf16[256,256]{1,0:T(8,128)(2,1)S(1)} %copy-done.9, ...), custom_call_target="tpu_custom_call" | custom-call | tf_op jit(solution)/shard_map/pallas_call | solution.py:515
  (8 shorter events, 0.0 us)
Async XLA Ops:
  0.0 1.1 %copy-start = (f32[5,16,16,128]{3,2,1,0:T(8,128)S(1)}, f32[5,16,16,128]{3,2,1,0:T(8,128)}, u32[]{:S(2)}) copy-start(f32[5,16,16,128]{3,2,1,0:T(8,128)} %param.8) | copy-start | bytes 1966084
  1.1 0.9 %copy-start.7 = (bf16[256,256]{1,0:T(8,128)(2,1)S(1)}, bf16[256,256]{1,0:T(8,128)(2,1)}, u32[]{:S(2)}) copy-start(bf16[256,256]{1,0:T(8,128)(2,1)} %constant.11.clone.sums_ref) | copy-start | bytes 393220
  2.0 25.3 %copy-start.4 = (bf16[256,256]{1,0:T(8,128)(2,1)S(1)}, bf16[256,256]{1,0:T(8,128)(2,1)}, u32[]{:S(2)}) copy-start(bf16[256,256]{1,0:T(8,128)(2,1)} %constant.12.clone.back_ref) | copy-start | bytes 393220
  2.0 25.3 %copy-start.6 = (bf16[256,256]{1,0:T(8,128)(2,1)S(1)}, bf16[256,256]{1,0:T(8,128)(2,1)}, u32[]{:S(2)}) copy-start(bf16[256,256]{1,0:T(8,128)(2,1)} %constant.10.clone.derive_ref) | copy-start | bytes 393220
  2.6 10.9 %collective-permute-start = (f32[8,16,128]{2,1,0:T(8,128)S(1)}, f32[8,16,128]{2,1,0:T(8,128)S(1)}, u32[]{:S(2)}, u32[]{:S(2)}) collective-permute-start(f32[8,16,128]{2,1,0:T(8,128)S(1)} %get-tuple-element.26), channel_id=1, source_target_pairs={{0,2},{2,0},{4,6},{6,4},{1,3},{3,1},{5,7},{7,5},{8,10},{10,8},{12,... | collective-permute-start | bytes 196616 | tf_op jit(solution)/shard_map/ppermute | solution.py:500
  5.7 7.8 %collective-permute-start.1 = (f32[8,16,128]{2,1,0:T(8,128)S(1)}, f32[8,16,128]{2,1,0:T(8,128)S(1)}, u32[]{:S(2)}, u32[]{:S(2)}) collective-permute-start(f32[8,16,128]{2,1,0:T(8,128)S(1)} %get-tuple-element.27), channel_id=1, source_target_pairs={{0,6},{2,4},{4,2},{6,0},{1,7},{3,5},{5,3},{7,1},{8,14},{10,12},{12... | collective-permute-start | bytes 196616 | tf_op jit(solution)/shard_map/ppermute | solution.py:500
  8.2 5.4 %collective-permute-start.2 = (f32[8,16,128]{2,1,0:T(8,128)S(1)}, f32[8,16,128]{2,1,0:T(8,128)S(1)}, u32[]{:S(2)}, u32[]{:S(2)}) collective-permute-start(f32[8,16,128]{2,1,0:T(8,128)S(1)} %get-tuple-element.28), channel_id=1, source_target_pairs={{0,8},{8,0},{16,24},{24,16},{1,9},{9,1},{17,25},{25,17},{2,10},{10... | collective-permute-start | bytes 196616 | tf_op jit(solution)/shard_map/ppermute | solution.py:500
  8.2 5.4 %collective-permute-start.3 = (f32[8,16,128]{2,1,0:T(8,128)S(1)}, f32[8,16,128]{2,1,0:T(8,128)S(1)}, u32[]{:S(2)}, u32[]{:S(2)}) collective-permute-start(f32[8,16,128]{2,1,0:T(8,128)S(1)} %get-tuple-element.29), channel_id=1, source_target_pairs={{0,24},{8,16},{16,8},{24,0},{1,25},{9,17},{17,9},{25,1},{2,26},{10... | collective-permute-start | bytes 196616 | tf_op jit(solution)/shard_map/ppermute | solution.py:500
  9.8 3.7 %collective-permute-start.4 = (f32[4,8,128]{2,1,0:T(8,128)S(1)}, f32[4,8,128]{2,1,0:T(8,128)S(1)}, u32[]{:S(2)}, u32[]{:S(2)}) collective-permute-start(f32[4,8,128]{2,1,0:T(8,128)S(1)} %get-tuple-element.30), channel_id=1, source_target_pairs={{0,1},{1,0},{2,3},{3,2},{4,5},{5,4},{6,7},{7,6},{8,9},{9,8},{10,11... | collective-permute-start | bytes 49160 | tf_op jit(solution)/shard_map/ppermute | solution.py:506
  13.6 1.3 %copy-start.1 = (f32[3,3,16,16,128]{4,3,2,1,0:T(8,128)S(1)}, f32[3,3,16,16,128]{4,3,2,1,0:T(8,128)}, u32[]{:S(2)}) copy-start(f32[3,3,16,16,128]{4,3,2,1,0:T(8,128)} %param.9) | copy-start | bytes 3538948
  14.8 0.9 %copy-start.2 = (f32[16,16,128]{2,1,0:T(8,128)S(1)}, f32[16,16,128]{2,1,0:T(8,128)}, u32[]{:S(2)}) copy-start(f32[16,16,128]{2,1,0:T(8,128)} %param.10) | copy-start | bytes 393220
  15.7 0.9 %copy-start.3 = (bf16[256,256]{1,0:T(8,128)(2,1)S(1)}, bf16[256,256]{1,0:T(8,128)(2,1)}, u32[]{:S(2)}) copy-start(bf16[256,256]{1,0:T(8,128)(2,1)} %constant.12.clone.back_ref) | copy-start | bytes 393220
  16.6 0.9 %copy-start.5 = (bf16[256,256]{1,0:T(8,128)(2,1)S(1)}, bf16[256,256]{1,0:T(8,128)(2,1)}, u32[]{:S(2)}) copy-start(bf16[256,256]{1,0:T(8,128)(2,1)} %constant.10.clone.derive_ref) | copy-start | bytes 393220
  20.3 6.2 %collective-permute-start.5 = (f32[10,16,128]{2,1,0:T(8,128)S(1)}, f32[10,16,128]{2,1,0:T(8,128)S(1)}, u32[]{:S(2)}, u32[]{:S(2)}) collective-permute-start(f32[10,16,128]{2,1,0:T(8,128)S(1)} %get-tuple-element.32), channel_id=1, source_target_pairs={{0,2},{2,0},{4,6},{6,4},{1,3},{3,1},{5,7},{7,5},{8,10},{10,8},{12,... | collective-permute-start | bytes 245768 | tf_op jit(solution)/shard_map/ppermute | solution.py:500
  21.0 6.2 %collective-permute-start.6 = (f32[10,16,128]{2,1,0:T(8,128)S(1)}, f32[10,16,128]{2,1,0:T(8,128)S(1)}, u32[]{:S(2)}, u32[]{:S(2)}) collective-permute-start(f32[10,16,128]{2,1,0:T(8,128)S(1)} %get-tuple-element.33), channel_id=1, source_target_pairs={{0,6},{2,4},{4,2},{6,0},{1,7},{3,5},{5,3},{7,1},{8,14},{10,12},{12... | collective-permute-start | bytes 245768 | tf_op jit(solution)/shard_map/ppermute | solution.py:500
  21.9 5.3 %collective-permute-start.7 = (f32[10,16,128]{2,1,0:T(8,128)S(1)}, f32[10,16,128]{2,1,0:T(8,128)S(1)}, u32[]{:S(2)}, u32[]{:S(2)}) collective-permute-start(f32[10,16,128]{2,1,0:T(8,128)S(1)} %get-tuple-element.34), channel_id=1, source_target_pairs={{0,8},{8,0},{16,24},{24,16},{1,9},{9,1},{17,25},{25,17},{2,10},{10... | collective-permute-start | bytes 245768 | tf_op jit(solution)/shard_map/ppermute | solution.py:500
  21.9 5.3 %collective-permute-start.8 = (f32[10,16,128]{2,1,0:T(8,128)S(1)}, f32[10,16,128]{2,1,0:T(8,128)S(1)}, u32[]{:S(2)}, u32[]{:S(2)}) collective-permute-start(f32[10,16,128]{2,1,0:T(8,128)S(1)} %get-tuple-element.35), channel_id=1, source_target_pairs={{0,24},{8,16},{16,8},{24,0},{1,25},{9,17},{17,9},{25,1},{2,26},{10... | collective-permute-start | bytes 245768 | tf_op jit(solution)/shard_map/ppermute | solution.py:500
  22.8 3.8 %collective-permute-start.9 = (f32[5,8,128]{2,1,0:T(8,128)S(1)}, f32[5,8,128]{2,1,0:T(8,128)S(1)}, u32[]{:S(2)}, u32[]{:S(2)}) collective-permute-start(f32[5,8,128]{2,1,0:T(8,128)S(1)} %get-tuple-element.36), channel_id=1, source_target_pairs={{0,1},{1,0},{2,3},{3,2},{4,5},{5,4},{6,7},{7,6},{8,9},{9,8},{10,11... | collective-permute-start | bytes 61448 | tf_op jit(solution)/shard_map/ppermute | solution.py:506
  27.3 26.5 %copy-start.8 = (bf16[256,256]{1,0:T(8,128)(2,1)S(1)}, bf16[256,256]{1,0:T(8,128)(2,1)}, u32[]{:S(2)}) copy-start(bf16[256,256]{1,0:T(8,128)(2,1)} %constant.14.clone.ends_ref) | copy-start | bytes 393220
  27.3 26.5 %copy-start.9 = (bf16[256,256]{1,0:T(8,128)(2,1)S(1)}, bf16[256,256]{1,0:T(8,128)(2,1)}, u32[]{:S(2)}) copy-start(bf16[256,256]{1,0:T(8,128)(2,1)} %constant.13.clone.smooth_ref) | copy-start | bytes 393220
  29.0 6.5 %collective-permute-start.10 = (f32[25,16,128]{2,1,0:T(8,128)S(1)}, f32[25,16,128]{2,1,0:T(8,128)S(1)}, u32[]{:S(2)}, u32[]{:S(2)}) collective-permute-start(f32[25,16,128]{2,1,0:T(8,128)S(1)} %get-tuple-element.38), channel_id=1, source_target_pairs={{0,2},{2,0},{4,6},{6,4},{1,3},{3,1},{5,7},{7,5},{8,10},{10,8},{12,... | collective-permute-start | bytes 614408 | tf_op jit(solution)/shard_map/ppermute | solution.py:500
  29.4 11.7 %collective-permute-start.11 = (f32[25,16,128]{2,1,0:T(8,128)S(1)}, f32[25,16,128]{2,1,0:T(8,128)S(1)}, u32[]{:S(2)}, u32[]{:S(2)}) collective-permute-start(f32[25,16,128]{2,1,0:T(8,128)S(1)} %get-tuple-element.39), channel_id=1, source_target_pairs={{0,6},{2,4},{4,2},{6,0},{1,7},{3,5},{5,3},{7,1},{8,14},{10,12},{12... | collective-permute-start | bytes 614408 | tf_op jit(solution)/shard_map/ppermute | solution.py:500
  41.9 1.5 %collective-permute-start.12 = (f32[25,16,128]{2,1,0:T(8,128)S(1)}, f32[25,16,128]{2,1,0:T(8,128)S(1)}, u32[]{:S(2)}, u32[]{:S(2)}) collective-permute-start(f32[25,16,128]{2,1,0:T(8,128)S(1)} %get-tuple-element.41), channel_id=1, source_target_pairs={{0,8},{8,0},{16,24},{24,16},{1,9},{9,1},{17,25},{25,17},{2,10},{10... | collective-permute-start | bytes 614408 | tf_op jit(solution)/shard_map/ppermute | solution.py:500
  42.0 6.9 %collective-permute-start.13 = (f32[25,16,128]{2,1,0:T(8,128)S(1)}, f32[25,16,128]{2,1,0:T(8,128)S(1)}, u32[]{:S(2)}, u32[]{:S(2)}) collective-permute-start(f32[25,16,128]{2,1,0:T(8,128)S(1)} %get-tuple-element.42), channel_id=1, source_target_pairs={{0,24},{8,16},{16,8},{24,0},{1,25},{9,17},{17,9},{25,1},{2,26},{10... | collective-permute-start | bytes 614408 | tf_op jit(solution)/shard_map/ppermute | solution.py:500
  49.4 4.4 %collective-permute-start.14 = (f32[5,24,128]{2,1,0:T(8,128)S(1)}, f32[5,24,128]{2,1,0:T(8,128)S(1)}, u32[]{:S(2)}, u32[]{:S(2)}) collective-permute-start(f32[5,24,128]{2,1,0:T(8,128)S(1)} %get-tuple-element.44), channel_id=1, source_target_pairs={{0,1},{1,0},{2,3},{3,2},{4,5},{5,4},{6,7},{7,6},{8,9},{9,8},{10,11... | collective-permute-start | bytes 184328 | tf_op jit(solution)/shard_map/ppermute | solution.py:506

commit v2 on v1

--- a/solution.py
+++ b/solution.py
@@ -268,12 +268,24 @@
 
 
 def primitive_kernel(
-    grid, u_ref, sums_ref, prim_ref, eta_first, eta_second, xi_first, xi_second, zeta_ref
+    grid,
+    u_hbm, sums_hbm,
+    u_ref, sums_ref, prim_ref, eta_first, eta_second, xi_first, xi_second, zeta_ref,
+    sums_sem, u_sems,
 ):
-    step = 4 * TILE
-
-    def body(index, carry):
-        rows = pl.ds(pl.multiple_of(index * step, step), step)
+    chunks = u_sems.shape[0]
+    step = grid.rows // chunks
+    copies = []
+    for index in range(chunks):
+        rows = pl.ds(index * step, step)
+        copy = pltpu.make_async_copy(u_hbm.at[:, rows, :], u_ref.at[:, rows, :], u_sems.at[index])
+        copy.start()
+        copies.append(copy)
+    weights = pltpu.make_async_copy(sums_hbm, sums_ref, sums_sem)
+    weights.start()
+    for index in range(chunks):
+        copies[index].wait()
+        rows = pl.ds(index * step, step)
         inverse = 1.0 / u_ref[0, rows, :]
         work = None
         for c in range(3):
@@ -283,9 +295,6 @@
             work = momentum * speed if work is None else work + momentum * speed
         pressure = 0.4 * (u_ref[4, rows, :] - 0.5 * work)
         prim_ref[3, rows, :] = pressure * inverse
-        return carry
-
-    lax.fori_loop(0, grid.rows // step, body, 0)
     for field in range(4):
         send_sums(
             lambda position, group: prim_ref[field, grid.eta_tile(position, group), :],
@@ -295,17 +304,24 @@
             lambda position, group: prim_ref[field, grid.xi_tile(position, group), :],
             grid.eta_groups, grid.nx, odd("xi"), xi_first, xi_second, field,
         )
+    weights.wait()
+    for field in range(4):
         zeta_ref[field] = pack_sums(prim_ref[field], sums_ref[...], grid)
 
 
-def flux_kernel(
-    grid,
-    u_ref, prim_ref, metrics_ref, jacobian_ref,
-    eta_a, eta_b, xi_a, xi_b, zeta_below, zeta_above,
-    derive_ref, back_ref, sums_ref,
-    contra_ref, eta_first, eta_second, xi_first, xi_second, zeta_ref,
-    slope_ref,
-):
+def fetch_kernel(count, *refs):
+    sources, results, sems = refs[:count], refs[count + 1 : 2 * count + 1], refs[-1]
+    copies = [
+        pltpu.make_async_copy(source, result, sems.at[index])
+        for index, (source, result) in enumerate(zip(sources, results))
+    ]
+    for copy in copies:
+        copy.start()
+    for copy in copies:
+        copy.wait()
+
+
+def slope_kernel(grid, prim_ref, eta_a, eta_b, xi_a, xi_b, derive_ref, slope_ref):
     for field in range(4):
         for group in range(grid.eta_groups):
             below, above = take_sums(xi_a, xi_b, odd("xi"), field, group)
@@ -317,10 +333,18 @@
             cells = [prim_ref[field, grid.eta_tile(i, group), :] for i in range(grid.ny)]
             for i, value in enumerate(derive_line(cells, below, above)):
                 slope_ref[1, field, grid.eta_tile(i, group), :] = value
+        slope_ref[2, field] = lane_product(prim_ref[field], derive_ref[...])
+
+
+def flux_kernel(
+    grid,
+    u_ref, prim_ref, metrics_ref, jacobian_ref, slope_ref, zeta_below, zeta_above, back_ref, sums_ref,
+    contra_ref, eta_first, eta_second, xi_first, xi_second, zeta_ref,
+    zeta_slope_ref,
+):
+    for field in range(4):
         halo = unpack_sums(zeta_below[field], zeta_above[field], grid)
-        slope_ref[2, field] = lane_product(prim_ref[field], derive_ref[...]) + lane_product(
-            halo, back_ref[...]
-        )
+        zeta_slope_ref[field] = slope_ref[2, field] + lane_product(halo, back_ref[...])
 
     step = TILE
 
@@ -333,7 +357,7 @@
         metrics = [[metrics_ref[3 * k + j, rows, :] for j in range(3)] for k in range(3)]
         physical = []
         for c in range(4):
-            slopes = [slope_ref[k, c, rows, :] for k in range(3)]
+            slopes = [slope_ref[0, c, rows, :], slope_ref[1, c, rows, :], zeta_slope_ref[c, rows, :]]
             physical.append(
                 [
                     jacobian
@@ -383,37 +407,36 @@
         zeta_ref[field] = pack_sums(contra_ref[2, field], sums_ref[...], grid)
 
 
-def step_kernel(
-    grid,
-    u_ref, jacobian_ref, contra_ref,
-    eta_a, eta_b, xi_a, xi_b, zeta_below, zeta_above,
-    derive_ref, back_ref,
-    state_ref, eta_first, eta_second,
-):
-    flag = odd("eta")
+def divergence_kernel(grid, contra_ref, eta_a, eta_b, xi_a, xi_b, derive_ref, total_ref):
     for field in range(5):
-        halo = unpack_sums(zeta_below[field], zeta_above[field], grid)
-        state_ref[field] = lane_product(contra_ref[2, field], derive_ref[...]) + lane_product(
-            halo, back_ref[...]
-        )
+        total_ref[field] = lane_product(contra_ref[2, field], derive_ref[...])
         for group in range(grid.xi_groups):
-            below, above = take_sums(eta_a, eta_b, flag, field, group)
+            below, above = take_sums(eta_a, eta_b, odd("eta"), field, group)
             cells = [contra_ref[1, field, grid.eta_tile(i, group), :] for i in range(grid.ny)]
             for i, value in enumerate(derive_line(cells, below, above)):
                 rows = grid.eta_tile(i, group)
-                state_ref[field, rows, :] = state_ref[field, rows, :] + value
+                total_ref[field, rows, :] = total_ref[field, rows, :] + value
         for group in range(grid.eta_groups):
             below, above = take_sums(xi_a, xi_b, odd("xi"), field, group)
             cells = [contra_ref[0, field, grid.xi_tile(i, group), :] for i in range(grid.nx)]
             for i, value in enumerate(derive_line(cells, below, above)):
                 rows = grid.xi_tile(i, group)
-                total = state_ref[field, rows, :] + value
-                state_ref[field, rows, :] = u_ref[field, rows, :] - (
-                    step_duration * jacobian_ref[rows, :]
-                ) * total
+                total_ref[field, rows, :] = total_ref[field, rows, :] + value
+
+
+def step_kernel(
+    grid,
+    u_ref, jacobian_ref, total_ref, zeta_below, zeta_above, back_ref,
+    state_ref, eta_first, eta_second,
+):
+    scale = step_duration * jacobian_ref[...]
+    for field in range(5):
+        halo = unpack_sums(zeta_below[field], zeta_above[field], grid)
+        total = total_ref[field] + lane_product(halo, back_ref[...])
+        state_ref[field] = u_ref[field] - scale * total
         send_cells(
             lambda position, group: state_ref[field, grid.eta_tile(position, group), :],
-            grid.xi_groups, grid.ny, flag, eta_first, eta_second, field,
+            grid.xi_groups, grid.ny, odd("eta"), eta_first, eta_second, field,
         )
 
 
@@ -473,7 +496,10 @@
             zeta_ref[field, group_rows(start // PACKED), :] = packed
 
 
-def zeta_filter_kernel(grid, state_ref, below_ref, above_ref, smooth_ref, ends_ref, result_ref):
+def zeta_filter_kernel(
+    grid, state_ref, below_ref, above_ref, smooth_ref, ends_ref, result_hbm, result_ref, sems
+):
+    copies = []
     tiles = grid.rows // TILE
     lane = lax.broadcasted_iota(jnp.int32, (TILE, LANES), 1)
     for field in range(5):
@@ -489,6 +515,11 @@
         result_ref[field] = lane_product(state_ref[field], smooth_ref[...]) + lane_product(
             halo, ends_ref[...]
         )
+        copy = pltpu.make_async_copy(result_ref.at[field], result_hbm.at[field], sems.at[field])
+        copy.start()
+        copies.append(copy)
+    for copy in copies:
+        copy.wait()
 
 
 def pair_swap(value, axis, parity):
@@ -510,14 +541,32 @@
     return lax.ppermute(value, axis, up), lax.ppermute(value, axis, down)
 
 
-def call(kernel, outs, *operands, scratch=()):
-    shapes = [jax.ShapeDtypeStruct(shape, jnp.float32) for shape in outs]
+HBM = pltpu.MemorySpace.HBM
+
+
+def call(kernel, outs, *operands, scratch=(), cost=1.0, far=(), far_outs=()):
+    shapes = [
+        out if isinstance(out, jax.ShapeDtypeStruct) else jax.ShapeDtypeStruct(out, jnp.float32)
+        for out in outs
+    ]
+    near = pltpu.MemorySpace.VMEM
     return pl.pallas_call(
         kernel,
         out_shape=shapes,
-        scratch_shapes=[pltpu.VMEM(shape, jnp.float32) for shape in scratch],
+        in_specs=[
+            pl.BlockSpec(memory_space=HBM if index in far else near) for index in range(len(operands))
+        ],
+        out_specs=[
+            pl.BlockSpec(memory_space=HBM if index in far_outs else near) for index in range(len(outs))
+        ],
+        scratch_shapes=scratch,
+        cost_estimate=pl.CostEstimate(flops=0, transcendentals=0, bytes_accessed=int(cost * 3.6e6)),
         compiler_params=pltpu.CompilerParams(vmem_limit_bytes=20 * 2**20),
     )(*operands)
+
+
+def like(value):
+    return jax.ShapeDtypeStruct(value.shape, value.dtype)
 
 
 def local(conserved_solution, metrics, jacobian):
@@ -536,28 +585,45 @@
         xi_b = pair_swap(xi_second, "xi", 1)
         below, above = ring_swap(zeta, "zeta")
         xi_a = pair_swap(xi_first, "xi", 0)
-        return eta_a, eta_b, xi_a, xi_b, below, above
+        return (eta_a, eta_b, xi_a, xi_b), (below, above)
 
     def sums_shapes(fields):
         return [(2 * fields, nx, nz)] * 2 + [(2 * fields, ny, nz)] * 2 + [(fields, TILE, LANES)]
 
-    prim, *sends = call(
+    chunks = 4
+    u, sums, prim, *sends = call(
         functools.partial(primitive_kernel, grid),
-        [(4, rows, nz)] + sums_shapes(4),
+        [like(u), like(tables["sums"]), (4, rows, nz)] + sums_shapes(4),
         u, tables["sums"],
-    )
-    got = exchange(*sends)
+        scratch=[pltpu.SemaphoreType.DMA, pltpu.SemaphoreType.DMA((chunks,))],
+        far=(0, 1),
+    )
+    sides, ends = exchange(*sends)
+    fetched = [metrics, jacobian] + [tables[name] for name in ("derive", "back", "smooth", "ends")]
+    metrics, jacobian, derive, back, smooth, smooth_ends = call(
+        functools.partial(fetch_kernel, len(fetched)),
+        [like(value) for value in fetched],
+        *fetched, sends[-1],
+        scratch=[pltpu.SemaphoreType.DMA((len(fetched),))],
+        far=tuple(range(len(fetched))),
+    )
+    (slopes,) = call(
+        functools.partial(slope_kernel, grid), [(3, 4, rows, nz)], prim, *sides, derive,
+    )
     contra, *sends = call(
         functools.partial(flux_kernel, grid),
         [(3, 5, rows, nz)] + sums_shapes(5),
-        u, prim, metrics, jacobian, *got, tables["derive"], tables["back"], tables["sums"],
-        scratch=[(3, 4, rows, nz)],
-    )
-    got = exchange(*sends)
+        u, prim, metrics, jacobian, slopes, *ends, back, sums,
+        scratch=[pltpu.VMEM((4, rows, nz), jnp.float32)],
+    )
+    sides, ends = exchange(*sends)
+    (total,) = call(
+        functools.partial(divergence_kernel, grid), [(5, rows, nz)], contra, *sides, derive,
+    )
     state, eta_first, eta_second = call(
         functools.partial(step_kernel, grid),
         [(5, rows, nz)] + [(5 * WIDTH, nx, nz)] * 2,
-        u, jacobian, contra, *got, tables["derive"], tables["back"],
+        u, jacobian, total, *ends, back,
     )
     eta_b = pair_swap(eta_second, "eta", 1)
     eta_a = pair_swap(eta_first, "eta", 0)
@@ -577,7 +643,9 @@
     (result,) = call(
         functools.partial(zeta_filter_kernel, grid),
         [(5, rows, nz)],
-        state, below, above, tables["smooth"], tables["ends"],
+        state, below, above, smooth, smooth_ends,
+        scratch=[pltpu.VMEM((5, rows, nz), jnp.float32), pltpu.SemaphoreType.DMA((5,))],
+        far_outs=(0,),
     )
     return result.reshape(5, nx, ny, nz)
 

time: 55.4 us -> 56.9 us (1.027)
  starting transfers between devices: 17.7 us -> 14.9 us
  Pallas kernels: 7.8 us -> 9.62 us
  local copies, waits for them, and re-layouts: 5.99 us -> 7.78 us
  waiting for transfers between devices: 23.6 us -> 24.2 us
    ppermute x12, waiting for transfers between devices: 16.4 us -> 20.4 us  [pair_swap(): return lax.ppermute(value, axis, pairs)]
    ppermute x3, waiting for transfers between devices: 7.25 us -> 3.77 us  [ring_swap(): other = lax.ppermute(value, axis, [(0, 1), (1, 0)])]
    ppermute x3, starting transfers between devices: 4.63 us -> 2.63 us  [ring_swap(): other = lax.ppermute(value, axis, [(0, 1), (1, 0)])]
    pallas_call x6 -> x9, Pallas kernels: 7.8 us -> 9.62 us  [call(): pl.pallas_call(kernel, out_shape=shapes, in_specs=[pl.BlockSpec(memory_sp...]
    unnamed x20 -> x16, local copies, waits for them, and re-layouts: 5.99 us -> 7.78 us
    ppermute x12, starting transfers between devices: 13 us -> 12.3 us  [pair_swap(): return lax.ppermute(value, axis, pairs)]
  transfers between devices with their start and end apart: 15 -> 15, of which waited for: 8 -> 7; matrix products, arithmetic and copies ran while one was open for 0% -> 0% of each run, Pallas kernels for 0% -> 6%
where the time goes in v2:
time: 56.9 us; the launch traced here: 56.6 us
  waiting for transfers between devices  24.2 us (43%)
  starting transfers between devices  14.9 us (26%)
  Pallas kernels  9.62 us (17%)
  local copies, waits for them, and re-layouts  7.78 us (14%)
    ppermute x12, waiting for transfers between devices, pair_swap(): return lax.ppermute(value, axis, pairs)  20.4 us
    ppermute x12, starting transfers between devices, pair_swap(): return lax.ppermute(value, axis, pairs)  12.3 us
    pallas_call x9, Pallas kernels, call(): pl.pallas_call(kernel, out_shape=shapes, in_specs=[pl.BlockSpec(memory_sp...  9.62 us
    unnamed x16, local copies, waits for them, and re-layouts  7.78 us
    ppermute x3, waiting for transfers between devices, ring_swap(): other = lax.ppermute(value, axis, [(0, 1), (1, 0)])  3.77 us
    ppermute x3, starting transfers between devices, ring_swap(): other = lax.ppermute(value, axis, [(0, 1), (1, 0)])  2.63 us
  transfers between devices with their start and end apart: 15, of which 7 were waited for; matrix products, arithmetic and copies ran while one was open for 0% of the time, Pallas kernels for 6%

profile of v2, /device:TPU:0, one launch (start us, length us, event | category | flops | bytes accessed | tf_op | source)
XLA Modules:
  0.0 56.6 jit_solution(17352250414130887920)
XLA Ops:
  0.0 0.0 copy-start.1
  0.0 1.1 %copy-done.1 = f32[5,16,16,128]{3,2,1,0:T(8,128)S(1)} copy-done((f32[5,16,16,128]{3,2,1,0:T(8,128)S(1)}, f32[5,16,16,128]{3,2,1,0:T(8,128)}, u32[]{:S(2)}) %copy-start.1) | copy-done | bytes 655384
  1.1 0.9 %copy-done.7 = bf16[256,256]{1,0:T(8,128)(2,1)S(1)} copy-done((bf16[256,256]{1,0:T(8,128)(2,1)S(1)}, bf16[256,256]{1,0:T(8,128)(2,1)}, u32[]{:S(2)}) %copy-start.7) | copy-done | bytes 131096
  2.0 1.0 %shard_map.82 = (f32[5,256,128]{2,1,0:T(8,128)S(1)}, bf16[256,256]{1,0:T(8,128)(2,1)S(1)}, f32[4,256,128]{2,1,0:T(8,128)S(1)}, f32[8,16,128]{2,1,0:T(8,128)S(1)}...) custom-call(f32[5,256,128]{2,1,0:T(8,128)S(1)} %bitcast.5, ...), custom_call_target="tpu_custom_call" | custom-call | bytes 3600000 | tf_op jit(solution)/shard_map/pallas_call | solution.py:553
  3.0 3.1 %collective-permute-start = (f32[8,16,128]{2,1,0:T(8,128)S(1)}, f32[8,16,128]{2,1,0:T(8,128)S(1)}, u32[]{:S(2)}, u32[]{:S(2)}) collective-permute-start(f32[8,16,128]{2,1,0:T(8,128)S(1)} %get-tuple-element.38), channel_id=1, source_target_pairs={{0,2},{2,0},{4,6},{6,4},{1,3},{3,1},{5,7},{7,5},{8,10},{10,8},{12,... | collective-permute-start | bytes 196616 | tf_op jit(solution)/shard_map/ppermute | solution.py:531
  6.1 2.5 %collective-permute-start.1 = (f32[8,16,128]{2,1,0:T(8,128)S(1)}, f32[8,16,128]{2,1,0:T(8,128)S(1)}, u32[]{:S(2)}, u32[]{:S(2)}) collective-permute-start(f32[8,16,128]{2,1,0:T(8,128)S(1)} %get-tuple-element.39), channel_id=1, source_target_pairs={{0,6},{2,4},{4,2},{6,0},{1,7},{3,5},{5,3},{7,1},{8,14},{10,12},{12... | collective-permute-start | bytes 196616 | tf_op jit(solution)/shard_map/ppermute | solution.py:531
  8.5 0.0 collective-permute-start.2
  8.6 1.6 %collective-permute-start.3 = (f32[8,16,128]{2,1,0:T(8,128)S(1)}, f32[8,16,128]{2,1,0:T(8,128)S(1)}, u32[]{:S(2)}, u32[]{:S(2)}) collective-permute-start(f32[8,16,128]{2,1,0:T(8,128)S(1)} %get-tuple-element.41), channel_id=1, source_target_pairs={{0,24},{8,16},{16,8},{24,0},{1,25},{9,17},{17,9},{25,1},{2,26},{10... | collective-permute-start | bytes 196616 | tf_op jit(solution)/shard_map/ppermute | solution.py:531
  10.2 1.5 %collective-permute-start.4 = (f32[4,8,128]{2,1,0:T(8,128)S(1)}, f32[4,8,128]{2,1,0:T(8,128)S(1)}, u32[]{:S(2)}, u32[]{:S(2)}) collective-permute-start(f32[4,8,128]{2,1,0:T(8,128)S(1)} %get-tuple-element.34.refs_6_), channel_id=1, source_target_pairs={{0,1},{1,0},{2,3},{3,2},{4,5},{5,4},{6,7},{7,6},{8,9},{9,8},{10,11... | collective-permute-start | bytes 49160 | tf_op jit(solution)/shard_map/ppermute | solution.py:537
  11.7 1.3 %copy-done = f32[3,3,16,16,128]{4,3,2,1,0:T(8,128)S(1)} copy-done((f32[3,3,16,16,128]{4,3,2,1,0:T(8,128)S(1)}, f32[3,3,16,16,128]{4,3,2,1,0:T(8,128)}, u32[]{:S(2)}) %copy-start) | copy-done | bytes 1179672
  12.9 0.9 %copy-done.2 = f32[16,16,128]{2,1,0:T(8,128)S(1)} copy-done((f32[16,16,128]{2,1,0:T(8,128)S(1)}, f32[16,16,128]{2,1,0:T(8,128)}, u32[]{:S(2)}) %copy-start.2) | copy-done | bytes 131096
  13.9 0.9 %copy-done.3 = bf16[256,256]{1,0:T(8,128)(2,1)S(1)} copy-done((bf16[256,256]{1,0:T(8,128)(2,1)S(1)}, bf16[256,256]{1,0:T(8,128)(2,1)}, u32[]{:S(2)}) %copy-start.3) | copy-done | bytes 131096
  14.8 0.9 %copy-done.4 = bf16[256,256]{1,0:T(8,128)(2,1)S(1)} copy-done((bf16[256,256]{1,0:T(8,128)(2,1)S(1)}, bf16[256,256]{1,0:T(8,128)(2,1)}, u32[]{:S(2)}) %copy-start.4) | copy-done | bytes 131096
  15.7 0.9 %copy-done.5 = bf16[256,256]{1,0:T(8,128)(2,1)S(1)} copy-done((bf16[256,256]{1,0:T(8,128)(2,1)S(1)}, bf16[256,256]{1,0:T(8,128)(2,1)}, u32[]{:S(2)}) %copy-start.5) | copy-done | bytes 131096
  16.6 0.9 %copy-done.6 = bf16[256,256]{1,0:T(8,128)(2,1)S(1)} copy-done((bf16[256,256]{1,0:T(8,128)(2,1)S(1)}, bf16[256,256]{1,0:T(8,128)(2,1)}, u32[]{:S(2)}) %copy-start.6) | copy-done | bytes 131096
  17.5 1.1 %shard_map.83 = (f32[9,256,128]{2,1,0:T(8,128)S(1)}, f32[256,128]{1,0:T(8,128)S(1)}, bf16[256,256]{1,0:T(8,128)(2,1)S(1)}, bf16[256,256]{1,0:T(8,128)(2,1)S(1)},...) custom-call(f32[9,256,128]{2,1,0:T(8,128)S(1)} %bitcast.4, f32[256,128]{1,0:T(8,128)S(1)} %bitcast.6, ...), custom_call_target="tpu_custom_call" | custom-call | bytes 3600000 | tf_op jit(solution)/shard_map/pallas_call | solution.py:553
  18.6 0.0 collective-permute-done.eta_a
  18.6 0.0 collective-permute-done.1.eta_b
  18.6 0.0 collective-permute-done.2.xi_a
  18.6 0.0 collective-permute-done.3.xi_b
  18.7 0.9 %shard_map.84.slope_ref = f32[3,4,256,128]{3,2,1,0:T(8,128)S(1)} custom-call(f32[4,256,128]{2,1,0:T(8,128)S(1)} %get-tuple-element.36.prim_ref, f32[8,16,128]{2,1,0:T(8,128)S(1)} %collective-permute-done.eta_a, f32[8,16,128]{2,1,0:T(8,128)S(1)} %collective-permute-done.1.eta_b, f32[8,16,128]{2,1,0:T(8,128)S(1)} %collective-permute-done.2.xi_a, ...), custom_call_target="tpu_custom_call" | custom-call | bytes 3600000 | tf_op jit(solution)/shard_map/pallas_call | solution.py:553
  19.6 0.0 collective-permute-done.4.zeta_below.zeta_above
  19.6 2.2 %shard_map.85 = (f32[3,5,256,128]{3,2,1,0:T(8,128)S(1)}, f32[10,16,128]{2,1,0:T(8,128)S(1)}, f32[10,16,128]{2,1,0:T(8,128)S(1)}, f32[10,16,128]{2,1,0:T(8,128)S(...) custom-call(f32[5,256,128]{2,1,0:T(8,128)S(1)} %get-tuple-element.33.u_ref, ...), custom_call_target="tpu_custom_call" | custom-call | bytes 3600000 | tf_op jit(solution)/shard_map/pallas_call | solution.py:553
  21.8 0.7 %collective-permute-start.5 = (f32[10,16,128]{2,1,0:T(8,128)S(1)}, f32[10,16,128]{2,1,0:T(8,128)S(1)}, u32[]{:S(2)}, u32[]{:S(2)}) collective-permute-start(f32[10,16,128]{2,1,0:T(8,128)S(1)} %get-tuple-element.46), channel_id=1, source_target_pairs={{0,2},{2,0},{4,6},{6,4},{1,3},{3,1},{5,7},{7,5},{8,10},{10,8},{12,... | collective-permute-start | bytes 245768 | tf_op jit(solution)/shard_map/ppermute | solution.py:531
  22.5 0.9 %collective-permute-start.6 = (f32[10,16,128]{2,1,0:T(8,128)S(1)}, f32[10,16,128]{2,1,0:T(8,128)S(1)}, u32[]{:S(2)}, u32[]{:S(2)}) collective-permute-start(f32[10,16,128]{2,1,0:T(8,128)S(1)} %get-tuple-element.47), channel_id=1, source_target_pairs={{0,6},{2,4},{4,2},{6,0},{1,7},{3,5},{5,3},{7,1},{8,14},{10,12},{12... | collective-permute-start | bytes 245768 | tf_op jit(solution)/shard_map/ppermute | solution.py:531
  23.4 0.0 collective-permute-start.7
  23.4 0.7 %collective-permute-start.8 = (f32[10,16,128]{2,1,0:T(8,128)S(1)}, f32[10,16,128]{2,1,0:T(8,128)S(1)}, u32[]{:S(2)}, u32[]{:S(2)}) collective-permute-start(f32[10,16,128]{2,1,0:T(8,128)S(1)} %get-tuple-element.49), channel_id=1, source_target_pairs={{0,24},{8,16},{16,8},{24,0},{1,25},{9,17},{17,9},{25,1},{2,26},{10... | collective-permute-start | bytes 245768 | tf_op jit(solution)/shard_map/ppermute | solution.py:531
  24.1 0.5 collective-permute-start.9
  24.6 1.7 %collective-permute-done.5.eta_a = f32[10,16,128]{2,1,0:T(8,128)S(1)} collective-permute-done((f32[10,16,128]{2,1,0:T(8,128)S(1)}, f32[10,16,128]{2,1,0:T(8,128)S(1)}, u32[]{:S(2)}, u32[]{:S(2)}) %collective-permute-start.5) | collective-permute-done | bytes 81952 | tf_op jit(solution)/shard_map/ppermute | solution.py:531
  26.3 2.6 %collective-permute-done.6.eta_b = f32[10,16,128]{2,1,0:T(8,128)S(1)} collective-permute-done((f32[10,16,128]{2,1,0:T(8,128)S(1)}, f32[10,16,128]{2,1,0:T(8,128)S(1)}, u32[]{:S(2)}, u32[]{:S(2)}) %collective-permute-start.6) | collective-permute-done | bytes 81952 | tf_op jit(solution)/shard_map/ppermute | solution.py:531
  28.9 0.0 collective-permute-done.7.xi_a
  28.9 0.0 collective-permute-done.8.xi_b
  28.9 1.3 %shard_map.86.total_ref = f32[5,256,128]{2,1,0:T(8,128)S(1)} custom-call(f32[3,5,256,128]{3,2,1,0:T(8,128)S(1)} %get-tuple-element.45.contra_ref, f32[10,16,128]{2,1,0:T(8,128)S(1)} %collective-permute-done.5.eta_a, f32[10,16,128]{2,1,0:T(8,128)S(1)} %collective-permute-done.6.eta_b, f32[10,16,128]{2,1,0:T(8,128)S(1)} %collective-permute-done.7.xi_a, ...), custom_call_target="tpu_custom_call" | custom-call | bytes 3600000 | tf_op jit(solution)/shard_map/pallas_call | solution.py:553
  30.2 0.0 collective-permute-done.9.zeta_below.zeta_above
  30.2 0.5 shard_map.87
  30.7 0.8 %collective-permute-start.10 = (f32[25,16,128]{2,1,0:T(8,128)S(1)}, f32[25,16,128]{2,1,0:T(8,128)S(1)}, u32[]{:S(2)}, u32[]{:S(2)}) collective-permute-start(f32[25,16,128]{2,1,0:T(8,128)S(1)} %get-tuple-element.52), channel_id=1, source_target_pairs={{0,2},{2,0},{4,6},{6,4},{1,3},{3,1},{5,7},{7,5},{8,10},{10,8},{12,... | collective-permute-start | bytes 614408 | tf_op jit(solution)/shard_map/ppermute | solution.py:531
  31.5 1.3 %collective-permute-start.11 = (f32[25,16,128]{2,1,0:T(8,128)S(1)}, f32[25,16,128]{2,1,0:T(8,128)S(1)}, u32[]{:S(2)}, u32[]{:S(2)}) collective-permute-start(f32[25,16,128]{2,1,0:T(8,128)S(1)} %get-tuple-element.53), channel_id=1, source_target_pairs={{0,6},{2,4},{4,2},{6,0},{1,7},{3,5},{5,3},{7,1},{8,14},{10,12},{12... | collective-permute-start | bytes 614408 | tf_op jit(solution)/shard_map/ppermute | solution.py:531
  32.8 4.4 %collective-permute-done.10.eta_a = f32[25,16,128]{2,1,0:T(8,128)S(1)} collective-permute-done((f32[25,16,128]{2,1,0:T(8,128)S(1)}, f32[25,16,128]{2,1,0:T(8,128)S(1)}, u32[]{:S(2)}, u32[]{:S(2)}) %collective-permute-start.10) | collective-permute-done | bytes 204832 | tf_op jit(solution)/shard_map/ppermute | solution.py:531
  37.2 5.5 %collective-permute-done.11.eta_b = f32[25,16,128]{2,1,0:T(8,128)S(1)} collective-permute-done((f32[25,16,128]{2,1,0:T(8,128)S(1)}, f32[25,16,128]{2,1,0:T(8,128)S(1)}, u32[]{:S(2)}, u32[]{:S(2)}) %collective-permute-start.11) | collective-permute-done | bytes 204832 | tf_op jit(solution)/shard_map/ppermute | solution.py:531
  42.7 0.7 %shard_map.88 = (f32[5,256,128]{2,1,0:T(8,128)S(1)}, f32[25,16,128]{2,1,0:T(8,128)S(1)}, f32[25,16,128]{2,1,0:T(8,128)S(1)}) custom-call(f32[5,256,128]{2,1,0:T(8,128)S(1)} %get-tuple-element.51.state_ref, f32[25,16,128]{2,1,0:T(8,128)S(1)} %collective-permute-done.10.eta_a, f32[25,16,128]{2,1,0:T(8,128)S(1)} %collective-permute-done.11.eta_b), custom_call_target="tpu_custom_call" | custom-call | bytes 3600000 | tf_op jit(solution)/shard_map/pallas_call | solution.py:553
  43.5 0.1 collective-permute-start.12
  43.5 0.7 %collective-permute-start.13 = (f32[25,16,128]{2,1,0:T(8,128)S(1)}, f32[25,16,128]{2,1,0:T(8,128)S(1)}, u32[]{:S(2)}, u32[]{:S(2)}) collective-permute-start(f32[25,16,128]{2,1,0:T(8,128)S(1)} %get-tuple-element.56), channel_id=1, source_target_pairs={{0,24},{8,16},{16,8},{24,0},{1,25},{9,17},{17,9},{25,1},{2,26},{10... | collective-permute-start | bytes 614408 | tf_op jit(solution)/shard_map/ppermute | solution.py:531
  44.2 0.8 %collective-permute-done.12.xi_a = f32[25,16,128]{2,1,0:T(8,128)S(1)} collective-permute-done((f32[25,16,128]{2,1,0:T(8,128)S(1)}, f32[25,16,128]{2,1,0:T(8,128)S(1)}, u32[]{:S(2)}, u32[]{:S(2)}) %collective-permute-start.12) | collective-permute-done | bytes 204832 | tf_op jit(solution)/shard_map/ppermute | solution.py:531
  45.0 5.4 %collective-permute-done.13.xi_b = f32[25,16,128]{2,1,0:T(8,128)S(1)} collective-permute-done((f32[25,16,128]{2,1,0:T(8,128)S(1)}, f32[25,16,128]{2,1,0:T(8,128)S(1)}, u32[]{:S(2)}, u32[]{:S(2)}) %collective-permute-start.13) | collective-permute-done | bytes 204832 | tf_op jit(solution)/shard_map/ppermute | solution.py:531
  50.4 0.6 %shard_map.89 = (f32[5,256,128]{2,1,0:T(8,128)S(1)}, f32[5,24,128]{2,1,0:T(8,128)S(1)}) custom-call(f32[5,256,128]{2,1,0:T(8,128)S(1)} %get-tuple-element.54.state_ref, f32[25,16,128]{2,1,0:T(8,128)S(1)} %collective-permute-done.12.xi_a, f32[25,16,128]{2,1,0:T(8,128)S(1)} %collective-permute-done.13.xi_b), custom_call_target="tpu_custom_call" | custom-call | bytes 3600000 | tf_op jit(solution)/shard_map/pallas_call | solution.py:553
  51.0 0.6 %collective-permute-start.14 = (f32[5,24,128]{2,1,0:T(8,128)S(1)}, f32[5,24,128]{2,1,0:T(8,128)S(1)}, u32[]{:S(2)}, u32[]{:S(2)}) collective-permute-start(f32[5,24,128]{2,1,0:T(8,128)S(1)} %get-tuple-element.58), channel_id=1, source_target_pairs={{0,1},{1,0},{2,3},{3,2},{4,5},{5,4},{6,7},{7,6},{8,9},{9,8},{10,11... | collective-permute-start | bytes 184328 | tf_op jit(solution)/shard_map/ppermute | solution.py:537
  51.6 3.8 %collective-permute-done.14.below_ref.above_ref = f32[5,24,128]{2,1,0:T(8,128)S(1)} collective-permute-done((f32[5,24,128]{2,1,0:T(8,128)S(1)}, f32[5,24,128]{2,1,0:T(8,128)S(1)}, u32[]{:S(2)}, u32[]{:S(2)}) %collective-permute-start.14) | collective-permute-done | bytes 61472 | tf_op jit(solution)/shard_map/ppermute | solution.py:537
  55.4 1.2 %shard_map.90 = f32[5,256,128]{2,1,0:T(8,128)} custom-call(f32[5,256,128]{2,1,0:T(8,128)S(1)} %get-tuple-element.57.state_ref, f32[5,24,128]{2,1,0:T(8,128)S(1)} %collective-permute-done.14.below_ref.above_ref, f32[5,24,128]{2,1,0:T(8,128)S(1)} %collective-permute-done.14.below_ref.above_ref, bf16[256,256]{1,0:T(8,128)(2,1)S(1)} %get-tuple-element.59.smooth_ref, ...), custom_call_target="tpu_custom_call" | custom-call | bytes 3600000 | tf_op jit(solution)/shard_map/pallas_call | solution.py:553
  (7 shorter events, 0.0 us)
Async XLA Ops:
  0.0 1.1 %copy-start.1 = (f32[5,16,16,128]{3,2,1,0:T(8,128)S(1)}, f32[5,16,16,128]{3,2,1,0:T(8,128)}, u32[]{:S(2)}) copy-start(f32[5,16,16,128]{3,2,1,0:T(8,128)} %param.8) | copy-start | bytes 1966084
  1.1 0.9 %copy-start.7 = (bf16[256,256]{1,0:T(8,128)(2,1)S(1)}, bf16[256,256]{1,0:T(8,128)(2,1)}, u32[]{:S(2)}) copy-start(bf16[256,256]{1,0:T(8,128)(2,1)} %constant.11.clone.sums_hbm) | copy-start | bytes 393220
  3.0 15.6 %collective-permute-start = (f32[8,16,128]{2,1,0:T(8,128)S(1)}, f32[8,16,128]{2,1,0:T(8,128)S(1)}, u32[]{:S(2)}, u32[]{:S(2)}) collective-permute-start(f32[8,16,128]{2,1,0:T(8,128)S(1)} %get-tuple-element.38), channel_id=1, source_target_pairs={{0,2},{2,0},{4,6},{6,4},{1,3},{3,1},{5,7},{7,5},{8,10},{10,8},{12,... | collective-permute-start | bytes 196616 | tf_op jit(solution)/shard_map/ppermute | solution.py:531
  6.1 12.6 %collective-permute-start.1 = (f32[8,16,128]{2,1,0:T(8,128)S(1)}, f32[8,16,128]{2,1,0:T(8,128)S(1)}, u32[]{:S(2)}, u32[]{:S(2)}) collective-permute-start(f32[8,16,128]{2,1,0:T(8,128)S(1)} %get-tuple-element.39), channel_id=1, source_target_pairs={{0,6},{2,4},{4,2},{6,0},{1,7},{3,5},{5,3},{7,1},{8,14},{10,12},{12... | collective-permute-start | bytes 196616 | tf_op jit(solution)/shard_map/ppermute | solution.py:531
  8.5 10.1 %collective-permute-start.2 = (f32[8,16,128]{2,1,0:T(8,128)S(1)}, f32[8,16,128]{2,1,0:T(8,128)S(1)}, u32[]{:S(2)}, u32[]{:S(2)}) collective-permute-start(f32[8,16,128]{2,1,0:T(8,128)S(1)} %get-tuple-element.40), channel_id=1, source_target_pairs={{0,8},{8,0},{16,24},{24,16},{1,9},{9,1},{17,25},{25,17},{2,10},{10... | collective-permute-start | bytes 196616 | tf_op jit(solution)/shard_map/ppermute | solution.py:531
  8.6 10.1 %collective-permute-start.3 = (f32[8,16,128]{2,1,0:T(8,128)S(1)}, f32[8,16,128]{2,1,0:T(8,128)S(1)}, u32[]{:S(2)}, u32[]{:S(2)}) collective-permute-start(f32[8,16,128]{2,1,0:T(8,128)S(1)} %get-tuple-element.41), channel_id=1, source_target_pairs={{0,24},{8,16},{16,8},{24,0},{1,25},{9,17},{17,9},{25,1},{2,26},{10... | collective-permute-start | bytes 196616 | tf_op jit(solution)/shard_map/ppermute | solution.py:531
  10.2 9.4 %collective-permute-start.4 = (f32[4,8,128]{2,1,0:T(8,128)S(1)}, f32[4,8,128]{2,1,0:T(8,128)S(1)}, u32[]{:S(2)}, u32[]{:S(2)}) collective-permute-start(f32[4,8,128]{2,1,0:T(8,128)S(1)} %get-tuple-element.34.refs_6_), channel_id=1, source_target_pairs={{0,1},{1,0},{2,3},{3,2},{4,5},{5,4},{6,7},{7,6},{8,9},{9,8},{10,11... | collective-permute-start | bytes 49160 | tf_op jit(solution)/shard_map/ppermute | solution.py:537
  11.7 1.3 %copy-start = (f32[3,3,16,16,128]{4,3,2,1,0:T(8,128)S(1)}, f32[3,3,16,16,128]{4,3,2,1,0:T(8,128)}, u32[]{:S(2)}) copy-start(f32[3,3,16,16,128]{4,3,2,1,0:T(8,128)} %param.9) | copy-start | bytes 3538948
  12.9 0.9 %copy-start.2 = (f32[16,16,128]{2,1,0:T(8,128)S(1)}, f32[16,16,128]{2,1,0:T(8,128)}, u32[]{:S(2)}) copy-start(f32[16,16,128]{2,1,0:T(8,128)} %param.10) | copy-start | bytes 393220
  13.9 0.9 %copy-start.3 = (bf16[256,256]{1,0:T(8,128)(2,1)S(1)}, bf16[256,256]{1,0:T(8,128)(2,1)}, u32[]{:S(2)}) copy-start(bf16[256,256]{1,0:T(8,128)(2,1)} %constant.14.clone.refs_5_) | copy-start | bytes 393220
  14.8 0.9 %copy-start.4 = (bf16[256,256]{1,0:T(8,128)(2,1)S(1)}, bf16[256,256]{1,0:T(8,128)(2,1)}, u32[]{:S(2)}) copy-start(bf16[256,256]{1,0:T(8,128)(2,1)} %constant.13.clone.refs_4_) | copy-start | bytes 393220
  15.7 0.9 %copy-start.5 = (bf16[256,256]{1,0:T(8,128)(2,1)S(1)}, bf16[256,256]{1,0:T(8,128)(2,1)}, u32[]{:S(2)}) copy-start(bf16[256,256]{1,0:T(8,128)(2,1)} %constant.12.clone.refs_3_) | copy-start | bytes 393220
  16.6 0.9 %copy-start.6 = (bf16[256,256]{1,0:T(8,128)(2,1)S(1)}, bf16[256,256]{1,0:T(8,128)(2,1)}, u32[]{:S(2)}) copy-start(bf16[256,256]{1,0:T(8,128)(2,1)} %constant.10.clone.refs_2_) | copy-start | bytes 393220
  21.8 4.5 %collective-permute-start.5 = (f32[10,16,128]{2,1,0:T(8,128)S(1)}, f32[10,16,128]{2,1,0:T(8,128)S(1)}, u32[]{:S(2)}, u32[]{:S(2)}) collective-permute-start(f32[10,16,128]{2,1,0:T(8,128)S(1)} %get-tuple-element.46), channel_id=1, source_target_pairs={{0,2},{2,0},{4,6},{6,4},{1,3},{3,1},{5,7},{7,5},{8,10},{10,8},{12,... | collective-permute-start | bytes 245768 | tf_op jit(solution)/shard_map/ppermute | solution.py:531
  22.5 6.3 %collective-permute-start.6 = (f32[10,16,128]{2,1,0:T(8,128)S(1)}, f32[10,16,128]{2,1,0:T(8,128)S(1)}, u32[]{:S(2)}, u32[]{:S(2)}) collective-permute-start(f32[10,16,128]{2,1,0:T(8,128)S(1)} %get-tuple-element.47), channel_id=1, source_target_pairs={{0,6},{2,4},{4,2},{6,0},{1,7},{3,5},{5,3},{7,1},{8,14},{10,12},{12... | collective-permute-start | bytes 245768 | tf_op jit(solution)/shard_map/ppermute | solution.py:531
  23.4 5.4 %collective-permute-start.7 = (f32[10,16,128]{2,1,0:T(8,128)S(1)}, f32[10,16,128]{2,1,0:T(8,128)S(1)}, u32[]{:S(2)}, u32[]{:S(2)}) collective-permute-start(f32[10,16,128]{2,1,0:T(8,128)S(1)} %get-tuple-element.48), channel_id=1, source_target_pairs={{0,8},{8,0},{16,24},{24,16},{1,9},{9,1},{17,25},{25,17},{2,10},{10... | collective-permute-start | bytes 245768 | tf_op jit(solution)/shard_map/ppermute | solution.py:531
  23.4 5.4 %collective-permute-start.8 = (f32[10,16,128]{2,1,0:T(8,128)S(1)}, f32[10,16,128]{2,1,0:T(8,128)S(1)}, u32[]{:S(2)}, u32[]{:S(2)}) collective-permute-start(f32[10,16,128]{2,1,0:T(8,128)S(1)} %get-tuple-element.49), channel_id=1, source_target_pairs={{0,24},{8,16},{16,8},{24,0},{1,25},{9,17},{17,9},{25,1},{2,26},{10... | collective-permute-start | bytes 245768 | tf_op jit(solution)/shard_map/ppermute | solution.py:531
  24.1 6.1 %collective-permute-start.9 = (f32[5,8,128]{2,1,0:T(8,128)S(1)}, f32[5,8,128]{2,1,0:T(8,128)S(1)}, u32[]{:S(2)}, u32[]{:S(2)}) collective-permute-start(f32[5,8,128]{2,1,0:T(8,128)S(1)} %get-tuple-element.50), channel_id=1, source_target_pairs={{0,1},{1,0},{2,3},{3,2},{4,5},{5,4},{6,7},{7,6},{8,9},{9,8},{10,11... | collective-permute-start | bytes 61448 | tf_op jit(solution)/shard_map/ppermute | solution.py:537
  30.7 6.5 %collective-permute-start.10 = (f32[25,16,128]{2,1,0:T(8,128)S(1)}, f32[25,16,128]{2,1,0:T(8,128)S(1)}, u32[]{:S(2)}, u32[]{:S(2)}) collective-permute-start(f32[25,16,128]{2,1,0:T(8,128)S(1)} %get-tuple-element.52), channel_id=1, source_target_pairs={{0,2},{2,0},{4,6},{6,4},{1,3},{3,1},{5,7},{7,5},{8,10},{10,8},{12,... | collective-permute-start | bytes 614408 | tf_op jit(solution)/shard_map/ppermute | solution.py:531
  31.5 11.2 %collective-permute-start.11 = (f32[25,16,128]{2,1,0:T(8,128)S(1)}, f32[25,16,128]{2,1,0:T(8,128)S(1)}, u32[]{:S(2)}, u32[]{:S(2)}) collective-permute-start(f32[25,16,128]{2,1,0:T(8,128)S(1)} %get-tuple-element.53), channel_id=1, source_target_pairs={{0,6},{2,4},{4,2},{6,0},{1,7},{3,5},{5,3},{7,1},{8,14},{10,12},{12... | collective-permute-start | bytes 614408 | tf_op jit(solution)/shard_map/ppermute | solution.py:531
  43.5 1.5 %collective-permute-start.12 = (f32[25,16,128]{2,1,0:T(8,128)S(1)}, f32[25,16,128]{2,1,0:T(8,128)S(1)}, u32[]{:S(2)}, u32[]{:S(2)}) collective-permute-start(f32[25,16,128]{2,1,0:T(8,128)S(1)} %get-tuple-element.55), channel_id=1, source_target_pairs={{0,8},{8,0},{16,24},{24,16},{1,9},{9,1},{17,25},{25,17},{2,10},{10... | collective-permute-start | bytes 614408 | tf_op jit(solution)/shard_map/ppermute | solution.py:531
  43.5 6.9 %collective-permute-start.13 = (f32[25,16,128]{2,1,0:T(8,128)S(1)}, f32[25,16,128]{2,1,0:T(8,128)S(1)}, u32[]{:S(2)}, u32[]{:S(2)}) collective-permute-start(f32[25,16,128]{2,1,0:T(8,128)S(1)} %get-tuple-element.56), channel_id=1, source_target_pairs={{0,24},{8,16},{16,8},{24,0},{1,25},{9,17},{17,9},{25,1},{2,26},{10... | collective-permute-start | bytes 614408 | tf_op jit(solution)/shard_map/ppermute | solution.py:531
  51.0 4.4 %collective-permute-start.14 = (f32[5,24,128]{2,1,0:T(8,128)S(1)}, f32[5,24,128]{2,1,0:T(8,128)S(1)}, u32[]{:S(2)}, u32[]{:S(2)}) collective-permute-start(f32[5,24,128]{2,1,0:T(8,128)S(1)} %get-tuple-element.58), channel_id=1, source_target_pairs={{0,1},{1,0},{2,3},{3,2},{4,5},{5,4},{6,7},{7,6},{8,9},{9,8},{10,11... | collective-permute-start | bytes 184328 | tf_op jit(solution)/shard_map/ppermute | solution.py:537

commit v3 on v2

--- a/solution.py
+++ b/solution.py
@@ -81,13 +81,6 @@
     return pivots[WIDTH - 2 :], row[:WIDTH], row[WIDTH : WIDTH + 3]
 
 
-def split_weights(table):
-    table = np.asarray(table, np.float32)
-    high = table.astype(jnp.bfloat16)
-    low = (table - high.astype(np.float32)).astype(jnp.bfloat16)
-    return np.block([[high, low], [high, np.zeros_like(low)]]).astype(jnp.bfloat16)
-
-
 def pad_rows(table):
     return np.concatenate([table, np.zeros((LANES - table.shape[0], table.shape[1]))], axis=0)
 
@@ -118,13 +111,11 @@
     )
     smooth = own_rows(*filter_system(length), length)
     ends = np.concatenate([smooth[:, :WIDTH], smooth[:, WIDTH + length :]], axis=1)
-    return {
-        "derive": split_weights(table[:, own].T),
-        "sums": split_weights(pad_columns(sums)),
-        "back": split_weights(pad_rows(back)),
-        "smooth": split_weights(smooth[:, own].T),
-        "ends": split_weights(pad_rows(ends.T)),
-    }
+    tables = [table[:, own].T, pad_columns(sums), pad_rows(back), smooth[:, own].T, pad_rows(ends.T)]
+    return np.stack(tables).astype(np.float32)
+
+
+DERIVE, SUMS, BACK, SMOOTH, ENDS = range(5)
 
 
 def twisted_solve(rights, pivots, off):
@@ -201,6 +192,13 @@
     return jnp.concatenate([high, low], axis=1)
 
 
+def split_weights(table):
+    high = table.astype(jnp.bfloat16)
+    low = (table - high.astype(jnp.float32)).astype(jnp.bfloat16)
+    top = jnp.concatenate([high, low], axis=1)
+    return jnp.concatenate([top, jnp.concatenate([high, jnp.zeros_like(low)], axis=1)], axis=0)
+
+
 def lane_product(values, weights):
     both = jnp.dot(split_values(values), weights, preferred_element_type=jnp.float32)
     return both[:, :LANES] + both[:, LANES:]
@@ -269,9 +267,9 @@
 
 def primitive_kernel(
     grid,
-    u_hbm, sums_hbm,
-    u_ref, sums_ref, prim_ref, eta_first, eta_second, xi_first, xi_second, zeta_ref,
-    sums_sem, u_sems,
+    u_hbm, tables_hbm,
+    u_ref, tables_ref, prim_ref, eta_first, eta_second, xi_first, xi_second, zeta_ref,
+    tables_sem, u_sems,
 ):
     chunks = u_sems.shape[0]
     step = grid.rows // chunks
@@ -281,7 +279,7 @@
         copy = pltpu.make_async_copy(u_hbm.at[:, rows, :], u_ref.at[:, rows, :], u_sems.at[index])
         copy.start()
         copies.append(copy)
-    weights = pltpu.make_async_copy(sums_hbm, sums_ref, sums_sem)
+    weights = pltpu.make_async_copy(tables_hbm, tables_ref, tables_sem)
     weights.start()
     for index in range(chunks):
         copies[index].wait()
@@ -305,8 +303,9 @@
             grid.eta_groups, grid.nx, odd("xi"), xi_first, xi_second, field,
         )
     weights.wait()
+    sums = split_weights(tables_ref[SUMS])
     for field in range(4):
-        zeta_ref[field] = pack_sums(prim_ref[field], sums_ref[...], grid)
+        zeta_ref[field] = pack_sums(prim_ref[field], sums, grid)
 
 
 def fetch_kernel(count, *refs):
@@ -321,7 +320,8 @@
         copy.wait()
 
 
-def slope_kernel(grid, prim_ref, eta_a, eta_b, xi_a, xi_b, derive_ref, slope_ref):
+def slope_kernel(grid, prim_ref, eta_a, eta_b, xi_a, xi_b, tables_ref, slope_ref):
+    derive = split_weights(tables_ref[DERIVE])
     for field in range(4):
         for group in range(grid.eta_groups):
             below, above = take_sums(xi_a, xi_b, odd("xi"), field, group)
@@ -333,18 +333,19 @@
             cells = [prim_ref[field, grid.eta_tile(i, group), :] for i in range(grid.ny)]
             for i, value in enumerate(derive_line(cells, below, above)):
                 slope_ref[1, field, grid.eta_tile(i, group), :] = value
-        slope_ref[2, field] = lane_product(prim_ref[field], derive_ref[...])
+        slope_ref[2, field] = lane_product(prim_ref[field], derive)
 
 
 def flux_kernel(
     grid,
-    u_ref, prim_ref, metrics_ref, jacobian_ref, slope_ref, zeta_below, zeta_above, back_ref, sums_ref,
+    u_ref, prim_ref, metrics_ref, jacobian_ref, slope_ref, zeta_below, zeta_above, tables_ref,
     contra_ref, eta_first, eta_second, xi_first, xi_second, zeta_ref,
     zeta_slope_ref,
 ):
+    back, sums = split_weights(tables_ref[BACK]), split_weights(tables_ref[SUMS])
     for field in range(4):
         halo = unpack_sums(zeta_below[field], zeta_above[field], grid)
-        zeta_slope_ref[field] = slope_ref[2, field] + lane_product(halo, back_ref[...])
+        zeta_slope_ref[field] = slope_ref[2, field] + lane_product(halo, back)
 
     step = TILE
 
@@ -404,12 +405,13 @@
             lambda position, group: contra_ref[0, field, grid.xi_tile(position, group), :],
             grid.eta_groups, grid.nx, odd("xi"), xi_first, xi_second, field,
         )
-        zeta_ref[field] = pack_sums(contra_ref[2, field], sums_ref[...], grid)
-
-
-def divergence_kernel(grid, contra_ref, eta_a, eta_b, xi_a, xi_b, derive_ref, total_ref):
+        zeta_ref[field] = pack_sums(contra_ref[2, field], sums, grid)
+
+
+def divergence_kernel(grid, contra_ref, eta_a, eta_b, xi_a, xi_b, tables_ref, total_ref):
+    derive = split_weights(tables_ref[DERIVE])
     for field in range(5):
-        total_ref[field] = lane_product(contra_ref[2, field], derive_ref[...])
+        total_ref[field] = lane_product(contra_ref[2, field], derive)
         for group in range(grid.xi_groups):
             below, above = take_sums(eta_a, eta_b, odd("eta"), field, group)
             cells = [contra_ref[1, field, grid.eta_tile(i, group), :] for i in range(grid.ny)]
@@ -426,13 +428,14 @@
 
 def step_kernel(
     grid,
-    u_ref, jacobian_ref, total_ref, zeta_below, zeta_above, back_ref,
+    u_ref, jacobian_ref, total_ref, zeta_below, zeta_above, tables_ref,
     state_ref, eta_first, eta_second,
 ):
+    back = split_weights(tables_ref[BACK])
     scale = step_duration * jacobian_ref[...]
     for field in range(5):
         halo = unpack_sums(zeta_below[field], zeta_above[field], grid)
-        total = total_ref[field] + lane_product(halo, back_ref[...])
+        total = total_ref[field] + lane_product(halo, back)
         state_ref[field] = u_ref[field] - scale * total
         send_cells(
             lambda position, group: state_ref[field, grid.eta_tile(position, group), :],
@@ -460,61 +463,78 @@
     return below, above
 
 
-def eta_filter_kernel(grid, state_ref, eta_a, eta_b, result_ref, xi_first, xi_second):
-    flag = odd("eta")
+def eta_filter_kernel(
+    grid, state_ref, eta_a, eta_b, result_ref, xi_first, xi_second, zeta_ref, edge_first, edge_second
+):
     for field in range(5):
         for group in range(grid.xi_groups):
-            below, above = take_cells(eta_a, eta_b, flag, field, group)
+            below, above = take_cells(eta_a, eta_b, odd("eta"), field, group)
             cells = [state_ref[field, grid.eta_tile(i, group), :] for i in range(grid.ny)]
             for i, value in enumerate(smooth_line(below + cells + above)):
                 result_ref[field, grid.eta_tile(i, group), :] = value
+    flag = odd("xi")
+    for field in range(5):
         send_cells(
             lambda position, group: result_ref[field, grid.xi_tile(position, group), :],
-            grid.eta_groups, grid.nx, odd("xi"), xi_first, xi_second, field,
+            grid.eta_groups, grid.nx, flag, xi_first, xi_second, field,
         )
-
-
-PACKED = 12
-
-
-def xi_filter_kernel(grid, state_ref, xi_a, xi_b, result_ref, zeta_ref):
+    lane = lax.broadcasted_iota(jnp.int32, (TILE, LANES), 1)
+    for position in range(grid.nx):
+        packed = None
+        for slot in range(5 * grid.eta_groups):
+            field, group = slot // grid.eta_groups, slot % grid.eta_groups
+            part = result_ref[field, grid.xi_tile(position, group), :]
+            part = pltpu.roll(part, WIDTH * (2 * slot + 1), axis=1)
+            packed = part if packed is None else jnp.where(lane >= 2 * WIDTH * slot, part, packed)
+        zeta_ref[group_rows(position), :] = packed
+    send_cells(
+        lambda position, group: zeta_ref[group_rows(position), :],
+        1, grid.nx, flag, edge_first, edge_second, 0,
+    )
+
+
+def xi_filter_kernel(grid, state_ref, xi_a, xi_b, tables_ref, result_ref):
+    smooth = split_weights(tables_ref[SMOOTH])
     flag = odd("xi")
-    tiles = grid.rows // TILE
     for field in range(5):
         for group in range(grid.eta_groups):
             below, above = take_cells(xi_a, xi_b, flag, field, group)
             cells = [state_ref[field, grid.xi_tile(i, group), :] for i in range(grid.nx)]
             for i, value in enumerate(smooth_line(below + cells + above)):
                 result_ref[field, grid.xi_tile(i, group), :] = value
-        lane = lax.broadcasted_iota(jnp.int32, (TILE, LANES), 1)
-        for start in range(0, tiles, PACKED):
-            packed = None
-            for slot in range(min(PACKED, tiles - start)):
-                part = result_ref[field, group_rows(start + slot), :]
-                part = pltpu.roll(part, WIDTH + 2 * WIDTH * slot, axis=1)
-                packed = part if packed is None else jnp.where(lane >= 2 * WIDTH * slot, part, packed)
-            zeta_ref[field, group_rows(start // PACKED), :] = packed
+        result_ref[field] = lane_product(result_ref[field], smooth)
 
 
 def zeta_filter_kernel(
-    grid, state_ref, below_ref, above_ref, smooth_ref, ends_ref, result_hbm, result_ref, sems
+    grid,
+    state_ref, below_ref, above_ref, a_below, a_above, b_below, b_above, tables_ref,
+    result_hbm,
+    result_ref, sems,
 ):
+    ends = split_weights(tables_ref[ENDS])
+    flag = odd("xi")
+    lane = lax.broadcasted_iota(jnp.int32, (TILE, LANES), 1)
+    from_below = lax.rem(lane, 2 * WIDTH) < WIDTH
+
+    def merge(below, above, index):
+        return jnp.where(from_below, below[group_rows(index), :], above[group_rows(index), :])
+
+    low, high = [], []
+    for step in range(WIDTH):
+        first, second = merge(a_below, a_above, step), merge(b_below, b_above, step)
+        low.insert(0, jnp.where(flag, first, second))
+        high.append(jnp.where(flag, second, first))
+    cells = [merge(below_ref, above_ref, position) for position in range(grid.nx)]
+    cells = smooth_line(low + cells + high)
     copies = []
-    tiles = grid.rows // TILE
-    lane = lax.broadcasted_iota(jnp.int32, (TILE, LANES), 1)
     for field in range(5):
         parts = []
-        for start in range(0, tiles, PACKED):
-            rows = group_rows(start // PACKED)
-            packed = jnp.where(
-                lax.rem(lane, 2 * WIDTH) < WIDTH, below_ref[field, rows, :], above_ref[field, rows, :]
-            )
-            for slot in range(min(PACKED, tiles - start)):
+        for packed in cells:
+            for group in range(grid.eta_groups):
+                slot = field * grid.eta_groups + group
                 parts.append(pltpu.roll(packed, LANES - 2 * WIDTH * slot, axis=1) if slot else packed)
         halo = jnp.concatenate(parts, axis=0)
-        result_ref[field] = lane_product(state_ref[field], smooth_ref[...]) + lane_product(
-            halo, ends_ref[...]
-        )
+        result_ref[field] = state_ref[field] + lane_product(halo, ends)
         copy = pltpu.make_async_copy(result_ref.at[field], result_hbm.at[field], sems.at[field])
         copy.start()
         copies.append(copy)
@@ -529,6 +549,21 @@
         step = 1 if index % 2 == parity else -1
         pairs.append((index, (index + step) % count))
     return lax.ppermute(value, axis, pairs)
+
+
+def diagonal_swap(value, parity):
+    nx, nz = lax.axis_size("xi"), lax.axis_size("zeta")
+
+    def send(shift):
+        pairs = []
+        for i in range(nx):
+            partner = (i + (1 if i % 2 == parity else -1)) % nx
+            for k in range(nz):
+                pairs.append((i * nz + k, partner * nz + (k + shift) % nz))
+        return lax.ppermute(value, ("xi", "zeta"), pairs)
+
+    below = send(1)
+    return (below, below) if nz == 2 else (below, send(-1))
 
 
 def ring_swap(value, axis):
@@ -550,6 +585,10 @@
         for out in outs
     ]
     near = pltpu.MemorySpace.VMEM
+    operands = [
+        pltpu.with_memory_space_constraint(value, HBM) if index in far else value
+        for index, value in enumerate(operands)
+    ]
     return pl.pallas_call(
         kernel,
         out_shape=shapes,
@@ -576,8 +615,7 @@
     u = conserved_solution.reshape(5, rows, nz)
     metrics = metrics.reshape(9, rows, nz)
     jacobian = jacobian.reshape(rows, nz)
-    tables = {name: jnp.asarray(table) for name, table in zeta_tables(nz).items()}
-    packs = -(-(rows // TILE) // PACKED)
+    tables = jnp.asarray(zeta_tables(nz))
 
     def exchange(eta_first, eta_second, xi_first, xi_second, zeta):
         eta_b = pair_swap(eta_second, "eta", 1)
@@ -591,59 +629,62 @@
         return [(2 * fields, nx, nz)] * 2 + [(2 * fields, ny, nz)] * 2 + [(fields, TILE, LANES)]
 
     chunks = 4
-    u, sums, prim, *sends = call(
+    u, tables, prim, *sends = call(
         functools.partial(primitive_kernel, grid),
-        [like(u), like(tables["sums"]), (4, rows, nz)] + sums_shapes(4),
-        u, tables["sums"],
+        [like(u), like(tables), (4, rows, nz)] + sums_shapes(4),
+        u, tables,
         scratch=[pltpu.SemaphoreType.DMA, pltpu.SemaphoreType.DMA((chunks,))],
         far=(0, 1),
     )
     sides, ends = exchange(*sends)
-    fetched = [metrics, jacobian] + [tables[name] for name in ("derive", "back", "smooth", "ends")]
-    metrics, jacobian, derive, back, smooth, smooth_ends = call(
-        functools.partial(fetch_kernel, len(fetched)),
-        [like(value) for value in fetched],
-        *fetched, sends[-1],
-        scratch=[pltpu.SemaphoreType.DMA((len(fetched),))],
-        far=tuple(range(len(fetched))),
+    metrics, jacobian = call(
+        functools.partial(fetch_kernel, 2),
+        [like(metrics), like(jacobian)],
+        metrics, jacobian, sends[-1],
+        scratch=[pltpu.SemaphoreType.DMA((2,))],
+        far=(0, 1),
     )
     (slopes,) = call(
-        functools.partial(slope_kernel, grid), [(3, 4, rows, nz)], prim, *sides, derive,
+        functools.partial(slope_kernel, grid), [(3, 4, rows, nz)], prim, *sides, tables,
     )
     contra, *sends = call(
         functools.partial(flux_kernel, grid),
         [(3, 5, rows, nz)] + sums_shapes(5),
-        u, prim, metrics, jacobian, slopes, *ends, back, sums,
+        u, prim, metrics, jacobian, slopes, *ends, tables,
         scratch=[pltpu.VMEM((4, rows, nz), jnp.float32)],
     )
     sides, ends = exchange(*sends)
     (total,) = call(
-        functools.partial(divergence_kernel, grid), [(5, rows, nz)], contra, *sides, derive,
+        functools.partial(divergence_kernel, grid), [(5, rows, nz)], contra, *sides, tables,
     )
     state, eta_first, eta_second = call(
         functools.partial(step_kernel, grid),
         [(5, rows, nz)] + [(5 * WIDTH, nx, nz)] * 2,
-        u, jacobian, total, *ends, back,
+        u, jacobian, total, *ends, tables,
     )
     eta_b = pair_swap(eta_second, "eta", 1)
     eta_a = pair_swap(eta_first, "eta", 0)
-    state, xi_first, xi_second = call(
+    state, xi_first, xi_second, zeta, edge_first, edge_second = call(
         functools.partial(eta_filter_kernel, grid),
-        [(5, rows, nz)] + [(5 * WIDTH, ny, nz)] * 2,
+        [(5, rows, nz)]
+        + [(5 * WIDTH, ny, nz)] * 2
+        + [(nx * TILE, LANES)]
+        + [(WIDTH, TILE, LANES)] * 2,
         state, eta_a, eta_b,
     )
     xi_b = pair_swap(xi_second, "xi", 1)
+    ends = ring_swap(zeta, "zeta")
+    edges_b = diagonal_swap(edge_second, 1)
+    edges_a = diagonal_swap(edge_first, 0)
     xi_a = pair_swap(xi_first, "xi", 0)
-    state, zeta = call(
-        functools.partial(xi_filter_kernel, grid),
-        [(5, rows, nz), (5, packs * TILE, LANES)],
-        state, xi_a, xi_b,
-    )
-    below, above = ring_swap(zeta, "zeta")
+    (state,) = call(
+        functools.partial(xi_filter_kernel, grid), [(5, rows, nz)], state, xi_a, xi_b, tables,
+    )
+    edges = [edge.reshape(WIDTH * TILE, LANES) for edge in (*edges_a, *edges_b)]
     (result,) = call(
         functools.partial(zeta_filter_kernel, grid),
         [(5, rows, nz)],
-        state, below, above, smooth, smooth_ends,
+        state, *ends, *edges, tables,
         scratch=[pltpu.VMEM((5, rows, nz), jnp.float32), pltpu.SemaphoreType.DMA((5,))],
         far_outs=(0,),
     )

time: 56.9 us -> 46.7 us (0.82)
  waiting for transfers between devices: 24.2 us -> 14.7 us
  local copies, waits for them, and re-layouts: 7.78 us -> 0 us
  starting transfers between devices: 14.9 us -> 20.9 us
  Pallas kernels: 9.62 us -> 10.8 us
    unnamed x16 -> x0, local copies, waits for them, and re-layouts: 7.78 us -> none
    ppermute x12, waiting for transfers between devices: 20.4 us -> 14.1 us  [pair_swap(): return lax.ppermute(value, axis, pairs)]
    ppermute x3, waiting for transfers between devices: 3.77 us -> 0.01 us  [ring_swap(): other = lax.ppermute(value, axis, [(0, 1), (1, 0)])]
    ppermute x0 -> x2, starting transfers between devices: none -> 2.16 us  [send(): return lax.ppermute(value, ('xi', 'zeta'), pairs)]
    ppermute x3, starting transfers between devices: 2.63 us -> 4.56 us  [ring_swap(): other = lax.ppermute(value, axis, [(0, 1), (1, 0)])]
    ppermute x12, starting transfers between devices: 12.3 us -> 14.2 us  [pair_swap(): return lax.ppermute(value, axis, pairs)]
    pallas_call x9, Pallas kernels: 9.62 us -> 10.8 us  [call(): pl.pallas_call(kernel, out_shape=shapes, in_specs=[pl.BlockSpec(memory_sp...]
    ppermute x0 -> x2, waiting for transfers between devices: none -> 0.65 us  [send(): return lax.ppermute(value, ('xi', 'zeta'), pairs)]
  transfers between devices with their start and end apart: 15 -> 17, of which waited for: 7 -> 5; matrix products, arithmetic and copies ran while one was open for 0% -> 0% of each run, Pallas kernels for 6% -> 9%
where the time goes in v3:
time: 46.7 us; the launch traced here: 46.5 us
  starting transfers between devices  20.9 us (45%)
  waiting for transfers between devices  14.7 us (31%)
  Pallas kernels  10.8 us (23%)
    ppermute x12, starting transfers between devices, pair_swap(): return lax.ppermute(value, axis, pairs)  14.2 us
    ppermute x12, waiting for transfers between devices, pair_swap(): return lax.ppermute(value, axis, pairs)  14.1 us
    pallas_call x9, Pallas kernels, call(): pl.pallas_call(kernel, out_shape=shapes, in_specs=[pl.BlockSpec(memory_sp...  10.8 us
    ppermute x3, starting transfers between devices, ring_swap(): other = lax.ppermute(value, axis, [(0, 1), (1, 0)])  4.56 us
    ppermute x2, starting transfers between devices, send(): return lax.ppermute(value, ('xi', 'zeta'), pairs)  2.16 us
  transfers between devices with their start and end apart: 17, of which 5 were waited for; matrix products, arithmetic and copies ran while one was open for 0% of the time, Pallas kernels for 9%

profile of v3, /device:TPU:0, one launch (start us, length us, event | category | flops | bytes accessed | tf_op | source)
XLA Modules:
  0.0 46.5 jit_solution(7557511728398859030)
XLA Ops:
  0.0 1.7 %shard_map.46 = (f32[5,256,128]{2,1,0:T(8,128)S(1)}, f32[5,128,128]{2,1,0:T(8,128)S(1)}, f32[4,256,128]{2,1,0:T(8,128)S(1)}, f32[8,16,128]{2,1,0:T(8,128)S(1)}, ...) custom-call(f32[5,256,128]{2,1,0:T(8,128)} %bitcast.11, ...), custom_call_target="tpu_custom_call" | custom-call | bytes 3600000 | tf_op jit(solution)/shard_map/pallas_call | solution.py:592
  1.7 3.1 %collective-permute-start = (f32[8,16,128]{2,1,0:T(8,128)S(1)}, f32[8,16,128]{2,1,0:T(8,128)S(1)}, u32[]{:S(2)}, u32[]{:S(2)}) collective-permute-start(f32[8,16,128]{2,1,0:T(8,128)S(1)} %get-tuple-element.35), channel_id=1, source_target_pairs={{0,2},{2,0},{4,6},{6,4},{1,3},{3,1},{5,7},{7,5},{8,10},{10,8},{12,... | collective-permute-start | bytes 196616 | tf_op jit(solution)/shard_map/ppermute | solution.py:551
  4.8 2.5 %collective-permute-start.1 = (f32[8,16,128]{2,1,0:T(8,128)S(1)}, f32[8,16,128]{2,1,0:T(8,128)S(1)}, u32[]{:S(2)}, u32[]{:S(2)}) collective-permute-start(f32[8,16,128]{2,1,0:T(8,128)S(1)} %get-tuple-element.36), channel_id=1, source_target_pairs={{0,6},{2,4},{4,2},{6,0},{1,7},{3,5},{5,3},{7,1},{8,14},{10,12},{12... | collective-permute-start | bytes 196616 | tf_op jit(solution)/shard_map/ppermute | solution.py:551
  7.3 0.0 collective-permute-start.2
  7.3 1.6 %collective-permute-start.3 = (f32[8,16,128]{2,1,0:T(8,128)S(1)}, f32[8,16,128]{2,1,0:T(8,128)S(1)}, u32[]{:S(2)}, u32[]{:S(2)}) collective-permute-start(f32[8,16,128]{2,1,0:T(8,128)S(1)} %get-tuple-element.38), channel_id=1, source_target_pairs={{0,24},{8,16},{16,8},{24,0},{1,25},{9,17},{17,9},{25,1},{2,26},{10... | collective-permute-start | bytes 196616 | tf_op jit(solution)/shard_map/ppermute | solution.py:551
  8.9 1.5 %collective-permute-start.4 = (f32[4,8,128]{2,1,0:T(8,128)S(1)}, f32[4,8,128]{2,1,0:T(8,128)S(1)}, u32[]{:S(2)}, u32[]{:S(2)}) collective-permute-start(f32[4,8,128]{2,1,0:T(8,128)S(1)} %get-tuple-element.31.refs_2_), channel_id=1, source_target_pairs={{0,1},{1,0},{2,3},{3,2},{4,5},{5,4},{6,7},{7,6},{8,9},{9,8},{10,11... | collective-permute-start | bytes 49160 | tf_op jit(solution)/shard_map/ppermute | solution.py:572
  10.4 1.3 %shard_map.47 = (f32[9,256,128]{2,1,0:T(8,128)S(1)}, f32[256,128]{1,0:T(8,128)S(1)}) custom-call(f32[9,256,128]{2,1,0:T(8,128)} %bitcast.10, f32[256,128]{1,0:T(8,128)} %bitcast.12, f32[4,8,128]{2,1,0:T(8,128)S(1)} %get-tuple-element.31.refs_2_), custom_call_target="tpu_custom_call" | custom-call | bytes 3600000 | tf_op jit(solution)/shard_map/pallas_call | solution.py:592
  11.7 0.0 collective-permute-done.eta_a
  11.7 0.0 collective-permute-done.1.eta_b
  11.7 0.0 collective-permute-done.2.xi_a
  11.8 0.0 collective-permute-done.3.xi_b
  11.8 0.9 %shard_map.48.slope_ref = f32[3,4,256,128]{3,2,1,0:T(8,128)S(1)} custom-call(f32[4,256,128]{2,1,0:T(8,128)S(1)} %get-tuple-element.33.prim_ref, f32[8,16,128]{2,1,0:T(8,128)S(1)} %collective-permute-done.eta_a, f32[8,16,128]{2,1,0:T(8,128)S(1)} %collective-permute-done.1.eta_b, f32[8,16,128]{2,1,0:T(8,128)S(1)} %collective-permute-done.2.xi_a, ...), custom_call_target="tpu_custom_call" | custom-call | bytes 3600000 | tf_op jit(solution)/shard_map/pallas_call | solution.py:592
  12.7 0.0 collective-permute-done.4.zeta_below.zeta_above
  12.7 2.2 %shard_map.49 = (f32[3,5,256,128]{3,2,1,0:T(8,128)S(1)}, f32[10,16,128]{2,1,0:T(8,128)S(1)}, f32[10,16,128]{2,1,0:T(8,128)S(1)}, f32[10,16,128]{2,1,0:T(8,128)S(...) custom-call(f32[5,256,128]{2,1,0:T(8,128)S(1)} %get-tuple-element.30.u_ref, ...), custom_call_target="tpu_custom_call" | custom-call | bytes 3600000 | tf_op jit(solution)/shard_map/pallas_call | solution.py:592
  14.9 0.7 %collective-permute-start.5 = (f32[10,16,128]{2,1,0:T(8,128)S(1)}, f32[10,16,128]{2,1,0:T(8,128)S(1)}, u32[]{:S(2)}, u32[]{:S(2)}) collective-permute-start(f32[10,16,128]{2,1,0:T(8,128)S(1)} %get-tuple-element.41), channel_id=1, source_target_pairs={{0,2},{2,0},{4,6},{6,4},{1,3},{3,1},{5,7},{7,5},{8,10},{10,8},{12,... | collective-permute-start | bytes 245768 | tf_op jit(solution)/shard_map/ppermute | solution.py:551
  15.6 1.0 %collective-permute-start.6 = (f32[10,16,128]{2,1,0:T(8,128)S(1)}, f32[10,16,128]{2,1,0:T(8,128)S(1)}, u32[]{:S(2)}, u32[]{:S(2)}) collective-permute-start(f32[10,16,128]{2,1,0:T(8,128)S(1)} %get-tuple-element.42), channel_id=1, source_target_pairs={{0,6},{2,4},{4,2},{6,0},{1,7},{3,5},{5,3},{7,1},{8,14},{10,12},{12... | collective-permute-start | bytes 245768 | tf_op jit(solution)/shard_map/ppermute | solution.py:551
  16.6 0.0 collective-permute-start.7
  16.7 1.6 %collective-permute-start.8 = (f32[10,16,128]{2,1,0:T(8,128)S(1)}, f32[10,16,128]{2,1,0:T(8,128)S(1)}, u32[]{:S(2)}, u32[]{:S(2)}) collective-permute-start(f32[10,16,128]{2,1,0:T(8,128)S(1)} %get-tuple-element.44), channel_id=1, source_target_pairs={{0,24},{8,16},{16,8},{24,0},{1,25},{9,17},{17,9},{25,1},{2,26},{10... | collective-permute-start | bytes 245768 | tf_op jit(solution)/shard_map/ppermute | solution.py:551
  18.2 1.5 %collective-permute-start.9 = (f32[5,8,128]{2,1,0:T(8,128)S(1)}, f32[5,8,128]{2,1,0:T(8,128)S(1)}, u32[]{:S(2)}, u32[]{:S(2)}) collective-permute-start(f32[5,8,128]{2,1,0:T(8,128)S(1)} %get-tuple-element.45), channel_id=1, source_target_pairs={{0,1},{1,0},{2,3},{3,2},{4,5},{5,4},{6,7},{7,6},{8,9},{9,8},{10,11... | collective-permute-start | bytes 61448 | tf_op jit(solution)/shard_map/ppermute | solution.py:572
  19.8 0.0 collective-permute-done.5.eta_a
  19.8 2.2 %collective-permute-done.6.eta_b = f32[10,16,128]{2,1,0:T(8,128)S(1)} collective-permute-done((f32[10,16,128]{2,1,0:T(8,128)S(1)}, f32[10,16,128]{2,1,0:T(8,128)S(1)}, u32[]{:S(2)}, u32[]{:S(2)}) %collective-permute-start.6) | collective-permute-done | bytes 81952 | tf_op jit(solution)/shard_map/ppermute | solution.py:551
  22.0 0.0 collective-permute-done.7.xi_a
  22.0 0.0 collective-permute-done.8.xi_b
  22.0 1.3 %shard_map.50.total_ref = f32[5,256,128]{2,1,0:T(8,128)S(1)} custom-call(f32[3,5,256,128]{3,2,1,0:T(8,128)S(1)} %get-tuple-element.40.contra_ref, f32[10,16,128]{2,1,0:T(8,128)S(1)} %collective-permute-done.5.eta_a, f32[10,16,128]{2,1,0:T(8,128)S(1)} %collective-permute-done.6.eta_b, f32[10,16,128]{2,1,0:T(8,128)S(1)} %collective-permute-done.7.xi_a, ...), custom_call_target="tpu_custom_call" | custom-call | bytes 3600000 | tf_op jit(solution)/shard_map/pallas_call | solution.py:592
  23.3 0.0 collective-permute-done.9.zeta_below.zeta_above
  23.4 0.5 %shard_map.51 = (f32[5,256,128]{2,1,0:T(8,128)S(1)}, f32[25,16,128]{2,1,0:T(8,128)S(1)}, f32[25,16,128]{2,1,0:T(8,128)S(1)}) custom-call(f32[5,256,128]{2,1,0:T(8,128)S(1)} %get-tuple-element.30.u_ref, f32[256,128]{1,0:T(8,128)S(1)} %get-tuple-element.32.jacobian_ref, f32[5,256,128]{2,1,0:T(8,128)S(1)} %shard_map.50.total_ref, ...), custom_call_target="tpu_custom_call" | custom-call | bytes 3600000 | tf_op jit(solution)/shard_map/pallas_call | solution.py:592
  23.9 0.8 %collective-permute-start.10 = (f32[25,16,128]{2,1,0:T(8,128)S(1)}, f32[25,16,128]{2,1,0:T(8,128)S(1)}, u32[]{:S(2)}, u32[]{:S(2)}) collective-permute-start(f32[25,16,128]{2,1,0:T(8,128)S(1)} %get-tuple-element.47), channel_id=1, source_target_pairs={{0,2},{2,0},{4,6},{6,4},{1,3},{3,1},{5,7},{7,5},{8,10},{10,8},{12,... | collective-permute-start | bytes 614408 | tf_op jit(solution)/shard_map/ppermute | solution.py:551
  24.6 1.6 %collective-permute-start.11 = (f32[25,16,128]{2,1,0:T(8,128)S(1)}, f32[25,16,128]{2,1,0:T(8,128)S(1)}, u32[]{:S(2)}, u32[]{:S(2)}) collective-permute-start(f32[25,16,128]{2,1,0:T(8,128)S(1)} %get-tuple-element.48), channel_id=1, source_target_pairs={{0,6},{2,4},{4,2},{6,0},{1,7},{3,5},{5,3},{7,1},{8,14},{10,12},{12... | collective-permute-start | bytes 614408 | tf_op jit(solution)/shard_map/ppermute | solution.py:551
  26.3 4.2 %collective-permute-done.10.eta_a = f32[25,16,128]{2,1,0:T(8,128)S(1)} collective-permute-done((f32[25,16,128]{2,1,0:T(8,128)S(1)}, f32[25,16,128]{2,1,0:T(8,128)S(1)}, u32[]{:S(2)}, u32[]{:S(2)}) %collective-permute-start.10) | collective-permute-done | bytes 204832 | tf_op jit(solution)/shard_map/ppermute | solution.py:551
  30.4 5.6 %collective-permute-done.11.eta_b = f32[25,16,128]{2,1,0:T(8,128)S(1)} collective-permute-done((f32[25,16,128]{2,1,0:T(8,128)S(1)}, f32[25,16,128]{2,1,0:T(8,128)S(1)}, u32[]{:S(2)}, u32[]{:S(2)}) %collective-permute-start.11) | collective-permute-done | bytes 204832 | tf_op jit(solution)/shard_map/ppermute | solution.py:551
  36.1 0.9 %shard_map.52 = (f32[5,256,128]{2,1,0:T(8,128)S(1)}, f32[25,16,128]{2,1,0:T(8,128)S(1)}, f32[25,16,128]{2,1,0:T(8,128)S(1)}, f32[128,128]{1,0:T(8,128)S(1)}, f32...) custom-call(f32[5,256,128]{2,1,0:T(8,128)S(1)} %get-tuple-element.46.state_ref, ...), custom_call_target="tpu_custom_call" | custom-call | bytes 3600000 | tf_op jit(solution)/shard_map/pallas_call | solution.py:592
  36.9 0.1 collective-permute-start.12
  37.0 1.2 %collective-permute-start.13 = (f32[25,16,128]{2,1,0:T(8,128)S(1)}, f32[25,16,128]{2,1,0:T(8,128)S(1)}, u32[]{:S(2)}, u32[]{:S(2)}) collective-permute-start(f32[25,16,128]{2,1,0:T(8,128)S(1)} %get-tuple-element.51), channel_id=1, source_target_pairs={{0,24},{8,16},{16,8},{24,0},{1,25},{9,17},{17,9},{25,1},{2,26},{10... | collective-permute-start | bytes 614408 | tf_op jit(solution)/shard_map/ppermute | solution.py:551
  38.2 1.5 %collective-permute-start.14 = (f32[128,128]{1,0:T(8,128)S(1)}, f32[128,128]{1,0:T(8,128)S(1)}, u32[]{:S(2)}, u32[]{:S(2)}) collective-permute-start(f32[128,128]{1,0:T(8,128)S(1)} %get-tuple-element.52), channel_id=1, source_target_pairs={{0,1},{1,0},{2,3},{3,2},{4,5},{5,4},{6,7},{7,6},{8,9},{9,8},{10,11... | collective-permute-start | bytes 196616 | tf_op jit(solution)/shard_map/ppermute | solution.py:572
  39.7 0.0 collective-permute-start.15
  39.7 2.2 %collective-permute-start.16 = (f32[5,8,128]{2,1,0:T(8,128)S(1)}, f32[5,8,128]{2,1,0:T(8,128)S(1)}, u32[]{:S(2)}, u32[]{:S(2)}) collective-permute-start(f32[5,8,128]{2,1,0:T(8,128)S(1)} %get-tuple-element.54), channel_id=1, source_target_pairs={{0,25},{1,24},{8,17},{9,16},{16,9},{17,8},{24,1},{25,0},{2,27},{3,... | collective-permute-start | bytes 61448 | tf_op jit(solution)/shard_map/ppermute | solution.py:563
  41.9 0.0 collective-permute-done.12.xi_a
  41.9 2.0 %collective-permute-done.13.xi_b = f32[25,16,128]{2,1,0:T(8,128)S(1)} collective-permute-done((f32[25,16,128]{2,1,0:T(8,128)S(1)}, f32[25,16,128]{2,1,0:T(8,128)S(1)}, u32[]{:S(2)}, u32[]{:S(2)}) %collective-permute-start.13) | collective-permute-done | bytes 204832 | tf_op jit(solution)/shard_map/ppermute | solution.py:551
  43.9 0.7 %shard_map.53.state_ref = f32[5,256,128]{2,1,0:T(8,128)S(1)} custom-call(f32[5,256,128]{2,1,0:T(8,128)S(1)} %get-tuple-element.49.state_ref, f32[25,16,128]{2,1,0:T(8,128)S(1)} %collective-permute-done.12.xi_a, f32[25,16,128]{2,1,0:T(8,128)S(1)} %collective-permute-done.13.xi_b, f32[5,128,128]{2,1,0:T(8,128)S(1)} %get-tuple-element.39.tables_ref), custom_call_target="tpu_custom_call" | custom-call | bytes 3600000 | tf_op jit(solution)/shard_map/pallas_call | solution.py:592
  44.6 0.0 collective-permute-done.15
  44.6 0.6 %collective-permute-done.16 = f32[5,8,128]{2,1,0:T(8,128)S(1)} collective-permute-done((f32[5,8,128]{2,1,0:T(8,128)S(1)}, f32[5,8,128]{2,1,0:T(8,128)S(1)}, u32[]{:S(2)}, u32[]{:S(2)}) %collective-permute-start.16) | collective-permute-done | bytes 20512 | tf_op jit(solution)/shard_map/ppermute | solution.py:563
  45.3 0.0 collective-permute-done.14.below_ref.above_ref
  45.3 1.2 %shard_map.54 = f32[5,256,128]{2,1,0:T(8,128)} custom-call(f32[5,256,128]{2,1,0:T(8,128)S(1)} %shard_map.53.state_ref, f32[128,128]{1,0:T(8,128)S(1)} %collective-permute-done.14.below_ref.above_ref, f32[128,128]{1,0:T(8,128)S(1)} %collective-permute-done.14.below_ref.above_ref, f32[40,128]{1,0:T(8,128)S(1)} %bitcast.6, f32[40,128]{1,0:T(8,128)S(1)} %bitcast.7, ...), custom_call_target="tpu_custom_call" | custom-call | bytes 3600000 | tf_op jit(solution)/shard_map/pallas_call | solution.py:592
Async XLA Ops:
  1.7 10.0 %collective-permute-start = (f32[8,16,128]{2,1,0:T(8,128)S(1)}, f32[8,16,128]{2,1,0:T(8,128)S(1)}, u32[]{:S(2)}, u32[]{:S(2)}) collective-permute-start(f32[8,16,128]{2,1,0:T(8,128)S(1)} %get-tuple-element.35), channel_id=1, source_target_pairs={{0,2},{2,0},{4,6},{6,4},{1,3},{3,1},{5,7},{7,5},{8,10},{10,8},{12,... | collective-permute-start | bytes 196616 | tf_op jit(solution)/shard_map/ppermute | solution.py:551
  4.8 6.9 %collective-permute-start.1 = (f32[8,16,128]{2,1,0:T(8,128)S(1)}, f32[8,16,128]{2,1,0:T(8,128)S(1)}, u32[]{:S(2)}, u32[]{:S(2)}) collective-permute-start(f32[8,16,128]{2,1,0:T(8,128)S(1)} %get-tuple-element.36), channel_id=1, source_target_pairs={{0,6},{2,4},{4,2},{6,0},{1,7},{3,5},{5,3},{7,1},{8,14},{10,12},{12... | collective-permute-start | bytes 196616 | tf_op jit(solution)/shard_map/ppermute | solution.py:551
  7.3 4.4 %collective-permute-start.2 = (f32[8,16,128]{2,1,0:T(8,128)S(1)}, f32[8,16,128]{2,1,0:T(8,128)S(1)}, u32[]{:S(2)}, u32[]{:S(2)}) collective-permute-start(f32[8,16,128]{2,1,0:T(8,128)S(1)} %get-tuple-element.37), channel_id=1, source_target_pairs={{0,8},{8,0},{16,24},{24,16},{1,9},{9,1},{17,25},{25,17},{2,10},{10... | collective-permute-start | bytes 196616 | tf_op jit(solution)/shard_map/ppermute | solution.py:551
  7.3 4.5 %collective-permute-start.3 = (f32[8,16,128]{2,1,0:T(8,128)S(1)}, f32[8,16,128]{2,1,0:T(8,128)S(1)}, u32[]{:S(2)}, u32[]{:S(2)}) collective-permute-start(f32[8,16,128]{2,1,0:T(8,128)S(1)} %get-tuple-element.38), channel_id=1, source_target_pairs={{0,24},{8,16},{16,8},{24,0},{1,25},{9,17},{17,9},{25,1},{2,26},{10... | collective-permute-start | bytes 196616 | tf_op jit(solution)/shard_map/ppermute | solution.py:551
  8.9 3.8 %collective-permute-start.4 = (f32[4,8,128]{2,1,0:T(8,128)S(1)}, f32[4,8,128]{2,1,0:T(8,128)S(1)}, u32[]{:S(2)}, u32[]{:S(2)}) collective-permute-start(f32[4,8,128]{2,1,0:T(8,128)S(1)} %get-tuple-element.31.refs_2_), channel_id=1, source_target_pairs={{0,1},{1,0},{2,3},{3,2},{4,5},{5,4},{6,7},{7,6},{8,9},{9,8},{10,11... | collective-permute-start | bytes 49160 | tf_op jit(solution)/shard_map/ppermute | solution.py:572
  14.9 4.9 %collective-permute-start.5 = (f32[10,16,128]{2,1,0:T(8,128)S(1)}, f32[10,16,128]{2,1,0:T(8,128)S(1)}, u32[]{:S(2)}, u32[]{:S(2)}) collective-permute-start(f32[10,16,128]{2,1,0:T(8,128)S(1)} %get-tuple-element.41), channel_id=1, source_target_pairs={{0,2},{2,0},{4,6},{6,4},{1,3},{3,1},{5,7},{7,5},{8,10},{10,8},{12,... | collective-permute-start | bytes 245768 | tf_op jit(solution)/shard_map/ppermute | solution.py:551
  15.6 6.3 %collective-permute-start.6 = (f32[10,16,128]{2,1,0:T(8,128)S(1)}, f32[10,16,128]{2,1,0:T(8,128)S(1)}, u32[]{:S(2)}, u32[]{:S(2)}) collective-permute-start(f32[10,16,128]{2,1,0:T(8,128)S(1)} %get-tuple-element.42), channel_id=1, source_target_pairs={{0,6},{2,4},{4,2},{6,0},{1,7},{3,5},{5,3},{7,1},{8,14},{10,12},{12... | collective-permute-start | bytes 245768 | tf_op jit(solution)/shard_map/ppermute | solution.py:551
  16.6 5.3 %collective-permute-start.7 = (f32[10,16,128]{2,1,0:T(8,128)S(1)}, f32[10,16,128]{2,1,0:T(8,128)S(1)}, u32[]{:S(2)}, u32[]{:S(2)}) collective-permute-start(f32[10,16,128]{2,1,0:T(8,128)S(1)} %get-tuple-element.43), channel_id=1, source_target_pairs={{0,8},{8,0},{16,24},{24,16},{1,9},{9,1},{17,25},{25,17},{2,10},{10... | collective-permute-start | bytes 245768 | tf_op jit(solution)/shard_map/ppermute | solution.py:551
  16.7 5.3 %collective-permute-start.8 = (f32[10,16,128]{2,1,0:T(8,128)S(1)}, f32[10,16,128]{2,1,0:T(8,128)S(1)}, u32[]{:S(2)}, u32[]{:S(2)}) collective-permute-start(f32[10,16,128]{2,1,0:T(8,128)S(1)} %get-tuple-element.44), channel_id=1, source_target_pairs={{0,24},{8,16},{16,8},{24,0},{1,25},{9,17},{17,9},{25,1},{2,26},{10... | collective-permute-start | bytes 245768 | tf_op jit(solution)/shard_map/ppermute | solution.py:551
  18.2 5.1 %collective-permute-start.9 = (f32[5,8,128]{2,1,0:T(8,128)S(1)}, f32[5,8,128]{2,1,0:T(8,128)S(1)}, u32[]{:S(2)}, u32[]{:S(2)}) collective-permute-start(f32[5,8,128]{2,1,0:T(8,128)S(1)} %get-tuple-element.45), channel_id=1, source_target_pairs={{0,1},{1,0},{2,3},{3,2},{4,5},{5,4},{6,7},{7,6},{8,9},{9,8},{10,11... | collective-permute-start | bytes 61448 | tf_op jit(solution)/shard_map/ppermute | solution.py:572
  23.9 6.6 %collective-permute-start.10 = (f32[25,16,128]{2,1,0:T(8,128)S(1)}, f32[25,16,128]{2,1,0:T(8,128)S(1)}, u32[]{:S(2)}, u32[]{:S(2)}) collective-permute-start(f32[25,16,128]{2,1,0:T(8,128)S(1)} %get-tuple-element.47), channel_id=1, source_target_pairs={{0,2},{2,0},{4,6},{6,4},{1,3},{3,1},{5,7},{7,5},{8,10},{10,8},{12,... | collective-permute-start | bytes 614408 | tf_op jit(solution)/shard_map/ppermute | solution.py:551
  24.6 11.4 %collective-permute-start.11 = (f32[25,16,128]{2,1,0:T(8,128)S(1)}, f32[25,16,128]{2,1,0:T(8,128)S(1)}, u32[]{:S(2)}, u32[]{:S(2)}) collective-permute-start(f32[25,16,128]{2,1,0:T(8,128)S(1)} %get-tuple-element.48), channel_id=1, source_target_pairs={{0,6},{2,4},{4,2},{6,0},{1,7},{3,5},{5,3},{7,1},{8,14},{10,12},{12... | collective-permute-start | bytes 614408 | tf_op jit(solution)/shard_map/ppermute | solution.py:551
  36.9 4.9 %collective-permute-start.12 = (f32[25,16,128]{2,1,0:T(8,128)S(1)}, f32[25,16,128]{2,1,0:T(8,128)S(1)}, u32[]{:S(2)}, u32[]{:S(2)}) collective-permute-start(f32[25,16,128]{2,1,0:T(8,128)S(1)} %get-tuple-element.50), channel_id=1, source_target_pairs={{0,8},{8,0},{16,24},{24,16},{1,9},{9,1},{17,25},{25,17},{2,10},{10... | collective-permute-start | bytes 614408 | tf_op jit(solution)/shard_map/ppermute | solution.py:551
  37.0 6.9 %collective-permute-start.13 = (f32[25,16,128]{2,1,0:T(8,128)S(1)}, f32[25,16,128]{2,1,0:T(8,128)S(1)}, u32[]{:S(2)}, u32[]{:S(2)}) collective-permute-start(f32[25,16,128]{2,1,0:T(8,128)S(1)} %get-tuple-element.51), channel_id=1, source_target_pairs={{0,24},{8,16},{16,8},{24,0},{1,25},{9,17},{17,9},{25,1},{2,26},{10... | collective-permute-start | bytes 614408 | tf_op jit(solution)/shard_map/ppermute | solution.py:551
  38.2 7.1 %collective-permute-start.14 = (f32[128,128]{1,0:T(8,128)S(1)}, f32[128,128]{1,0:T(8,128)S(1)}, u32[]{:S(2)}, u32[]{:S(2)}) collective-permute-start(f32[128,128]{1,0:T(8,128)S(1)} %get-tuple-element.52), channel_id=1, source_target_pairs={{0,1},{1,0},{2,3},{3,2},{4,5},{5,4},{6,7},{7,6},{8,9},{9,8},{10,11... | collective-permute-start | bytes 196616 | tf_op jit(solution)/shard_map/ppermute | solution.py:572
  39.7 4.9 %collective-permute-start.15 = (f32[5,8,128]{2,1,0:T(8,128)S(1)}, f32[5,8,128]{2,1,0:T(8,128)S(1)}, u32[]{:S(2)}, u32[]{:S(2)}) collective-permute-start(f32[5,8,128]{2,1,0:T(8,128)S(1)} %get-tuple-element.53), channel_id=1, source_target_pairs={{0,9},{1,8},{8,1},{9,0},{16,25},{17,24},{24,17},{25,16},{2,11},{3,... | collective-permute-start | bytes 61448 | tf_op jit(solution)/shard_map/ppermute | solution.py:563
  39.7 5.6 %collective-permute-start.16 = (f32[5,8,128]{2,1,0:T(8,128)S(1)}, f32[5,8,128]{2,1,0:T(8,128)S(1)}, u32[]{:S(2)}, u32[]{:S(2)}) collective-permute-start(f32[5,8,128]{2,1,0:T(8,128)S(1)} %get-tuple-element.54), channel_id=1, source_target_pairs={{0,25},{1,24},{8,17},{9,16},{16,9},{17,8},{24,1},{25,0},{2,27},{3,... | collective-permute-start | bytes 61448 | tf_op jit(solution)/shard_map/ppermute | solution.py:563

commit v4 on v3

--- a/solution.py
+++ b/solution.py
@@ -141,23 +141,32 @@
     return answer
 
 
-def derive_line(cells, below, above):
+def derive_source(cells):
     count = len(cells)
-    pivots, _, edge = derivative_parts(count)
+    _, _, edge = derivative_parts(count)
     near, far = 7.0 / 9.0, 1.0 / 36.0
     rights = [None] * count
-    rights[0] = below[0] + edge[0] * cells[0] + edge[1] * cells[1] + edge[2] * cells[2]
-    rights[1] = near * (cells[2] - cells[0]) + far * (cells[3] - below[1])
+    rights[0] = edge[0] * cells[0] + edge[1] * cells[1] + edge[2] * cells[2]
+    rights[1] = near * (cells[2] - cells[0]) + far * cells[3]
     for step in range(2, count - 2):
         rights[step] = near * (cells[step + 1] - cells[step - 1]) + far * (
             cells[step + 2] - cells[step - 2]
         )
-    rights[count - 2] = near * (cells[count - 1] - cells[count - 3]) + far * (
-        above[1] - cells[count - 4]
-    )
-    rights[count - 1] = above[0] - (
+    rights[count - 2] = near * (cells[count - 1] - cells[count - 3]) - far * cells[count - 4]
+    rights[count - 1] = -(
         edge[0] * cells[count - 1] + edge[1] * cells[count - 2] + edge[2] * cells[count - 3]
     )
+    return rights
+
+
+def derive_solve(rights, below, above):
+    pivots, _, _ = derivative_parts(len(rights))
+    rights = list(rights)
+    far = 1.0 / 36.0
+    rights[0] = rights[0] + below[0]
+    rights[1] = rights[1] - far * below[1]
+    rights[-2] = rights[-2] + far * above[1]
+    rights[-1] = rights[-1] + above[0]
     return twisted_solve(rights, pivots, 1.0 / 3.0)
 
 
@@ -169,20 +178,34 @@
     return total, cells[0]
 
 
-def smooth_line(cells):
-    count = len(cells) - 2 * WIDTH
+def smooth_source(cells):
+    count = len(cells)
     coeffs = filter_coefficients()
+    rights = []
+    for step in range(count):
+        total = coeffs[0] * cells[step]
+        for offset in range(1, WIDTH + 1):
+            around = [cells[i] for i in (step - offset, step + offset) if 0 <= i < count]
+            around = around[0] + around[1] if len(around) == 2 else around[0]
+            total = total + (0.5 * coeffs[offset]) * around
+        rights.append(total)
+    return rights
+
+
+def smooth_solve(rights, below, above):
+    count = len(rights)
+    coeffs = filter_coefficients()
+    rights = list(rights)
+    for step in range(WIDTH):
+        for cell in range(WIDTH - step):
+            factor = 0.5 * coeffs[step + cell + 1]
+            if step == 0 and cell == 0:
+                factor = factor - 0.4
+            rights[step] = rights[step] + factor * below[cell]
+            rights[count - 1 - step] = rights[count - 1 - step] + factor * above[cell]
     pivots = [1.0]
     for _ in range(count):
         pivots.append(1.0 - 0.16 / pivots[-1])
-    rights = []
-    for step in range(WIDTH, WIDTH + count):
-        total = coeffs[0] * cells[step]
-        for offset in range(1, WIDTH + 1):
-            total = total + (0.5 * coeffs[offset]) * (cells[step + offset] + cells[step - offset])
-        rights.append(total)
-    rights[0] = rights[0] - 0.4 * cells[WIDTH - 1]
-    rights[-1] = rights[-1] - 0.4 * cells[WIDTH + count]
     return twisted_solve(rights, pivots, 0.4)
 
 
@@ -215,6 +238,9 @@
 
     def eta_tile(self, position, group):
         return pl.ds(position + group * TILE * self.ny, TILE, stride=self.ny)
+
+    def eta_major(self, position, group):
+        return pl.ds(position * self.nx + group * TILE, TILE)
 
 
 def group_rows(group):
@@ -276,13 +302,17 @@
     copies = []
     for index in range(chunks):
         rows = pl.ds(index * step, step)
-        copy = pltpu.make_async_copy(u_hbm.at[:, rows, :], u_ref.at[:, rows, :], u_sems.at[index])
-        copy.start()
-        copies.append(copy)
+        for field in range(5):
+            copy = pltpu.make_async_copy(
+                u_hbm.at[field, rows, :], u_ref.at[field, rows, :], u_sems.at[index, field]
+            )
+            copy.start()
+            copies.append(copy)
     weights = pltpu.make_async_copy(tables_hbm, tables_ref, tables_sem)
     weights.start()
     for index in range(chunks):
-        copies[index].wait()
+        for copy in copies[5 * index : 5 * index + 5]:
+            copy.wait()
         rows = pl.ds(index * step, step)
         inverse = 1.0 / u_ref[0, rows, :]
         work = None
@@ -320,32 +350,54 @@
         copy.wait()
 
 
-def slope_kernel(grid, prim_ref, eta_a, eta_b, xi_a, xi_b, tables_ref, slope_ref):
+def derive_source_kernel(grid, fields, value_ref, tables_ref, xi_ref, eta_ref, zeta_ref):
+    parts = [value_ref.at[k] for k in range(3)] if len(value_ref.shape) == 4 else [value_ref] * 3
+    xi_value, eta_value, zeta_value = parts
     derive = split_weights(tables_ref[DERIVE])
+    for field in range(fields):
+        zeta_ref[field] = lane_product(zeta_value[field], derive)
+        for group in range(grid.eta_groups):
+            cells = [xi_value[field, grid.xi_tile(i, group), :] for i in range(grid.nx)]
+            for i, value in enumerate(derive_source(cells)):
+                xi_ref[field, grid.xi_tile(i, group), :] = value
+        for group in range(grid.xi_groups):
+            cells = [eta_value[field, grid.eta_tile(i, group), :] for i in range(grid.ny)]
+            for i, value in enumerate(derive_source(cells)):
+                eta_ref[field, grid.eta_major(i, group), :] = value
+
+
+def xi_derivative(grid, source_ref, xi_a, xi_b, field, group):
+    below, above = take_sums(xi_a, xi_b, odd("xi"), field, group)
+    rights = [source_ref[field, grid.xi_tile(i, group), :] for i in range(grid.nx)]
+    return derive_solve(rights, below, above)
+
+
+def eta_derivative(grid, source_ref, eta_a, eta_b, field, group):
+    below, above = take_sums(eta_a, eta_b, odd("eta"), field, group)
+    rights = [source_ref[field, grid.eta_major(i, group), :] for i in range(grid.ny)]
+    return derive_solve(rights, below, above)
+
+
+def slope_kernel(grid, xi_source, eta_source, eta_a, eta_b, xi_a, xi_b, slope_ref):
     for field in range(4):
         for group in range(grid.eta_groups):
-            below, above = take_sums(xi_a, xi_b, odd("xi"), field, group)
-            cells = [prim_ref[field, grid.xi_tile(i, group), :] for i in range(grid.nx)]
-            for i, value in enumerate(derive_line(cells, below, above)):
+            for i, value in enumerate(xi_derivative(grid, xi_source, xi_a, xi_b, field, group)):
                 slope_ref[0, field, grid.xi_tile(i, group), :] = value
         for group in range(grid.xi_groups):
-            below, above = take_sums(eta_a, eta_b, odd("eta"), field, group)
-            cells = [prim_ref[field, grid.eta_tile(i, group), :] for i in range(grid.ny)]
-            for i, value in enumerate(derive_line(cells, below, above)):
+            for i, value in enumerate(eta_derivative(grid, eta_source, eta_a, eta_b, field, group)):
                 slope_ref[1, field, grid.eta_tile(i, group), :] = value
-        slope_ref[2, field] = lane_product(prim_ref[field], derive)
 
 
 def flux_kernel(
     grid,
-    u_ref, prim_ref, metrics_ref, jacobian_ref, slope_ref, zeta_below, zeta_above, tables_ref,
+    u_ref, prim_ref, metrics_ref, jacobian_ref, slope_ref, own_ref, zeta_below, zeta_above, tables_ref,
     contra_ref, eta_first, eta_second, xi_first, xi_second, zeta_ref,
     zeta_slope_ref,
 ):
     back, sums = split_weights(tables_ref[BACK]), split_weights(tables_ref[SUMS])
     for field in range(4):
         halo = unpack_sums(zeta_below[field], zeta_above[field], grid)
-        zeta_slope_ref[field] = slope_ref[2, field] + lane_product(halo, back)
+        zeta_slope_ref[field] = own_ref[field] + lane_product(halo, back)
 
     step = TILE
 
@@ -354,38 +406,33 @@
         u = [u_ref[c, rows, :] for c in range(5)]
         speed = [prim_ref[c, rows, :] for c in range(3)]
         pressure = prim_ref[3, rows, :] * u[0]
-        jacobian = jacobian_ref[rows, :]
         metrics = [[metrics_ref[3 * k + j, rows, :] for j in range(3)] for k in range(3)]
+        scaled = (viscosity * jacobian_ref[rows, :])
+        scaled = [[scaled * metrics[k][j] for j in range(3)] for k in range(3)]
         physical = []
         for c in range(4):
             slopes = [slope_ref[0, c, rows, :], slope_ref[1, c, rows, :], zeta_slope_ref[c, rows, :]]
             physical.append(
                 [
-                    jacobian
-                    * (
-                        metrics[0][j] * slopes[0] + metrics[1][j] * slopes[1] + metrics[2][j] * slopes[2]
-                    )
+                    scaled[0][j] * slopes[0] + scaled[1][j] * slopes[1] + scaled[2][j] * slopes[2]
                     for j in range(3)
                 ]
             )
-        spread = (2.0 / 3.0 * viscosity) * (physical[0][0] + physical[1][1] + physical[2][2])
+        spread = (2.0 / 3.0) * (physical[0][0] + physical[1][1] + physical[2][2])
         stress = [[None] * 3 for _ in range(3)]
+        momentum = [[None] * 3 for _ in range(3)]
         for c in range(3):
-            stress[c][c] = (2.0 * viscosity) * physical[c][c] - spread
+            stress[c][c] = (physical[c][c] + physical[c][c]) - spread
+            momentum[c][c] = (u[1 + c] * speed[c] + pressure) - stress[c][c]
             for j in range(c):
-                stress[c][j] = stress[j][c] = viscosity * (physical[c][j] + physical[j][c])
+                stress[c][j] = stress[j][c] = physical[c][j] + physical[j][c]
+                momentum[c][j] = momentum[j][c] = u[1 + c] * speed[j] - stress[c][j]
         total = u[4] + pressure
         fluxes = []
         for j in range(3):
-            parts = [u[1 + j]]
-            for c in range(3):
-                carried = u[1 + c] * speed[j] - stress[c][j]
-                if c == j:
-                    carried = carried + pressure
-                parts.append(carried)
             worked = speed[0] * stress[0][j] + speed[1] * stress[1][j] + speed[2] * stress[2][j]
-            parts.append(total * speed[j] - worked - conduction * physical[3][j])
-            fluxes.append(parts)
+            energy = (total * speed[j] - worked) - (conduction / viscosity) * physical[3][j]
+            fluxes.append([u[1 + j], momentum[0][j], momentum[1][j], momentum[2][j], energy])
         for k in range(3):
             for f in range(5):
                 contra_ref[k, f, rows, :] = (
@@ -395,7 +442,7 @@
                 )
         return carry
 
-    lax.fori_loop(0, grid.rows // step, body, 0)
+    lax.fori_loop(0, grid.rows // step, body, 0, unroll=4)
     for field in range(5):
         send_sums(
             lambda position, group: contra_ref[1, field, grid.eta_tile(position, group), :],
@@ -408,20 +455,14 @@
         zeta_ref[field] = pack_sums(contra_ref[2, field], sums, grid)
 
 
-def divergence_kernel(grid, contra_ref, eta_a, eta_b, xi_a, xi_b, tables_ref, total_ref):
-    derive = split_weights(tables_ref[DERIVE])
-    for field in range(5):
-        total_ref[field] = lane_product(contra_ref[2, field], derive)
+def divergence_kernel(grid, xi_source, eta_source, own_ref, eta_a, eta_b, xi_a, xi_b, total_ref):
+    for field in range(5):
         for group in range(grid.xi_groups):
-            below, above = take_sums(eta_a, eta_b, odd("eta"), field, group)
-            cells = [contra_ref[1, field, grid.eta_tile(i, group), :] for i in range(grid.ny)]
-            for i, value in enumerate(derive_line(cells, below, above)):
+            for i, value in enumerate(eta_derivative(grid, eta_source, eta_a, eta_b, field, group)):
                 rows = grid.eta_tile(i, group)
-                total_ref[field, rows, :] = total_ref[field, rows, :] + value
+                total_ref[field, rows, :] = own_ref[field, rows, :] + value
         for group in range(grid.eta_groups):
-            below, above = take_sums(xi_a, xi_b, odd("xi"), field, group)
-            cells = [contra_ref[0, field, grid.xi_tile(i, group), :] for i in range(grid.nx)]
-            for i, value in enumerate(derive_line(cells, below, above)):
+            for i, value in enumerate(xi_derivative(grid, xi_source, xi_a, xi_b, field, group)):
                 rows = grid.xi_tile(i, group)
                 total_ref[field, rows, :] = total_ref[field, rows, :] + value
 
@@ -458,19 +499,35 @@
     for step in range(WIDTH):
         first = first_ref[WIDTH * field + step, group_rows(group), :]
         second = second_ref[WIDTH * field + step, group_rows(group), :]
-        below.insert(0, jnp.where(flag, first, second))
+        below.append(jnp.where(flag, first, second))
         above.append(jnp.where(flag, second, first))
     return below, above
 
 
+def eta_source_kernel(grid, state_ref, source_ref):
+    for field in range(5):
+        for group in range(grid.xi_groups):
+            cells = [state_ref[field, grid.eta_tile(i, group), :] for i in range(grid.ny)]
+            for i, value in enumerate(smooth_source(cells)):
+                source_ref[field, grid.eta_major(i, group), :] = value
+
+
+def xi_source_kernel(grid, state_ref, source_ref):
+    for field in range(5):
+        for group in range(grid.eta_groups):
+            cells = [state_ref[field, grid.xi_tile(i, group), :] for i in range(grid.nx)]
+            for i, value in enumerate(smooth_source(cells)):
+                source_ref[field, grid.xi_tile(i, group), :] = value
+
+
 def eta_filter_kernel(
-    grid, state_ref, eta_a, eta_b, result_ref, xi_first, xi_second, zeta_ref, edge_first, edge_second
+    grid, source_ref, eta_a, eta_b, result_ref, xi_first, xi_second, zeta_ref, edge_first, edge_second
 ):
     for field in range(5):
         for group in range(grid.xi_groups):
             below, above = take_cells(eta_a, eta_b, odd("eta"), field, group)
-            cells = [state_ref[field, grid.eta_tile(i, group), :] for i in range(grid.ny)]
-            for i, value in enumerate(smooth_line(below + cells + above)):
+            rights = [source_ref[field, grid.eta_major(i, group), :] for i in range(grid.ny)]
+            for i, value in enumerate(smooth_solve(rights, below, above)):
                 result_ref[field, grid.eta_tile(i, group), :] = value
     flag = odd("xi")
     for field in range(5):
@@ -493,14 +550,14 @@
     )
 
 
-def xi_filter_kernel(grid, state_ref, xi_a, xi_b, tables_ref, result_ref):
+def xi_filter_kernel(grid, source_ref, xi_a, xi_b, tables_ref, result_ref):
     smooth = split_weights(tables_ref[SMOOTH])
     flag = odd("xi")
     for field in range(5):
         for group in range(grid.eta_groups):
             below, above = take_cells(xi_a, xi_b, flag, field, group)
-            cells = [state_ref[field, grid.xi_tile(i, group), :] for i in range(grid.nx)]
-            for i, value in enumerate(smooth_line(below + cells + above)):
+            rights = [source_ref[field, grid.xi_tile(i, group), :] for i in range(grid.nx)]
+            for i, value in enumerate(smooth_solve(rights, below, above)):
                 result_ref[field, grid.xi_tile(i, group), :] = value
         result_ref[field] = lane_product(result_ref[field], smooth)
 
@@ -522,10 +579,10 @@
     low, high = [], []
     for step in range(WIDTH):
         first, second = merge(a_below, a_above, step), merge(b_below, b_above, step)
-        low.insert(0, jnp.where(flag, first, second))
+        low.append(jnp.where(flag, first, second))
         high.append(jnp.where(flag, second, first))
     cells = [merge(below_ref, above_ref, position) for position in range(grid.nx)]
-    cells = smooth_line(low + cells + high)
+    cells = smooth_solve(smooth_source(cells), low, high)
     copies = []
     for field in range(5):
         parts = []
@@ -628,12 +685,12 @@
     def sums_shapes(fields):
         return [(2 * fields, nx, nz)] * 2 + [(2 * fields, ny, nz)] * 2 + [(fields, TILE, LANES)]
 
-    chunks = 4
+    chunks = 2
     u, tables, prim, *sends = call(
         functools.partial(primitive_kernel, grid),
         [like(u), like(tables), (4, rows, nz)] + sums_shapes(4),
         u, tables,
-        scratch=[pltpu.SemaphoreType.DMA, pltpu.SemaphoreType.DMA((chunks,))],
+        scratch=[pltpu.SemaphoreType.DMA, pltpu.SemaphoreType.DMA((chunks, 5))],
         far=(0, 1),
     )
     sides, ends = exchange(*sends)
@@ -644,18 +701,28 @@
         scratch=[pltpu.SemaphoreType.DMA((2,))],
         far=(0, 1),
     )
+    xi_source, eta_source, own = call(
+        functools.partial(derive_source_kernel, grid, 4),
+        [(4, rows, nz)] * 3,
+        prim, tables,
+    )
     (slopes,) = call(
-        functools.partial(slope_kernel, grid), [(3, 4, rows, nz)], prim, *sides, tables,
+        functools.partial(slope_kernel, grid), [(2, 4, rows, nz)], xi_source, eta_source, *sides,
     )
     contra, *sends = call(
         functools.partial(flux_kernel, grid),
         [(3, 5, rows, nz)] + sums_shapes(5),
-        u, prim, metrics, jacobian, slopes, *ends, tables,
+        u, prim, metrics, jacobian, slopes, own, *ends, tables,
         scratch=[pltpu.VMEM((4, rows, nz), jnp.float32)],
     )
     sides, ends = exchange(*sends)
+    xi_source, eta_source, own = call(
+        functools.partial(derive_source_kernel, grid, 5), [(5, rows, nz)] * 3, contra, tables,
+    )
     (total,) = call(
-        functools.partial(divergence_kernel, grid), [(5, rows, nz)], contra, *sides, tables,
+        functools.partial(divergence_kernel, grid),
+        [(5, rows, nz)],
+        xi_source, eta_source, own, *sides,
     )
     state, eta_first, eta_second = call(
         functools.partial(step_kernel, grid),
@@ -664,21 +731,23 @@
     )
     eta_b = pair_swap(eta_second, "eta", 1)
     eta_a = pair_swap(eta_first, "eta", 0)
+    (source,) = call(functools.partial(eta_source_kernel, grid), [(5, rows, nz)], state)
     state, xi_first, xi_second, zeta, edge_first, edge_second = call(
         functools.partial(eta_filter_kernel, grid),
         [(5, rows, nz)]
         + [(5 * WIDTH, ny, nz)] * 2
         + [(nx * TILE, LANES)]
         + [(WIDTH, TILE, LANES)] * 2,
-        state, eta_a, eta_b,
+        source, eta_a, eta_b,
     )
     xi_b = pair_swap(xi_second, "xi", 1)
     ends = ring_swap(zeta, "zeta")
     edges_b = diagonal_swap(edge_second, 1)
     edges_a = diagonal_swap(edge_first, 0)
     xi_a = pair_swap(xi_first, "xi", 0)
+    (source,) = call(functools.partial(xi_source_kernel, grid), [(5, rows, nz)], state)
     (state,) = call(
-        functools.partial(xi_filter_kernel, grid), [(5, rows, nz)], state, xi_a, xi_b, tables,
+        functools.partial(xi_filter_kernel, grid), [(5, rows, nz)], source, xi_a, xi_b, tables,
     )
     edges = [edge.reshape(WIDTH * TILE, LANES) for edge in (*edges_a, *edges_b)]
     (result,) = call(

time: 46.7 us -> 45 us (0.964)
  starting transfers between devices: 20.9 us -> 20 us
  Pallas kernels: 10.8 us -> 10.3 us
    ppermute x12, starting transfers between devices: 14.2 us -> 13.1 us  [pair_swap(): return lax.ppermute(value, axis, pairs)]
    ppermute x12, waiting for transfers between devices: 14.1 us -> 13.4 us  [pair_swap(): return lax.ppermute(value, axis, pairs)]
    pallas_call x9 -> x13, Pallas kernels: 10.8 us -> 10.3 us  [call(): pl.pallas_call(kernel, out_shape=shapes, in_specs=[pl.BlockSpec(memory_sp...]
  transfers between devices with their start and end apart: 17 -> 17, of which waited for: 5 -> 5; matrix products, arithmetic and copies ran while one was open for 0% -> 0% of each run, Pallas kernels for 9% -> 10%
where the time goes in v4:
time: 45 us; the launch traced here: 44.8 us
  starting transfers between devices  20 us (44%)
  waiting for transfers between devices  14.4 us (32%)
  Pallas kernels  10.3 us (23%)
    ppermute x12, waiting for transfers between devices, pair_swap(): return lax.ppermute(value, axis, pairs)  13.4 us
    ppermute x12, starting transfers between devices, pair_swap(): return lax.ppermute(value, axis, pairs)  13.1 us
    pallas_call x13, Pallas kernels, call(): pl.pallas_call(kernel, out_shape=shapes, in_specs=[pl.BlockSpec(memory_sp...  10.3 us
    ppermute x3, starting transfers between devices, ring_swap(): other = lax.ppermute(value, axis, [(0, 1), (1, 0)])  4.56 us
    ppermute x2, starting transfers between devices, send(): return lax.ppermute(value, ('xi', 'zeta'), pairs)  2.38 us
    ppermute x2, waiting for transfers between devices, send(): return lax.ppermute(value, ('xi', 'zeta'), pairs)  0.91 us
  transfers between devices with their start and end apart: 17, of which 5 were waited for; matrix products, arithmetic and copies ran while one was open for 0% of the time, Pallas kernels for 10%

profile of v4, /device:TPU:0, one launch (start us, length us, event | category | flops | bytes accessed | tf_op | source)
XLA Modules:
  0.0 44.8 jit_solution(11496186913768370974)
XLA Ops:
  0.0 1.8 %shard_map.46 = (f32[5,256,128]{2,1,0:T(8,128)S(1)}, f32[5,128,128]{2,1,0:T(8,128)S(1)}, f32[4,256,128]{2,1,0:T(8,128)S(1)}, f32[8,16,128]{2,1,0:T(8,128)S(1)}, ...) custom-call(f32[5,256,128]{2,1,0:T(8,128)} %bitcast.11, ...), custom_call_target="tpu_custom_call" | custom-call | bytes 3600000 | tf_op jit(solution)/shard_map/pallas_call | solution.py:649
  1.8 3.1 %collective-permute-start = (f32[8,16,128]{2,1,0:T(8,128)S(1)}, f32[8,16,128]{2,1,0:T(8,128)S(1)}, u32[]{:S(2)}, u32[]{:S(2)}) collective-permute-start(f32[8,16,128]{2,1,0:T(8,128)S(1)} %get-tuple-element.44), channel_id=1, source_target_pairs={{0,2},{2,0},{4,6},{6,4},{1,3},{3,1},{5,7},{7,5},{8,10},{10,8},{12,... | collective-permute-start | bytes 196616 | tf_op jit(solution)/shard_map/ppermute | solution.py:608
  4.9 2.5 %collective-permute-start.1 = (f32[8,16,128]{2,1,0:T(8,128)S(1)}, f32[8,16,128]{2,1,0:T(8,128)S(1)}, u32[]{:S(2)}, u32[]{:S(2)}) collective-permute-start(f32[8,16,128]{2,1,0:T(8,128)S(1)} %get-tuple-element.45), channel_id=1, source_target_pairs={{0,6},{2,4},{4,2},{6,0},{1,7},{3,5},{5,3},{7,1},{8,14},{10,12},{12... | collective-permute-start | bytes 196616 | tf_op jit(solution)/shard_map/ppermute | solution.py:608
  7.3 0.0 collective-permute-start.2
  7.3 1.6 %collective-permute-start.3 = (f32[8,16,128]{2,1,0:T(8,128)S(1)}, f32[8,16,128]{2,1,0:T(8,128)S(1)}, u32[]{:S(2)}, u32[]{:S(2)}) collective-permute-start(f32[8,16,128]{2,1,0:T(8,128)S(1)} %get-tuple-element.47), channel_id=1, source_target_pairs={{0,24},{8,16},{16,8},{24,0},{1,25},{9,17},{17,9},{25,1},{2,26},{10... | collective-permute-start | bytes 196616 | tf_op jit(solution)/shard_map/ppermute | solution.py:608
  8.9 1.5 %collective-permute-start.4 = (f32[4,8,128]{2,1,0:T(8,128)S(1)}, f32[4,8,128]{2,1,0:T(8,128)S(1)}, u32[]{:S(2)}, u32[]{:S(2)}) collective-permute-start(f32[4,8,128]{2,1,0:T(8,128)S(1)} %get-tuple-element.37.refs_2_), channel_id=1, source_target_pairs={{0,1},{1,0},{2,3},{3,2},{4,5},{5,4},{6,7},{7,6},{8,9},{9,8},{10,11... | collective-permute-start | bytes 49160 | tf_op jit(solution)/shard_map/ppermute | solution.py:629
  10.5 1.3 %shard_map.47 = (f32[9,256,128]{2,1,0:T(8,128)S(1)}, f32[256,128]{1,0:T(8,128)S(1)}) custom-call(f32[9,256,128]{2,1,0:T(8,128)} %bitcast.10, f32[256,128]{1,0:T(8,128)} %bitcast.12, f32[4,8,128]{2,1,0:T(8,128)S(1)} %get-tuple-element.37.refs_2_), custom_call_target="tpu_custom_call" | custom-call | bytes 3600000 | tf_op jit(solution)/shard_map/pallas_call | solution.py:649
  11.8 0.5 %shard_map.48 = (f32[4,256,128]{2,1,0:T(8,128)S(1)}, f32[4,256,128]{2,1,0:T(8,128)S(1)}, f32[4,256,128]{2,1,0:T(8,128)S(1)}) custom-call(f32[4,256,128]{2,1,0:T(8,128)S(1)} %get-tuple-element.39.value_ref.prim_ref, f32[5,128,128]{2,1,0:T(8,128)S(1)} %get-tuple-element.41.tables_ref), custom_call_target="tpu_custom_call" | custom-call | bytes 3600000 | tf_op jit(solution)/shard_map/pallas_call | solution.py:649
  12.3 0.0 collective-permute-done.eta_a
  12.3 0.0 collective-permute-done.1.eta_b
  12.3 0.0 collective-permute-done.2.xi_a
  12.3 0.0 collective-permute-done.3.xi_b
  12.3 0.3 shard_map.49.slope_ref
  12.7 0.0 collective-permute-done.4.zeta_below.zeta_above
  12.7 1.8 %shard_map.50 = (f32[3,5,256,128]{3,2,1,0:T(8,128)S(1)}, f32[10,16,128]{2,1,0:T(8,128)S(1)}, f32[10,16,128]{2,1,0:T(8,128)S(1)}, f32[10,16,128]{2,1,0:T(8,128)S(...) custom-call(f32[5,256,128]{2,1,0:T(8,128)S(1)} %get-tuple-element.36.u_ref, ...), custom_call_target="tpu_custom_call" | custom-call | bytes 3600000 | tf_op jit(solution)/shard_map/pallas_call | solution.py:649
  14.5 0.7 %collective-permute-start.5 = (f32[10,16,128]{2,1,0:T(8,128)S(1)}, f32[10,16,128]{2,1,0:T(8,128)S(1)}, u32[]{:S(2)}, u32[]{:S(2)}) collective-permute-start(f32[10,16,128]{2,1,0:T(8,128)S(1)} %get-tuple-element.53), channel_id=1, source_target_pairs={{0,2},{2,0},{4,6},{6,4},{1,3},{3,1},{5,7},{7,5},{8,10},{10,8},{12,... | collective-permute-start | bytes 245768 | tf_op jit(solution)/shard_map/ppermute | solution.py:608
  15.3 0.9 %collective-permute-start.6 = (f32[10,16,128]{2,1,0:T(8,128)S(1)}, f32[10,16,128]{2,1,0:T(8,128)S(1)}, u32[]{:S(2)}, u32[]{:S(2)}) collective-permute-start(f32[10,16,128]{2,1,0:T(8,128)S(1)} %get-tuple-element.54), channel_id=1, source_target_pairs={{0,6},{2,4},{4,2},{6,0},{1,7},{3,5},{5,3},{7,1},{8,14},{10,12},{12... | collective-permute-start | bytes 245768 | tf_op jit(solution)/shard_map/ppermute | solution.py:608
  16.2 0.0 collective-permute-start.7
  16.2 1.2 %collective-permute-start.8 = (f32[10,16,128]{2,1,0:T(8,128)S(1)}, f32[10,16,128]{2,1,0:T(8,128)S(1)}, u32[]{:S(2)}, u32[]{:S(2)}) collective-permute-start(f32[10,16,128]{2,1,0:T(8,128)S(1)} %get-tuple-element.56), channel_id=1, source_target_pairs={{0,24},{8,16},{16,8},{24,0},{1,25},{9,17},{17,9},{25,1},{2,26},{10... | collective-permute-start | bytes 245768 | tf_op jit(solution)/shard_map/ppermute | solution.py:608
  17.3 1.5 %collective-permute-start.9 = (f32[5,8,128]{2,1,0:T(8,128)S(1)}, f32[5,8,128]{2,1,0:T(8,128)S(1)}, u32[]{:S(2)}, u32[]{:S(2)}) collective-permute-start(f32[5,8,128]{2,1,0:T(8,128)S(1)} %get-tuple-element.57), channel_id=1, source_target_pairs={{0,1},{1,0},{2,3},{3,2},{4,5},{5,4},{6,7},{7,6},{8,9},{9,8},{10,11... | collective-permute-start | bytes 61448 | tf_op jit(solution)/shard_map/ppermute | solution.py:629
  18.9 0.6 %shard_map.51 = (f32[5,256,128]{2,1,0:T(8,128)S(1)}, f32[5,256,128]{2,1,0:T(8,128)S(1)}, f32[5,256,128]{2,1,0:T(8,128)S(1)}) custom-call(f32[3,5,256,128]{3,2,1,0:T(8,128)S(1)} %get-tuple-element.49.value_ref, f32[5,128,128]{2,1,0:T(8,128)S(1)} %get-tuple-element.41.tables_ref), custom_call_target="tpu_custom_call" | custom-call | bytes 3600000 | tf_op jit(solution)/shard_map/pallas_call | solution.py:649
  19.4 0.0 collective-permute-done.5.eta_a
  19.5 2.2 %collective-permute-done.6.eta_b = f32[10,16,128]{2,1,0:T(8,128)S(1)} collective-permute-done((f32[10,16,128]{2,1,0:T(8,128)S(1)}, f32[10,16,128]{2,1,0:T(8,128)S(1)}, u32[]{:S(2)}, u32[]{:S(2)}) %collective-permute-start.6) | collective-permute-done | bytes 81952 | tf_op jit(solution)/shard_map/ppermute | solution.py:608
  21.6 0.0 collective-permute-done.7.xi_a
  21.6 0.0 collective-permute-done.8.xi_b
  21.6 0.6 %shard_map.52.total_ref = f32[5,256,128]{2,1,0:T(8,128)S(1)} custom-call(f32[5,256,128]{2,1,0:T(8,128)S(1)} %get-tuple-element.50.xi_source, f32[5,256,128]{2,1,0:T(8,128)S(1)} %get-tuple-element.51.eta_source, f32[5,256,128]{2,1,0:T(8,128)S(1)} %get-tuple-element.52.own_ref, f32[10,16,128]{2,1,0:T(8,128)S(1)} %collective-permute-done.5.eta_a, ...), custom_call_target="tpu_custom_call" | custom-call | bytes 3600000 | tf_op jit(solution)/shard_map/pallas_call | solution.py:649
  22.2 0.0 collective-permute-done.9.zeta_below.zeta_above
  22.3 0.5 %shard_map.53 = (f32[5,256,128]{2,1,0:T(8,128)S(1)}, f32[25,16,128]{2,1,0:T(8,128)S(1)}, f32[25,16,128]{2,1,0:T(8,128)S(1)}) custom-call(f32[5,256,128]{2,1,0:T(8,128)S(1)} %get-tuple-element.36.u_ref, f32[256,128]{1,0:T(8,128)S(1)} %get-tuple-element.38.jacobian_ref, f32[5,256,128]{2,1,0:T(8,128)S(1)} %shard_map.52.total_ref, ...), custom_call_target="tpu_custom_call" | custom-call | bytes 3600000 | tf_op jit(solution)/shard_map/pallas_call | solution.py:649
  22.8 0.7 %collective-permute-start.10 = (f32[25,16,128]{2,1,0:T(8,128)S(1)}, f32[25,16,128]{2,1,0:T(8,128)S(1)}, u32[]{:S(2)}, u32[]{:S(2)}) collective-permute-start(f32[25,16,128]{2,1,0:T(8,128)S(1)} %get-tuple-element.59), channel_id=1, source_target_pairs={{0,2},{2,0},{4,6},{6,4},{1,3},{3,1},{5,7},{7,5},{8,10},{10,8},{12,... | collective-permute-start | bytes 614408 | tf_op jit(solution)/shard_map/ppermute | solution.py:608
  23.5 1.3 %collective-permute-start.11 = (f32[25,16,128]{2,1,0:T(8,128)S(1)}, f32[25,16,128]{2,1,0:T(8,128)S(1)}, u32[]{:S(2)}, u32[]{:S(2)}) collective-permute-start(f32[25,16,128]{2,1,0:T(8,128)S(1)} %get-tuple-element.60), channel_id=1, source_target_pairs={{0,6},{2,4},{4,2},{6,0},{1,7},{3,5},{5,3},{7,1},{8,14},{10,12},{12... | collective-permute-start | bytes 614408 | tf_op jit(solution)/shard_map/ppermute | solution.py:608
  24.8 0.4 shard_map.54.source_ref
  25.2 4.0 %collective-permute-done.10.eta_a = f32[25,16,128]{2,1,0:T(8,128)S(1)} collective-permute-done((f32[25,16,128]{2,1,0:T(8,128)S(1)}, f32[25,16,128]{2,1,0:T(8,128)S(1)}, u32[]{:S(2)}, u32[]{:S(2)}) %collective-permute-start.10) | collective-permute-done | bytes 204832 | tf_op jit(solution)/shard_map/ppermute | solution.py:608
  29.2 5.5 %collective-permute-done.11.eta_b = f32[25,16,128]{2,1,0:T(8,128)S(1)} collective-permute-done((f32[25,16,128]{2,1,0:T(8,128)S(1)}, f32[25,16,128]{2,1,0:T(8,128)S(1)}, u32[]{:S(2)}, u32[]{:S(2)}) %collective-permute-start.11) | collective-permute-done | bytes 204832 | tf_op jit(solution)/shard_map/ppermute | solution.py:608
  34.8 0.5 %shard_map.55 = (f32[5,256,128]{2,1,0:T(8,128)S(1)}, f32[25,16,128]{2,1,0:T(8,128)S(1)}, f32[25,16,128]{2,1,0:T(8,128)S(1)}, f32[128,128]{1,0:T(8,128)S(1)}, f32...) custom-call(f32[5,256,128]{2,1,0:T(8,128)S(1)} %shard_map.54.source_ref, ...), custom_call_target="tpu_custom_call" | custom-call | bytes 3600000 | tf_op jit(solution)/shard_map/pallas_call | solution.py:649
  35.3 0.1 collective-permute-start.12
  35.4 0.9 %collective-permute-start.13 = (f32[25,16,128]{2,1,0:T(8,128)S(1)}, f32[25,16,128]{2,1,0:T(8,128)S(1)}, u32[]{:S(2)}, u32[]{:S(2)}) collective-permute-start(f32[25,16,128]{2,1,0:T(8,128)S(1)} %get-tuple-element.63), channel_id=1, source_target_pairs={{0,24},{8,16},{16,8},{24,0},{1,25},{9,17},{17,9},{25,1},{2,26},{10... | collective-permute-start | bytes 614408 | tf_op jit(solution)/shard_map/ppermute | solution.py:608
  36.3 1.5 %collective-permute-start.14 = (f32[128,128]{1,0:T(8,128)S(1)}, f32[128,128]{1,0:T(8,128)S(1)}, u32[]{:S(2)}, u32[]{:S(2)}) collective-permute-start(f32[128,128]{1,0:T(8,128)S(1)} %get-tuple-element.64), channel_id=1, source_target_pairs={{0,1},{1,0},{2,3},{3,2},{4,5},{5,4},{6,7},{7,6},{8,9},{9,8},{10,11... | collective-permute-start | bytes 196616 | tf_op jit(solution)/shard_map/ppermute | solution.py:629
  37.8 0.0 collective-permute-start.15
  37.8 2.4 %collective-permute-start.16 = (f32[5,8,128]{2,1,0:T(8,128)S(1)}, f32[5,8,128]{2,1,0:T(8,128)S(1)}, u32[]{:S(2)}, u32[]{:S(2)}) collective-permute-start(f32[5,8,128]{2,1,0:T(8,128)S(1)} %get-tuple-element.66), channel_id=1, source_target_pairs={{0,25},{1,24},{8,17},{9,16},{16,9},{17,8},{24,1},{25,0},{2,27},{3,... | collective-permute-start | bytes 61448 | tf_op jit(solution)/shard_map/ppermute | solution.py:620
  40.2 0.3 shard_map.56.source_ref
  40.5 0.0 collective-permute-done.12.xi_a
  40.5 1.7 %collective-permute-done.13.xi_b = f32[25,16,128]{2,1,0:T(8,128)S(1)} collective-permute-done((f32[25,16,128]{2,1,0:T(8,128)S(1)}, f32[25,16,128]{2,1,0:T(8,128)S(1)}, u32[]{:S(2)}, u32[]{:S(2)}) %collective-permute-start.13) | collective-permute-done | bytes 204832 | tf_op jit(solution)/shard_map/ppermute | solution.py:608
  42.2 0.5 %shard_map.57.state_ref = f32[5,256,128]{2,1,0:T(8,128)S(1)} custom-call(f32[5,256,128]{2,1,0:T(8,128)S(1)} %shard_map.56.source_ref, f32[25,16,128]{2,1,0:T(8,128)S(1)} %collective-permute-done.12.xi_a, f32[25,16,128]{2,1,0:T(8,128)S(1)} %collective-permute-done.13.xi_b, f32[5,128,128]{2,1,0:T(8,128)S(1)} %get-tuple-element.41.tables_ref), custom_call_target="tpu_custom_call" | custom-call | bytes 3600000 | tf_op jit(solution)/shard_map/pallas_call | solution.py:649
  42.7 0.0 collective-permute-done.15
  42.7 0.9 %collective-permute-done.16 = f32[5,8,128]{2,1,0:T(8,128)S(1)} collective-permute-done((f32[5,8,128]{2,1,0:T(8,128)S(1)}, f32[5,8,128]{2,1,0:T(8,128)S(1)}, u32[]{:S(2)}, u32[]{:S(2)}) %collective-permute-start.16) | collective-permute-done | bytes 20512 | tf_op jit(solution)/shard_map/ppermute | solution.py:620
  43.6 0.0 collective-permute-done.14.below_ref.above_ref
  43.6 1.2 %shard_map.58 = f32[5,256,128]{2,1,0:T(8,128)} custom-call(f32[5,256,128]{2,1,0:T(8,128)S(1)} %shard_map.57.state_ref, f32[128,128]{1,0:T(8,128)S(1)} %collective-permute-done.14.below_ref.above_ref, f32[128,128]{1,0:T(8,128)S(1)} %collective-permute-done.14.below_ref.above_ref, f32[40,128]{1,0:T(8,128)S(1)} %bitcast.6, f32[40,128]{1,0:T(8,128)S(1)} %bitcast.7, ...), custom_call_target="tpu_custom_call" | custom-call | bytes 3600000 | tf_op jit(solution)/shard_map/pallas_call | solution.py:649
Async XLA Ops:
  1.8 10.5 %collective-permute-start = (f32[8,16,128]{2,1,0:T(8,128)S(1)}, f32[8,16,128]{2,1,0:T(8,128)S(1)}, u32[]{:S(2)}, u32[]{:S(2)}) collective-permute-start(f32[8,16,128]{2,1,0:T(8,128)S(1)} %get-tuple-element.44), channel_id=1, source_target_pairs={{0,2},{2,0},{4,6},{6,4},{1,3},{3,1},{5,7},{7,5},{8,10},{10,8},{12,... | collective-permute-start | bytes 196616 | tf_op jit(solution)/shard_map/ppermute | solution.py:608
  4.9 7.4 %collective-permute-start.1 = (f32[8,16,128]{2,1,0:T(8,128)S(1)}, f32[8,16,128]{2,1,0:T(8,128)S(1)}, u32[]{:S(2)}, u32[]{:S(2)}) collective-permute-start(f32[8,16,128]{2,1,0:T(8,128)S(1)} %get-tuple-element.45), channel_id=1, source_target_pairs={{0,6},{2,4},{4,2},{6,0},{1,7},{3,5},{5,3},{7,1},{8,14},{10,12},{12... | collective-permute-start | bytes 196616 | tf_op jit(solution)/shard_map/ppermute | solution.py:608
  7.3 5.0 %collective-permute-start.2 = (f32[8,16,128]{2,1,0:T(8,128)S(1)}, f32[8,16,128]{2,1,0:T(8,128)S(1)}, u32[]{:S(2)}, u32[]{:S(2)}) collective-permute-start(f32[8,16,128]{2,1,0:T(8,128)S(1)} %get-tuple-element.46), channel_id=1, source_target_pairs={{0,8},{8,0},{16,24},{24,16},{1,9},{9,1},{17,25},{25,17},{2,10},{10... | collective-permute-start | bytes 196616 | tf_op jit(solution)/shard_map/ppermute | solution.py:608
  7.3 5.0 %collective-permute-start.3 = (f32[8,16,128]{2,1,0:T(8,128)S(1)}, f32[8,16,128]{2,1,0:T(8,128)S(1)}, u32[]{:S(2)}, u32[]{:S(2)}) collective-permute-start(f32[8,16,128]{2,1,0:T(8,128)S(1)} %get-tuple-element.47), channel_id=1, source_target_pairs={{0,24},{8,16},{16,8},{24,0},{1,25},{9,17},{17,9},{25,1},{2,26},{10... | collective-permute-start | bytes 196616 | tf_op jit(solution)/shard_map/ppermute | solution.py:608
  8.9 3.7 %collective-permute-start.4 = (f32[4,8,128]{2,1,0:T(8,128)S(1)}, f32[4,8,128]{2,1,0:T(8,128)S(1)}, u32[]{:S(2)}, u32[]{:S(2)}) collective-permute-start(f32[4,8,128]{2,1,0:T(8,128)S(1)} %get-tuple-element.37.refs_2_), channel_id=1, source_target_pairs={{0,1},{1,0},{2,3},{3,2},{4,5},{5,4},{6,7},{7,6},{8,9},{9,8},{10,11... | collective-permute-start | bytes 49160 | tf_op jit(solution)/shard_map/ppermute | solution.py:629
  14.5 4.9 %collective-permute-start.5 = (f32[10,16,128]{2,1,0:T(8,128)S(1)}, f32[10,16,128]{2,1,0:T(8,128)S(1)}, u32[]{:S(2)}, u32[]{:S(2)}) collective-permute-start(f32[10,16,128]{2,1,0:T(8,128)S(1)} %get-tuple-element.53), channel_id=1, source_target_pairs={{0,2},{2,0},{4,6},{6,4},{1,3},{3,1},{5,7},{7,5},{8,10},{10,8},{12,... | collective-permute-start | bytes 245768 | tf_op jit(solution)/shard_map/ppermute | solution.py:608
  15.3 6.3 %collective-permute-start.6 = (f32[10,16,128]{2,1,0:T(8,128)S(1)}, f32[10,16,128]{2,1,0:T(8,128)S(1)}, u32[]{:S(2)}, u32[]{:S(2)}) collective-permute-start(f32[10,16,128]{2,1,0:T(8,128)S(1)} %get-tuple-element.54), channel_id=1, source_target_pairs={{0,6},{2,4},{4,2},{6,0},{1,7},{3,5},{5,3},{7,1},{8,14},{10,12},{12... | collective-permute-start | bytes 245768 | tf_op jit(solution)/shard_map/ppermute | solution.py:608
  16.2 5.5 %collective-permute-start.7 = (f32[10,16,128]{2,1,0:T(8,128)S(1)}, f32[10,16,128]{2,1,0:T(8,128)S(1)}, u32[]{:S(2)}, u32[]{:S(2)}) collective-permute-start(f32[10,16,128]{2,1,0:T(8,128)S(1)} %get-tuple-element.55), channel_id=1, source_target_pairs={{0,8},{8,0},{16,24},{24,16},{1,9},{9,1},{17,25},{25,17},{2,10},{10... | collective-permute-start | bytes 245768 | tf_op jit(solution)/shard_map/ppermute | solution.py:608
  16.2 5.5 %collective-permute-start.8 = (f32[10,16,128]{2,1,0:T(8,128)S(1)}, f32[10,16,128]{2,1,0:T(8,128)S(1)}, u32[]{:S(2)}, u32[]{:S(2)}) collective-permute-start(f32[10,16,128]{2,1,0:T(8,128)S(1)} %get-tuple-element.56), channel_id=1, source_target_pairs={{0,24},{8,16},{16,8},{24,0},{1,25},{9,17},{17,9},{25,1},{2,26},{10... | collective-permute-start | bytes 245768 | tf_op jit(solution)/shard_map/ppermute | solution.py:608
  17.3 4.9 %collective-permute-start.9 = (f32[5,8,128]{2,1,0:T(8,128)S(1)}, f32[5,8,128]{2,1,0:T(8,128)S(1)}, u32[]{:S(2)}, u32[]{:S(2)}) collective-permute-start(f32[5,8,128]{2,1,0:T(8,128)S(1)} %get-tuple-element.57), channel_id=1, source_target_pairs={{0,1},{1,0},{2,3},{3,2},{4,5},{5,4},{6,7},{7,6},{8,9},{9,8},{10,11... | collective-permute-start | bytes 61448 | tf_op jit(solution)/shard_map/ppermute | solution.py:629
  22.8 6.5 %collective-permute-start.10 = (f32[25,16,128]{2,1,0:T(8,128)S(1)}, f32[25,16,128]{2,1,0:T(8,128)S(1)}, u32[]{:S(2)}, u32[]{:S(2)}) collective-permute-start(f32[25,16,128]{2,1,0:T(8,128)S(1)} %get-tuple-element.59), channel_id=1, source_target_pairs={{0,2},{2,0},{4,6},{6,4},{1,3},{3,1},{5,7},{7,5},{8,10},{10,8},{12,... | collective-permute-start | bytes 614408 | tf_op jit(solution)/shard_map/ppermute | solution.py:608
  23.5 11.3 %collective-permute-start.11 = (f32[25,16,128]{2,1,0:T(8,128)S(1)}, f32[25,16,128]{2,1,0:T(8,128)S(1)}, u32[]{:S(2)}, u32[]{:S(2)}) collective-permute-start(f32[25,16,128]{2,1,0:T(8,128)S(1)} %get-tuple-element.60), channel_id=1, source_target_pairs={{0,6},{2,4},{4,2},{6,0},{1,7},{3,5},{5,3},{7,1},{8,14},{10,12},{12... | collective-permute-start | bytes 614408 | tf_op jit(solution)/shard_map/ppermute | solution.py:608
  35.3 5.2 %collective-permute-start.12 = (f32[25,16,128]{2,1,0:T(8,128)S(1)}, f32[25,16,128]{2,1,0:T(8,128)S(1)}, u32[]{:S(2)}, u32[]{:S(2)}) collective-permute-start(f32[25,16,128]{2,1,0:T(8,128)S(1)} %get-tuple-element.62), channel_id=1, source_target_pairs={{0,8},{8,0},{16,24},{24,16},{1,9},{9,1},{17,25},{25,17},{2,10},{10... | collective-permute-start | bytes 614408 | tf_op jit(solution)/shard_map/ppermute | solution.py:608
  35.4 6.9 %collective-permute-start.13 = (f32[25,16,128]{2,1,0:T(8,128)S(1)}, f32[25,16,128]{2,1,0:T(8,128)S(1)}, u32[]{:S(2)}, u32[]{:S(2)}) collective-permute-start(f32[25,16,128]{2,1,0:T(8,128)S(1)} %get-tuple-element.63), channel_id=1, source_target_pairs={{0,24},{8,16},{16,8},{24,0},{1,25},{9,17},{17,9},{25,1},{2,26},{10... | collective-permute-start | bytes 614408 | tf_op jit(solution)/shard_map/ppermute | solution.py:608
  36.3 7.3 %collective-permute-start.14 = (f32[128,128]{1,0:T(8,128)S(1)}, f32[128,128]{1,0:T(8,128)S(1)}, u32[]{:S(2)}, u32[]{:S(2)}) collective-permute-start(f32[128,128]{1,0:T(8,128)S(1)} %get-tuple-element.64), channel_id=1, source_target_pairs={{0,1},{1,0},{2,3},{3,2},{4,5},{5,4},{6,7},{7,6},{8,9},{9,8},{10,11... | collective-permute-start | bytes 196616 | tf_op jit(solution)/shard_map/ppermute | solution.py:629
  37.8 4.9 %collective-permute-start.15 = (f32[5,8,128]{2,1,0:T(8,128)S(1)}, f32[5,8,128]{2,1,0:T(8,128)S(1)}, u32[]{:S(2)}, u32[]{:S(2)}) collective-permute-start(f32[5,8,128]{2,1,0:T(8,128)S(1)} %get-tuple-element.65), channel_id=1, source_target_pairs={{0,9},{1,8},{8,1},{9,0},{16,25},{17,24},{24,17},{25,16},{2,11},{3,... | collective-permute-start | bytes 61448 | tf_op jit(solution)/shard_map/ppermute | solution.py:620
  37.8 5.8 %collective-permute-start.16 = (f32[5,8,128]{2,1,0:T(8,128)S(1)}, f32[5,8,128]{2,1,0:T(8,128)S(1)}, u32[]{:S(2)}, u32[]{:S(2)}) collective-permute-start(f32[5,8,128]{2,1,0:T(8,128)S(1)} %get-tuple-element.66), channel_id=1, source_target_pairs={{0,25},{1,24},{8,17},{9,16},{16,9},{17,8},{24,1},{25,0},{2,27},{3,... | collective-permute-start | bytes 61448 | tf_op jit(solution)/shard_map/ppermute | solution.py:620

commit v5 on v4

--- a/solution.py
+++ b/solution.py
@@ -273,13 +273,13 @@
 
 def pack_sums(values, weights, grid):
     sums = lane_product(values, weights)
-    packed = None
+    parts = []
     for group in range(grid.rows // TILE):
         part = sums[group * TILE : (group + 1) * TILE]
-        if group:
-            part = pltpu.roll(part, 4 * group, axis=1)
-        packed = part if packed is None else packed + part
-    return packed
+        parts.append(pltpu.roll(part, 4 * group, axis=1) if group else part)
+    while len(parts) > 1:
+        parts = [sum(parts[i + 1 : i + 2], parts[i]) for i in range(0, len(parts), 2)]
+    return parts[0]
 
 
 def unpack_sums(below, above, grid):
@@ -293,9 +293,10 @@
 
 def primitive_kernel(
     grid,
-    u_hbm, tables_hbm,
-    u_ref, tables_ref, prim_ref, eta_first, eta_second, xi_first, xi_second, zeta_ref,
-    tables_sem, u_sems,
+    u_hbm, tables_hbm, metrics_hbm, jacobian_hbm,
+    u_ref, tables_ref, metrics_ref, jacobian_ref,
+    prim_ref, mass_ref, eta_first, eta_second, xi_first, xi_second, zeta_ref,
+    u_sems, late_sems,
 ):
     chunks = u_sems.shape[0]
     step = grid.rows // chunks
@@ -308,8 +309,16 @@
             )
             copy.start()
             copies.append(copy)
-    weights = pltpu.make_async_copy(tables_hbm, tables_ref, tables_sem)
-    weights.start()
+    late = [
+        pltpu.make_async_copy(source, result, late_sems.at[index])
+        for index, (source, result) in enumerate(
+            [(tables_hbm, tables_ref)]
+            + [(metrics_hbm.at[k], metrics_ref.at[k]) for k in range(9)]
+            + [(jacobian_hbm, jacobian_ref)]
+        )
+    ]
+    for copy in late:
+        copy.start()
     for index in range(chunks):
         for copy in copies[5 * index : 5 * index + 5]:
             copy.wait()
@@ -323,47 +332,59 @@
             work = momentum * speed if work is None else work + momentum * speed
         pressure = 0.4 * (u_ref[4, rows, :] - 0.5 * work)
         prim_ref[3, rows, :] = pressure * inverse
+
+    def send(xi_value, eta_value, field):
+        send_sums(
+            lambda position, group: eta_value[grid.eta_tile(position, group), :],
+            grid.xi_groups, grid.ny, odd("eta"), eta_first, eta_second, field,
+        )
+        send_sums(
+            lambda position, group: xi_value[grid.xi_tile(position, group), :],
+            grid.eta_groups, grid.nx, odd("xi"), xi_first, xi_second, field,
+        )
+
     for field in range(4):
-        send_sums(
-            lambda position, group: prim_ref[field, grid.eta_tile(position, group), :],
-            grid.xi_groups, grid.ny, odd("eta"), eta_first, eta_second, field,
-        )
-        send_sums(
-            lambda position, group: prim_ref[field, grid.xi_tile(position, group), :],
-            grid.eta_groups, grid.nx, odd("xi"), xi_first, xi_second, field,
-        )
-    weights.wait()
+        send(prim_ref.at[field], prim_ref.at[field], field)
+    for copy in late:
+        copy.wait()
+    for k in range(3):
+        for index in range(chunks):
+            rows = pl.ds(index * step, step)
+            mass_ref[k, rows, :] = (
+                metrics_ref[3 * k, rows, :] * u_ref[1, rows, :]
+                + metrics_ref[3 * k + 1, rows, :] * u_ref[2, rows, :]
+                + metrics_ref[3 * k + 2, rows, :] * u_ref[3, rows, :]
+            )
+    send(mass_ref.at[0], mass_ref.at[1], 4)
     sums = split_weights(tables_ref[SUMS])
+    for field in range(5):
+        values = prim_ref[field] if field < 4 else mass_ref[2]
+        zeta_ref[field] = pack_sums(values, sums, grid)
+
+
+def derive_sources(grid, xi_value, eta_value, zeta_value, derive, field, xi_ref, eta_ref, zeta_ref):
+    zeta_ref[field] = lane_product(zeta_value[...], derive)
+    for group in range(grid.eta_groups):
+        cells = [xi_value[grid.xi_tile(i, group), :] for i in range(grid.nx)]
+        for i, value in enumerate(derive_source(cells)):
+            xi_ref[field, grid.xi_tile(i, group), :] = value
+    for group in range(grid.xi_groups):
+        cells = [eta_value[grid.eta_tile(i, group), :] for i in range(grid.ny)]
+        for i, value in enumerate(derive_source(cells)):
+            eta_ref[field, grid.eta_major(i, group), :] = value
+
+
+def primitive_source_kernel(grid, prim_ref, mass_ref, tables_ref, *results):
+    derive = split_weights(tables_ref[DERIVE])
     for field in range(4):
-        zeta_ref[field] = pack_sums(prim_ref[field], sums, grid)
-
-
-def fetch_kernel(count, *refs):
-    sources, results, sems = refs[:count], refs[count + 1 : 2 * count + 1], refs[-1]
-    copies = [
-        pltpu.make_async_copy(source, result, sems.at[index])
-        for index, (source, result) in enumerate(zip(sources, results))
-    ]
-    for copy in copies:
-        copy.start()
-    for copy in copies:
-        copy.wait()
-
-
-def derive_source_kernel(grid, fields, value_ref, tables_ref, xi_ref, eta_ref, zeta_ref):
-    parts = [value_ref.at[k] for k in range(3)] if len(value_ref.shape) == 4 else [value_ref] * 3
-    xi_value, eta_value, zeta_value = parts
+        derive_sources(grid, *[prim_ref.at[field]] * 3, derive, field, *results)
+    derive_sources(grid, *[mass_ref.at[k] for k in range(3)], derive, 4, *results)
+
+
+def contra_source_kernel(grid, contra_ref, tables_ref, *results):
     derive = split_weights(tables_ref[DERIVE])
-    for field in range(fields):
-        zeta_ref[field] = lane_product(zeta_value[field], derive)
-        for group in range(grid.eta_groups):
-            cells = [xi_value[field, grid.xi_tile(i, group), :] for i in range(grid.nx)]
-            for i, value in enumerate(derive_source(cells)):
-                xi_ref[field, grid.xi_tile(i, group), :] = value
-        for group in range(grid.xi_groups):
-            cells = [eta_value[field, grid.eta_tile(i, group), :] for i in range(grid.ny)]
-            for i, value in enumerate(derive_source(cells)):
-                eta_ref[field, grid.eta_major(i, group), :] = value
+    for field in range(4):
+        derive_sources(grid, *[contra_ref.at[k, field] for k in range(3)], derive, field, *results)
 
 
 def xi_derivative(grid, source_ref, xi_a, xi_b, field, group):
@@ -378,7 +399,18 @@
     return derive_solve(rights, below, above)
 
 
-def slope_kernel(grid, xi_source, eta_source, eta_a, eta_b, xi_a, xi_b, slope_ref):
+def add_derivatives(grid, xi_source, eta_source, own_ref, eta_a, eta_b, xi_a, xi_b, field, total_ref):
+    for group in range(grid.xi_groups):
+        for i, value in enumerate(eta_derivative(grid, eta_source, eta_a, eta_b, field, group)):
+            rows = grid.eta_tile(i, group)
+            total_ref[rows, :] = own_ref[field, rows, :] + value
+    for group in range(grid.eta_groups):
+        for i, value in enumerate(xi_derivative(grid, xi_source, xi_a, xi_b, field, group)):
+            rows = grid.xi_tile(i, group)
+            total_ref[rows, :] = total_ref[rows, :] + value
+
+
+def slope_kernel(grid, xi_source, eta_source, own_ref, eta_a, eta_b, xi_b, xi_a, slope_ref, mass_total_ref):
     for field in range(4):
         for group in range(grid.eta_groups):
             for i, value in enumerate(xi_derivative(grid, xi_source, xi_a, xi_b, field, group)):
@@ -386,18 +418,29 @@
         for group in range(grid.xi_groups):
             for i, value in enumerate(eta_derivative(grid, eta_source, eta_a, eta_b, field, group)):
                 slope_ref[1, field, grid.eta_tile(i, group), :] = value
+    add_derivatives(
+        grid, xi_source, eta_source, own_ref, eta_a, eta_b, xi_a, xi_b, 4, mass_total_ref
+    )
 
 
 def flux_kernel(
     grid,
-    u_ref, prim_ref, metrics_ref, jacobian_ref, slope_ref, own_ref, zeta_below, zeta_above, tables_ref,
-    contra_ref, eta_first, eta_second, xi_first, xi_second, zeta_ref,
+    u_ref, prim_ref, metrics_ref, jacobian_ref, slope_ref, own_ref, mass_total_ref,
+    zeta_below, zeta_above, tables_ref,
+    contra_ref, mass_ref, eta_first, eta_second, xi_first, xi_second, zeta_ref,
     zeta_slope_ref,
 ):
     back, sums = split_weights(tables_ref[BACK]), split_weights(tables_ref[SUMS])
     for field in range(4):
         halo = unpack_sums(zeta_below[field], zeta_above[field], grid)
         zeta_slope_ref[field] = own_ref[field] + lane_product(halo, back)
+    halo = unpack_sums(zeta_below[4], zeta_above[4], grid)
+    total = mass_total_ref[...] + lane_product(halo, back)
+    mass_ref[...] = u_ref[0] - (step_duration * jacobian_ref[...]) * total
+    send_cells(
+        lambda position, group: mass_ref[grid.eta_tile(position, group), :],
+        grid.xi_groups, grid.ny, odd("eta"), eta_first, eta_second, 2 * 4,
+    )
 
     step = TILE
 
@@ -432,9 +475,9 @@
         for j in range(3):
             worked = speed[0] * stress[0][j] + speed[1] * stress[1][j] + speed[2] * stress[2][j]
             energy = (total * speed[j] - worked) - (conduction / viscosity) * physical[3][j]
-            fluxes.append([u[1 + j], momentum[0][j], momentum[1][j], momentum[2][j], energy])
+            fluxes.append([momentum[0][j], momentum[1][j], momentum[2][j], energy])
         for k in range(3):
-            for f in range(5):
+            for f in range(4):
                 contra_ref[k, f, rows, :] = (
                     metrics[k][0] * fluxes[0][f]
                     + metrics[k][1] * fluxes[1][f]
@@ -443,7 +486,7 @@
         return carry
 
     lax.fori_loop(0, grid.rows // step, body, 0, unroll=4)
-    for field in range(5):
+    for field in range(4):
         send_sums(
             lambda position, group: contra_ref[1, field, grid.eta_tile(position, group), :],
             grid.xi_groups, grid.ny, odd("eta"), eta_first, eta_second, field,
@@ -455,16 +498,11 @@
         zeta_ref[field] = pack_sums(contra_ref[2, field], sums, grid)
 
 
-def divergence_kernel(grid, xi_source, eta_source, own_ref, eta_a, eta_b, xi_a, xi_b, total_ref):
-    for field in range(5):
-        for group in range(grid.xi_groups):
-            for i, value in enumerate(eta_derivative(grid, eta_source, eta_a, eta_b, field, group)):
-                rows = grid.eta_tile(i, group)
-                total_ref[field, rows, :] = own_ref[field, rows, :] + value
-        for group in range(grid.eta_groups):
-            for i, value in enumerate(xi_derivative(grid, xi_source, xi_a, xi_b, field, group)):
-                rows = grid.xi_tile(i, group)
-                total_ref[field, rows, :] = total_ref[field, rows, :] + value
+def divergence_kernel(grid, xi_source, eta_source, own_ref, eta_a, eta_b, xi_b, xi_a, total_ref):
+    for field in range(4):
+        add_derivatives(
+            grid, xi_source, eta_source, own_ref, eta_a, eta_b, xi_a, xi_b, field, total_ref.at[field]
+        )
 
 
 def step_kernel(
@@ -474,73 +512,98 @@
 ):
     back = split_weights(tables_ref[BACK])
     scale = step_duration * jacobian_ref[...]
-    for field in range(5):
+    for field in range(4):
         halo = unpack_sums(zeta_below[field], zeta_above[field], grid)
         total = total_ref[field] + lane_product(halo, back)
-        state_ref[field] = u_ref[field] - scale * total
+        state_ref[field] = u_ref[1 + field] - scale * total
         send_cells(
             lambda position, group: state_ref[field, grid.eta_tile(position, group), :],
-            grid.xi_groups, grid.ny, odd("eta"), eta_first, eta_second, field,
-        )
-
-
-def send_cells(read, groups, count, flag, first_ref, second_ref, field):
+            grid.xi_groups, grid.ny, odd("eta"), eta_first, eta_second, WIDTH * field,
+        )
+
+
+def send_cells(read, groups, count, flag, first_ref, second_ref, base):
     for group in range(groups):
         for step in range(WIDTH):
             low = read(step, group)
             top = read(count - 1 - step, group)
-            index = WIDTH * field + step
-            first_ref[index, group_rows(group), :] = jnp.where(flag, low, top)
-            second_ref[index, group_rows(group), :] = jnp.where(flag, top, low)
-
-
-def take_cells(first_ref, second_ref, flag, field, group):
+            first_ref[base + step, group_rows(group), :] = jnp.where(flag, low, top)
+            second_ref[base + step, group_rows(group), :] = jnp.where(flag, top, low)
+
+
+def take_cells(first_ref, second_ref, flag, base, group):
     below, above = [], []
     for step in range(WIDTH):
-        first = first_ref[WIDTH * field + step, group_rows(group), :]
-        second = second_ref[WIDTH * field + step, group_rows(group), :]
+        first = first_ref[base + step, group_rows(group), :]
+        second = second_ref[base + step, group_rows(group), :]
         below.append(jnp.where(flag, first, second))
         above.append(jnp.where(flag, second, first))
     return below, above
 
 
-def eta_source_kernel(grid, state_ref, source_ref):
-    for field in range(5):
-        for group in range(grid.xi_groups):
-            cells = [state_ref[field, grid.eta_tile(i, group), :] for i in range(grid.ny)]
-            for i, value in enumerate(smooth_source(cells)):
-                source_ref[field, grid.eta_major(i, group), :] = value
-
-
-def xi_source_kernel(grid, state_ref, source_ref):
-    for field in range(5):
-        for group in range(grid.eta_groups):
-            cells = [state_ref[field, grid.xi_tile(i, group), :] for i in range(grid.nx)]
-            for i, value in enumerate(smooth_source(cells)):
-                source_ref[field, grid.xi_tile(i, group), :] = value
+def eta_sources(grid, state_ref, source_ref):
+    for group in range(grid.xi_groups):
+        cells = [state_ref[grid.eta_tile(i, group), :] for i in range(grid.ny)]
+        for i, value in enumerate(smooth_source(cells)):
+            source_ref[grid.eta_major(i, group), :] = value
+
+
+def xi_sources(grid, state_ref, source_ref):
+    for group in range(grid.eta_groups):
+        cells = [state_ref[grid.xi_tile(i, group), :] for i in range(grid.nx)]
+        for i, value in enumerate(smooth_source(cells)):
+            source_ref[grid.xi_tile(i, group), :] = value
+
+
+def eta_filter(grid, source_ref, eta_a, eta_b, base, result_ref):
+    for group in range(grid.xi_groups):
+        below, above = take_cells(eta_a, eta_b, odd("eta"), base, group)
+        rights = [source_ref[grid.eta_major(i, group), :] for i in range(grid.ny)]
+        for i, value in enumerate(smooth_solve(rights, below, above)):
+            result_ref[grid.eta_tile(i, group), :] = value
+
+
+def xi_filter(grid, source_ref, xi_a, xi_b, base, smooth, result_ref):
+    for group in range(grid.eta_groups):
+        below, above = take_cells(xi_a, xi_b, odd("xi"), base, group)
+        rights = [source_ref[grid.xi_tile(i, group), :] for i in range(grid.nx)]
+        for i, value in enumerate(smooth_solve(rights, below, above)):
+            result_ref[grid.xi_tile(i, group), :] = value
+    result_ref[...] = lane_product(result_ref[...], smooth)
+
+
+def source_kernel(grid, form, state_ref, source_ref):
+    for field in range(state_ref.shape[0]):
+        form(grid, state_ref.at[field], source_ref.at[field])
+
+
+def mass_eta_kernel(grid, source_ref, eta_a, eta_b, order_ref, result_ref, next_ref, xi_first, xi_second):
+    eta_filter(grid, source_ref.at[0], eta_a, eta_b, 2 * 4, result_ref.at[0])
+    send_cells(
+        lambda position, group: result_ref[0, grid.xi_tile(position, group), :],
+        grid.eta_groups, grid.nx, odd("xi"), xi_first, xi_second, 0,
+    )
+    xi_sources(grid, result_ref.at[0], next_ref.at[0])
 
 
 def eta_filter_kernel(
-    grid, source_ref, eta_a, eta_b, result_ref, xi_first, xi_second, zeta_ref, edge_first, edge_second
+    grid, source_ref, mass_ref, order_ref, eta_b, eta_a,
+    result_ref, xi_first, xi_second, zeta_ref, edge_first, edge_second,
 ):
-    for field in range(5):
-        for group in range(grid.xi_groups):
-            below, above = take_cells(eta_a, eta_b, odd("eta"), field, group)
-            rights = [source_ref[field, grid.eta_major(i, group), :] for i in range(grid.ny)]
-            for i, value in enumerate(smooth_solve(rights, below, above)):
-                result_ref[field, grid.eta_tile(i, group), :] = value
     flag = odd("xi")
-    for field in range(5):
+    for field in range(4):
+        eta_filter(grid, source_ref.at[field], eta_a, eta_b, WIDTH * field, result_ref.at[field])
         send_cells(
             lambda position, group: result_ref[field, grid.xi_tile(position, group), :],
-            grid.eta_groups, grid.nx, flag, xi_first, xi_second, field,
+            grid.eta_groups, grid.nx, flag, xi_first, xi_second, WIDTH * field,
         )
     lane = lax.broadcasted_iota(jnp.int32, (TILE, LANES), 1)
     for position in range(grid.nx):
         packed = None
         for slot in range(5 * grid.eta_groups):
             field, group = slot // grid.eta_groups, slot % grid.eta_groups
-            part = result_ref[field, grid.xi_tile(position, group), :]
+            rows = grid.xi_tile(position, group)
+            part = result_ref[field - 1, rows, :] if field else mass_ref[0, rows, :]
             part = pltpu.roll(part, WIDTH * (2 * slot + 1), axis=1)
             packed = part if packed is None else jnp.where(lane >= 2 * WIDTH * slot, part, packed)
         zeta_ref[group_rows(position), :] = packed
@@ -552,19 +615,15 @@
 
 def xi_filter_kernel(grid, source_ref, xi_a, xi_b, tables_ref, result_ref):
     smooth = split_weights(tables_ref[SMOOTH])
-    flag = odd("xi")
-    for field in range(5):
-        for group in range(grid.eta_groups):
-            below, above = take_cells(xi_a, xi_b, flag, field, group)
-            rights = [source_ref[field, grid.xi_tile(i, group), :] for i in range(grid.nx)]
-            for i, value in enumerate(smooth_solve(rights, below, above)):
-                result_ref[field, grid.xi_tile(i, group), :] = value
-        result_ref[field] = lane_product(result_ref[field], smooth)
+    for field in range(source_ref.shape[0]):
+        xi_filter(
+            grid, source_ref.at[field], xi_a, xi_b, WIDTH * field, smooth, result_ref.at[field]
+        )
 
 
 def zeta_filter_kernel(
     grid,
-    state_ref, below_ref, above_ref, a_below, a_above, b_below, b_above, tables_ref,
+    mass_ref, state_ref, below_ref, above_ref, a_below, a_above, b_below, b_above, tables_ref,
     result_hbm,
     result_ref, sems,
 ):
@@ -591,7 +650,8 @@
                 slot = field * grid.eta_groups + group
                 parts.append(pltpu.roll(packed, LANES - 2 * WIDTH * slot, axis=1) if slot else packed)
         halo = jnp.concatenate(parts, axis=0)
-        result_ref[field] = state_ref[field] + lane_product(halo, ends)
+        own = state_ref[field - 1] if field else mass_ref[0]
+        result_ref[field] = own + lane_product(halo, ends)
         copy = pltpu.make_async_copy(result_ref.at[field], result_hbm.at[field], sems.at[field])
         copy.start()
         copies.append(copy)
@@ -680,81 +740,91 @@
         xi_b = pair_swap(xi_second, "xi", 1)
         below, above = ring_swap(zeta, "zeta")
         xi_a = pair_swap(xi_first, "xi", 0)
-        return (eta_a, eta_b, xi_a, xi_b), (below, above)
-
-    def sums_shapes(fields):
-        return [(2 * fields, nx, nz)] * 2 + [(2 * fields, ny, nz)] * 2 + [(fields, TILE, LANES)]
-
+        return (eta_a, eta_b, xi_b, xi_a), (below, above)
+
+    block = (rows, nz)
     chunks = 2
-    u, tables, prim, *sends = call(
+    u, tables, metrics, jacobian, prim, mass, *sends = call(
         functools.partial(primitive_kernel, grid),
-        [like(u), like(tables), (4, rows, nz)] + sums_shapes(4),
-        u, tables,
-        scratch=[pltpu.SemaphoreType.DMA, pltpu.SemaphoreType.DMA((chunks, 5))],
-        far=(0, 1),
-    )
-    sides, ends = exchange(*sends)
-    metrics, jacobian = call(
-        functools.partial(fetch_kernel, 2),
-        [like(metrics), like(jacobian)],
-        metrics, jacobian, sends[-1],
-        scratch=[pltpu.SemaphoreType.DMA((2,))],
-        far=(0, 1),
-    )
-    xi_source, eta_source, own = call(
-        functools.partial(derive_source_kernel, grid, 4),
-        [(4, rows, nz)] * 3,
-        prim, tables,
-    )
-    (slopes,) = call(
-        functools.partial(slope_kernel, grid), [(2, 4, rows, nz)], xi_source, eta_source, *sides,
-    )
-    contra, *sends = call(
-        functools.partial(flux_kernel, grid),
-        [(3, 5, rows, nz)] + sums_shapes(5),
-        u, prim, metrics, jacobian, slopes, own, *ends, tables,
-        scratch=[pltpu.VMEM((4, rows, nz), jnp.float32)],
+        [like(u), like(tables), like(metrics), like(jacobian), (4, *block), (3, *block)]
+        + [(2 * 5, nx, nz)] * 2
+        + [(2 * 5, ny, nz)] * 2
+        + [(5, TILE, LANES)],
+        u, tables, metrics, jacobian,
+        scratch=[pltpu.SemaphoreType.DMA((chunks, 5)), pltpu.SemaphoreType.DMA((11,))],
+        far=(0, 1, 2, 3),
     )
     sides, ends = exchange(*sends)
     xi_source, eta_source, own = call(
-        functools.partial(derive_source_kernel, grid, 5), [(5, rows, nz)] * 3, contra, tables,
+        functools.partial(primitive_source_kernel, grid), [(5, *block)] * 3, prim, mass, tables,
+    )
+    slopes, mass_total = call(
+        functools.partial(slope_kernel, grid),
+        [(2, 4, *block), block],
+        xi_source, eta_source, own, *sides,
+    )
+    contra, mass, *sends = call(
+        functools.partial(flux_kernel, grid),
+        [(3, 4, *block), block]
+        + [(2 * 4 + WIDTH, nx, nz)] * 2
+        + [(2 * 4, ny, nz)] * 2
+        + [(4, TILE, LANES)],
+        u, prim, metrics, jacobian, slopes, own, mass_total, *ends, tables,
+        scratch=[pltpu.VMEM((4, *block), jnp.float32)],
+    )
+    sides, ends = exchange(*sends)
+    xi_source, eta_source, own = call(
+        functools.partial(contra_source_kernel, grid), [(4, *block)] * 3, contra, tables,
+    )
+    (mass_source,) = call(
+        functools.partial(source_kernel, grid, eta_sources), [(1, *block)], mass.reshape(1, *block),
     )
     (total,) = call(
         functools.partial(divergence_kernel, grid),
-        [(5, rows, nz)],
+        [(4, *block)],
         xi_source, eta_source, own, *sides,
     )
     state, eta_first, eta_second = call(
         functools.partial(step_kernel, grid),
-        [(5, rows, nz)] + [(5 * WIDTH, nx, nz)] * 2,
+        [(4, *block)] + [(4 * WIDTH, nx, nz)] * 2,
         u, jacobian, total, *ends, tables,
+    )
+    mass, mass_source, xi_first, xi_second = call(
+        functools.partial(mass_eta_kernel, grid),
+        [(1, *block)] * 2 + [(WIDTH, ny, nz)] * 2,
+        mass_source, sides[0], sides[1], eta_first,
     )
     eta_b = pair_swap(eta_second, "eta", 1)
     eta_a = pair_swap(eta_first, "eta", 0)
-    (source,) = call(functools.partial(eta_source_kernel, grid), [(5, rows, nz)], state)
+    xi_b = pair_swap(xi_second, "xi", 1)
+    xi_a = pair_swap(xi_first, "xi", 0)
+    (source,) = call(functools.partial(source_kernel, grid, eta_sources), [(4, *block)], state)
+    (mass_part,) = call(
+        functools.partial(xi_filter_kernel, grid), [(1, *block)], mass_source, xi_a, xi_b, tables,
+    )
     state, xi_first, xi_second, zeta, edge_first, edge_second = call(
         functools.partial(eta_filter_kernel, grid),
-        [(5, rows, nz)]
-        + [(5 * WIDTH, ny, nz)] * 2
+        [(4, *block)]
+        + [(4 * WIDTH, ny, nz)] * 2
         + [(nx * TILE, LANES)]
         + [(WIDTH, TILE, LANES)] * 2,
-        source, eta_a, eta_b,
+        source, mass, mass_part, eta_b, eta_a,
     )
     xi_b = pair_swap(xi_second, "xi", 1)
     ends = ring_swap(zeta, "zeta")
     edges_b = diagonal_swap(edge_second, 1)
     edges_a = diagonal_swap(edge_first, 0)
     xi_a = pair_swap(xi_first, "xi", 0)
-    (source,) = call(functools.partial(xi_source_kernel, grid), [(5, rows, nz)], state)
+    (source,) = call(functools.partial(source_kernel, grid, xi_sources), [(4, *block)], state)
     (state,) = call(
-        functools.partial(xi_filter_kernel, grid), [(5, rows, nz)], source, xi_a, xi_b, tables,
+        functools.partial(xi_filter_kernel, grid), [(4, *block)], source, xi_a, xi_b, tables,
     )
     edges = [edge.reshape(WIDTH * TILE, LANES) for edge in (*edges_a, *edges_b)]
     (result,) = call(
         functools.partial(zeta_filter_kernel, grid),
-        [(5, rows, nz)],
-        state, *ends, *edges, tables,
-        scratch=[pltpu.VMEM((5, rows, nz), jnp.float32), pltpu.SemaphoreType.DMA((5,))],
+        [(5, *block)],
+        mass_part, state, *ends, *edges, tables,
+        scratch=[pltpu.VMEM((5, *block), jnp.float32), pltpu.SemaphoreType.DMA((5,))],
         far_outs=(0,),
     )
     return result.reshape(5, nx, ny, nz)

time: 45 us -> 43.5 us (0.967)
  waiting for transfers between devices: 14.4 us -> 11 us
  starting transfers between devices: 20 us -> 22.5 us
  Pallas kernels: 10.3 us -> 9.73 us
    ppermute x12 -> x14, waiting for transfers between devices: 13.4 us -> 9.73 us  [pair_swap(): return lax.ppermute(value, axis, pairs)]
    ppermute x12 -> x14, starting transfers between devices: 13.1 us -> 15.3 us  [pair_swap(): return lax.ppermute(value, axis, pairs)]
    pallas_call x13 -> x15, Pallas kernels: 10.3 us -> 9.73 us  [call(): pl.pallas_call(kernel, out_shape=shapes, in_specs=[pl.BlockSpec(memory_sp...]
  transfers between devices with their start and end apart: 17 -> 19, of which waited for: 5 -> 10; matrix products, arithmetic and copies ran while one was open for 0% -> 0% of each run, Pallas kernels for 10% -> 8%
where the time goes in v5:
time: 43.5 us; the launch traced here: 43.3 us
  starting transfers between devices  22.5 us (52%)
  waiting for transfers between devices  11 us (25%)
  Pallas kernels  9.73 us (22%)
    ppermute x14, starting transfers between devices, pair_swap(): return lax.ppermute(value, axis, pairs)  15.3 us
    ppermute x14, waiting for transfers between devices, pair_swap(): return lax.ppermute(value, axis, pairs)  9.73 us
    pallas_call x15, Pallas kernels, call(): pl.pallas_call(kernel, out_shape=shapes, in_specs=[pl.BlockSpec(memory_sp...  9.73 us
    ppermute x3, starting transfers between devices, ring_swap(): other = lax.ppermute(value, axis, [(0, 1), (1, 0)])  4.58 us
    ppermute x2, starting transfers between devices, send(): return lax.ppermute(value, ('xi', 'zeta'), pairs)  2.59 us
    ppermute x2, waiting for transfers between devices, send(): return lax.ppermute(value, ('xi', 'zeta'), pairs)  1.01 us
  transfers between devices with their start and end apart: 19, of which 10 were waited for; matrix products, arithmetic and copies ran while one was open for 0% of the time, Pallas kernels for 8%

profile of v5, /device:TPU:0, one launch (start us, length us, event | category | flops | bytes accessed | tf_op | source)
XLA Modules:
  0.0 43.3 jit_solution(12350601001083785068)
XLA Ops:
  0.0 2.4 %shard_map.46 = (f32[5,256,128]{2,1,0:T(8,128)S(1)}, f32[5,128,128]{2,1,0:T(8,128)S(1)}, f32[9,256,128]{2,1,0:T(8,128)S(1)}, f32[256,128]{1,0:T(8,128)S(1)}, f32...) custom-call(f32[5,256,128]{2,1,0:T(8,128)} %bitcast.13, ...), custom_call_target="tpu_custom_call" | custom-call | bytes 3600000 | tf_op jit(solution)/shard_map/pallas_call | solution.py:709
  2.4 3.1 %collective-permute-start = (f32[10,16,128]{2,1,0:T(8,128)S(1)}, f32[10,16,128]{2,1,0:T(8,128)S(1)}, u32[]{:S(2)}, u32[]{:S(2)}) collective-permute-start(f32[10,16,128]{2,1,0:T(8,128)S(1)} %get-tuple-element.53), channel_id=1, source_target_pairs={{0,2},{2,0},{4,6},{6,4},{1,3},{3,1},{5,7},{7,5},{8,10},{10,8},{12,... | collective-permute-start | bytes 245768 | tf_op jit(solution)/shard_map/ppermute | solution.py:668
  5.5 2.5 %collective-permute-start.1 = (f32[10,16,128]{2,1,0:T(8,128)S(1)}, f32[10,16,128]{2,1,0:T(8,128)S(1)}, u32[]{:S(2)}, u32[]{:S(2)}) collective-permute-start(f32[10,16,128]{2,1,0:T(8,128)S(1)} %get-tuple-element.54), channel_id=1, source_target_pairs={{0,6},{2,4},{4,2},{6,0},{1,7},{3,5},{5,3},{7,1},{8,14},{10,12},{12... | collective-permute-start | bytes 245768 | tf_op jit(solution)/shard_map/ppermute | solution.py:668
  8.0 0.4 collective-permute-start.2
  8.4 1.2 %collective-permute-start.3 = (f32[10,16,128]{2,1,0:T(8,128)S(1)}, f32[10,16,128]{2,1,0:T(8,128)S(1)}, u32[]{:S(2)}, u32[]{:S(2)}) collective-permute-start(f32[10,16,128]{2,1,0:T(8,128)S(1)} %get-tuple-element.56), channel_id=1, source_target_pairs={{0,8},{8,0},{16,24},{24,16},{1,9},{9,1},{17,25},{25,17},{2,10},{10... | collective-permute-start | bytes 245768 | tf_op jit(solution)/shard_map/ppermute | solution.py:668
  9.6 1.5 %collective-permute-start.4 = (f32[5,8,128]{2,1,0:T(8,128)S(1)}, f32[5,8,128]{2,1,0:T(8,128)S(1)}, u32[]{:S(2)}, u32[]{:S(2)}) collective-permute-start(f32[5,8,128]{2,1,0:T(8,128)S(1)} %get-tuple-element.59), channel_id=1, source_target_pairs={{0,1},{1,0},{2,3},{3,2},{4,5},{5,4},{6,7},{7,6},{8,9},{9,8},{10,11... | collective-permute-start | bytes 61448 | tf_op jit(solution)/shard_map/ppermute | solution.py:689
  11.1 0.6 %shard_map.47 = (f32[5,256,128]{2,1,0:T(8,128)S(1)}, f32[5,256,128]{2,1,0:T(8,128)S(1)}, f32[5,256,128]{2,1,0:T(8,128)S(1)}) custom-call(f32[4,256,128]{2,1,0:T(8,128)S(1)} %get-tuple-element.45.prim_ref, f32[3,256,128]{2,1,0:T(8,128)S(1)} %get-tuple-element.48.mass_ref, f32[5,128,128]{2,1,0:T(8,128)S(1)} %get-tuple-element.49.tables_ref), custom_call_target="tpu_custom_call" | custom-call | bytes 3600000 | tf_op jit(solution)/shard_map/pallas_call | solution.py:709
  11.7 0.0 collective-permute-done.eta_a
  11.7 0.4 %collective-permute-done.1.eta_b = f32[10,16,128]{2,1,0:T(8,128)S(1)} collective-permute-done((f32[10,16,128]{2,1,0:T(8,128)S(1)}, f32[10,16,128]{2,1,0:T(8,128)S(1)}, u32[]{:S(2)}, u32[]{:S(2)}) %collective-permute-start.1) | collective-permute-done | bytes 81952 | tf_op jit(solution)/shard_map/ppermute | solution.py:668
  12.1 0.5 %collective-permute-done.2.xi_b = f32[10,16,128]{2,1,0:T(8,128)S(1)} collective-permute-done((f32[10,16,128]{2,1,0:T(8,128)S(1)}, f32[10,16,128]{2,1,0:T(8,128)S(1)}, u32[]{:S(2)}, u32[]{:S(2)}) %collective-permute-start.2) | collective-permute-done | bytes 81952 | tf_op jit(solution)/shard_map/ppermute | solution.py:668
  12.7 0.0 collective-permute-done.3.xi_a
  12.7 0.5 %shard_map.48 = (f32[2,4,256,128]{3,2,1,0:T(8,128)S(1)}, f32[256,128]{1,0:T(8,128)S(1)}) custom-call(f32[5,256,128]{2,1,0:T(8,128)S(1)} %get-tuple-element.50.xi_source, f32[5,256,128]{2,1,0:T(8,128)S(1)} %get-tuple-element.51.eta_source, f32[5,256,128]{2,1,0:T(8,128)S(1)} %get-tuple-element.52.own_ref, f32[10,16,128]{2,1,0:T(8,128)S(1)} %collective-permute-done.eta_a, ...), custom_call_target="tpu_custom_call" | custom-call | bytes 3600000 | tf_op jit(solution)/shard_map/pallas_call | solution.py:709
  13.2 0.2 collective-permute-done.4.zeta_below.zeta_above
  13.4 1.8 %shard_map.49 = (f32[3,4,256,128]{3,2,1,0:T(8,128)S(1)}, f32[256,128]{1,0:T(8,128)S(1)}, f32[13,16,128]{2,1,0:T(8,128)S(1)}, f32[13,16,128]{2,1,0:T(8,128)S(1)},...) custom-call(f32[5,256,128]{2,1,0:T(8,128)S(1)} %get-tuple-element.44.u_ref, ...), custom_call_target="tpu_custom_call" | custom-call | bytes 3600000 | tf_op jit(solution)/shard_map/pallas_call | solution.py:709
  15.2 0.7 %collective-permute-start.5 = (f32[13,16,128]{2,1,0:T(8,128)S(1)}, f32[13,16,128]{2,1,0:T(8,128)S(1)}, u32[]{:S(2)}, u32[]{:S(2)}) collective-permute-start(f32[13,16,128]{2,1,0:T(8,128)S(1)} %get-tuple-element.61), channel_id=1, source_target_pairs={{0,2},{2,0},{4,6},{6,4},{1,3},{3,1},{5,7},{7,5},{8,10},{10,8},{12,... | collective-permute-start | bytes 319496 | tf_op jit(solution)/shard_map/ppermute | solution.py:668
  15.9 1.7 %collective-permute-start.6 = (f32[13,16,128]{2,1,0:T(8,128)S(1)}, f32[13,16,128]{2,1,0:T(8,128)S(1)}, u32[]{:S(2)}, u32[]{:S(2)}) collective-permute-start(f32[13,16,128]{2,1,0:T(8,128)S(1)} %get-tuple-element.62), channel_id=1, source_target_pairs={{0,6},{2,4},{4,2},{6,0},{1,7},{3,5},{5,3},{7,1},{8,14},{10,12},{12... | collective-permute-start | bytes 319496 | tf_op jit(solution)/shard_map/ppermute | solution.py:668
  17.6 0.0 collective-permute-start.7
  17.6 1.6 %collective-permute-start.8 = (f32[8,16,128]{2,1,0:T(8,128)S(1)}, f32[8,16,128]{2,1,0:T(8,128)S(1)}, u32[]{:S(2)}, u32[]{:S(2)}) collective-permute-start(f32[8,16,128]{2,1,0:T(8,128)S(1)} %get-tuple-element.68), channel_id=1, source_target_pairs={{0,8},{8,0},{16,24},{24,16},{1,9},{9,1},{17,25},{25,17},{2,10},{10... | collective-permute-start | bytes 196616 | tf_op jit(solution)/shard_map/ppermute | solution.py:668
  19.2 1.5 %collective-permute-start.9 = (f32[4,8,128]{2,1,0:T(8,128)S(1)}, f32[4,8,128]{2,1,0:T(8,128)S(1)}, u32[]{:S(2)}, u32[]{:S(2)}) collective-permute-start(f32[4,8,128]{2,1,0:T(8,128)S(1)} %get-tuple-element.69), channel_id=1, source_target_pairs={{0,1},{1,0},{2,3},{3,2},{4,5},{5,4},{6,7},{7,6},{8,9},{9,8},{10,11... | collective-permute-start | bytes 49160 | tf_op jit(solution)/shard_map/ppermute | solution.py:689
  20.7 0.5 %shard_map.51 = (f32[4,256,128]{2,1,0:T(8,128)S(1)}, f32[4,256,128]{2,1,0:T(8,128)S(1)}, f32[4,256,128]{2,1,0:T(8,128)S(1)}) custom-call(f32[3,4,256,128]{3,2,1,0:T(8,128)S(1)} %get-tuple-element.63.contra_ref, f32[5,128,128]{2,1,0:T(8,128)S(1)} %get-tuple-element.49.tables_ref), custom_call_target="tpu_custom_call" | custom-call | bytes 3600000 | tf_op jit(solution)/shard_map/pallas_call | solution.py:709
  21.2 0.7 %collective-permute-done.7.xi_b = f32[8,16,128]{2,1,0:T(8,128)S(1)} collective-permute-done((f32[8,16,128]{2,1,0:T(8,128)S(1)}, f32[8,16,128]{2,1,0:T(8,128)S(1)}, u32[]{:S(2)}, u32[]{:S(2)}) %collective-permute-start.7) | collective-permute-done | bytes 65568 | tf_op jit(solution)/shard_map/ppermute | solution.py:668
  21.9 0.7 %collective-permute-done.6.eta_b = f32[13,16,128]{2,1,0:T(8,128)S(1)} collective-permute-done((f32[13,16,128]{2,1,0:T(8,128)S(1)}, f32[13,16,128]{2,1,0:T(8,128)S(1)}, u32[]{:S(2)}, u32[]{:S(2)}) %collective-permute-start.6) | collective-permute-done | bytes 106528 | tf_op jit(solution)/shard_map/ppermute | solution.py:668
  22.6 0.5 %shard_map.52.total_ref = f32[4,256,128]{2,1,0:T(8,128)S(1)} custom-call(f32[4,256,128]{2,1,0:T(8,128)S(1)} %get-tuple-element.64.xi_source, f32[4,256,128]{2,1,0:T(8,128)S(1)} %get-tuple-element.65.eta_source, f32[4,256,128]{2,1,0:T(8,128)S(1)} %get-tuple-element.66.own_ref, f32[13,16,128]{2,1,0:T(8,128)S(1)} %collective-permute-done.5.eta_a, ...), custom_call_target="tpu_custom_call" | custom-call | bytes 3600000 | tf_op jit(solution)/shard_map/pallas_call | solution.py:709
  23.1 0.0 collective-permute-done.9.zeta_below.zeta_above
  23.1 0.4 %shard_map.53 = (f32[4,256,128]{2,1,0:T(8,128)S(1)}, f32[20,16,128]{2,1,0:T(8,128)S(1)}, f32[20,16,128]{2,1,0:T(8,128)S(1)}) custom-call(f32[5,256,128]{2,1,0:T(8,128)S(1)} %get-tuple-element.44.u_ref, f32[256,128]{1,0:T(8,128)S(1)} %get-tuple-element.47.jacobian_ref, f32[4,256,128]{2,1,0:T(8,128)S(1)} %shard_map.52.total_ref, ...), custom_call_target="tpu_custom_call" | custom-call | bytes 3600000 | tf_op jit(solution)/shard_map/pallas_call | solution.py:709
  23.5 2.4 %collective-permute-start.12 = (f32[20,16,128]{2,1,0:T(8,128)S(1)}, f32[20,16,128]{2,1,0:T(8,128)S(1)}, u32[]{:S(2)}, u32[]{:S(2)}) collective-permute-start(f32[20,16,128]{2,1,0:T(8,128)S(1)} %get-tuple-element.76), channel_id=1, source_target_pairs={{0,6},{2,4},{4,2},{6,0},{1,7},{3,5},{5,3},{7,1},{8,14},{10,12},{12... | collective-permute-start | bytes 491528 | tf_op jit(solution)/shard_map/ppermute | solution.py:668
  25.9 0.1 shard_map.50.source_ref
  26.0 0.2 shard_map.54
  26.1 0.1 collective-permute-start.10
  26.2 0.9 %collective-permute-start.11 = (f32[5,16,128]{2,1,0:T(8,128)S(1)}, f32[5,16,128]{2,1,0:T(8,128)S(1)}, u32[]{:S(2)}, u32[]{:S(2)}) collective-permute-start(f32[5,16,128]{2,1,0:T(8,128)S(1)} %get-tuple-element.73), channel_id=1, source_target_pairs={{0,24},{8,16},{16,8},{24,0},{1,25},{9,17},{17,9},{25,1},{2,26},{10... | collective-permute-start | bytes 122888 | tf_op jit(solution)/shard_map/ppermute | solution.py:668
  27.1 0.3 shard_map.56.source_ref
  27.4 0.0 collective-permute-done.10.xi_a
  27.5 2.3 %collective-permute-done.11.xi_b = f32[5,16,128]{2,1,0:T(8,128)S(1)} collective-permute-done((f32[5,16,128]{2,1,0:T(8,128)S(1)}, f32[5,16,128]{2,1,0:T(8,128)S(1)}, u32[]{:S(2)}, u32[]{:S(2)}) %collective-permute-start.11) | collective-permute-done | bytes 40992 | tf_op jit(solution)/shard_map/ppermute | solution.py:668
  29.7 0.2 shard_map.55.order_ref.mass_ref
  29.9 2.6 %collective-permute-done.12.eta_b = f32[20,16,128]{2,1,0:T(8,128)S(1)} collective-permute-done((f32[20,16,128]{2,1,0:T(8,128)S(1)}, f32[20,16,128]{2,1,0:T(8,128)S(1)}, u32[]{:S(2)}, u32[]{:S(2)}) %collective-permute-start.12) | collective-permute-done | bytes 163872 | tf_op jit(solution)/shard_map/ppermute | solution.py:668
  32.5 1.6 %collective-permute-done.13.eta_a = f32[20,16,128]{2,1,0:T(8,128)S(1)} collective-permute-done((f32[20,16,128]{2,1,0:T(8,128)S(1)}, f32[20,16,128]{2,1,0:T(8,128)S(1)}, u32[]{:S(2)}, u32[]{:S(2)}) %collective-permute-start.13) | collective-permute-done | bytes 163872 | tf_op jit(solution)/shard_map/ppermute | solution.py:668
  34.2 0.4 %shard_map.57 = (f32[4,256,128]{2,1,0:T(8,128)S(1)}, f32[20,16,128]{2,1,0:T(8,128)S(1)}, f32[20,16,128]{2,1,0:T(8,128)S(1)}, f32[128,128]{1,0:T(8,128)S(1)}, f32...) custom-call(f32[4,256,128]{2,1,0:T(8,128)S(1)} %shard_map.56.source_ref, f32[1,256,128]{2,1,0:T(8,128)S(1)} %get-tuple-element.75.mass_ref, ...), custom_call_target="tpu_custom_call" | custom-call | bytes 3600000 | tf_op jit(solution)/shard_map/pallas_call | solution.py:709
  34.6 0.1 collective-permute-start.14
  34.7 0.8 %collective-permute-start.15 = (f32[20,16,128]{2,1,0:T(8,128)S(1)}, f32[20,16,128]{2,1,0:T(8,128)S(1)}, u32[]{:S(2)}, u32[]{:S(2)}) collective-permute-start(f32[20,16,128]{2,1,0:T(8,128)S(1)} %get-tuple-element.79), channel_id=1, source_target_pairs={{0,24},{8,16},{16,8},{24,0},{1,25},{9,17},{17,9},{25,1},{2,26},{10... | collective-permute-start | bytes 491528 | tf_op jit(solution)/shard_map/ppermute | solution.py:668
  35.5 1.5 %collective-permute-start.16 = (f32[128,128]{1,0:T(8,128)S(1)}, f32[128,128]{1,0:T(8,128)S(1)}, u32[]{:S(2)}, u32[]{:S(2)}) collective-permute-start(f32[128,128]{1,0:T(8,128)S(1)} %get-tuple-element.80), channel_id=1, source_target_pairs={{0,1},{1,0},{2,3},{3,2},{4,5},{5,4},{6,7},{7,6},{8,9},{9,8},{10,11... | collective-permute-start | bytes 196616 | tf_op jit(solution)/shard_map/ppermute | solution.py:689
  37.0 2.6 %collective-permute-start.18 = (f32[5,8,128]{2,1,0:T(8,128)S(1)}, f32[5,8,128]{2,1,0:T(8,128)S(1)}, u32[]{:S(2)}, u32[]{:S(2)}) collective-permute-start(f32[5,8,128]{2,1,0:T(8,128)S(1)} %get-tuple-element.82), channel_id=1, source_target_pairs={{0,25},{1,24},{8,17},{9,16},{16,9},{17,8},{24,1},{25,0},{2,27},{3,... | collective-permute-start | bytes 61448 | tf_op jit(solution)/shard_map/ppermute | solution.py:680
  39.6 0.2 shard_map.58.source_ref
  39.8 0.0 collective-permute-done.14.xi_a
  39.8 0.9 %collective-permute-done.15.xi_b = f32[20,16,128]{2,1,0:T(8,128)S(1)} collective-permute-done((f32[20,16,128]{2,1,0:T(8,128)S(1)}, f32[20,16,128]{2,1,0:T(8,128)S(1)}, u32[]{:S(2)}, u32[]{:S(2)}) %collective-permute-start.15) | collective-permute-done | bytes 163872 | tf_op jit(solution)/shard_map/ppermute | solution.py:668
  40.7 0.4 shard_map.59.state_ref
  41.1 0.0 collective-permute-done.17
  41.1 1.0 %collective-permute-done.18 = f32[5,8,128]{2,1,0:T(8,128)S(1)} collective-permute-done((f32[5,8,128]{2,1,0:T(8,128)S(1)}, f32[5,8,128]{2,1,0:T(8,128)S(1)}, u32[]{:S(2)}, u32[]{:S(2)}) %collective-permute-start.18) | collective-permute-done | bytes 20512 | tf_op jit(solution)/shard_map/ppermute | solution.py:680
  42.1 1.2 %shard_map.60 = f32[5,256,128]{2,1,0:T(8,128)} custom-call(f32[1,256,128]{2,1,0:T(8,128)S(1)} %shard_map.55.order_ref.mass_ref, f32[4,256,128]{2,1,0:T(8,128)S(1)} %shard_map.59.state_ref, f32[128,128]{1,0:T(8,128)S(1)} %collective-permute-done.16.below_ref.above_ref, f32[128,128]{1,0:T(8,128)S(1)} %collective-permute-done.16.below_ref.above_ref, ...), custom_call_target="tpu_custom_call" | custom-call | bytes 3600000 | tf_op jit(solution)/shard_map/pallas_call | solution.py:709
  (5 shorter events, 0.0 us)
Async XLA Ops:
  2.4 9.3 %collective-permute-start = (f32[10,16,128]{2,1,0:T(8,128)S(1)}, f32[10,16,128]{2,1,0:T(8,128)S(1)}, u32[]{:S(2)}, u32[]{:S(2)}) collective-permute-start(f32[10,16,128]{2,1,0:T(8,128)S(1)} %get-tuple-element.53), channel_id=1, source_target_pairs={{0,2},{2,0},{4,6},{6,4},{1,3},{3,1},{5,7},{7,5},{8,10},{10,8},{12,... | collective-permute-start | bytes 245768 | tf_op jit(solution)/shard_map/ppermute | solution.py:668
  5.5 6.6 %collective-permute-start.1 = (f32[10,16,128]{2,1,0:T(8,128)S(1)}, f32[10,16,128]{2,1,0:T(8,128)S(1)}, u32[]{:S(2)}, u32[]{:S(2)}) collective-permute-start(f32[10,16,128]{2,1,0:T(8,128)S(1)} %get-tuple-element.54), channel_id=1, source_target_pairs={{0,6},{2,4},{4,2},{6,0},{1,7},{3,5},{5,3},{7,1},{8,14},{10,12},{12... | collective-permute-start | bytes 245768 | tf_op jit(solution)/shard_map/ppermute | solution.py:668
  8.0 4.7 %collective-permute-start.2 = (f32[10,16,128]{2,1,0:T(8,128)S(1)}, f32[10,16,128]{2,1,0:T(8,128)S(1)}, u32[]{:S(2)}, u32[]{:S(2)}) collective-permute-start(f32[10,16,128]{2,1,0:T(8,128)S(1)} %get-tuple-element.55), channel_id=1, source_target_pairs={{0,24},{8,16},{16,8},{24,0},{1,25},{9,17},{17,9},{25,1},{2,26},{10... | collective-permute-start | bytes 245768 | tf_op jit(solution)/shard_map/ppermute | solution.py:668
  8.4 4.3 %collective-permute-start.3 = (f32[10,16,128]{2,1,0:T(8,128)S(1)}, f32[10,16,128]{2,1,0:T(8,128)S(1)}, u32[]{:S(2)}, u32[]{:S(2)}) collective-permute-start(f32[10,16,128]{2,1,0:T(8,128)S(1)} %get-tuple-element.56), channel_id=1, source_target_pairs={{0,8},{8,0},{16,24},{24,16},{1,9},{9,1},{17,25},{25,17},{2,10},{10... | collective-permute-start | bytes 245768 | tf_op jit(solution)/shard_map/ppermute | solution.py:668
  9.6 3.8 %collective-permute-start.4 = (f32[5,8,128]{2,1,0:T(8,128)S(1)}, f32[5,8,128]{2,1,0:T(8,128)S(1)}, u32[]{:S(2)}, u32[]{:S(2)}) collective-permute-start(f32[5,8,128]{2,1,0:T(8,128)S(1)} %get-tuple-element.59), channel_id=1, source_target_pairs={{0,1},{1,0},{2,3},{3,2},{4,5},{5,4},{6,7},{7,6},{8,9},{9,8},{10,11... | collective-permute-start | bytes 61448 | tf_op jit(solution)/shard_map/ppermute | solution.py:689
  15.2 6.8 %collective-permute-start.5 = (f32[13,16,128]{2,1,0:T(8,128)S(1)}, f32[13,16,128]{2,1,0:T(8,128)S(1)}, u32[]{:S(2)}, u32[]{:S(2)}) collective-permute-start(f32[13,16,128]{2,1,0:T(8,128)S(1)} %get-tuple-element.61), channel_id=1, source_target_pairs={{0,2},{2,0},{4,6},{6,4},{1,3},{3,1},{5,7},{7,5},{8,10},{10,8},{12,... | collective-permute-start | bytes 319496 | tf_op jit(solution)/shard_map/ppermute | solution.py:668
  15.9 6.7 %collective-permute-start.6 = (f32[13,16,128]{2,1,0:T(8,128)S(1)}, f32[13,16,128]{2,1,0:T(8,128)S(1)}, u32[]{:S(2)}, u32[]{:S(2)}) collective-permute-start(f32[13,16,128]{2,1,0:T(8,128)S(1)} %get-tuple-element.62), channel_id=1, source_target_pairs={{0,6},{2,4},{4,2},{6,0},{1,7},{3,5},{5,3},{7,1},{8,14},{10,12},{12... | collective-permute-start | bytes 319496 | tf_op jit(solution)/shard_map/ppermute | solution.py:668
  17.6 4.3 %collective-permute-start.7 = (f32[8,16,128]{2,1,0:T(8,128)S(1)}, f32[8,16,128]{2,1,0:T(8,128)S(1)}, u32[]{:S(2)}, u32[]{:S(2)}) collective-permute-start(f32[8,16,128]{2,1,0:T(8,128)S(1)} %get-tuple-element.67), channel_id=1, source_target_pairs={{0,24},{8,16},{16,8},{24,0},{1,25},{9,17},{17,9},{25,1},{2,26},{10... | collective-permute-start | bytes 196616 | tf_op jit(solution)/shard_map/ppermute | solution.py:668
  17.6 4.3 %collective-permute-start.8 = (f32[8,16,128]{2,1,0:T(8,128)S(1)}, f32[8,16,128]{2,1,0:T(8,128)S(1)}, u32[]{:S(2)}, u32[]{:S(2)}) collective-permute-start(f32[8,16,128]{2,1,0:T(8,128)S(1)} %get-tuple-element.68), channel_id=1, source_target_pairs={{0,8},{8,0},{16,24},{24,16},{1,9},{9,1},{17,25},{25,17},{2,10},{10... | collective-permute-start | bytes 196616 | tf_op jit(solution)/shard_map/ppermute | solution.py:668
  19.2 3.9 %collective-permute-start.9 = (f32[4,8,128]{2,1,0:T(8,128)S(1)}, f32[4,8,128]{2,1,0:T(8,128)S(1)}, u32[]{:S(2)}, u32[]{:S(2)}) collective-permute-start(f32[4,8,128]{2,1,0:T(8,128)S(1)} %get-tuple-element.69), channel_id=1, source_target_pairs={{0,1},{1,0},{2,3},{3,2},{4,5},{5,4},{6,7},{7,6},{8,9},{9,8},{10,11... | collective-permute-start | bytes 49160 | tf_op jit(solution)/shard_map/ppermute | solution.py:689
  23.5 9.0 %collective-permute-start.12 = (f32[20,16,128]{2,1,0:T(8,128)S(1)}, f32[20,16,128]{2,1,0:T(8,128)S(1)}, u32[]{:S(2)}, u32[]{:S(2)}) collective-permute-start(f32[20,16,128]{2,1,0:T(8,128)S(1)} %get-tuple-element.76), channel_id=1, source_target_pairs={{0,6},{2,4},{4,2},{6,0},{1,7},{3,5},{5,3},{7,1},{8,14},{10,12},{12... | collective-permute-start | bytes 491528 | tf_op jit(solution)/shard_map/ppermute | solution.py:668
  25.9 8.3 %collective-permute-start.13 = (f32[20,16,128]{2,1,0:T(8,128)S(1)}, f32[20,16,128]{2,1,0:T(8,128)S(1)}, u32[]{:S(2)}, u32[]{:S(2)}) collective-permute-start(f32[20,16,128]{2,1,0:T(8,128)S(1)} %get-tuple-element.70.order_ref), channel_id=1, source_target_pairs={{0,2},{2,0},{4,6},{6,4},{1,3},{3,1},{5,7},{7,5},{8,10},{10,8},{12,... | collective-permute-start | bytes 491528 | tf_op jit(solution)/shard_map/ppermute | solution.py:668
  26.1 1.3 %collective-permute-start.10 = (f32[5,16,128]{2,1,0:T(8,128)S(1)}, f32[5,16,128]{2,1,0:T(8,128)S(1)}, u32[]{:S(2)}, u32[]{:S(2)}) collective-permute-start(f32[5,16,128]{2,1,0:T(8,128)S(1)} %get-tuple-element.72), channel_id=1, source_target_pairs={{0,8},{8,0},{16,24},{24,16},{1,9},{9,1},{17,25},{25,17},{2,10},{10... | collective-permute-start | bytes 122888 | tf_op jit(solution)/shard_map/ppermute | solution.py:668
  26.2 3.5 %collective-permute-start.11 = (f32[5,16,128]{2,1,0:T(8,128)S(1)}, f32[5,16,128]{2,1,0:T(8,128)S(1)}, u32[]{:S(2)}, u32[]{:S(2)}) collective-permute-start(f32[5,16,128]{2,1,0:T(8,128)S(1)} %get-tuple-element.73), channel_id=1, source_target_pairs={{0,24},{8,16},{16,8},{24,0},{1,25},{9,17},{17,9},{25,1},{2,26},{10... | collective-permute-start | bytes 122888 | tf_op jit(solution)/shard_map/ppermute | solution.py:668
  34.6 5.2 %collective-permute-start.14 = (f32[20,16,128]{2,1,0:T(8,128)S(1)}, f32[20,16,128]{2,1,0:T(8,128)S(1)}, u32[]{:S(2)}, u32[]{:S(2)}) collective-permute-start(f32[20,16,128]{2,1,0:T(8,128)S(1)} %get-tuple-element.78), channel_id=1, source_target_pairs={{0,8},{8,0},{16,24},{24,16},{1,9},{9,1},{17,25},{25,17},{2,10},{10... | collective-permute-start | bytes 491528 | tf_op jit(solution)/shard_map/ppermute | solution.py:668
  34.7 6.0 %collective-permute-start.15 = (f32[20,16,128]{2,1,0:T(8,128)S(1)}, f32[20,16,128]{2,1,0:T(8,128)S(1)}, u32[]{:S(2)}, u32[]{:S(2)}) collective-permute-start(f32[20,16,128]{2,1,0:T(8,128)S(1)} %get-tuple-element.79), channel_id=1, source_target_pairs={{0,24},{8,16},{16,8},{24,0},{1,25},{9,17},{17,9},{25,1},{2,26},{10... | collective-permute-start | bytes 491528 | tf_op jit(solution)/shard_map/ppermute | solution.py:668
  35.5 6.7 %collective-permute-start.16 = (f32[128,128]{1,0:T(8,128)S(1)}, f32[128,128]{1,0:T(8,128)S(1)}, u32[]{:S(2)}, u32[]{:S(2)}) collective-permute-start(f32[128,128]{1,0:T(8,128)S(1)} %get-tuple-element.80), channel_id=1, source_target_pairs={{0,1},{1,0},{2,3},{3,2},{4,5},{5,4},{6,7},{7,6},{8,9},{9,8},{10,11... | collective-permute-start | bytes 196616 | tf_op jit(solution)/shard_map/ppermute | solution.py:689
  37.0 4.1 %collective-permute-start.17 = (f32[5,8,128]{2,1,0:T(8,128)S(1)}, f32[5,8,128]{2,1,0:T(8,128)S(1)}, u32[]{:S(2)}, u32[]{:S(2)}) collective-permute-start(f32[5,8,128]{2,1,0:T(8,128)S(1)} %get-tuple-element.81), channel_id=1, source_target_pairs={{0,9},{1,8},{8,1},{9,0},{16,25},{17,24},{24,17},{25,16},{2,11},{3,... | collective-permute-start | bytes 61448 | tf_op jit(solution)/shard_map/ppermute | solution.py:680
  37.0 5.1 %collective-permute-start.18 = (f32[5,8,128]{2,1,0:T(8,128)S(1)}, f32[5,8,128]{2,1,0:T(8,128)S(1)}, u32[]{:S(2)}, u32[]{:S(2)}) collective-permute-start(f32[5,8,128]{2,1,0:T(8,128)S(1)} %get-tuple-element.82), channel_id=1, source_target_pairs={{0,25},{1,24},{8,17},{9,16},{16,9},{17,8},{24,1},{25,0},{2,27},{3,... | collective-permute-start | bytes 61448 | tf_op jit(solution)/shard_map/ppermute | solution.py:680

commit v6 on v5

--- a/solution.py
+++ b/solution.py
@@ -410,7 +410,7 @@
             total_ref[rows, :] = total_ref[rows, :] + value
 
 
-def slope_kernel(grid, xi_source, eta_source, own_ref, eta_a, eta_b, xi_b, xi_a, slope_ref, mass_total_ref):
+def slope_kernel(grid, xi_source, eta_source, own_ref, eta_b, eta_a, xi_b, xi_a, slope_ref, mass_total_ref):
     for field in range(4):
         for group in range(grid.eta_groups):
             for i, value in enumerate(xi_derivative(grid, xi_source, xi_a, xi_b, field, group)):
@@ -427,10 +427,10 @@
     grid,
     u_ref, prim_ref, metrics_ref, jacobian_ref, slope_ref, own_ref, mass_total_ref,
     zeta_below, zeta_above, tables_ref,
-    contra_ref, mass_ref, eta_first, eta_second, xi_first, xi_second, zeta_ref,
+    contra_ref, mass_ref, eta_first, eta_second,
     zeta_slope_ref,
 ):
-    back, sums = split_weights(tables_ref[BACK]), split_weights(tables_ref[SUMS])
+    back = split_weights(tables_ref[BACK])
     for field in range(4):
         halo = unpack_sums(zeta_below[field], zeta_above[field], grid)
         zeta_slope_ref[field] = own_ref[field] + lane_product(halo, back)
@@ -491,6 +491,11 @@
             lambda position, group: contra_ref[1, field, grid.eta_tile(position, group), :],
             grid.xi_groups, grid.ny, odd("eta"), eta_first, eta_second, field,
         )
+
+
+def contra_sums_kernel(grid, contra_ref, tables_ref, xi_first, xi_second, zeta_ref):
+    sums = split_weights(tables_ref[SUMS])
+    for field in range(4):
         send_sums(
             lambda position, group: contra_ref[0, field, grid.xi_tile(position, group), :],
             grid.eta_groups, grid.nx, odd("xi"), xi_first, xi_second, field,
@@ -498,7 +503,7 @@
         zeta_ref[field] = pack_sums(contra_ref[2, field], sums, grid)
 
 
-def divergence_kernel(grid, xi_source, eta_source, own_ref, eta_a, eta_b, xi_b, xi_a, total_ref):
+def divergence_kernel(grid, xi_source, eta_source, own_ref, eta_b, eta_a, xi_b, xi_a, total_ref):
     for field in range(4):
         add_derivatives(
             grid, xi_source, eta_source, own_ref, eta_a, eta_b, xi_a, xi_b, field, total_ref.at[field]
@@ -541,6 +546,25 @@
     return below, above
 
 
+def send_faces(grid, read, flag, first_ref, second_ref, base):
+    for group in range(grid.eta_groups):
+        for step in range(WIDTH):
+            low = read(step, group)
+            top = read(grid.nx - WIDTH + step, group)
+            first_ref[base + step, group_rows(group), :] = jnp.where(flag, low, top)
+            second_ref[base + step, group_rows(group), :] = jnp.where(flag, top, low)
+
+
+def take_faces(first_ref, second_ref, flag, base, group):
+    below, above = [], []
+    for step in range(WIDTH):
+        low, top = base + step, base + WIDTH - 1 - step
+        rows = group_rows(group)
+        below.append(jnp.where(flag, first_ref[top, rows, :], second_ref[top, rows, :]))
+        above.append(jnp.where(flag, second_ref[low, rows, :], first_ref[low, rows, :]))
+    return below, above
+
+
 def eta_sources(grid, state_ref, source_ref):
     for group in range(grid.xi_groups):
         cells = [state_ref[grid.eta_tile(i, group), :] for i in range(grid.ny)]
@@ -565,7 +589,7 @@
 
 def xi_filter(grid, source_ref, xi_a, xi_b, base, smooth, result_ref):
     for group in range(grid.eta_groups):
-        below, above = take_cells(xi_a, xi_b, odd("xi"), base, group)
+        below, above = take_faces(xi_a, xi_b, odd("xi"), base, group)
         rights = [source_ref[grid.xi_tile(i, group), :] for i in range(grid.nx)]
         for i, value in enumerate(smooth_solve(rights, below, above)):
             result_ref[grid.xi_tile(i, group), :] = value
@@ -577,26 +601,69 @@
         form(grid, state_ref.at[field], source_ref.at[field])
 
 
-def mass_eta_kernel(grid, source_ref, eta_a, eta_b, order_ref, result_ref, next_ref, xi_first, xi_second):
-    eta_filter(grid, source_ref.at[0], eta_a, eta_b, 2 * 4, result_ref.at[0])
-    send_cells(
-        lambda position, group: result_ref[0, grid.xi_tile(position, group), :],
-        grid.eta_groups, grid.nx, odd("xi"), xi_first, xi_second, 0,
-    )
-    xi_sources(grid, result_ref.at[0], next_ref.at[0])
-
-
-def eta_filter_kernel(
-    grid, source_ref, mass_ref, order_ref, eta_b, eta_a,
-    result_ref, xi_first, xi_second, zeta_ref, edge_first, edge_second,
+def face_kernel(
+    grid, state_ref, source_ref, eta_a, eta_b, result_ref, next_ref, xi_first, xi_second
 ):
     flag = odd("xi")
+    eta_filter(grid, source_ref.at[0], eta_a, eta_b, 2 * 4, result_ref.at[0])
+    for field in range(5):
+        values = state_ref.at[field] if field < 4 else result_ref.at[0]
+        send_faces(
+            grid, lambda position, group: values[grid.xi_tile(position, group), :],
+            flag, xi_first, xi_second, WIDTH * field,
+        )
+    xi_sources(grid, result_ref.at[0], next_ref.at[0])
+
+
+PLANES = 3 * TILE
+
+
+def halo_source_kernel(grid, first_ref, second_ref, first_source, second_source):
+    for faces, source in ((first_ref, first_source), (second_ref, second_source)):
+        for tile in range(PLANES // TILE):
+            cells = [
+                faces[pl.ds(tile * TILE * grid.ny + i, TILE, stride=grid.ny), :] for i in range(grid.ny)
+            ]
+            for i, value in enumerate(smooth_source(cells)):
+                source[pl.ds(i * PLANES + tile * TILE, TILE), :] = value
+
+
+def edge_kernel(grid, order_ref, eta_a, eta_b, first_ref, second_ref):
+    flag = odd("xi")
+    eta_flag = odd("eta")
+    for side in range(2):
+        for step in range(WIDTH):
+            start = (side * WIDTH + step) * PLANES
+            for field in range(4):
+                one, other = eta_a[WIDTH * field + step], eta_b[WIDTH * field + step]
+                cells = jnp.where(eta_flag, other, one) if side else jnp.where(eta_flag, one, other)
+                low, top = cells[:WIDTH], cells[grid.nx - WIDTH :]
+                rows = pl.ds(start + WIDTH * field, WIDTH)
+                first_ref[rows, :] = jnp.where(flag, low, top)
+                second_ref[rows, :] = jnp.where(flag, top, low)
+            rest = pl.ds(start + 4 * WIDTH, PLANES - 4 * WIDTH)
+            first_ref[rest, :] = jnp.zeros((PLANES - 4 * WIDTH, LANES), jnp.float32)
+            second_ref[rest, :] = jnp.zeros((PLANES - 4 * WIDTH, LANES), jnp.float32)
+
+
+def filter_halo(grid, source_ref, edge_ref, result_ref):
+    for tile in range(PLANES // TILE):
+        ends = [
+            [edge_ref[pl.ds((side * WIDTH + i) * PLANES + tile * TILE, TILE), :] for i in range(WIDTH)]
+            for side in range(2)
+        ]
+        rights = [source_ref[pl.ds(i * PLANES + tile * TILE, TILE), :] for i in range(grid.ny)]
+        for i, value in enumerate(smooth_solve(rights, *ends)):
+            result_ref[pl.ds(tile * TILE * grid.ny + i, TILE, stride=grid.ny), :] = value
+
+
+def eta_filter_kernel(
+    grid, source_ref, mass_ref, eta_b, eta_a,
+    result_ref, zeta_ref, edge_first, edge_second,
+):
+    flag = odd("xi")
     for field in range(4):
         eta_filter(grid, source_ref.at[field], eta_a, eta_b, WIDTH * field, result_ref.at[field])
-        send_cells(
-            lambda position, group: result_ref[field, grid.xi_tile(position, group), :],
-            grid.eta_groups, grid.nx, flag, xi_first, xi_second, WIDTH * field,
-        )
     lane = lax.broadcasted_iota(jnp.int32, (TILE, LANES), 1)
     for position in range(grid.nx):
         packed = None
@@ -613,17 +680,37 @@
     )
 
 
-def xi_filter_kernel(grid, source_ref, xi_a, xi_b, tables_ref, result_ref):
+def mass_xi_kernel(grid, source_ref, xi_a, xi_b, tables_ref, result_ref):
     smooth = split_weights(tables_ref[SMOOTH])
-    for field in range(source_ref.shape[0]):
+    xi_filter(grid, source_ref.at[0], xi_a, xi_b, WIDTH * 4, smooth, result_ref.at[0])
+
+
+def xi_filter_kernel(
+    grid, source_ref, first_source, second_source, edge_b, edge_a, tables_ref, result_ref,
+    first_ref, second_ref,
+):
+    smooth = split_weights(tables_ref[SMOOTH])
+    filter_halo(grid, first_source, edge_a, first_ref)
+    filter_halo(grid, second_source, edge_b, second_ref)
+
+    class Layers:
+        def __init__(self, ref):
+            self.ref = ref
+
+        def __getitem__(self, index):
+            layer, rows, _ = index
+            return self.ref[pl.ds(layer * grid.ny + rows.start, rows.size), :]
+
+    for field in range(4):
         xi_filter(
-            grid, source_ref.at[field], xi_a, xi_b, WIDTH * field, smooth, result_ref.at[field]
+            grid, source_ref.at[field], Layers(first_ref), Layers(second_ref), WIDTH * field, smooth,
+            result_ref.at[field],
         )
 
 
 def zeta_filter_kernel(
     grid,
-    mass_ref, state_ref, below_ref, above_ref, a_below, a_above, b_below, b_above, tables_ref,
+    mass_ref, state_ref, b_below, b_above, below_ref, above_ref, a_below, a_above, tables_ref,
     result_hbm,
     result_ref, sems,
 ):
@@ -740,7 +827,7 @@
         xi_b = pair_swap(xi_second, "xi", 1)
         below, above = ring_swap(zeta, "zeta")
         xi_a = pair_swap(xi_first, "xi", 0)
-        return (eta_a, eta_b, xi_b, xi_a), (below, above)
+        return (eta_b, eta_a, xi_b, xi_a), (below, above)
 
     block = (rows, nz)
     chunks = 2
@@ -763,16 +850,18 @@
         [(2, 4, *block), block],
         xi_source, eta_source, own, *sides,
     )
-    contra, mass, *sends = call(
+    contra, mass, *eta_sends = call(
         functools.partial(flux_kernel, grid),
-        [(3, 4, *block), block]
-        + [(2 * 4 + WIDTH, nx, nz)] * 2
-        + [(2 * 4, ny, nz)] * 2
-        + [(4, TILE, LANES)],
+        [(3, 4, *block), block] + [(2 * 4 + WIDTH, nx, nz)] * 2,
         u, prim, metrics, jacobian, slopes, own, mass_total, *ends, tables,
         scratch=[pltpu.VMEM((4, *block), jnp.float32)],
     )
-    sides, ends = exchange(*sends)
+    sends = call(
+        functools.partial(contra_sums_kernel, grid),
+        [(2 * 4, ny, nz)] * 2 + [(4, TILE, LANES)],
+        contra, tables,
+    )
+    sides, ends = exchange(*eta_sends, *sends)
     xi_source, eta_source, own = call(
         functools.partial(contra_source_kernel, grid), [(4, *block)] * 3, contra, tables,
     )
@@ -789,41 +878,50 @@
         [(4, *block)] + [(4 * WIDTH, nx, nz)] * 2,
         u, jacobian, total, *ends, tables,
     )
-    mass, mass_source, xi_first, xi_second = call(
-        functools.partial(mass_eta_kernel, grid),
-        [(1, *block)] * 2 + [(WIDTH, ny, nz)] * 2,
-        mass_source, sides[0], sides[1], eta_first,
-    )
     eta_b = pair_swap(eta_second, "eta", 1)
     eta_a = pair_swap(eta_first, "eta", 0)
+    mass, mass_source, xi_first, xi_second = call(
+        functools.partial(face_kernel, grid),
+        [(1, *block)] * 2 + [(5 * WIDTH, ny, nz)] * 2,
+        state, mass_source, sides[1], sides[0],
+    )
     xi_b = pair_swap(xi_second, "xi", 1)
     xi_a = pair_swap(xi_first, "xi", 0)
     (source,) = call(functools.partial(source_kernel, grid, eta_sources), [(4, *block)], state)
     (mass_part,) = call(
-        functools.partial(xi_filter_kernel, grid), [(1, *block)], mass_source, xi_a, xi_b, tables,
-    )
-    state, xi_first, xi_second, zeta, edge_first, edge_second = call(
+        functools.partial(mass_xi_kernel, grid), [(1, *block)], mass_source, xi_a, xi_b, tables,
+    )
+    layers = 5 * WIDTH * ny
+    halo_first, halo_second = call(
+        functools.partial(halo_source_kernel, grid),
+        [(ny * PLANES, nz)] * 2,
+        xi_a.reshape(layers, nz), xi_b.reshape(layers, nz),
+    )
+    edge_first, edge_second = call(
+        functools.partial(edge_kernel, grid), [(2 * WIDTH * PLANES, nz)] * 2, source, eta_a, eta_b,
+    )
+    edge_b = pair_swap(edge_second, "xi", 1)
+    edge_a = pair_swap(edge_first, "xi", 0)
+    state, zeta, corner_first, corner_second = call(
         functools.partial(eta_filter_kernel, grid),
-        [(4, *block)]
-        + [(4 * WIDTH, ny, nz)] * 2
-        + [(nx * TILE, LANES)]
-        + [(WIDTH, TILE, LANES)] * 2,
-        source, mass, mass_part, eta_b, eta_a,
-    )
-    xi_b = pair_swap(xi_second, "xi", 1)
+        [(4, *block), (nx * TILE, LANES)] + [(WIDTH, TILE, LANES)] * 2,
+        source, mass, eta_b, eta_a,
+    )
     ends = ring_swap(zeta, "zeta")
-    edges_b = diagonal_swap(edge_second, 1)
-    edges_a = diagonal_swap(edge_first, 0)
-    xi_a = pair_swap(xi_first, "xi", 0)
+    edges_b = diagonal_swap(corner_second, 1)
+    edges_a = diagonal_swap(corner_first, 0)
     (source,) = call(functools.partial(source_kernel, grid, xi_sources), [(4, *block)], state)
     (state,) = call(
-        functools.partial(xi_filter_kernel, grid), [(4, *block)], source, xi_a, xi_b, tables,
+        functools.partial(xi_filter_kernel, grid),
+        [(4, *block)],
+        source, halo_first, halo_second, edge_b, edge_a, tables,
+        scratch=[pltpu.VMEM((PLANES * ny, nz), jnp.float32)] * 2,
     )
     edges = [edge.reshape(WIDTH * TILE, LANES) for edge in (*edges_a, *edges_b)]
     (result,) = call(
         functools.partial(zeta_filter_kernel, grid),
         [(5, *block)],
-        mass_part, state, *ends, *edges, tables,
+        mass_part, state, *edges[2:], *ends, *edges[:2], tables,
         scratch=[pltpu.VMEM((5, *block), jnp.float32), pltpu.SemaphoreType.DMA((5,))],
         far_outs=(0,),
     )

time: 43.5 us -> 42.5 us (0.977)
  waiting for transfers between devices: 11 us -> 10.1 us
  starting transfers between devices: 22.5 us -> 21.9 us
  Pallas kernels: 9.73 us -> 10.2 us
    ppermute x14, starting transfers between devices: 15.3 us -> 14.3 us  [pair_swap(): return lax.ppermute(value, axis, pairs)]
    ppermute x2, waiting for transfers between devices: 1.01 us -> 0.53 us  [send(): return lax.ppermute(value, ('xi', 'zeta'), pairs)]
    ppermute x2, starting transfers between devices: 2.59 us -> 3.04 us  [send(): return lax.ppermute(value, ('xi', 'zeta'), pairs)]
    pallas_call x15 -> x18, Pallas kernels: 9.73 us -> 10.2 us  [call(): pl.pallas_call(kernel, out_shape=shapes, in_specs=[pl.BlockSpec(memory_sp...]
  transfers between devices with their start and end apart: 19 -> 19, of which waited for: 10 -> 10; matrix products, arithmetic and copies ran while one was open for 0% -> 0% of each run, Pallas kernels for 8% -> 11%
where the time goes in v6:
time: 42.5 us; the launch traced here: 42.4 us
  starting transfers between devices  21.9 us (52%)
  Pallas kernels  10.2 us (24%)
  waiting for transfers between devices  10.1 us (24%)
    ppermute x14, starting transfers between devices, pair_swap(): return lax.ppermute(value, axis, pairs)  14.3 us
    pallas_call x18, Pallas kernels, call(): pl.pallas_call(kernel, out_shape=shapes, in_specs=[pl.BlockSpec(memory_sp...  10.2 us
    ppermute x14, waiting for transfers between devices, pair_swap(): return lax.ppermute(value, axis, pairs)  9.37 us
    ppermute x3, starting transfers between devices, ring_swap(): other = lax.ppermute(value, axis, [(0, 1), (1, 0)])  4.62 us
    ppermute x2, starting transfers between devices, send(): return lax.ppermute(value, ('xi', 'zeta'), pairs)  3.04 us
  transfers between devices with their start and end apart: 19, of which 10 were waited for; matrix products, arithmetic and copies ran while one was open for 0% of the time, Pallas kernels for 11%

profile of v6, /device:TPU:0, one launch (start us, length us, event | category | flops | bytes accessed | tf_op | source)
XLA Modules:
  0.0 42.4 jit_solution(327072010246446535)
XLA Ops:
  0.0 2.4 %shard_map.46 = (f32[5,256,128]{2,1,0:T(8,128)S(1)}, f32[5,128,128]{2,1,0:T(8,128)S(1)}, f32[9,256,128]{2,1,0:T(8,128)S(1)}, f32[256,128]{1,0:T(8,128)S(1)}, f32...) custom-call(f32[5,256,128]{2,1,0:T(8,128)} %bitcast.17, ...), custom_call_target="tpu_custom_call" | custom-call | bytes 3600000 | tf_op jit(solution)/shard_map/pallas_call | solution.py:796
  2.4 5.1 %collective-permute-start = (f32[10,16,128]{2,1,0:T(8,128)S(1)}, f32[10,16,128]{2,1,0:T(8,128)S(1)}, u32[]{:S(2)}, u32[]{:S(2)}) collective-permute-start(f32[10,16,128]{2,1,0:T(8,128)S(1)} %get-tuple-element.55), channel_id=1, source_target_pairs={{0,6},{2,4},{4,2},{6,0},{1,7},{3,5},{5,3},{7,1},{8,14},{10,12},{12... | collective-permute-start | bytes 245768 | tf_op jit(solution)/shard_map/ppermute | solution.py:755
  7.5 0.0 collective-permute-start.1
  7.5 0.7 %collective-permute-start.2 = (f32[10,16,128]{2,1,0:T(8,128)S(1)}, f32[10,16,128]{2,1,0:T(8,128)S(1)}, u32[]{:S(2)}, u32[]{:S(2)}) collective-permute-start(f32[10,16,128]{2,1,0:T(8,128)S(1)} %get-tuple-element.57), channel_id=1, source_target_pairs={{0,24},{8,16},{16,8},{24,0},{1,25},{9,17},{17,9},{25,1},{2,26},{10... | collective-permute-start | bytes 245768 | tf_op jit(solution)/shard_map/ppermute | solution.py:755
  8.2 1.0 %collective-permute-start.3 = (f32[10,16,128]{2,1,0:T(8,128)S(1)}, f32[10,16,128]{2,1,0:T(8,128)S(1)}, u32[]{:S(2)}, u32[]{:S(2)}) collective-permute-start(f32[10,16,128]{2,1,0:T(8,128)S(1)} %get-tuple-element.58), channel_id=1, source_target_pairs={{0,8},{8,0},{16,24},{24,16},{1,9},{9,1},{17,25},{25,17},{2,10},{10... | collective-permute-start | bytes 245768 | tf_op jit(solution)/shard_map/ppermute | solution.py:755
  9.1 1.5 %collective-permute-start.4 = (f32[5,8,128]{2,1,0:T(8,128)S(1)}, f32[5,8,128]{2,1,0:T(8,128)S(1)}, u32[]{:S(2)}, u32[]{:S(2)}) collective-permute-start(f32[5,8,128]{2,1,0:T(8,128)S(1)} %get-tuple-element.61), channel_id=1, source_target_pairs={{0,1},{1,0},{2,3},{3,2},{4,5},{5,4},{6,7},{7,6},{8,9},{9,8},{10,11... | collective-permute-start | bytes 61448 | tf_op jit(solution)/shard_map/ppermute | solution.py:776
  10.7 0.6 %shard_map.47 = (f32[5,256,128]{2,1,0:T(8,128)S(1)}, f32[5,256,128]{2,1,0:T(8,128)S(1)}, f32[5,256,128]{2,1,0:T(8,128)S(1)}) custom-call(f32[4,256,128]{2,1,0:T(8,128)S(1)} %get-tuple-element.48.prim_ref, f32[3,256,128]{2,1,0:T(8,128)S(1)} %get-tuple-element.50.mass_ref, f32[5,128,128]{2,1,0:T(8,128)S(1)} %get-tuple-element.51.tables_ref), custom_call_target="tpu_custom_call" | custom-call | bytes 3600000 | tf_op jit(solution)/shard_map/pallas_call | solution.py:796
  11.2 0.0 collective-permute-done.eta_b
  11.3 0.7 %collective-permute-done.1.eta_a = f32[10,16,128]{2,1,0:T(8,128)S(1)} collective-permute-done((f32[10,16,128]{2,1,0:T(8,128)S(1)}, f32[10,16,128]{2,1,0:T(8,128)S(1)}, u32[]{:S(2)}, u32[]{:S(2)}) %collective-permute-start.1) | collective-permute-done | bytes 81952 | tf_op jit(solution)/shard_map/ppermute | solution.py:755
  12.0 0.2 collective-permute-done.2.xi_b
  12.2 0.5 %shard_map.48 = (f32[2,4,256,128]{3,2,1,0:T(8,128)S(1)}, f32[256,128]{1,0:T(8,128)S(1)}) custom-call(f32[5,256,128]{2,1,0:T(8,128)S(1)} %get-tuple-element.52.xi_source, f32[5,256,128]{2,1,0:T(8,128)S(1)} %get-tuple-element.53.eta_source, f32[5,256,128]{2,1,0:T(8,128)S(1)} %get-tuple-element.54.own_ref, f32[10,16,128]{2,1,0:T(8,128)S(1)} %collective-permute-done.eta_b, ...), custom_call_target="tpu_custom_call" | custom-call | bytes 3600000 | tf_op jit(solution)/shard_map/pallas_call | solution.py:796
  12.7 0.2 collective-permute-done.4.zeta_below.zeta_above
  12.9 1.4 %shard_map.49 = (f32[3,4,256,128]{3,2,1,0:T(8,128)S(1)}, f32[256,128]{1,0:T(8,128)S(1)}, f32[13,16,128]{2,1,0:T(8,128)S(1)}, f32[13,16,128]{2,1,0:T(8,128)S(1)}) custom-call(f32[5,256,128]{2,1,0:T(8,128)S(1)} %get-tuple-element.46.u_ref, f32[4,256,128]{2,1,0:T(8,128)S(1)} %get-tuple-element.48.prim_ref, f32[9,256,128]{2,1,0:T(8,128)S(1)} %get-tuple-element.49.metrics_ref, ...), custom_call_target="tpu_custom_call" | custom-call | bytes 3600000 | tf_op jit(solution)/shard_map/pallas_call | solution.py:796
  14.3 2.0 %collective-permute-start.5 = (f32[13,16,128]{2,1,0:T(8,128)S(1)}, f32[13,16,128]{2,1,0:T(8,128)S(1)}, u32[]{:S(2)}, u32[]{:S(2)}) collective-permute-start(f32[13,16,128]{2,1,0:T(8,128)S(1)} %get-tuple-element.66), channel_id=1, source_target_pairs={{0,6},{2,4},{4,2},{6,0},{1,7},{3,5},{5,3},{7,1},{8,14},{10,12},{12... | collective-permute-start | bytes 319496 | tf_op jit(solution)/shard_map/ppermute | solution.py:755
  16.4 0.1 collective-permute-start.6
  16.5 0.4 shard_map.51
  16.9 0.1 collective-permute-start.7
  17.0 1.5 %collective-permute-start.8 = (f32[8,16,128]{2,1,0:T(8,128)S(1)}, f32[8,16,128]{2,1,0:T(8,128)S(1)}, u32[]{:S(2)}, u32[]{:S(2)}) collective-permute-start(f32[8,16,128]{2,1,0:T(8,128)S(1)} %get-tuple-element.69), channel_id=1, source_target_pairs={{0,8},{8,0},{16,24},{24,16},{1,9},{9,1},{17,25},{25,17},{2,10},{10... | collective-permute-start | bytes 196616 | tf_op jit(solution)/shard_map/ppermute | solution.py:755
  18.4 1.5 %collective-permute-start.9 = (f32[4,8,128]{2,1,0:T(8,128)S(1)}, f32[4,8,128]{2,1,0:T(8,128)S(1)}, u32[]{:S(2)}, u32[]{:S(2)}) collective-permute-start(f32[4,8,128]{2,1,0:T(8,128)S(1)} %get-tuple-element.70), channel_id=1, source_target_pairs={{0,1},{1,0},{2,3},{3,2},{4,5},{5,4},{6,7},{7,6},{8,9},{9,8},{10,11... | collective-permute-start | bytes 49160 | tf_op jit(solution)/shard_map/ppermute | solution.py:776
  20.0 0.5 %shard_map.50 = (f32[4,256,128]{2,1,0:T(8,128)S(1)}, f32[4,256,128]{2,1,0:T(8,128)S(1)}, f32[4,256,128]{2,1,0:T(8,128)S(1)}) custom-call(f32[3,4,256,128]{3,2,1,0:T(8,128)S(1)} %get-tuple-element.62.contra_ref, f32[5,128,128]{2,1,0:T(8,128)S(1)} %get-tuple-element.51.tables_ref), custom_call_target="tpu_custom_call" | custom-call | bytes 3600000 | tf_op jit(solution)/shard_map/pallas_call | solution.py:796
  20.5 0.8 %collective-permute-done.7.xi_b = f32[8,16,128]{2,1,0:T(8,128)S(1)} collective-permute-done((f32[8,16,128]{2,1,0:T(8,128)S(1)}, f32[8,16,128]{2,1,0:T(8,128)S(1)}, u32[]{:S(2)}, u32[]{:S(2)}) %collective-permute-start.7) | collective-permute-done | bytes 65568 | tf_op jit(solution)/shard_map/ppermute | solution.py:755
  21.3 0.8 %collective-permute-done.5.eta_b = f32[13,16,128]{2,1,0:T(8,128)S(1)} collective-permute-done((f32[13,16,128]{2,1,0:T(8,128)S(1)}, f32[13,16,128]{2,1,0:T(8,128)S(1)}, u32[]{:S(2)}, u32[]{:S(2)}) %collective-permute-start.5) | collective-permute-done | bytes 106528 | tf_op jit(solution)/shard_map/ppermute | solution.py:755
  22.0 0.2 collective-permute-done.6.eta_a
  22.2 0.5 %shard_map.52.total_ref = f32[4,256,128]{2,1,0:T(8,128)S(1)} custom-call(f32[4,256,128]{2,1,0:T(8,128)S(1)} %get-tuple-element.63.xi_source, f32[4,256,128]{2,1,0:T(8,128)S(1)} %get-tuple-element.64.eta_source, f32[4,256,128]{2,1,0:T(8,128)S(1)} %get-tuple-element.65.own_ref, f32[13,16,128]{2,1,0:T(8,128)S(1)} %collective-permute-done.5.eta_b, ...), custom_call_target="tpu_custom_call" | custom-call | bytes 3600000 | tf_op jit(solution)/shard_map/pallas_call | solution.py:796
  22.7 0.4 %shard_map.53 = (f32[4,256,128]{2,1,0:T(8,128)S(1)}, f32[20,16,128]{2,1,0:T(8,128)S(1)}, f32[20,16,128]{2,1,0:T(8,128)S(1)}) custom-call(f32[5,256,128]{2,1,0:T(8,128)S(1)} %get-tuple-element.46.u_ref, f32[256,128]{1,0:T(8,128)S(1)} %get-tuple-element.47.jacobian_ref, f32[4,256,128]{2,1,0:T(8,128)S(1)} %shard_map.52.total_ref, ...), custom_call_target="tpu_custom_call" | custom-call | bytes 3600000 | tf_op jit(solution)/shard_map/pallas_call | solution.py:796
  23.2 2.1 %collective-permute-start.12 = (f32[20,16,128]{2,1,0:T(8,128)S(1)}, f32[20,16,128]{2,1,0:T(8,128)S(1)}, u32[]{:S(2)}, u32[]{:S(2)}) collective-permute-start(f32[20,16,128]{2,1,0:T(8,128)S(1)} %get-tuple-element.77), channel_id=1, source_target_pairs={{0,6},{2,4},{4,2},{6,0},{1,7},{3,5},{5,3},{7,1},{8,14},{10,12},{12... | collective-permute-start | bytes 491528 | tf_op jit(solution)/shard_map/ppermute | solution.py:755
  25.3 0.1 collective-permute-start.13
  25.5 0.1 shard_map.54.source_ref
  25.5 0.2 shard_map.55
  25.7 0.1 collective-permute-start.10
  25.8 1.1 %collective-permute-start.11 = (f32[25,16,128]{2,1,0:T(8,128)S(1)}, f32[25,16,128]{2,1,0:T(8,128)S(1)}, u32[]{:S(2)}, u32[]{:S(2)}) collective-permute-start(f32[25,16,128]{2,1,0:T(8,128)S(1)} %get-tuple-element.75), channel_id=1, source_target_pairs={{0,24},{8,16},{16,8},{24,0},{1,25},{9,17},{17,9},{25,1},{2,26},{10... | collective-permute-start | bytes 614408 | tf_op jit(solution)/shard_map/ppermute | solution.py:755
  26.9 0.3 shard_map.57.source_ref.order_ref
  27.2 4.8 %collective-permute-done.12.eta_b = f32[20,16,128]{2,1,0:T(8,128)S(1)} collective-permute-done((f32[20,16,128]{2,1,0:T(8,128)S(1)}, f32[20,16,128]{2,1,0:T(8,128)S(1)}, u32[]{:S(2)}, u32[]{:S(2)}) %collective-permute-start.12) | collective-permute-done | bytes 163872 | tf_op jit(solution)/shard_map/ppermute | solution.py:755
  32.1 1.8 %collective-permute-done.13.eta_a = f32[20,16,128]{2,1,0:T(8,128)S(1)} collective-permute-done((f32[20,16,128]{2,1,0:T(8,128)S(1)}, f32[20,16,128]{2,1,0:T(8,128)S(1)}, u32[]{:S(2)}, u32[]{:S(2)}) %collective-permute-start.13) | collective-permute-done | bytes 163872 | tf_op jit(solution)/shard_map/ppermute | solution.py:755
  33.8 0.1 shard_map.61
  33.9 0.1 collective-permute-start.14
  34.0 0.3 collective-permute-start.15
  34.2 0.4 %shard_map.58 = (f32[4,256,128]{2,1,0:T(8,128)S(1)}, f32[128,128]{1,0:T(8,128)S(1)}, f32[5,8,128]{2,1,0:T(8,128)S(1)}, f32[5,8,128]{2,1,0:T(8,128)S(1)}) custom-call(f32[4,256,128]{2,1,0:T(8,128)S(1)} %shard_map.57.source_ref.order_ref, f32[1,256,128]{2,1,0:T(8,128)S(1)} %get-tuple-element.76.mass_ref, f32[20,16,128]{2,1,0:T(8,128)S(1)} %collective-permute-done.12.eta_b, ...), custom_call_target="tpu_custom_call" | custom-call | bytes 3600000 | tf_op jit(solution)/shard_map/pallas_call | solution.py:796
  34.7 1.6 %collective-permute-start.17 = (f32[128,128]{1,0:T(8,128)S(1)}, f32[128,128]{1,0:T(8,128)S(1)}, u32[]{:S(2)}, u32[]{:S(2)}) collective-permute-start(f32[128,128]{1,0:T(8,128)S(1)} %get-tuple-element.85), channel_id=1, source_target_pairs={{0,1},{1,0},{2,3},{3,2},{4,5},{5,4},{6,7},{7,6},{8,9},{9,8},{10,11... | collective-permute-start | bytes 196616 | tf_op jit(solution)/shard_map/ppermute | solution.py:776
  36.3 1.1 %collective-permute-start.16 = (f32[5,8,128]{2,1,0:T(8,128)S(1)}, f32[5,8,128]{2,1,0:T(8,128)S(1)}, u32[]{:S(2)}, u32[]{:S(2)}) collective-permute-start(f32[5,8,128]{2,1,0:T(8,128)S(1)} %get-tuple-element.84), channel_id=1, source_target_pairs={{0,25},{1,24},{8,17},{9,16},{16,9},{17,8},{24,1},{25,0},{2,27},{3,... | collective-permute-start | bytes 61448 | tf_op jit(solution)/shard_map/ppermute | solution.py:767
  37.4 1.9 %collective-permute-start.18 = (f32[5,8,128]{2,1,0:T(8,128)S(1)}, f32[5,8,128]{2,1,0:T(8,128)S(1)}, u32[]{:S(2)}, u32[]{:S(2)}) collective-permute-start(f32[5,8,128]{2,1,0:T(8,128)S(1)} %get-tuple-element.86), channel_id=1, source_target_pairs={{0,9},{1,8},{8,1},{9,0},{16,25},{17,24},{24,17},{25,16},{2,11},{3,... | collective-permute-start | bytes 61448 | tf_op jit(solution)/shard_map/ppermute | solution.py:767
  39.3 0.2 shard_map.59.source_ref
  39.6 0.2 shard_map.60
  39.8 0.2 shard_map.56.mass_ref
  40.0 0.6 %shard_map.62.state_ref = f32[4,256,128]{2,1,0:T(8,128)S(1)} custom-call(f32[4,256,128]{2,1,0:T(8,128)S(1)} %shard_map.59.source_ref, f32[384,128]{1,0:T(8,128)S(1)} %get-tuple-element.80.first_source, f32[384,128]{1,0:T(8,128)S(1)} %get-tuple-element.81.second_source, f32[240,128]{1,0:T(8,128)S(1)} %collective-permute-done.14.edge_b, ...), custom_call_target="tpu_custom_call" | custom-call | bytes 3600000 | tf_op jit(solution)/shard_map/pallas_call | solution.py:796
  40.6 0.4 collective-permute-done.16
  41.0 0.2 collective-permute-done.18
  41.2 1.2 %shard_map.63 = f32[5,256,128]{2,1,0:T(8,128)} custom-call(f32[1,256,128]{2,1,0:T(8,128)S(1)} %shard_map.56.mass_ref, f32[4,256,128]{2,1,0:T(8,128)S(1)} %shard_map.62.state_ref, f32[40,128]{1,0:T(8,128)S(1)} %bitcast.12, f32[40,128]{1,0:T(8,128)S(1)} %bitcast.13, f32[128,128]{1,0:T(8,128)S(1)} %collective-permute-done.17.below_ref.above_ref, ...), custom_call_target="tpu_custom_call" | custom-call | bytes 3600000 | tf_op jit(solution)/shard_map/pallas_call | solution.py:796
  (8 shorter events, 0.0 us)
Async XLA Ops:
  2.4 8.8 %collective-permute-start = (f32[10,16,128]{2,1,0:T(8,128)S(1)}, f32[10,16,128]{2,1,0:T(8,128)S(1)}, u32[]{:S(2)}, u32[]{:S(2)}) collective-permute-start(f32[10,16,128]{2,1,0:T(8,128)S(1)} %get-tuple-element.55), channel_id=1, source_target_pairs={{0,6},{2,4},{4,2},{6,0},{1,7},{3,5},{5,3},{7,1},{8,14},{10,12},{12... | collective-permute-start | bytes 245768 | tf_op jit(solution)/shard_map/ppermute | solution.py:755
  7.5 4.5 %collective-permute-start.1 = (f32[10,16,128]{2,1,0:T(8,128)S(1)}, f32[10,16,128]{2,1,0:T(8,128)S(1)}, u32[]{:S(2)}, u32[]{:S(2)}) collective-permute-start(f32[10,16,128]{2,1,0:T(8,128)S(1)} %get-tuple-element.56), channel_id=1, source_target_pairs={{0,2},{2,0},{4,6},{6,4},{1,3},{3,1},{5,7},{7,5},{8,10},{10,8},{12,... | collective-permute-start | bytes 245768 | tf_op jit(solution)/shard_map/ppermute | solution.py:755
  7.5 4.7 %collective-permute-start.2 = (f32[10,16,128]{2,1,0:T(8,128)S(1)}, f32[10,16,128]{2,1,0:T(8,128)S(1)}, u32[]{:S(2)}, u32[]{:S(2)}) collective-permute-start(f32[10,16,128]{2,1,0:T(8,128)S(1)} %get-tuple-element.57), channel_id=1, source_target_pairs={{0,24},{8,16},{16,8},{24,0},{1,25},{9,17},{17,9},{25,1},{2,26},{10... | collective-permute-start | bytes 245768 | tf_op jit(solution)/shard_map/ppermute | solution.py:755
  8.2 4.0 %collective-permute-start.3 = (f32[10,16,128]{2,1,0:T(8,128)S(1)}, f32[10,16,128]{2,1,0:T(8,128)S(1)}, u32[]{:S(2)}, u32[]{:S(2)}) collective-permute-start(f32[10,16,128]{2,1,0:T(8,128)S(1)} %get-tuple-element.58), channel_id=1, source_target_pairs={{0,8},{8,0},{16,24},{24,16},{1,9},{9,1},{17,25},{25,17},{2,10},{10... | collective-permute-start | bytes 245768 | tf_op jit(solution)/shard_map/ppermute | solution.py:755
  9.1 3.8 %collective-permute-start.4 = (f32[5,8,128]{2,1,0:T(8,128)S(1)}, f32[5,8,128]{2,1,0:T(8,128)S(1)}, u32[]{:S(2)}, u32[]{:S(2)}) collective-permute-start(f32[5,8,128]{2,1,0:T(8,128)S(1)} %get-tuple-element.61), channel_id=1, source_target_pairs={{0,1},{1,0},{2,3},{3,2},{4,5},{5,4},{6,7},{7,6},{8,9},{9,8},{10,11... | collective-permute-start | bytes 61448 | tf_op jit(solution)/shard_map/ppermute | solution.py:776
  14.3 7.7 %collective-permute-start.5 = (f32[13,16,128]{2,1,0:T(8,128)S(1)}, f32[13,16,128]{2,1,0:T(8,128)S(1)}, u32[]{:S(2)}, u32[]{:S(2)}) collective-permute-start(f32[13,16,128]{2,1,0:T(8,128)S(1)} %get-tuple-element.66), channel_id=1, source_target_pairs={{0,6},{2,4},{4,2},{6,0},{1,7},{3,5},{5,3},{7,1},{8,14},{10,12},{12... | collective-permute-start | bytes 319496 | tf_op jit(solution)/shard_map/ppermute | solution.py:755
  16.4 5.9 %collective-permute-start.6 = (f32[13,16,128]{2,1,0:T(8,128)S(1)}, f32[13,16,128]{2,1,0:T(8,128)S(1)}, u32[]{:S(2)}, u32[]{:S(2)}) collective-permute-start(f32[13,16,128]{2,1,0:T(8,128)S(1)} %get-tuple-element.67), channel_id=1, source_target_pairs={{0,2},{2,0},{4,6},{6,4},{1,3},{3,1},{5,7},{7,5},{8,10},{10,8},{12,... | collective-permute-start | bytes 319496 | tf_op jit(solution)/shard_map/ppermute | solution.py:755
  16.9 4.4 %collective-permute-start.7 = (f32[8,16,128]{2,1,0:T(8,128)S(1)}, f32[8,16,128]{2,1,0:T(8,128)S(1)}, u32[]{:S(2)}, u32[]{:S(2)}) collective-permute-start(f32[8,16,128]{2,1,0:T(8,128)S(1)} %get-tuple-element.68), channel_id=1, source_target_pairs={{0,24},{8,16},{16,8},{24,0},{1,25},{9,17},{17,9},{25,1},{2,26},{10... | collective-permute-start | bytes 196616 | tf_op jit(solution)/shard_map/ppermute | solution.py:755
  17.0 4.3 %collective-permute-start.8 = (f32[8,16,128]{2,1,0:T(8,128)S(1)}, f32[8,16,128]{2,1,0:T(8,128)S(1)}, u32[]{:S(2)}, u32[]{:S(2)}) collective-permute-start(f32[8,16,128]{2,1,0:T(8,128)S(1)} %get-tuple-element.69), channel_id=1, source_target_pairs={{0,8},{8,0},{16,24},{24,16},{1,9},{9,1},{17,25},{25,17},{2,10},{10... | collective-permute-start | bytes 196616 | tf_op jit(solution)/shard_map/ppermute | solution.py:755
  18.4 4.3 %collective-permute-start.9 = (f32[4,8,128]{2,1,0:T(8,128)S(1)}, f32[4,8,128]{2,1,0:T(8,128)S(1)}, u32[]{:S(2)}, u32[]{:S(2)}) collective-permute-start(f32[4,8,128]{2,1,0:T(8,128)S(1)} %get-tuple-element.70), channel_id=1, source_target_pairs={{0,1},{1,0},{2,3},{3,2},{4,5},{5,4},{6,7},{7,6},{8,9},{9,8},{10,11... | collective-permute-start | bytes 49160 | tf_op jit(solution)/shard_map/ppermute | solution.py:776
  23.2 8.9 %collective-permute-start.12 = (f32[20,16,128]{2,1,0:T(8,128)S(1)}, f32[20,16,128]{2,1,0:T(8,128)S(1)}, u32[]{:S(2)}, u32[]{:S(2)}) collective-permute-start(f32[20,16,128]{2,1,0:T(8,128)S(1)} %get-tuple-element.77), channel_id=1, source_target_pairs={{0,6},{2,4},{4,2},{6,0},{1,7},{3,5},{5,3},{7,1},{8,14},{10,12},{12... | collective-permute-start | bytes 491528 | tf_op jit(solution)/shard_map/ppermute | solution.py:755
  25.3 8.5 %collective-permute-start.13 = (f32[20,16,128]{2,1,0:T(8,128)S(1)}, f32[20,16,128]{2,1,0:T(8,128)S(1)}, u32[]{:S(2)}, u32[]{:S(2)}) collective-permute-start(f32[20,16,128]{2,1,0:T(8,128)S(1)} %get-tuple-element.78), channel_id=1, source_target_pairs={{0,2},{2,0},{4,6},{6,4},{1,3},{3,1},{5,7},{7,5},{8,10},{10,8},{12,... | collective-permute-start | bytes 491528 | tf_op jit(solution)/shard_map/ppermute | solution.py:755
  25.7 10.6 %collective-permute-start.10 = (f32[25,16,128]{2,1,0:T(8,128)S(1)}, f32[25,16,128]{2,1,0:T(8,128)S(1)}, u32[]{:S(2)}, u32[]{:S(2)}) collective-permute-start(f32[25,16,128]{2,1,0:T(8,128)S(1)} %get-tuple-element.74), channel_id=1, source_target_pairs={{0,8},{8,0},{16,24},{24,16},{1,9},{9,1},{17,25},{25,17},{2,10},{10... | collective-permute-start | bytes 614408 | tf_op jit(solution)/shard_map/ppermute | solution.py:755
  25.8 11.6 %collective-permute-start.11 = (f32[25,16,128]{2,1,0:T(8,128)S(1)}, f32[25,16,128]{2,1,0:T(8,128)S(1)}, u32[]{:S(2)}, u32[]{:S(2)}) collective-permute-start(f32[25,16,128]{2,1,0:T(8,128)S(1)} %get-tuple-element.75), channel_id=1, source_target_pairs={{0,24},{8,16},{16,8},{24,0},{1,25},{9,17},{17,9},{25,1},{2,26},{10... | collective-permute-start | bytes 614408 | tf_op jit(solution)/shard_map/ppermute | solution.py:755
  33.9 6.2 %collective-permute-start.14 = (f32[240,128]{1,0:T(8,128)S(1)}, f32[240,128]{1,0:T(8,128)S(1)}, u32[]{:S(2)}, u32[]{:S(2)}) collective-permute-start(f32[240,128]{1,0:T(8,128)S(1)} %get-tuple-element.82), channel_id=1, source_target_pairs={{0,24},{8,16},{16,8},{24,0},{1,25},{9,17},{17,9},{25,1},{2,26},{10... | collective-permute-start | bytes 368648 | tf_op jit(solution)/shard_map/ppermute | solution.py:755
  34.0 6.1 %collective-permute-start.15 = (f32[240,128]{1,0:T(8,128)S(1)}, f32[240,128]{1,0:T(8,128)S(1)}, u32[]{:S(2)}, u32[]{:S(2)}) collective-permute-start(f32[240,128]{1,0:T(8,128)S(1)} %get-tuple-element.83), channel_id=1, source_target_pairs={{0,8},{8,0},{16,24},{24,16},{1,9},{9,1},{17,25},{25,17},{2,10},{10... | collective-permute-start | bytes 368648 | tf_op jit(solution)/shard_map/ppermute | solution.py:755
  34.7 6.5 %collective-permute-start.17 = (f32[128,128]{1,0:T(8,128)S(1)}, f32[128,128]{1,0:T(8,128)S(1)}, u32[]{:S(2)}, u32[]{:S(2)}) collective-permute-start(f32[128,128]{1,0:T(8,128)S(1)} %get-tuple-element.85), channel_id=1, source_target_pairs={{0,1},{1,0},{2,3},{3,2},{4,5},{5,4},{6,7},{7,6},{8,9},{9,8},{10,11... | collective-permute-start | bytes 196616 | tf_op jit(solution)/shard_map/ppermute | solution.py:776
  36.3 4.7 %collective-permute-start.16 = (f32[5,8,128]{2,1,0:T(8,128)S(1)}, f32[5,8,128]{2,1,0:T(8,128)S(1)}, u32[]{:S(2)}, u32[]{:S(2)}) collective-permute-start(f32[5,8,128]{2,1,0:T(8,128)S(1)} %get-tuple-element.84), channel_id=1, source_target_pairs={{0,25},{1,24},{8,17},{9,16},{16,9},{17,8},{24,1},{25,0},{2,27},{3,... | collective-permute-start | bytes 61448 | tf_op jit(solution)/shard_map/ppermute | solution.py:767
  37.4 3.8 %collective-permute-start.18 = (f32[5,8,128]{2,1,0:T(8,128)S(1)}, f32[5,8,128]{2,1,0:T(8,128)S(1)}, u32[]{:S(2)}, u32[]{:S(2)}) collective-permute-start(f32[5,8,128]{2,1,0:T(8,128)S(1)} %get-tuple-element.86), channel_id=1, source_target_pairs={{0,9},{1,8},{8,1},{9,0},{16,25},{17,24},{24,17},{25,16},{2,11},{3,... | collective-permute-start | bytes 61448 | tf_op jit(solution)/shard_map/ppermute | solution.py:767

commit v7 on v6

--- a/solution.py
+++ b/solution.py
@@ -112,10 +112,10 @@
     smooth = own_rows(*filter_system(length), length)
     ends = np.concatenate([smooth[:, :WIDTH], smooth[:, WIDTH + length :]], axis=1)
     tables = [table[:, own].T, pad_columns(sums), pad_rows(back), smooth[:, own].T, pad_rows(ends.T)]
-    return np.stack(tables).astype(np.float32)
-
-
-DERIVE, SUMS, BACK, SMOOTH, ENDS = range(5)
+    return tables.pop(1).astype(np.float32), np.stack(tables).astype(np.float32)
+
+
+DERIVE, BACK, SMOOTH, ENDS = range(4)
 
 
 def twisted_solve(rights, pivots, off):
@@ -293,35 +293,31 @@
 
 def primitive_kernel(
     grid,
-    u_hbm, tables_hbm, metrics_hbm, jacobian_hbm,
-    u_ref, tables_ref, metrics_ref, jacobian_ref,
+    u_hbm, sums_hbm, metrics_hbm,
+    u_ref, sums_ref, metrics_ref,
     prim_ref, mass_ref, eta_first, eta_second, xi_first, xi_second, zeta_ref,
     u_sems, late_sems,
 ):
     chunks = u_sems.shape[0]
     step = grid.rows // chunks
+    weights = pltpu.make_async_copy(sums_hbm, sums_ref, late_sems.at[0])
+    weights.start()
     copies = []
     for index in range(chunks):
         rows = pl.ds(index * step, step)
-        for field in range(5):
-            copy = pltpu.make_async_copy(
-                u_hbm.at[field, rows, :], u_ref.at[field, rows, :], u_sems.at[index, field]
-            )
-            copy.start()
-            copies.append(copy)
+        copy = pltpu.make_async_copy(u_hbm.at[:, rows, :], u_ref.at[:, rows, :], u_sems.at[index])
+        copy.start()
+        copies.append(copy)
     late = [
         pltpu.make_async_copy(source, result, late_sems.at[index])
         for index, (source, result) in enumerate(
-            [(tables_hbm, tables_ref)]
-            + [(metrics_hbm.at[k], metrics_ref.at[k]) for k in range(9)]
-            + [(jacobian_hbm, jacobian_ref)]
+            [(sums_hbm, sums_ref)] + [(metrics_hbm, metrics_ref)]
         )
     ]
-    for copy in late:
+    for copy in late[1:]:
         copy.start()
     for index in range(chunks):
-        for copy in copies[5 * index : 5 * index + 5]:
-            copy.wait()
+        copies[index].wait()
         rows = pl.ds(index * step, step)
         inverse = 1.0 / u_ref[0, rows, :]
         work = None
@@ -345,7 +341,11 @@
 
     for field in range(4):
         send(prim_ref.at[field], prim_ref.at[field], field)
-    for copy in late:
+    weights.wait()
+    sums = split_weights(sums_ref[...])
+    for field in range(4):
+        zeta_ref[field] = pack_sums(prim_ref[field], sums, grid)
+    for copy in late[1:]:
         copy.wait()
     for k in range(3):
         for index in range(chunks):
@@ -356,10 +356,19 @@
                 + metrics_ref[3 * k + 2, rows, :] * u_ref[3, rows, :]
             )
     send(mass_ref.at[0], mass_ref.at[1], 4)
-    sums = split_weights(tables_ref[SUMS])
-    for field in range(5):
-        values = prim_ref[field] if field < 4 else mass_ref[2]
-        zeta_ref[field] = pack_sums(values, sums, grid)
+    zeta_ref[4] = pack_sums(mass_ref[2], sums, grid)
+
+
+def fetch_kernel(count, *refs):
+    sources, results, sems = refs[:count], refs[count + 1 : 2 * count + 1], refs[-1]
+    copies = [
+        pltpu.make_async_copy(source, result, sems.at[index])
+        for index, (source, result) in enumerate(zip(sources, results))
+    ]
+    for copy in copies:
+        copy.start()
+    for copy in copies:
+        copy.wait()
 
 
 def derive_sources(grid, xi_value, eta_value, zeta_value, derive, field, xi_ref, eta_ref, zeta_ref):
@@ -410,7 +419,7 @@
             total_ref[rows, :] = total_ref[rows, :] + value
 
 
-def slope_kernel(grid, xi_source, eta_source, own_ref, eta_b, eta_a, xi_b, xi_a, slope_ref, mass_total_ref):
+def slope_kernel(grid, xi_source, eta_source, own_ref, eta_a, eta_b, xi_b, xi_a, slope_ref, mass_total_ref):
     for field in range(4):
         for group in range(grid.eta_groups):
             for i, value in enumerate(xi_derivative(grid, xi_source, xi_a, xi_b, field, group)):
@@ -493,8 +502,8 @@
         )
 
 
-def contra_sums_kernel(grid, contra_ref, tables_ref, xi_first, xi_second, zeta_ref):
-    sums = split_weights(tables_ref[SUMS])
+def contra_sums_kernel(grid, contra_ref, sums_ref, xi_first, xi_second, zeta_ref):
+    sums = split_weights(sums_ref[...])
     for field in range(4):
         send_sums(
             lambda position, group: contra_ref[0, field, grid.xi_tile(position, group), :],
@@ -503,7 +512,7 @@
         zeta_ref[field] = pack_sums(contra_ref[2, field], sums, grid)
 
 
-def divergence_kernel(grid, xi_source, eta_source, own_ref, eta_b, eta_a, xi_b, xi_a, total_ref):
+def divergence_kernel(grid, xi_source, eta_source, own_ref, eta_a, eta_b, xi_b, xi_a, total_ref):
     for field in range(4):
         add_derivatives(
             grid, xi_source, eta_source, own_ref, eta_a, eta_b, xi_a, xi_b, field, total_ref.at[field]
@@ -628,7 +637,7 @@
                 source[pl.ds(i * PLANES + tile * TILE, TILE), :] = value
 
 
-def edge_kernel(grid, order_ref, eta_a, eta_b, first_ref, second_ref):
+def edge_kernel(grid, order_ref, eta_b, eta_a, first_ref, second_ref):
     flag = odd("xi")
     eta_flag = odd("eta")
     for side in range(2):
@@ -658,7 +667,7 @@
 
 
 def eta_filter_kernel(
-    grid, source_ref, mass_ref, eta_b, eta_a,
+    grid, source_ref, mass_ref, eta_a, eta_b,
     result_ref, zeta_ref, edge_first, edge_second,
 ):
     flag = odd("xi")
@@ -819,7 +828,7 @@
     u = conserved_solution.reshape(5, rows, nz)
     metrics = metrics.reshape(9, rows, nz)
     jacobian = jacobian.reshape(rows, nz)
-    tables = jnp.asarray(zeta_tables(nz))
+    sums, tables = (jnp.asarray(table) for table in zeta_tables(nz))
 
     def exchange(eta_first, eta_second, xi_first, xi_second, zeta):
         eta_b = pair_swap(eta_second, "eta", 1)
@@ -827,19 +836,26 @@
         xi_b = pair_swap(xi_second, "xi", 1)
         below, above = ring_swap(zeta, "zeta")
         xi_a = pair_swap(xi_first, "xi", 0)
-        return (eta_b, eta_a, xi_b, xi_a), (below, above)
+        return (eta_a, eta_b, xi_b, xi_a), (below, above)
 
     block = (rows, nz)
     chunks = 2
-    u, tables, metrics, jacobian, prim, mass, *sends = call(
+    u, sums, metrics, prim, mass, *sends = call(
         functools.partial(primitive_kernel, grid),
-        [like(u), like(tables), like(metrics), like(jacobian), (4, *block), (3, *block)]
+        [like(u), like(sums), like(metrics), (4, *block), (3, *block)]
         + [(2 * 5, nx, nz)] * 2
         + [(2 * 5, ny, nz)] * 2
         + [(5, TILE, LANES)],
-        u, tables, metrics, jacobian,
-        scratch=[pltpu.SemaphoreType.DMA((chunks, 5)), pltpu.SemaphoreType.DMA((11,))],
-        far=(0, 1, 2, 3),
+        u, sums, metrics,
+        scratch=[pltpu.SemaphoreType.DMA((chunks,)), pltpu.SemaphoreType.DMA((10,))],
+        far=(0, 1, 2),
+    )
+    tables, jacobian = call(
+        functools.partial(fetch_kernel, 2),
+        [like(tables), like(jacobian)],
+        tables, jacobian, sends[-1],
+        scratch=[pltpu.SemaphoreType.DMA((2,))],
+        far=(0, 1),
     )
     sides, ends = exchange(*sends)
     xi_source, eta_source, own = call(
@@ -859,7 +875,7 @@
     sends = call(
         functools.partial(contra_sums_kernel, grid),
         [(2 * 4, ny, nz)] * 2 + [(4, TILE, LANES)],
-        contra, tables,
+        contra, sums,
     )
     sides, ends = exchange(*eta_sends, *sends)
     xi_source, eta_source, own = call(
@@ -883,7 +899,7 @@
     mass, mass_source, xi_first, xi_second = call(
         functools.partial(face_kernel, grid),
         [(1, *block)] * 2 + [(5 * WIDTH, ny, nz)] * 2,
-        state, mass_source, sides[1], sides[0],
+        state, mass_source, sides[0], sides[1],
     )
     xi_b = pair_swap(xi_second, "xi", 1)
     xi_a = pair_swap(xi_first, "xi", 0)
@@ -898,14 +914,14 @@
         xi_a.reshape(layers, nz), xi_b.reshape(layers, nz),
     )
     edge_first, edge_second = call(
-        functools.partial(edge_kernel, grid), [(2 * WIDTH * PLANES, nz)] * 2, source, eta_a, eta_b,
+        functools.partial(edge_kernel, grid), [(2 * WIDTH * PLANES, nz)] * 2, source, eta_b, eta_a,
     )
     edge_b = pair_swap(edge_second, "xi", 1)
     edge_a = pair_swap(edge_first, "xi", 0)
     state, zeta, corner_first, corner_second = call(
         functools.partial(eta_filter_kernel, grid),
         [(4, *block), (nx * TILE, LANES)] + [(WIDTH, TILE, LANES)] * 2,
-        source, mass, eta_b, eta_a,
+        source, mass, eta_a, eta_b,
     )
     ends = ring_swap(zeta, "zeta")
     edges_b = diagonal_swap(corner_second, 1)

time: 42.5 us -> 41.5 us (0.976)
  waiting for transfers between devices: 10.1 us -> 7.21 us
  starting transfers between devices: 21.9 us -> 23 us
  Pallas kernels: 10.2 us -> 11 us
    ppermute x14, waiting for transfers between devices: 9.37 us -> 6.18 us  [pair_swap(): return lax.ppermute(value, axis, pairs)]
    ppermute x14, starting transfers between devices: 14.3 us -> 16 us  [pair_swap(): return lax.ppermute(value, axis, pairs)]
    pallas_call x18 -> x19, Pallas kernels: 10.2 us -> 11 us  [call(): pl.pallas_call(kernel, out_shape=shapes, in_specs=[pl.BlockSpec(memory_sp...]
    ppermute x2, starting transfers between devices: 3.04 us -> 2.36 us  [send(): return lax.ppermute(value, ('xi', 'zeta'), pairs)]
  transfers between devices with their start and end apart: 19 -> 19, of which waited for: 10 -> 7; matrix products, arithmetic and copies ran while one was open for 0% -> 0% of each run, Pallas kernels for 11% -> 14%
where the time goes in v7:
time: 41.5 us; the launch traced here: 41.4 us
  starting transfers between devices  23 us (55%)
  Pallas kernels  11 us (27%)
  waiting for transfers between devices  7.21 us (17%)
    ppermute x14, starting transfers between devices, pair_swap(): return lax.ppermute(value, axis, pairs)  16 us
    pallas_call x19, Pallas kernels, call(): pl.pallas_call(kernel, out_shape=shapes, in_specs=[pl.BlockSpec(memory_sp...  11 us
    ppermute x14, waiting for transfers between devices, pair_swap(): return lax.ppermute(value, axis, pairs)  6.18 us
    ppermute x3, starting transfers between devices, ring_swap(): other = lax.ppermute(value, axis, [(0, 1), (1, 0)])  4.64 us
    ppermute x2, starting transfers between devices, send(): return lax.ppermute(value, ('xi', 'zeta'), pairs)  2.36 us
  transfers between devices with their start and end apart: 19, of which 7 were waited for; matrix products, arithmetic and copies ran while one was open for 0% of the time, Pallas kernels for 14%

profile of v7, /device:TPU:0, one launch (start us, length us, event | category | flops | bytes accessed | tf_op | source)
XLA Modules:
  0.0 41.4 jit_solution(15755576015624834603)
XLA Ops:
  0.0 2.2 %shard_map.55 = (f32[5,256,128]{2,1,0:T(8,128)S(1)}, f32[128,128]{1,0:T(8,128)S(1)}, f32[9,256,128]{2,1,0:T(8,128)S(1)}, f32[4,256,128]{2,1,0:T(8,128)S(1)}, f32...) custom-call(f32[5,256,128]{2,1,0:T(8,128)} %bitcast.17, ...), custom_call_target="tpu_custom_call" | custom-call | bytes 3600000 | tf_op jit(solution)/shard_map/pallas_call | solution.py:805
  2.2 3.1 %collective-permute-start = (f32[10,16,128]{2,1,0:T(8,128)S(1)}, f32[10,16,128]{2,1,0:T(8,128)S(1)}, u32[]{:S(2)}, u32[]{:S(2)}) collective-permute-start(f32[10,16,128]{2,1,0:T(8,128)S(1)} %get-tuple-element.57), channel_id=1, source_target_pairs={{0,2},{2,0},{4,6},{6,4},{1,3},{3,1},{5,7},{7,5},{8,10},{10,8},{12,... | collective-permute-start | bytes 245768 | tf_op jit(solution)/shard_map/ppermute | solution.py:764
  5.3 2.5 %collective-permute-start.1 = (f32[10,16,128]{2,1,0:T(8,128)S(1)}, f32[10,16,128]{2,1,0:T(8,128)S(1)}, u32[]{:S(2)}, u32[]{:S(2)}) collective-permute-start(f32[10,16,128]{2,1,0:T(8,128)S(1)} %get-tuple-element.58), channel_id=1, source_target_pairs={{0,6},{2,4},{4,2},{6,0},{1,7},{3,5},{5,3},{7,1},{8,14},{10,12},{12... | collective-permute-start | bytes 245768 | tf_op jit(solution)/shard_map/ppermute | solution.py:764
  7.8 0.4 collective-permute-start.2
  8.1 1.2 %collective-permute-start.3 = (f32[10,16,128]{2,1,0:T(8,128)S(1)}, f32[10,16,128]{2,1,0:T(8,128)S(1)}, u32[]{:S(2)}, u32[]{:S(2)}) collective-permute-start(f32[10,16,128]{2,1,0:T(8,128)S(1)} %get-tuple-element.60), channel_id=1, source_target_pairs={{0,8},{8,0},{16,24},{24,16},{1,9},{9,1},{17,25},{25,17},{2,10},{10... | collective-permute-start | bytes 245768 | tf_op jit(solution)/shard_map/ppermute | solution.py:764
  9.4 1.5 %collective-permute-start.4 = (f32[5,8,128]{2,1,0:T(8,128)S(1)}, f32[5,8,128]{2,1,0:T(8,128)S(1)}, u32[]{:S(2)}, u32[]{:S(2)}) collective-permute-start(f32[5,8,128]{2,1,0:T(8,128)S(1)} %get-tuple-element.48.refs_2_), channel_id=1, source_target_pairs={{0,1},{1,0},{2,3},{3,2},{4,5},{5,4},{6,7},{7,6},{8,9},{9,8},{10,11... | collective-permute-start | bytes 61448 | tf_op jit(solution)/shard_map/ppermute | solution.py:785
  10.9 1.0 %shard_map.56 = (f32[4,128,128]{2,1,0:T(8,128)S(1)}, f32[256,128]{1,0:T(8,128)S(1)}) custom-call(f32[4,128,128]{2,1,0:T(8,128)} %constant.5.clone.refs_0_, f32[256,128]{1,0:T(8,128)} %bitcast.18, f32[5,8,128]{2,1,0:T(8,128)S(1)} %get-tuple-element.48.refs_2_), custom_call_target="tpu_custom_call" | custom-call | bytes 3600000 | tf_op jit(solution)/shard_map/pallas_call | solution.py:805
  11.9 0.6 %shard_map.57 = (f32[5,256,128]{2,1,0:T(8,128)S(1)}, f32[5,256,128]{2,1,0:T(8,128)S(1)}, f32[5,256,128]{2,1,0:T(8,128)S(1)}) custom-call(f32[4,256,128]{2,1,0:T(8,128)S(1)} %get-tuple-element.50.prim_ref, f32[3,256,128]{2,1,0:T(8,128)S(1)} %get-tuple-element.52.mass_ref, f32[4,128,128]{2,1,0:T(8,128)S(1)} %get-tuple-element.53.tables_ref), custom_call_target="tpu_custom_call" | custom-call | bytes 3600000 | tf_op jit(solution)/shard_map/pallas_call | solution.py:805
  12.5 0.0 collective-permute-done.1.eta_b
  12.5 0.0 collective-permute-done.2.xi_b
  12.5 0.5 %shard_map.58 = (f32[2,4,256,128]{3,2,1,0:T(8,128)S(1)}, f32[256,128]{1,0:T(8,128)S(1)}) custom-call(f32[5,256,128]{2,1,0:T(8,128)S(1)} %get-tuple-element.54.xi_source, f32[5,256,128]{2,1,0:T(8,128)S(1)} %get-tuple-element.55.eta_source, f32[5,256,128]{2,1,0:T(8,128)S(1)} %get-tuple-element.56.own_ref, f32[10,16,128]{2,1,0:T(8,128)S(1)} %collective-permute-done.eta_a, ...), custom_call_target="tpu_custom_call" | custom-call | bytes 3600000 | tf_op jit(solution)/shard_map/pallas_call | solution.py:805
  13.0 0.2 collective-permute-done.4.zeta_below.zeta_above
  13.1 1.4 %shard_map.59 = (f32[3,4,256,128]{3,2,1,0:T(8,128)S(1)}, f32[256,128]{1,0:T(8,128)S(1)}, f32[13,16,128]{2,1,0:T(8,128)S(1)}, f32[13,16,128]{2,1,0:T(8,128)S(1)}) custom-call(f32[5,256,128]{2,1,0:T(8,128)S(1)} %get-tuple-element.47.u_ref, f32[4,256,128]{2,1,0:T(8,128)S(1)} %get-tuple-element.50.prim_ref, f32[9,256,128]{2,1,0:T(8,128)S(1)} %get-tuple-element.51.metrics_ref, ...), custom_call_target="tpu_custom_call" | custom-call | bytes 3600000 | tf_op jit(solution)/shard_map/pallas_call | solution.py:805
  14.6 0.7 %collective-permute-start.5 = (f32[13,16,128]{2,1,0:T(8,128)S(1)}, f32[13,16,128]{2,1,0:T(8,128)S(1)}, u32[]{:S(2)}, u32[]{:S(2)}) collective-permute-start(f32[13,16,128]{2,1,0:T(8,128)S(1)} %get-tuple-element.67), channel_id=1, source_target_pairs={{0,2},{2,0},{4,6},{6,4},{1,3},{3,1},{5,7},{7,5},{8,10},{10,8},{12,... | collective-permute-start | bytes 319496 | tf_op jit(solution)/shard_map/ppermute | solution.py:764
  15.3 1.7 %collective-permute-start.6 = (f32[13,16,128]{2,1,0:T(8,128)S(1)}, f32[13,16,128]{2,1,0:T(8,128)S(1)}, u32[]{:S(2)}, u32[]{:S(2)}) collective-permute-start(f32[13,16,128]{2,1,0:T(8,128)S(1)} %get-tuple-element.68), channel_id=1, source_target_pairs={{0,6},{2,4},{4,2},{6,0},{1,7},{3,5},{5,3},{7,1},{8,14},{10,12},{12... | collective-permute-start | bytes 319496 | tf_op jit(solution)/shard_map/ppermute | solution.py:764
  17.0 0.4 shard_map.61
  17.3 0.1 collective-permute-start.7
  17.4 1.6 %collective-permute-start.8 = (f32[8,16,128]{2,1,0:T(8,128)S(1)}, f32[8,16,128]{2,1,0:T(8,128)S(1)}, u32[]{:S(2)}, u32[]{:S(2)}) collective-permute-start(f32[8,16,128]{2,1,0:T(8,128)S(1)} %get-tuple-element.71), channel_id=1, source_target_pairs={{0,8},{8,0},{16,24},{24,16},{1,9},{9,1},{17,25},{25,17},{2,10},{10... | collective-permute-start | bytes 196616 | tf_op jit(solution)/shard_map/ppermute | solution.py:764
  19.0 1.5 %collective-permute-start.9 = (f32[4,8,128]{2,1,0:T(8,128)S(1)}, f32[4,8,128]{2,1,0:T(8,128)S(1)}, u32[]{:S(2)}, u32[]{:S(2)}) collective-permute-start(f32[4,8,128]{2,1,0:T(8,128)S(1)} %get-tuple-element.72), channel_id=1, source_target_pairs={{0,1},{1,0},{2,3},{3,2},{4,5},{5,4},{6,7},{7,6},{8,9},{9,8},{10,11... | collective-permute-start | bytes 49160 | tf_op jit(solution)/shard_map/ppermute | solution.py:785
  20.5 0.5 %shard_map.60 = (f32[4,256,128]{2,1,0:T(8,128)S(1)}, f32[4,256,128]{2,1,0:T(8,128)S(1)}, f32[4,256,128]{2,1,0:T(8,128)S(1)}) custom-call(f32[3,4,256,128]{3,2,1,0:T(8,128)S(1)} %get-tuple-element.63.contra_ref, f32[4,128,128]{2,1,0:T(8,128)S(1)} %get-tuple-element.53.tables_ref), custom_call_target="tpu_custom_call" | custom-call | bytes 3600000 | tf_op jit(solution)/shard_map/pallas_call | solution.py:805
  21.0 0.7 %collective-permute-done.7.xi_b = f32[8,16,128]{2,1,0:T(8,128)S(1)} collective-permute-done((f32[8,16,128]{2,1,0:T(8,128)S(1)}, f32[8,16,128]{2,1,0:T(8,128)S(1)}, u32[]{:S(2)}, u32[]{:S(2)}) %collective-permute-start.7) | collective-permute-done | bytes 65568 | tf_op jit(solution)/shard_map/ppermute | solution.py:764
  21.8 0.0 collective-permute-done.5.eta_a
  21.8 0.2 collective-permute-done.6.eta_b
  22.0 0.5 %shard_map.62.total_ref = f32[4,256,128]{2,1,0:T(8,128)S(1)} custom-call(f32[4,256,128]{2,1,0:T(8,128)S(1)} %get-tuple-element.64.xi_source, f32[4,256,128]{2,1,0:T(8,128)S(1)} %get-tuple-element.65.eta_source, f32[4,256,128]{2,1,0:T(8,128)S(1)} %get-tuple-element.66.own_ref, f32[13,16,128]{2,1,0:T(8,128)S(1)} %collective-permute-done.5.eta_a, ...), custom_call_target="tpu_custom_call" | custom-call | bytes 3600000 | tf_op jit(solution)/shard_map/pallas_call | solution.py:805
  22.5 0.3 collective-permute-done.9.zeta_below.zeta_above
  22.8 0.4 %shard_map.63 = (f32[4,256,128]{2,1,0:T(8,128)S(1)}, f32[20,16,128]{2,1,0:T(8,128)S(1)}, f32[20,16,128]{2,1,0:T(8,128)S(1)}) custom-call(f32[5,256,128]{2,1,0:T(8,128)S(1)} %get-tuple-element.47.u_ref, f32[256,128]{1,0:T(8,128)S(1)} %get-tuple-element.49.jacobian_ref, f32[4,256,128]{2,1,0:T(8,128)S(1)} %shard_map.62.total_ref, ...), custom_call_target="tpu_custom_call" | custom-call | bytes 3600000 | tf_op jit(solution)/shard_map/pallas_call | solution.py:805
  23.2 1.3 %collective-permute-start.12 = (f32[20,16,128]{2,1,0:T(8,128)S(1)}, f32[20,16,128]{2,1,0:T(8,128)S(1)}, u32[]{:S(2)}, u32[]{:S(2)}) collective-permute-start(f32[20,16,128]{2,1,0:T(8,128)S(1)} %get-tuple-element.79), channel_id=1, source_target_pairs={{0,2},{2,0},{4,6},{6,4},{1,3},{3,1},{5,7},{7,5},{8,10},{10,8},{12,... | collective-permute-start | bytes 491528 | tf_op jit(solution)/shard_map/ppermute | solution.py:764
  24.5 1.5 %collective-permute-start.13 = (f32[20,16,128]{2,1,0:T(8,128)S(1)}, f32[20,16,128]{2,1,0:T(8,128)S(1)}, u32[]{:S(2)}, u32[]{:S(2)}) collective-permute-start(f32[20,16,128]{2,1,0:T(8,128)S(1)} %get-tuple-element.80), channel_id=1, source_target_pairs={{0,6},{2,4},{4,2},{6,0},{1,7},{3,5},{5,3},{7,1},{8,14},{10,12},{12... | collective-permute-start | bytes 491528 | tf_op jit(solution)/shard_map/ppermute | solution.py:764
  25.9 0.1 shard_map.64.source_ref
  26.0 0.2 shard_map.65
  26.2 0.1 collective-permute-start.10
  26.3 0.9 %collective-permute-start.11 = (f32[25,16,128]{2,1,0:T(8,128)S(1)}, f32[25,16,128]{2,1,0:T(8,128)S(1)}, u32[]{:S(2)}, u32[]{:S(2)}) collective-permute-start(f32[25,16,128]{2,1,0:T(8,128)S(1)} %get-tuple-element.77), channel_id=1, source_target_pairs={{0,24},{8,16},{16,8},{24,0},{1,25},{9,17},{17,9},{25,1},{2,26},{10... | collective-permute-start | bytes 614408 | tf_op jit(solution)/shard_map/ppermute | solution.py:764
  27.2 0.3 shard_map.67.source_ref.order_ref
  27.5 3.2 %collective-permute-done.12.eta_a = f32[20,16,128]{2,1,0:T(8,128)S(1)} collective-permute-done((f32[20,16,128]{2,1,0:T(8,128)S(1)}, f32[20,16,128]{2,1,0:T(8,128)S(1)}, u32[]{:S(2)}, u32[]{:S(2)}) %collective-permute-start.12) | collective-permute-done | bytes 163872 | tf_op jit(solution)/shard_map/ppermute | solution.py:764
  30.7 2.0 %collective-permute-done.13.eta_b = f32[20,16,128]{2,1,0:T(8,128)S(1)} collective-permute-done((f32[20,16,128]{2,1,0:T(8,128)S(1)}, f32[20,16,128]{2,1,0:T(8,128)S(1)}, u32[]{:S(2)}, u32[]{:S(2)}) %collective-permute-start.13) | collective-permute-done | bytes 163872 | tf_op jit(solution)/shard_map/ppermute | solution.py:764
  32.7 0.1 shard_map.71
  32.8 0.1 collective-permute-start.14
  32.9 0.9 %collective-permute-start.15 = (f32[240,128]{1,0:T(8,128)S(1)}, f32[240,128]{1,0:T(8,128)S(1)}, u32[]{:S(2)}, u32[]{:S(2)}) collective-permute-start(f32[240,128]{1,0:T(8,128)S(1)} %get-tuple-element.85), channel_id=1, source_target_pairs={{0,8},{8,0},{16,24},{24,16},{1,9},{9,1},{17,25},{25,17},{2,10},{10... | collective-permute-start | bytes 368648 | tf_op jit(solution)/shard_map/ppermute | solution.py:764
  33.8 0.4 %shard_map.68 = (f32[4,256,128]{2,1,0:T(8,128)S(1)}, f32[128,128]{1,0:T(8,128)S(1)}, f32[5,8,128]{2,1,0:T(8,128)S(1)}, f32[5,8,128]{2,1,0:T(8,128)S(1)}) custom-call(f32[4,256,128]{2,1,0:T(8,128)S(1)} %shard_map.67.source_ref.order_ref, f32[1,256,128]{2,1,0:T(8,128)S(1)} %get-tuple-element.78.mass_ref, f32[20,16,128]{2,1,0:T(8,128)S(1)} %collective-permute-done.12.eta_a, ...), custom_call_target="tpu_custom_call" | custom-call | bytes 3600000 | tf_op jit(solution)/shard_map/pallas_call | solution.py:805
  34.3 1.6 %collective-permute-start.17 = (f32[128,128]{1,0:T(8,128)S(1)}, f32[128,128]{1,0:T(8,128)S(1)}, u32[]{:S(2)}, u32[]{:S(2)}) collective-permute-start(f32[128,128]{1,0:T(8,128)S(1)} %get-tuple-element.87), channel_id=1, source_target_pairs={{0,1},{1,0},{2,3},{3,2},{4,5},{5,4},{6,7},{7,6},{8,9},{9,8},{10,11... | collective-permute-start | bytes 196616 | tf_op jit(solution)/shard_map/ppermute | solution.py:785
  35.9 0.4 %collective-permute-start.16 = (f32[5,8,128]{2,1,0:T(8,128)S(1)}, f32[5,8,128]{2,1,0:T(8,128)S(1)}, u32[]{:S(2)}, u32[]{:S(2)}) collective-permute-start(f32[5,8,128]{2,1,0:T(8,128)S(1)} %get-tuple-element.86), channel_id=1, source_target_pairs={{0,25},{1,24},{8,17},{9,16},{16,9},{17,8},{24,1},{25,0},{2,27},{3,... | collective-permute-start | bytes 61448 | tf_op jit(solution)/shard_map/ppermute | solution.py:776
  36.3 1.9 %collective-permute-start.18 = (f32[5,8,128]{2,1,0:T(8,128)S(1)}, f32[5,8,128]{2,1,0:T(8,128)S(1)}, u32[]{:S(2)}, u32[]{:S(2)}) collective-permute-start(f32[5,8,128]{2,1,0:T(8,128)S(1)} %get-tuple-element.88), channel_id=1, source_target_pairs={{0,9},{1,8},{8,1},{9,0},{16,25},{17,24},{24,17},{25,16},{2,11},{3,... | collective-permute-start | bytes 61448 | tf_op jit(solution)/shard_map/ppermute | solution.py:776
  38.2 0.2 shard_map.69.source_ref
  38.5 0.2 shard_map.70
  38.7 0.2 shard_map.66.mass_ref
  39.0 0.6 %shard_map.72.state_ref = f32[4,256,128]{2,1,0:T(8,128)S(1)} custom-call(f32[4,256,128]{2,1,0:T(8,128)S(1)} %shard_map.69.source_ref, f32[384,128]{1,0:T(8,128)S(1)} %get-tuple-element.82.first_source, f32[384,128]{1,0:T(8,128)S(1)} %get-tuple-element.83.second_source, f32[240,128]{1,0:T(8,128)S(1)} %collective-permute-done.14.edge_b, ...), custom_call_target="tpu_custom_call" | custom-call | bytes 3600000 | tf_op jit(solution)/shard_map/pallas_call | solution.py:805
  39.6 0.6 %collective-permute-done.16 = f32[5,8,128]{2,1,0:T(8,128)S(1)} collective-permute-done((f32[5,8,128]{2,1,0:T(8,128)S(1)}, f32[5,8,128]{2,1,0:T(8,128)S(1)}, u32[]{:S(2)}, u32[]{:S(2)}) %collective-permute-start.16) | collective-permute-done | bytes 20512 | tf_op jit(solution)/shard_map/ppermute | solution.py:776
  40.1 1.2 %shard_map.73 = f32[5,256,128]{2,1,0:T(8,128)} custom-call(f32[1,256,128]{2,1,0:T(8,128)S(1)} %shard_map.66.mass_ref, f32[4,256,128]{2,1,0:T(8,128)S(1)} %shard_map.72.state_ref, f32[40,128]{1,0:T(8,128)S(1)} %bitcast.12, f32[40,128]{1,0:T(8,128)S(1)} %bitcast.13, f32[128,128]{1,0:T(8,128)S(1)} %collective-permute-done.17.below_ref.above_ref, ...), custom_call_target="tpu_custom_call" | custom-call | bytes 3600000 | tf_op jit(solution)/shard_map/pallas_call | solution.py:805
  (9 shorter events, 0.0 us)
Async XLA Ops:
  2.2 10.3 %collective-permute-start = (f32[10,16,128]{2,1,0:T(8,128)S(1)}, f32[10,16,128]{2,1,0:T(8,128)S(1)}, u32[]{:S(2)}, u32[]{:S(2)}) collective-permute-start(f32[10,16,128]{2,1,0:T(8,128)S(1)} %get-tuple-element.57), channel_id=1, source_target_pairs={{0,2},{2,0},{4,6},{6,4},{1,3},{3,1},{5,7},{7,5},{8,10},{10,8},{12,... | collective-permute-start | bytes 245768 | tf_op jit(solution)/shard_map/ppermute | solution.py:764
  5.3 7.2 %collective-permute-start.1 = (f32[10,16,128]{2,1,0:T(8,128)S(1)}, f32[10,16,128]{2,1,0:T(8,128)S(1)}, u32[]{:S(2)}, u32[]{:S(2)}) collective-permute-start(f32[10,16,128]{2,1,0:T(8,128)S(1)} %get-tuple-element.58), channel_id=1, source_target_pairs={{0,6},{2,4},{4,2},{6,0},{1,7},{3,5},{5,3},{7,1},{8,14},{10,12},{12... | collective-permute-start | bytes 245768 | tf_op jit(solution)/shard_map/ppermute | solution.py:764
  7.8 4.7 %collective-permute-start.2 = (f32[10,16,128]{2,1,0:T(8,128)S(1)}, f32[10,16,128]{2,1,0:T(8,128)S(1)}, u32[]{:S(2)}, u32[]{:S(2)}) collective-permute-start(f32[10,16,128]{2,1,0:T(8,128)S(1)} %get-tuple-element.59), channel_id=1, source_target_pairs={{0,24},{8,16},{16,8},{24,0},{1,25},{9,17},{17,9},{25,1},{2,26},{10... | collective-permute-start | bytes 245768 | tf_op jit(solution)/shard_map/ppermute | solution.py:764
  8.1 4.4 %collective-permute-start.3 = (f32[10,16,128]{2,1,0:T(8,128)S(1)}, f32[10,16,128]{2,1,0:T(8,128)S(1)}, u32[]{:S(2)}, u32[]{:S(2)}) collective-permute-start(f32[10,16,128]{2,1,0:T(8,128)S(1)} %get-tuple-element.60), channel_id=1, source_target_pairs={{0,8},{8,0},{16,24},{24,16},{1,9},{9,1},{17,25},{25,17},{2,10},{10... | collective-permute-start | bytes 245768 | tf_op jit(solution)/shard_map/ppermute | solution.py:764
  9.4 3.8 %collective-permute-start.4 = (f32[5,8,128]{2,1,0:T(8,128)S(1)}, f32[5,8,128]{2,1,0:T(8,128)S(1)}, u32[]{:S(2)}, u32[]{:S(2)}) collective-permute-start(f32[5,8,128]{2,1,0:T(8,128)S(1)} %get-tuple-element.48.refs_2_), channel_id=1, source_target_pairs={{0,1},{1,0},{2,3},{3,2},{4,5},{5,4},{6,7},{7,6},{8,9},{9,8},{10,11... | collective-permute-start | bytes 61448 | tf_op jit(solution)/shard_map/ppermute | solution.py:785
  14.6 7.2 %collective-permute-start.5 = (f32[13,16,128]{2,1,0:T(8,128)S(1)}, f32[13,16,128]{2,1,0:T(8,128)S(1)}, u32[]{:S(2)}, u32[]{:S(2)}) collective-permute-start(f32[13,16,128]{2,1,0:T(8,128)S(1)} %get-tuple-element.67), channel_id=1, source_target_pairs={{0,2},{2,0},{4,6},{6,4},{1,3},{3,1},{5,7},{7,5},{8,10},{10,8},{12,... | collective-permute-start | bytes 319496 | tf_op jit(solution)/shard_map/ppermute | solution.py:764
  15.3 6.7 %collective-permute-start.6 = (f32[13,16,128]{2,1,0:T(8,128)S(1)}, f32[13,16,128]{2,1,0:T(8,128)S(1)}, u32[]{:S(2)}, u32[]{:S(2)}) collective-permute-start(f32[13,16,128]{2,1,0:T(8,128)S(1)} %get-tuple-element.68), channel_id=1, source_target_pairs={{0,6},{2,4},{4,2},{6,0},{1,7},{3,5},{5,3},{7,1},{8,14},{10,12},{12... | collective-permute-start | bytes 319496 | tf_op jit(solution)/shard_map/ppermute | solution.py:764
  17.3 4.4 %collective-permute-start.7 = (f32[8,16,128]{2,1,0:T(8,128)S(1)}, f32[8,16,128]{2,1,0:T(8,128)S(1)}, u32[]{:S(2)}, u32[]{:S(2)}) collective-permute-start(f32[8,16,128]{2,1,0:T(8,128)S(1)} %get-tuple-element.70), channel_id=1, source_target_pairs={{0,24},{8,16},{16,8},{24,0},{1,25},{9,17},{17,9},{25,1},{2,26},{10... | collective-permute-start | bytes 196616 | tf_op jit(solution)/shard_map/ppermute | solution.py:764
  17.4 4.3 %collective-permute-start.8 = (f32[8,16,128]{2,1,0:T(8,128)S(1)}, f32[8,16,128]{2,1,0:T(8,128)S(1)}, u32[]{:S(2)}, u32[]{:S(2)}) collective-permute-start(f32[8,16,128]{2,1,0:T(8,128)S(1)} %get-tuple-element.71), channel_id=1, source_target_pairs={{0,8},{8,0},{16,24},{24,16},{1,9},{9,1},{17,25},{25,17},{2,10},{10... | collective-permute-start | bytes 196616 | tf_op jit(solution)/shard_map/ppermute | solution.py:764
  19.0 3.7 %collective-permute-start.9 = (f32[4,8,128]{2,1,0:T(8,128)S(1)}, f32[4,8,128]{2,1,0:T(8,128)S(1)}, u32[]{:S(2)}, u32[]{:S(2)}) collective-permute-start(f32[4,8,128]{2,1,0:T(8,128)S(1)} %get-tuple-element.72), channel_id=1, source_target_pairs={{0,1},{1,0},{2,3},{3,2},{4,5},{5,4},{6,7},{7,6},{8,9},{9,8},{10,11... | collective-permute-start | bytes 49160 | tf_op jit(solution)/shard_map/ppermute | solution.py:785
  23.2 7.5 %collective-permute-start.12 = (f32[20,16,128]{2,1,0:T(8,128)S(1)}, f32[20,16,128]{2,1,0:T(8,128)S(1)}, u32[]{:S(2)}, u32[]{:S(2)}) collective-permute-start(f32[20,16,128]{2,1,0:T(8,128)S(1)} %get-tuple-element.79), channel_id=1, source_target_pairs={{0,2},{2,0},{4,6},{6,4},{1,3},{3,1},{5,7},{7,5},{8,10},{10,8},{12,... | collective-permute-start | bytes 491528 | tf_op jit(solution)/shard_map/ppermute | solution.py:764
  24.5 8.3 %collective-permute-start.13 = (f32[20,16,128]{2,1,0:T(8,128)S(1)}, f32[20,16,128]{2,1,0:T(8,128)S(1)}, u32[]{:S(2)}, u32[]{:S(2)}) collective-permute-start(f32[20,16,128]{2,1,0:T(8,128)S(1)} %get-tuple-element.80), channel_id=1, source_target_pairs={{0,6},{2,4},{4,2},{6,0},{1,7},{3,5},{5,3},{7,1},{8,14},{10,12},{12... | collective-permute-start | bytes 491528 | tf_op jit(solution)/shard_map/ppermute | solution.py:764
  26.2 9.7 %collective-permute-start.10 = (f32[25,16,128]{2,1,0:T(8,128)S(1)}, f32[25,16,128]{2,1,0:T(8,128)S(1)}, u32[]{:S(2)}, u32[]{:S(2)}) collective-permute-start(f32[25,16,128]{2,1,0:T(8,128)S(1)} %get-tuple-element.76), channel_id=1, source_target_pairs={{0,8},{8,0},{16,24},{24,16},{1,9},{9,1},{17,25},{25,17},{2,10},{10... | collective-permute-start | bytes 614408 | tf_op jit(solution)/shard_map/ppermute | solution.py:764
  26.3 10.0 %collective-permute-start.11 = (f32[25,16,128]{2,1,0:T(8,128)S(1)}, f32[25,16,128]{2,1,0:T(8,128)S(1)}, u32[]{:S(2)}, u32[]{:S(2)}) collective-permute-start(f32[25,16,128]{2,1,0:T(8,128)S(1)} %get-tuple-element.77), channel_id=1, source_target_pairs={{0,24},{8,16},{16,8},{24,0},{1,25},{9,17},{17,9},{25,1},{2,26},{10... | collective-permute-start | bytes 614408 | tf_op jit(solution)/shard_map/ppermute | solution.py:764
  32.8 6.1 %collective-permute-start.14 = (f32[240,128]{1,0:T(8,128)S(1)}, f32[240,128]{1,0:T(8,128)S(1)}, u32[]{:S(2)}, u32[]{:S(2)}) collective-permute-start(f32[240,128]{1,0:T(8,128)S(1)} %get-tuple-element.84), channel_id=1, source_target_pairs={{0,24},{8,16},{16,8},{24,0},{1,25},{9,17},{17,9},{25,1},{2,26},{10... | collective-permute-start | bytes 368648 | tf_op jit(solution)/shard_map/ppermute | solution.py:764
  32.9 6.1 %collective-permute-start.15 = (f32[240,128]{1,0:T(8,128)S(1)}, f32[240,128]{1,0:T(8,128)S(1)}, u32[]{:S(2)}, u32[]{:S(2)}) collective-permute-start(f32[240,128]{1,0:T(8,128)S(1)} %get-tuple-element.85), channel_id=1, source_target_pairs={{0,8},{8,0},{16,24},{24,16},{1,9},{9,1},{17,25},{25,17},{2,10},{10... | collective-permute-start | bytes 368648 | tf_op jit(solution)/shard_map/ppermute | solution.py:764
  34.3 5.9 %collective-permute-start.17 = (f32[128,128]{1,0:T(8,128)S(1)}, f32[128,128]{1,0:T(8,128)S(1)}, u32[]{:S(2)}, u32[]{:S(2)}) collective-permute-start(f32[128,128]{1,0:T(8,128)S(1)} %get-tuple-element.87), channel_id=1, source_target_pairs={{0,1},{1,0},{2,3},{3,2},{4,5},{5,4},{6,7},{7,6},{8,9},{9,8},{10,11... | collective-permute-start | bytes 196616 | tf_op jit(solution)/shard_map/ppermute | solution.py:785
  35.9 4.3 %collective-permute-start.16 = (f32[5,8,128]{2,1,0:T(8,128)S(1)}, f32[5,8,128]{2,1,0:T(8,128)S(1)}, u32[]{:S(2)}, u32[]{:S(2)}) collective-permute-start(f32[5,8,128]{2,1,0:T(8,128)S(1)} %get-tuple-element.86), channel_id=1, source_target_pairs={{0,25},{1,24},{8,17},{9,16},{16,9},{17,8},{24,1},{25,0},{2,27},{3,... | collective-permute-start | bytes 61448 | tf_op jit(solution)/shard_map/ppermute | solution.py:776
  36.3 3.8 %collective-permute-start.18 = (f32[5,8,128]{2,1,0:T(8,128)S(1)}, f32[5,8,128]{2,1,0:T(8,128)S(1)}, u32[]{:S(2)}, u32[]{:S(2)}) collective-permute-start(f32[5,8,128]{2,1,0:T(8,128)S(1)} %get-tuple-element.88), channel_id=1, source_target_pairs={{0,9},{1,8},{8,1},{9,0},{16,25},{17,24},{24,17},{25,16},{2,11},{3,... | collective-permute-start | bytes 61448 | tf_op jit(solution)/shard_map/ppermute | solution.py:776

commit v8 on v7

--- a/solution.py
+++ b/solution.py
@@ -408,44 +408,44 @@
     return derive_solve(rights, below, above)
 
 
-def add_derivatives(grid, xi_source, eta_source, own_ref, eta_a, eta_b, xi_a, xi_b, field, total_ref):
-    for group in range(grid.xi_groups):
-        for i, value in enumerate(eta_derivative(grid, eta_source, eta_a, eta_b, field, group)):
-            rows = grid.eta_tile(i, group)
-            total_ref[rows, :] = own_ref[field, rows, :] + value
-    for group in range(grid.eta_groups):
-        for i, value in enumerate(xi_derivative(grid, xi_source, xi_a, xi_b, field, group)):
-            rows = grid.xi_tile(i, group)
-            total_ref[rows, :] = total_ref[rows, :] + value
-
-
-def slope_kernel(grid, xi_source, eta_source, own_ref, eta_a, eta_b, xi_b, xi_a, slope_ref, mass_total_ref):
-    for field in range(4):
+def eta_slope_kernel(grid, source_ref, own_ref, eta_a, eta_b, slope_ref, mass_total_ref):
+    for field in range(5):
+        for group in range(grid.xi_groups):
+            for i, value in enumerate(eta_derivative(grid, source_ref, eta_a, eta_b, field, group)):
+                rows = grid.eta_tile(i, group)
+                if field < 4:
+                    slope_ref[field, rows, :] = value
+                else:
+                    mass_total_ref[rows, :] = own_ref[4, rows, :] + value
+
+
+def zeta_slope_kernel(grid, own_ref, part_ref, below_ref, above_ref, tables_ref, slope_ref, mass_total_ref):
+    back = split_weights(tables_ref[BACK])
+    for field in range(5):
+        beyond = lane_product(unpack_sums(below_ref[field], above_ref[field], grid), back)
+        if field < 4:
+            slope_ref[field] = own_ref[field] + beyond
+        else:
+            mass_total_ref[...] = part_ref[...] + beyond
+
+
+def xi_slope_kernel(grid, source_ref, part_ref, xi_b, xi_a, slope_ref, mass_total_ref):
+    for field in range(5):
         for group in range(grid.eta_groups):
-            for i, value in enumerate(xi_derivative(grid, xi_source, xi_a, xi_b, field, group)):
-                slope_ref[0, field, grid.xi_tile(i, group), :] = value
-        for group in range(grid.xi_groups):
-            for i, value in enumerate(eta_derivative(grid, eta_source, eta_a, eta_b, field, group)):
-                slope_ref[1, field, grid.eta_tile(i, group), :] = value
-    add_derivatives(
-        grid, xi_source, eta_source, own_ref, eta_a, eta_b, xi_a, xi_b, 4, mass_total_ref
-    )
+            for i, value in enumerate(xi_derivative(grid, source_ref, xi_a, xi_b, field, group)):
+                rows = grid.xi_tile(i, group)
+                if field < 4:
+                    slope_ref[field, rows, :] = value
+                else:
+                    mass_total_ref[rows, :] = part_ref[rows, :] + value
 
 
 def flux_kernel(
     grid,
-    u_ref, prim_ref, metrics_ref, jacobian_ref, slope_ref, own_ref, mass_total_ref,
-    zeta_below, zeta_above, tables_ref,
+    u_ref, prim_ref, metrics_ref, jacobian_ref, xi_slope_ref, eta_slope_ref, zeta_slope_ref, mass_total_ref,
     contra_ref, mass_ref, eta_first, eta_second,
-    zeta_slope_ref,
 ):
-    back = split_weights(tables_ref[BACK])
-    for field in range(4):
-        halo = unpack_sums(zeta_below[field], zeta_above[field], grid)
-        zeta_slope_ref[field] = own_ref[field] + lane_product(halo, back)
-    halo = unpack_sums(zeta_below[4], zeta_above[4], grid)
-    total = mass_total_ref[...] + lane_product(halo, back)
-    mass_ref[...] = u_ref[0] - (step_duration * jacobian_ref[...]) * total
+    mass_ref[...] = u_ref[0] - (step_duration * jacobian_ref[...]) * mass_total_ref[...]
     send_cells(
         lambda position, group: mass_ref[grid.eta_tile(position, group), :],
         grid.xi_groups, grid.ny, odd("eta"), eta_first, eta_second, 2 * 4,
@@ -463,7 +463,7 @@
         scaled = [[scaled * metrics[k][j] for j in range(3)] for k in range(3)]
         physical = []
         for c in range(4):
-            slopes = [slope_ref[0, c, rows, :], slope_ref[1, c, rows, :], zeta_slope_ref[c, rows, :]]
+            slopes = [ref[c, rows, :] for ref in (xi_slope_ref, eta_slope_ref, zeta_slope_ref)]
             physical.append(
                 [
                     scaled[0][j] * slopes[0] + scaled[1][j] * slopes[1] + scaled[2][j] * slopes[2]
@@ -512,23 +512,30 @@
         zeta_ref[field] = pack_sums(contra_ref[2, field], sums, grid)
 
 
-def divergence_kernel(grid, xi_source, eta_source, own_ref, eta_a, eta_b, xi_b, xi_a, total_ref):
-    for field in range(4):
-        add_derivatives(
-            grid, xi_source, eta_source, own_ref, eta_a, eta_b, xi_a, xi_b, field, total_ref.at[field]
-        )
+def xi_divergence_kernel(grid, source_ref, own_ref, xi_b, xi_a, total_ref):
+    for field in range(4):
+        for group in range(grid.eta_groups):
+            for i, value in enumerate(xi_derivative(grid, source_ref, xi_a, xi_b, field, group)):
+                rows = grid.xi_tile(i, group)
+                total_ref[field, rows, :] = own_ref[field, rows, :] + value
+
+
+def zeta_divergence_kernel(grid, part_ref, below_ref, above_ref, tables_ref, total_ref):
+    back = split_weights(tables_ref[BACK])
+    for field in range(4):
+        beyond = lane_product(unpack_sums(below_ref[field], above_ref[field], grid), back)
+        total_ref[field] = part_ref[field] + beyond
 
 
 def step_kernel(
-    grid,
-    u_ref, jacobian_ref, total_ref, zeta_below, zeta_above, tables_ref,
-    state_ref, eta_first, eta_second,
+    grid, u_ref, jacobian_ref, source_ref, total_ref, eta_a, eta_b, state_ref, eta_first, eta_second
 ):
-    back = split_weights(tables_ref[BACK])
     scale = step_duration * jacobian_ref[...]
     for field in range(4):
-        halo = unpack_sums(zeta_below[field], zeta_above[field], grid)
-        total = total_ref[field] + lane_product(halo, back)
+        for group in range(grid.xi_groups):
+            for i, value in enumerate(eta_derivative(grid, source_ref, eta_a, eta_b, field, group)):
+                state_ref[field, grid.eta_tile(i, group), :] = value
+        total = total_ref[field] + state_ref[field]
         state_ref[field] = u_ref[1 + field] - scale * total
         send_cells(
             lambda position, group: state_ref[field, grid.eta_tile(position, group), :],
@@ -836,7 +843,7 @@
         xi_b = pair_swap(xi_second, "xi", 1)
         below, above = ring_swap(zeta, "zeta")
         xi_a = pair_swap(xi_first, "xi", 0)
-        return (eta_a, eta_b, xi_b, xi_a), (below, above)
+        return (eta_a, eta_b), (xi_b, xi_a), (below, above)
 
     block = (rows, nz)
     chunks = 2
@@ -857,27 +864,34 @@
         scratch=[pltpu.SemaphoreType.DMA((2,))],
         far=(0, 1),
     )
-    sides, ends = exchange(*sends)
+    eta_sides, xi_sides, ends = exchange(*sends)
     xi_source, eta_source, own = call(
         functools.partial(primitive_source_kernel, grid), [(5, *block)] * 3, prim, mass, tables,
     )
-    slopes, mass_total = call(
-        functools.partial(slope_kernel, grid),
-        [(2, 4, *block), block],
-        xi_source, eta_source, own, *sides,
+    eta_slope, mass_total = call(
+        functools.partial(eta_slope_kernel, grid), [(4, *block), block], eta_source, own, *eta_sides,
+    )
+    xi_slope, mass_total = call(
+        functools.partial(xi_slope_kernel, grid),
+        [(4, *block), block],
+        xi_source, mass_total, *xi_sides,
+    )
+    zeta_slope, mass_total = call(
+        functools.partial(zeta_slope_kernel, grid),
+        [(4, *block), block],
+        own, mass_total, *ends, tables,
     )
     contra, mass, *eta_sends = call(
         functools.partial(flux_kernel, grid),
         [(3, 4, *block), block] + [(2 * 4 + WIDTH, nx, nz)] * 2,
-        u, prim, metrics, jacobian, slopes, own, mass_total, *ends, tables,
-        scratch=[pltpu.VMEM((4, *block), jnp.float32)],
+        u, prim, metrics, jacobian, xi_slope, eta_slope, zeta_slope, mass_total,
     )
     sends = call(
         functools.partial(contra_sums_kernel, grid),
         [(2 * 4, ny, nz)] * 2 + [(4, TILE, LANES)],
         contra, sums,
     )
-    sides, ends = exchange(*eta_sends, *sends)
+    eta_sides, xi_sides, ends = exchange(*eta_sends, *sends)
     xi_source, eta_source, own = call(
         functools.partial(contra_source_kernel, grid), [(4, *block)] * 3, contra, tables,
     )
@@ -885,21 +899,22 @@
         functools.partial(source_kernel, grid, eta_sources), [(1, *block)], mass.reshape(1, *block),
     )
     (total,) = call(
-        functools.partial(divergence_kernel, grid),
-        [(4, *block)],
-        xi_source, eta_source, own, *sides,
+        functools.partial(xi_divergence_kernel, grid), [(4, *block)], xi_source, own, *xi_sides,
+    )
+    (total,) = call(
+        functools.partial(zeta_divergence_kernel, grid), [(4, *block)], total, *ends, tables,
     )
     state, eta_first, eta_second = call(
         functools.partial(step_kernel, grid),
         [(4, *block)] + [(4 * WIDTH, nx, nz)] * 2,
-        u, jacobian, total, *ends, tables,
+        u, jacobian, eta_source, total, *eta_sides,
     )
     eta_b = pair_swap(eta_second, "eta", 1)
     eta_a = pair_swap(eta_first, "eta", 0)
     mass, mass_source, xi_first, xi_second = call(
         functools.partial(face_kernel, grid),
         [(1, *block)] * 2 + [(5 * WIDTH, ny, nz)] * 2,
-        state, mass_source, sides[0], sides[1],
+        state, mass_source, *eta_sides,
     )
     xi_b = pair_swap(xi_second, "xi", 1)
     xi_a = pair_swap(xi_first, "xi", 0)

time: 41.5 us -> 41.5 us (level)
    ppermute x3, waiting for transfers between devices: 0.45 us -> 1 us  [ring_swap(): other = lax.ppermute(value, axis, [(0, 1), (1, 0)])]
    pallas_call x19 -> x22, Pallas kernels: 11 us -> 11 us  [call(): pl.pallas_call(kernel, out_shape=shapes, in_specs=[pl.BlockSpec(memory_sp...]
  transfers between devices with their start and end apart: 19 -> 19, of which waited for: 7 -> 5; matrix products, arithmetic and copies ran while one was open for 0% -> 0% of each run, Pallas kernels for 14% -> 14%
where the time goes in v8:
time: 41.5 us; the launch traced here: 41.4 us
  starting transfers between devices  22.6 us (54%)
  Pallas kernels  11 us (27%)
  waiting for transfers between devices  7.49 us (18%)
    ppermute x14, starting transfers between devices, pair_swap(): return lax.ppermute(value, axis, pairs)  15.8 us
    pallas_call x22, Pallas kernels, call(): pl.pallas_call(kernel, out_shape=shapes, in_specs=[pl.BlockSpec(memory_sp...  11 us
    ppermute x14, waiting for transfers between devices, pair_swap(): return lax.ppermute(value, axis, pairs)  5.81 us
    ppermute x3, starting transfers between devices, ring_swap(): other = lax.ppermute(value, axis, [(0, 1), (1, 0)])  4.6 us
    ppermute x2, starting transfers between devices, send(): return lax.ppermute(value, ('xi', 'zeta'), pairs)  2.22 us
    ppermute x3, waiting for transfers between devices, ring_swap(): other = lax.ppermute(value, axis, [(0, 1), (1, 0)])  1 us
  transfers between devices with their start and end apart: 19, of which 5 were waited for; matrix products, arithmetic and copies ran while one was open for 0% of the time, Pallas kernels for 14%

profile of v8, /device:TPU:0, one launch (start us, length us, event | category | flops | bytes accessed | tf_op | source)
XLA Modules:
  0.0 41.4 jit_solution(5373232749687247952)
XLA Ops:
  0.0 2.2 %shard_map.55 = (f32[5,256,128]{2,1,0:T(8,128)S(1)}, f32[128,128]{1,0:T(8,128)S(1)}, f32[9,256,128]{2,1,0:T(8,128)S(1)}, f32[4,256,128]{2,1,0:T(8,128)S(1)}, f32...) custom-call(f32[5,256,128]{2,1,0:T(8,128)} %bitcast.17, ...), custom_call_target="tpu_custom_call" | custom-call | bytes 3600000 | tf_op jit(solution)/shard_map/pallas_call | solution.py:812
  2.2 3.1 %collective-permute-start = (f32[10,16,128]{2,1,0:T(8,128)S(1)}, f32[10,16,128]{2,1,0:T(8,128)S(1)}, u32[]{:S(2)}, u32[]{:S(2)}) collective-permute-start(f32[10,16,128]{2,1,0:T(8,128)S(1)} %get-tuple-element.61), channel_id=1, source_target_pairs={{0,2},{2,0},{4,6},{6,4},{1,3},{3,1},{5,7},{7,5},{8,10},{10,8},{12,... | collective-permute-start | bytes 245768 | tf_op jit(solution)/shard_map/ppermute | solution.py:771
  5.3 2.5 %collective-permute-start.1 = (f32[10,16,128]{2,1,0:T(8,128)S(1)}, f32[10,16,128]{2,1,0:T(8,128)S(1)}, u32[]{:S(2)}, u32[]{:S(2)}) collective-permute-start(f32[10,16,128]{2,1,0:T(8,128)S(1)} %get-tuple-element.62), channel_id=1, source_target_pairs={{0,6},{2,4},{4,2},{6,0},{1,7},{3,5},{5,3},{7,1},{8,14},{10,12},{12... | collective-permute-start | bytes 245768 | tf_op jit(solution)/shard_map/ppermute | solution.py:771
  7.8 0.4 collective-permute-start.2
  8.1 1.2 %collective-permute-start.3 = (f32[10,16,128]{2,1,0:T(8,128)S(1)}, f32[10,16,128]{2,1,0:T(8,128)S(1)}, u32[]{:S(2)}, u32[]{:S(2)}) collective-permute-start(f32[10,16,128]{2,1,0:T(8,128)S(1)} %get-tuple-element.65), channel_id=1, source_target_pairs={{0,8},{8,0},{16,24},{24,16},{1,9},{9,1},{17,25},{25,17},{2,10},{10... | collective-permute-start | bytes 245768 | tf_op jit(solution)/shard_map/ppermute | solution.py:771
  9.4 1.5 %collective-permute-start.4 = (f32[5,8,128]{2,1,0:T(8,128)S(1)}, f32[5,8,128]{2,1,0:T(8,128)S(1)}, u32[]{:S(2)}, u32[]{:S(2)}) collective-permute-start(f32[5,8,128]{2,1,0:T(8,128)S(1)} %get-tuple-element.52.refs_2_), channel_id=1, source_target_pairs={{0,1},{1,0},{2,3},{3,2},{4,5},{5,4},{6,7},{7,6},{8,9},{9,8},{10,11... | collective-permute-start | bytes 61448 | tf_op jit(solution)/shard_map/ppermute | solution.py:792
  10.9 1.0 %shard_map.56 = (f32[4,128,128]{2,1,0:T(8,128)S(1)}, f32[256,128]{1,0:T(8,128)S(1)}) custom-call(f32[4,128,128]{2,1,0:T(8,128)} %constant.5.clone.refs_0_, f32[256,128]{1,0:T(8,128)} %bitcast.18, f32[5,8,128]{2,1,0:T(8,128)S(1)} %get-tuple-element.52.refs_2_), custom_call_target="tpu_custom_call" | custom-call | bytes 3600000 | tf_op jit(solution)/shard_map/pallas_call | solution.py:812
  11.9 0.6 %shard_map.57 = (f32[5,256,128]{2,1,0:T(8,128)S(1)}, f32[5,256,128]{2,1,0:T(8,128)S(1)}, f32[5,256,128]{2,1,0:T(8,128)S(1)}) custom-call(f32[4,256,128]{2,1,0:T(8,128)S(1)} %get-tuple-element.54.prim_ref, f32[3,256,128]{2,1,0:T(8,128)S(1)} %get-tuple-element.56.mass_ref, f32[4,128,128]{2,1,0:T(8,128)S(1)} %get-tuple-element.57.tables_ref), custom_call_target="tpu_custom_call" | custom-call | bytes 3600000 | tf_op jit(solution)/shard_map/pallas_call | solution.py:812
  12.5 0.0 collective-permute-done.1.eta_b
  12.5 0.3 shard_map.58
  12.8 0.0 collective-permute-done.2.xi_b
  12.8 0.2 shard_map.59
  13.0 0.1 collective-permute-done.4.below_ref.above_ref
  13.1 0.4 shard_map.60
  13.5 1.0 %shard_map.61 = (f32[3,4,256,128]{3,2,1,0:T(8,128)S(1)}, f32[256,128]{1,0:T(8,128)S(1)}, f32[13,16,128]{2,1,0:T(8,128)S(1)}, f32[13,16,128]{2,1,0:T(8,128)S(1)}) custom-call(f32[5,256,128]{2,1,0:T(8,128)S(1)} %get-tuple-element.51.u_ref, f32[4,256,128]{2,1,0:T(8,128)S(1)} %get-tuple-element.54.prim_ref, f32[9,256,128]{2,1,0:T(8,128)S(1)} %get-tuple-element.55.metrics_ref, ...), custom_call_target="tpu_custom_call" | custom-call | bytes 3600000 | tf_op jit(solution)/shard_map/pallas_call | solution.py:812
  14.6 0.7 %collective-permute-start.8 = (f32[13,16,128]{2,1,0:T(8,128)S(1)}, f32[13,16,128]{2,1,0:T(8,128)S(1)}, u32[]{:S(2)}, u32[]{:S(2)}) collective-permute-start(f32[13,16,128]{2,1,0:T(8,128)S(1)} %get-tuple-element.79), channel_id=1, source_target_pairs={{0,2},{2,0},{4,6},{6,4},{1,3},{3,1},{5,7},{7,5},{8,10},{10,8},{12,... | collective-permute-start | bytes 319496 | tf_op jit(solution)/shard_map/ppermute | solution.py:771
  15.3 1.7 %collective-permute-start.9 = (f32[13,16,128]{2,1,0:T(8,128)S(1)}, f32[13,16,128]{2,1,0:T(8,128)S(1)}, u32[]{:S(2)}, u32[]{:S(2)}) collective-permute-start(f32[13,16,128]{2,1,0:T(8,128)S(1)} %get-tuple-element.80), channel_id=1, source_target_pairs={{0,6},{2,4},{4,2},{6,0},{1,7},{3,5},{5,3},{7,1},{8,14},{10,12},{12... | collective-permute-start | bytes 319496 | tf_op jit(solution)/shard_map/ppermute | solution.py:771
  17.0 0.4 shard_map.63
  17.4 0.1 collective-permute-start.5
  17.5 1.6 %collective-permute-start.6 = (f32[8,16,128]{2,1,0:T(8,128)S(1)}, f32[8,16,128]{2,1,0:T(8,128)S(1)}, u32[]{:S(2)}, u32[]{:S(2)}) collective-permute-start(f32[8,16,128]{2,1,0:T(8,128)S(1)} %get-tuple-element.77), channel_id=1, source_target_pairs={{0,8},{8,0},{16,24},{24,16},{1,9},{9,1},{17,25},{25,17},{2,10},{10... | collective-permute-start | bytes 196616 | tf_op jit(solution)/shard_map/ppermute | solution.py:771
  19.1 1.5 %collective-permute-start.7 = (f32[4,8,128]{2,1,0:T(8,128)S(1)}, f32[4,8,128]{2,1,0:T(8,128)S(1)}, u32[]{:S(2)}, u32[]{:S(2)}) collective-permute-start(f32[4,8,128]{2,1,0:T(8,128)S(1)} %get-tuple-element.78), channel_id=1, source_target_pairs={{0,1},{1,0},{2,3},{3,2},{4,5},{5,4},{6,7},{7,6},{8,9},{9,8},{10,11... | collective-permute-start | bytes 49160 | tf_op jit(solution)/shard_map/ppermute | solution.py:792
  20.6 0.5 %shard_map.62 = (f32[4,256,128]{2,1,0:T(8,128)S(1)}, f32[4,256,128]{2,1,0:T(8,128)S(1)}, f32[4,256,128]{2,1,0:T(8,128)S(1)}) custom-call(f32[3,4,256,128]{3,2,1,0:T(8,128)S(1)} %get-tuple-element.71.contra_ref, f32[4,128,128]{2,1,0:T(8,128)S(1)} %get-tuple-element.57.tables_ref), custom_call_target="tpu_custom_call" | custom-call | bytes 3600000 | tf_op jit(solution)/shard_map/pallas_call | solution.py:812
  21.1 0.7 %collective-permute-done.5.xi_b = f32[8,16,128]{2,1,0:T(8,128)S(1)} collective-permute-done((f32[8,16,128]{2,1,0:T(8,128)S(1)}, f32[8,16,128]{2,1,0:T(8,128)S(1)}, u32[]{:S(2)}, u32[]{:S(2)}) %collective-permute-start.5) | collective-permute-done | bytes 65568 | tf_op jit(solution)/shard_map/ppermute | solution.py:771
  21.8 0.1 shard_map.64.part_ref
  22.0 0.8 %collective-permute-done.7.below_ref.above_ref = f32[4,8,128]{2,1,0:T(8,128)S(1)} collective-permute-done((f32[4,8,128]{2,1,0:T(8,128)S(1)}, f32[4,8,128]{2,1,0:T(8,128)S(1)}, u32[]{:S(2)}, u32[]{:S(2)}) %collective-permute-start.7) | collective-permute-done | bytes 16416 | tf_op jit(solution)/shard_map/ppermute | solution.py:792
  22.8 0.4 shard_map.65.total_ref
  23.2 0.4 %shard_map.66 = (f32[4,256,128]{2,1,0:T(8,128)S(1)}, f32[20,16,128]{2,1,0:T(8,128)S(1)}, f32[20,16,128]{2,1,0:T(8,128)S(1)}) custom-call(f32[5,256,128]{2,1,0:T(8,128)S(1)} %get-tuple-element.51.u_ref, f32[256,128]{1,0:T(8,128)S(1)} %get-tuple-element.53.jacobian_ref, f32[4,256,128]{2,1,0:T(8,128)S(1)} %get-tuple-element.72.source_ref, ...), custom_call_target="tpu_custom_call" | custom-call | bytes 3600000 | tf_op jit(solution)/shard_map/pallas_call | solution.py:812
  23.6 0.2 collective-permute-start.12
  23.9 1.7 %collective-permute-start.13 = (f32[20,16,128]{2,1,0:T(8,128)S(1)}, f32[20,16,128]{2,1,0:T(8,128)S(1)}, u32[]{:S(2)}, u32[]{:S(2)}) collective-permute-start(f32[20,16,128]{2,1,0:T(8,128)S(1)} %get-tuple-element.88), channel_id=1, source_target_pairs={{0,6},{2,4},{4,2},{6,0},{1,7},{3,5},{5,3},{7,1},{8,14},{10,12},{12... | collective-permute-start | bytes 491528 | tf_op jit(solution)/shard_map/ppermute | solution.py:771
  25.6 0.1 shard_map.67.source_ref
  25.7 0.2 shard_map.68
  25.9 0.1 collective-permute-start.10
  25.9 1.4 %collective-permute-start.11 = (f32[25,16,128]{2,1,0:T(8,128)S(1)}, f32[25,16,128]{2,1,0:T(8,128)S(1)}, u32[]{:S(2)}, u32[]{:S(2)}) collective-permute-start(f32[25,16,128]{2,1,0:T(8,128)S(1)} %get-tuple-element.85), channel_id=1, source_target_pairs={{0,24},{8,16},{16,8},{24,0},{1,25},{9,17},{17,9},{25,1},{2,26},{10... | collective-permute-start | bytes 614408 | tf_op jit(solution)/shard_map/ppermute | solution.py:771
  27.3 0.3 shard_map.70.source_ref.order_ref
  27.6 5.1 %collective-permute-done.12.eta_a = f32[20,16,128]{2,1,0:T(8,128)S(1)} collective-permute-done((f32[20,16,128]{2,1,0:T(8,128)S(1)}, f32[20,16,128]{2,1,0:T(8,128)S(1)}, u32[]{:S(2)}, u32[]{:S(2)}) %collective-permute-start.12) | collective-permute-done | bytes 163872 | tf_op jit(solution)/shard_map/ppermute | solution.py:771
  32.7 0.1 shard_map.74
  32.7 0.1 collective-permute-start.14
  32.8 1.1 %collective-permute-start.15 = (f32[240,128]{1,0:T(8,128)S(1)}, f32[240,128]{1,0:T(8,128)S(1)}, u32[]{:S(2)}, u32[]{:S(2)}) collective-permute-start(f32[240,128]{1,0:T(8,128)S(1)} %get-tuple-element.93), channel_id=1, source_target_pairs={{0,8},{8,0},{16,24},{24,16},{1,9},{9,1},{17,25},{25,17},{2,10},{10... | collective-permute-start | bytes 368648 | tf_op jit(solution)/shard_map/ppermute | solution.py:771
  33.9 0.4 %shard_map.71 = (f32[4,256,128]{2,1,0:T(8,128)S(1)}, f32[128,128]{1,0:T(8,128)S(1)}, f32[5,8,128]{2,1,0:T(8,128)S(1)}, f32[5,8,128]{2,1,0:T(8,128)S(1)}) custom-call(f32[4,256,128]{2,1,0:T(8,128)S(1)} %shard_map.70.source_ref.order_ref, f32[1,256,128]{2,1,0:T(8,128)S(1)} %get-tuple-element.86.mass_ref, f32[20,16,128]{2,1,0:T(8,128)S(1)} %collective-permute-done.12.eta_a, ...), custom_call_target="tpu_custom_call" | custom-call | bytes 3600000 | tf_op jit(solution)/shard_map/pallas_call | solution.py:812
  34.3 1.6 %collective-permute-start.17 = (f32[128,128]{1,0:T(8,128)S(1)}, f32[128,128]{1,0:T(8,128)S(1)}, u32[]{:S(2)}, u32[]{:S(2)}) collective-permute-start(f32[128,128]{1,0:T(8,128)S(1)} %get-tuple-element.95), channel_id=1, source_target_pairs={{0,1},{1,0},{2,3},{3,2},{4,5},{5,4},{6,7},{7,6},{8,9},{9,8},{10,11... | collective-permute-start | bytes 196616 | tf_op jit(solution)/shard_map/ppermute | solution.py:792
  35.9 0.3 collective-permute-start.16
  36.2 1.9 %collective-permute-start.18 = (f32[5,8,128]{2,1,0:T(8,128)S(1)}, f32[5,8,128]{2,1,0:T(8,128)S(1)}, u32[]{:S(2)}, u32[]{:S(2)}) collective-permute-start(f32[5,8,128]{2,1,0:T(8,128)S(1)} %get-tuple-element.96), channel_id=1, source_target_pairs={{0,9},{1,8},{8,1},{9,0},{16,25},{17,24},{24,17},{25,16},{2,11},{3,... | collective-permute-start | bytes 61448 | tf_op jit(solution)/shard_map/ppermute | solution.py:783
  38.1 0.2 shard_map.72.source_ref
  38.4 0.2 shard_map.73
  38.6 0.2 shard_map.69.mass_ref
  38.9 0.6 %shard_map.75.state_ref = f32[4,256,128]{2,1,0:T(8,128)S(1)} custom-call(f32[4,256,128]{2,1,0:T(8,128)S(1)} %shard_map.72.source_ref, f32[384,128]{1,0:T(8,128)S(1)} %get-tuple-element.90.first_source, f32[384,128]{1,0:T(8,128)S(1)} %get-tuple-element.91.second_source, f32[240,128]{1,0:T(8,128)S(1)} %collective-permute-done.14.edge_b, ...), custom_call_target="tpu_custom_call" | custom-call | bytes 3600000 | tf_op jit(solution)/shard_map/pallas_call | solution.py:812
  39.5 0.7 %collective-permute-done.16 = f32[5,8,128]{2,1,0:T(8,128)S(1)} collective-permute-done((f32[5,8,128]{2,1,0:T(8,128)S(1)}, f32[5,8,128]{2,1,0:T(8,128)S(1)}, u32[]{:S(2)}, u32[]{:S(2)}) %collective-permute-start.16) | collective-permute-done | bytes 20512 | tf_op jit(solution)/shard_map/ppermute | solution.py:783
  40.2 1.2 %shard_map.76 = f32[5,256,128]{2,1,0:T(8,128)} custom-call(f32[1,256,128]{2,1,0:T(8,128)S(1)} %shard_map.69.mass_ref, f32[4,256,128]{2,1,0:T(8,128)S(1)} %shard_map.75.state_ref, f32[40,128]{1,0:T(8,128)S(1)} %bitcast.12, f32[40,128]{1,0:T(8,128)S(1)} %bitcast.13, f32[128,128]{1,0:T(8,128)S(1)} %collective-permute-done.17.below_ref.above_ref, ...), custom_call_target="tpu_custom_call" | custom-call | bytes 3600000 | tf_op jit(solution)/shard_map/pallas_call | solution.py:812
  (12 shorter events, 0.0 us)
Async XLA Ops:
  2.2 10.3 %collective-permute-start = (f32[10,16,128]{2,1,0:T(8,128)S(1)}, f32[10,16,128]{2,1,0:T(8,128)S(1)}, u32[]{:S(2)}, u32[]{:S(2)}) collective-permute-start(f32[10,16,128]{2,1,0:T(8,128)S(1)} %get-tuple-element.61), channel_id=1, source_target_pairs={{0,2},{2,0},{4,6},{6,4},{1,3},{3,1},{5,7},{7,5},{8,10},{10,8},{12,... | collective-permute-start | bytes 245768 | tf_op jit(solution)/shard_map/ppermute | solution.py:771
  5.3 7.2 %collective-permute-start.1 = (f32[10,16,128]{2,1,0:T(8,128)S(1)}, f32[10,16,128]{2,1,0:T(8,128)S(1)}, u32[]{:S(2)}, u32[]{:S(2)}) collective-permute-start(f32[10,16,128]{2,1,0:T(8,128)S(1)} %get-tuple-element.62), channel_id=1, source_target_pairs={{0,6},{2,4},{4,2},{6,0},{1,7},{3,5},{5,3},{7,1},{8,14},{10,12},{12... | collective-permute-start | bytes 245768 | tf_op jit(solution)/shard_map/ppermute | solution.py:771
  7.8 5.1 %collective-permute-start.2 = (f32[10,16,128]{2,1,0:T(8,128)S(1)}, f32[10,16,128]{2,1,0:T(8,128)S(1)}, u32[]{:S(2)}, u32[]{:S(2)}) collective-permute-start(f32[10,16,128]{2,1,0:T(8,128)S(1)} %get-tuple-element.64), channel_id=1, source_target_pairs={{0,24},{8,16},{16,8},{24,0},{1,25},{9,17},{17,9},{25,1},{2,26},{10... | collective-permute-start | bytes 245768 | tf_op jit(solution)/shard_map/ppermute | solution.py:771
  8.1 4.7 %collective-permute-start.3 = (f32[10,16,128]{2,1,0:T(8,128)S(1)}, f32[10,16,128]{2,1,0:T(8,128)S(1)}, u32[]{:S(2)}, u32[]{:S(2)}) collective-permute-start(f32[10,16,128]{2,1,0:T(8,128)S(1)} %get-tuple-element.65), channel_id=1, source_target_pairs={{0,8},{8,0},{16,24},{24,16},{1,9},{9,1},{17,25},{25,17},{2,10},{10... | collective-permute-start | bytes 245768 | tf_op jit(solution)/shard_map/ppermute | solution.py:771
  9.4 3.8 %collective-permute-start.4 = (f32[5,8,128]{2,1,0:T(8,128)S(1)}, f32[5,8,128]{2,1,0:T(8,128)S(1)}, u32[]{:S(2)}, u32[]{:S(2)}) collective-permute-start(f32[5,8,128]{2,1,0:T(8,128)S(1)} %get-tuple-element.52.refs_2_), channel_id=1, source_target_pairs={{0,1},{1,0},{2,3},{3,2},{4,5},{5,4},{6,7},{7,6},{8,9},{9,8},{10,11... | collective-permute-start | bytes 61448 | tf_op jit(solution)/shard_map/ppermute | solution.py:792
  14.6 8.6 %collective-permute-start.8 = (f32[13,16,128]{2,1,0:T(8,128)S(1)}, f32[13,16,128]{2,1,0:T(8,128)S(1)}, u32[]{:S(2)}, u32[]{:S(2)}) collective-permute-start(f32[13,16,128]{2,1,0:T(8,128)S(1)} %get-tuple-element.79), channel_id=1, source_target_pairs={{0,2},{2,0},{4,6},{6,4},{1,3},{3,1},{5,7},{7,5},{8,10},{10,8},{12,... | collective-permute-start | bytes 319496 | tf_op jit(solution)/shard_map/ppermute | solution.py:771
  15.3 7.8 %collective-permute-start.9 = (f32[13,16,128]{2,1,0:T(8,128)S(1)}, f32[13,16,128]{2,1,0:T(8,128)S(1)}, u32[]{:S(2)}, u32[]{:S(2)}) collective-permute-start(f32[13,16,128]{2,1,0:T(8,128)S(1)} %get-tuple-element.80), channel_id=1, source_target_pairs={{0,6},{2,4},{4,2},{6,0},{1,7},{3,5},{5,3},{7,1},{8,14},{10,12},{12... | collective-permute-start | bytes 319496 | tf_op jit(solution)/shard_map/ppermute | solution.py:771
  17.4 4.4 %collective-permute-start.5 = (f32[8,16,128]{2,1,0:T(8,128)S(1)}, f32[8,16,128]{2,1,0:T(8,128)S(1)}, u32[]{:S(2)}, u32[]{:S(2)}) collective-permute-start(f32[8,16,128]{2,1,0:T(8,128)S(1)} %get-tuple-element.76), channel_id=1, source_target_pairs={{0,24},{8,16},{16,8},{24,0},{1,25},{9,17},{17,9},{25,1},{2,26},{10... | collective-permute-start | bytes 196616 | tf_op jit(solution)/shard_map/ppermute | solution.py:771
  17.5 4.3 %collective-permute-start.6 = (f32[8,16,128]{2,1,0:T(8,128)S(1)}, f32[8,16,128]{2,1,0:T(8,128)S(1)}, u32[]{:S(2)}, u32[]{:S(2)}) collective-permute-start(f32[8,16,128]{2,1,0:T(8,128)S(1)} %get-tuple-element.77), channel_id=1, source_target_pairs={{0,8},{8,0},{16,24},{24,16},{1,9},{9,1},{17,25},{25,17},{2,10},{10... | collective-permute-start | bytes 196616 | tf_op jit(solution)/shard_map/ppermute | solution.py:771
  19.1 3.7 %collective-permute-start.7 = (f32[4,8,128]{2,1,0:T(8,128)S(1)}, f32[4,8,128]{2,1,0:T(8,128)S(1)}, u32[]{:S(2)}, u32[]{:S(2)}) collective-permute-start(f32[4,8,128]{2,1,0:T(8,128)S(1)} %get-tuple-element.78), channel_id=1, source_target_pairs={{0,1},{1,0},{2,3},{3,2},{4,5},{5,4},{6,7},{7,6},{8,9},{9,8},{10,11... | collective-permute-start | bytes 49160 | tf_op jit(solution)/shard_map/ppermute | solution.py:792
  23.6 9.0 %collective-permute-start.12 = (f32[20,16,128]{2,1,0:T(8,128)S(1)}, f32[20,16,128]{2,1,0:T(8,128)S(1)}, u32[]{:S(2)}, u32[]{:S(2)}) collective-permute-start(f32[20,16,128]{2,1,0:T(8,128)S(1)} %get-tuple-element.87), channel_id=1, source_target_pairs={{0,2},{2,0},{4,6},{6,4},{1,3},{3,1},{5,7},{7,5},{8,10},{10,8},{12,... | collective-permute-start | bytes 491528 | tf_op jit(solution)/shard_map/ppermute | solution.py:771
  23.9 8.8 %collective-permute-start.13 = (f32[20,16,128]{2,1,0:T(8,128)S(1)}, f32[20,16,128]{2,1,0:T(8,128)S(1)}, u32[]{:S(2)}, u32[]{:S(2)}) collective-permute-start(f32[20,16,128]{2,1,0:T(8,128)S(1)} %get-tuple-element.88), channel_id=1, source_target_pairs={{0,6},{2,4},{4,2},{6,0},{1,7},{3,5},{5,3},{7,1},{8,14},{10,12},{12... | collective-permute-start | bytes 491528 | tf_op jit(solution)/shard_map/ppermute | solution.py:771
  25.9 10.1 %collective-permute-start.10 = (f32[25,16,128]{2,1,0:T(8,128)S(1)}, f32[25,16,128]{2,1,0:T(8,128)S(1)}, u32[]{:S(2)}, u32[]{:S(2)}) collective-permute-start(f32[25,16,128]{2,1,0:T(8,128)S(1)} %get-tuple-element.84), channel_id=1, source_target_pairs={{0,8},{8,0},{16,24},{24,16},{1,9},{9,1},{17,25},{25,17},{2,10},{10... | collective-permute-start | bytes 614408 | tf_op jit(solution)/shard_map/ppermute | solution.py:771
  25.9 10.3 %collective-permute-start.11 = (f32[25,16,128]{2,1,0:T(8,128)S(1)}, f32[25,16,128]{2,1,0:T(8,128)S(1)}, u32[]{:S(2)}, u32[]{:S(2)}) collective-permute-start(f32[25,16,128]{2,1,0:T(8,128)S(1)} %get-tuple-element.85), channel_id=1, source_target_pairs={{0,24},{8,16},{16,8},{24,0},{1,25},{9,17},{17,9},{25,1},{2,26},{10... | collective-permute-start | bytes 614408 | tf_op jit(solution)/shard_map/ppermute | solution.py:771
  32.7 6.1 %collective-permute-start.14 = (f32[240,128]{1,0:T(8,128)S(1)}, f32[240,128]{1,0:T(8,128)S(1)}, u32[]{:S(2)}, u32[]{:S(2)}) collective-permute-start(f32[240,128]{1,0:T(8,128)S(1)} %get-tuple-element.92), channel_id=1, source_target_pairs={{0,24},{8,16},{16,8},{24,0},{1,25},{9,17},{17,9},{25,1},{2,26},{10... | collective-permute-start | bytes 368648 | tf_op jit(solution)/shard_map/ppermute | solution.py:771
  32.8 6.1 %collective-permute-start.15 = (f32[240,128]{1,0:T(8,128)S(1)}, f32[240,128]{1,0:T(8,128)S(1)}, u32[]{:S(2)}, u32[]{:S(2)}) collective-permute-start(f32[240,128]{1,0:T(8,128)S(1)} %get-tuple-element.93), channel_id=1, source_target_pairs={{0,8},{8,0},{16,24},{24,16},{1,9},{9,1},{17,25},{25,17},{2,10},{10... | collective-permute-start | bytes 368648 | tf_op jit(solution)/shard_map/ppermute | solution.py:771
  34.3 5.8 %collective-permute-start.17 = (f32[128,128]{1,0:T(8,128)S(1)}, f32[128,128]{1,0:T(8,128)S(1)}, u32[]{:S(2)}, u32[]{:S(2)}) collective-permute-start(f32[128,128]{1,0:T(8,128)S(1)} %get-tuple-element.95), channel_id=1, source_target_pairs={{0,1},{1,0},{2,3},{3,2},{4,5},{5,4},{6,7},{7,6},{8,9},{9,8},{10,11... | collective-permute-start | bytes 196616 | tf_op jit(solution)/shard_map/ppermute | solution.py:792
  35.9 4.2 %collective-permute-start.16 = (f32[5,8,128]{2,1,0:T(8,128)S(1)}, f32[5,8,128]{2,1,0:T(8,128)S(1)}, u32[]{:S(2)}, u32[]{:S(2)}) collective-permute-start(f32[5,8,128]{2,1,0:T(8,128)S(1)} %get-tuple-element.94), channel_id=1, source_target_pairs={{0,25},{1,24},{8,17},{9,16},{16,9},{17,8},{24,1},{25,0},{2,27},{3,... | collective-permute-start | bytes 61448 | tf_op jit(solution)/shard_map/ppermute | solution.py:783
  36.2 3.9 %collective-permute-start.18 = (f32[5,8,128]{2,1,0:T(8,128)S(1)}, f32[5,8,128]{2,1,0:T(8,128)S(1)}, u32[]{:S(2)}, u32[]{:S(2)}) collective-permute-start(f32[5,8,128]{2,1,0:T(8,128)S(1)} %get-tuple-element.96), channel_id=1, source_target_pairs={{0,9},{1,8},{8,1},{9,0},{16,25},{17,24},{24,17},{25,16},{2,11},{3,... | collective-permute-start | bytes 61448 | tf_op jit(solution)/shard_map/ppermute | solution.py:783

commit v9 on v7

--- a/solution.py
+++ b/solution.py
@@ -689,7 +689,7 @@
     )
 
 
-def mass_xi_kernel(grid, source_ref, xi_a, xi_b, tables_ref, result_ref):
+def mass_xi_kernel(grid, source_ref, xi_a, xi_b, tables_ref, order_ref, result_ref):
     smooth = split_weights(tables_ref[SMOOTH])
     xi_filter(grid, source_ref.at[0], xi_a, xi_b, WIDTH * 4, smooth, result_ref.at[0])
 
@@ -904,9 +904,6 @@
     xi_b = pair_swap(xi_second, "xi", 1)
     xi_a = pair_swap(xi_first, "xi", 0)
     (source,) = call(functools.partial(source_kernel, grid, eta_sources), [(4, *block)], state)
-    (mass_part,) = call(
-        functools.partial(mass_xi_kernel, grid), [(1, *block)], mass_source, xi_a, xi_b, tables,
-    )
     layers = 5 * WIDTH * ny
     halo_first, halo_second = call(
         functools.partial(halo_source_kernel, grid),
@@ -933,6 +930,9 @@
         source, halo_first, halo_second, edge_b, edge_a, tables,
         scratch=[pltpu.VMEM((PLANES * ny, nz), jnp.float32)] * 2,
     )
+    (mass_part,) = call(
+        functools.partial(mass_xi_kernel, grid), [(1, *block)], mass_source, xi_a, xi_b, tables, state,
+    )
     edges = [edge.reshape(WIDTH * TILE, LANES) for edge in (*edges_a, *edges_b)]
     (result,) = call(
         functools.partial(zeta_filter_kernel, grid),

time: 41.5 us -> 41.5 us (level)
  no operation moved by 1% of the time
where the time goes in v9:
time: 41.5 us; the launch traced here: 41.4 us
  starting transfers between devices  23 us (55%)
  Pallas kernels  11 us (27%)
  waiting for transfers between devices  7.21 us (17%)
    ppermute x14, starting transfers between devices, pair_swap(): return lax.ppermute(value, axis, pairs)  16 us
    pallas_call x19, Pallas kernels, call(): pl.pallas_call(kernel, out_shape=shapes, in_specs=[pl.BlockSpec(memory_sp...  11 us
    ppermute x14, waiting for transfers between devices, pair_swap(): return lax.ppermute(value, axis, pairs)  6.18 us
    ppermute x3, starting transfers between devices, ring_swap(): other = lax.ppermute(value, axis, [(0, 1), (1, 0)])  4.64 us
    ppermute x2, starting transfers between devices, send(): return lax.ppermute(value, ('xi', 'zeta'), pairs)  2.36 us
  transfers between devices with their start and end apart: 19, of which 7 were waited for; matrix products, arithmetic and copies ran while one was open for 0% of the time, Pallas kernels for 14%

profile of v9, /device:TPU:0, one launch (start us, length us, event | category | flops | bytes accessed | tf_op | source)
XLA Modules:
  0.0 41.4 jit_solution(672876759362932195)
XLA Ops:
  0.0 2.2 %shard_map.55 = (f32[5,256,128]{2,1,0:T(8,128)S(1)}, f32[128,128]{1,0:T(8,128)S(1)}, f32[9,256,128]{2,1,0:T(8,128)S(1)}, f32[4,256,128]{2,1,0:T(8,128)S(1)}, f32...) custom-call(f32[5,256,128]{2,1,0:T(8,128)} %bitcast.17, ...), custom_call_target="tpu_custom_call" | custom-call | bytes 3600000 | tf_op jit(solution)/shard_map/pallas_call | solution.py:805
  2.2 3.1 %collective-permute-start = (f32[10,16,128]{2,1,0:T(8,128)S(1)}, f32[10,16,128]{2,1,0:T(8,128)S(1)}, u32[]{:S(2)}, u32[]{:S(2)}) collective-permute-start(f32[10,16,128]{2,1,0:T(8,128)S(1)} %get-tuple-element.57), channel_id=1, source_target_pairs={{0,2},{2,0},{4,6},{6,4},{1,3},{3,1},{5,7},{7,5},{8,10},{10,8},{12,... | collective-permute-start | bytes 245768 | tf_op jit(solution)/shard_map/ppermute | solution.py:764
  5.3 2.5 %collective-permute-start.1 = (f32[10,16,128]{2,1,0:T(8,128)S(1)}, f32[10,16,128]{2,1,0:T(8,128)S(1)}, u32[]{:S(2)}, u32[]{:S(2)}) collective-permute-start(f32[10,16,128]{2,1,0:T(8,128)S(1)} %get-tuple-element.58), channel_id=1, source_target_pairs={{0,6},{2,4},{4,2},{6,0},{1,7},{3,5},{5,3},{7,1},{8,14},{10,12},{12... | collective-permute-start | bytes 245768 | tf_op jit(solution)/shard_map/ppermute | solution.py:764
  7.8 0.4 collective-permute-start.2
  8.1 1.2 %collective-permute-start.3 = (f32[10,16,128]{2,1,0:T(8,128)S(1)}, f32[10,16,128]{2,1,0:T(8,128)S(1)}, u32[]{:S(2)}, u32[]{:S(2)}) collective-permute-start(f32[10,16,128]{2,1,0:T(8,128)S(1)} %get-tuple-element.60), channel_id=1, source_target_pairs={{0,8},{8,0},{16,24},{24,16},{1,9},{9,1},{17,25},{25,17},{2,10},{10... | collective-permute-start | bytes 245768 | tf_op jit(solution)/shard_map/ppermute | solution.py:764
  9.4 1.5 %collective-permute-start.4 = (f32[5,8,128]{2,1,0:T(8,128)S(1)}, f32[5,8,128]{2,1,0:T(8,128)S(1)}, u32[]{:S(2)}, u32[]{:S(2)}) collective-permute-start(f32[5,8,128]{2,1,0:T(8,128)S(1)} %get-tuple-element.48.refs_2_), channel_id=1, source_target_pairs={{0,1},{1,0},{2,3},{3,2},{4,5},{5,4},{6,7},{7,6},{8,9},{9,8},{10,11... | collective-permute-start | bytes 61448 | tf_op jit(solution)/shard_map/ppermute | solution.py:785
  10.9 1.0 %shard_map.56 = (f32[4,128,128]{2,1,0:T(8,128)S(1)}, f32[256,128]{1,0:T(8,128)S(1)}) custom-call(f32[4,128,128]{2,1,0:T(8,128)} %constant.5.clone.refs_0_, f32[256,128]{1,0:T(8,128)} %bitcast.18, f32[5,8,128]{2,1,0:T(8,128)S(1)} %get-tuple-element.48.refs_2_), custom_call_target="tpu_custom_call" | custom-call | bytes 3600000 | tf_op jit(solution)/shard_map/pallas_call | solution.py:805
  11.9 0.6 %shard_map.57 = (f32[5,256,128]{2,1,0:T(8,128)S(1)}, f32[5,256,128]{2,1,0:T(8,128)S(1)}, f32[5,256,128]{2,1,0:T(8,128)S(1)}) custom-call(f32[4,256,128]{2,1,0:T(8,128)S(1)} %get-tuple-element.50.prim_ref, f32[3,256,128]{2,1,0:T(8,128)S(1)} %get-tuple-element.52.mass_ref, f32[4,128,128]{2,1,0:T(8,128)S(1)} %get-tuple-element.53.tables_ref), custom_call_target="tpu_custom_call" | custom-call | bytes 3600000 | tf_op jit(solution)/shard_map/pallas_call | solution.py:805
  12.5 0.0 collective-permute-done.1.eta_b
  12.5 0.0 collective-permute-done.2.xi_b
  12.5 0.5 %shard_map.58 = (f32[2,4,256,128]{3,2,1,0:T(8,128)S(1)}, f32[256,128]{1,0:T(8,128)S(1)}) custom-call(f32[5,256,128]{2,1,0:T(8,128)S(1)} %get-tuple-element.54.xi_source, f32[5,256,128]{2,1,0:T(8,128)S(1)} %get-tuple-element.55.eta_source, f32[5,256,128]{2,1,0:T(8,128)S(1)} %get-tuple-element.56.own_ref, f32[10,16,128]{2,1,0:T(8,128)S(1)} %collective-permute-done.eta_a, ...), custom_call_target="tpu_custom_call" | custom-call | bytes 3600000 | tf_op jit(solution)/shard_map/pallas_call | solution.py:805
  13.0 0.2 collective-permute-done.4.zeta_below.zeta_above
  13.1 1.4 %shard_map.59 = (f32[3,4,256,128]{3,2,1,0:T(8,128)S(1)}, f32[256,128]{1,0:T(8,128)S(1)}, f32[13,16,128]{2,1,0:T(8,128)S(1)}, f32[13,16,128]{2,1,0:T(8,128)S(1)}) custom-call(f32[5,256,128]{2,1,0:T(8,128)S(1)} %get-tuple-element.47.u_ref, f32[4,256,128]{2,1,0:T(8,128)S(1)} %get-tuple-element.50.prim_ref, f32[9,256,128]{2,1,0:T(8,128)S(1)} %get-tuple-element.51.metrics_ref, ...), custom_call_target="tpu_custom_call" | custom-call | bytes 3600000 | tf_op jit(solution)/shard_map/pallas_call | solution.py:805
  14.6 0.7 %collective-permute-start.5 = (f32[13,16,128]{2,1,0:T(8,128)S(1)}, f32[13,16,128]{2,1,0:T(8,128)S(1)}, u32[]{:S(2)}, u32[]{:S(2)}) collective-permute-start(f32[13,16,128]{2,1,0:T(8,128)S(1)} %get-tuple-element.67), channel_id=1, source_target_pairs={{0,2},{2,0},{4,6},{6,4},{1,3},{3,1},{5,7},{7,5},{8,10},{10,8},{12,... | collective-permute-start | bytes 319496 | tf_op jit(solution)/shard_map/ppermute | solution.py:764
  15.3 1.7 %collective-permute-start.6 = (f32[13,16,128]{2,1,0:T(8,128)S(1)}, f32[13,16,128]{2,1,0:T(8,128)S(1)}, u32[]{:S(2)}, u32[]{:S(2)}) collective-permute-start(f32[13,16,128]{2,1,0:T(8,128)S(1)} %get-tuple-element.68), channel_id=1, source_target_pairs={{0,6},{2,4},{4,2},{6,0},{1,7},{3,5},{5,3},{7,1},{8,14},{10,12},{12... | collective-permute-start | bytes 319496 | tf_op jit(solution)/shard_map/ppermute | solution.py:764
  17.0 0.4 shard_map.61
  17.3 0.1 collective-permute-start.7
  17.4 1.6 %collective-permute-start.8 = (f32[8,16,128]{2,1,0:T(8,128)S(1)}, f32[8,16,128]{2,1,0:T(8,128)S(1)}, u32[]{:S(2)}, u32[]{:S(2)}) collective-permute-start(f32[8,16,128]{2,1,0:T(8,128)S(1)} %get-tuple-element.71), channel_id=1, source_target_pairs={{0,8},{8,0},{16,24},{24,16},{1,9},{9,1},{17,25},{25,17},{2,10},{10... | collective-permute-start | bytes 196616 | tf_op jit(solution)/shard_map/ppermute | solution.py:764
  19.0 1.5 %collective-permute-start.9 = (f32[4,8,128]{2,1,0:T(8,128)S(1)}, f32[4,8,128]{2,1,0:T(8,128)S(1)}, u32[]{:S(2)}, u32[]{:S(2)}) collective-permute-start(f32[4,8,128]{2,1,0:T(8,128)S(1)} %get-tuple-element.72), channel_id=1, source_target_pairs={{0,1},{1,0},{2,3},{3,2},{4,5},{5,4},{6,7},{7,6},{8,9},{9,8},{10,11... | collective-permute-start | bytes 49160 | tf_op jit(solution)/shard_map/ppermute | solution.py:785
  20.5 0.5 %shard_map.60 = (f32[4,256,128]{2,1,0:T(8,128)S(1)}, f32[4,256,128]{2,1,0:T(8,128)S(1)}, f32[4,256,128]{2,1,0:T(8,128)S(1)}) custom-call(f32[3,4,256,128]{3,2,1,0:T(8,128)S(1)} %get-tuple-element.63.contra_ref, f32[4,128,128]{2,1,0:T(8,128)S(1)} %get-tuple-element.53.tables_ref), custom_call_target="tpu_custom_call" | custom-call | bytes 3600000 | tf_op jit(solution)/shard_map/pallas_call | solution.py:805
  21.0 0.7 %collective-permute-done.7.xi_b = f32[8,16,128]{2,1,0:T(8,128)S(1)} collective-permute-done((f32[8,16,128]{2,1,0:T(8,128)S(1)}, f32[8,16,128]{2,1,0:T(8,128)S(1)}, u32[]{:S(2)}, u32[]{:S(2)}) %collective-permute-start.7) | collective-permute-done | bytes 65568 | tf_op jit(solution)/shard_map/ppermute | solution.py:764
  21.8 0.0 collective-permute-done.5.eta_a
  21.8 0.2 collective-permute-done.6.eta_b
  22.0 0.5 %shard_map.62.total_ref = f32[4,256,128]{2,1,0:T(8,128)S(1)} custom-call(f32[4,256,128]{2,1,0:T(8,128)S(1)} %get-tuple-element.64.xi_source, f32[4,256,128]{2,1,0:T(8,128)S(1)} %get-tuple-element.65.eta_source, f32[4,256,128]{2,1,0:T(8,128)S(1)} %get-tuple-element.66.own_ref, f32[13,16,128]{2,1,0:T(8,128)S(1)} %collective-permute-done.5.eta_a, ...), custom_call_target="tpu_custom_call" | custom-call | bytes 3600000 | tf_op jit(solution)/shard_map/pallas_call | solution.py:805
  22.5 0.3 collective-permute-done.9.zeta_below.zeta_above
  22.8 0.4 %shard_map.63 = (f32[4,256,128]{2,1,0:T(8,128)S(1)}, f32[20,16,128]{2,1,0:T(8,128)S(1)}, f32[20,16,128]{2,1,0:T(8,128)S(1)}) custom-call(f32[5,256,128]{2,1,0:T(8,128)S(1)} %get-tuple-element.47.u_ref, f32[256,128]{1,0:T(8,128)S(1)} %get-tuple-element.49.jacobian_ref, f32[4,256,128]{2,1,0:T(8,128)S(1)} %shard_map.62.total_ref, ...), custom_call_target="tpu_custom_call" | custom-call | bytes 3600000 | tf_op jit(solution)/shard_map/pallas_call | solution.py:805
  23.2 1.3 %collective-permute-start.12 = (f32[20,16,128]{2,1,0:T(8,128)S(1)}, f32[20,16,128]{2,1,0:T(8,128)S(1)}, u32[]{:S(2)}, u32[]{:S(2)}) collective-permute-start(f32[20,16,128]{2,1,0:T(8,128)S(1)} %get-tuple-element.79), channel_id=1, source_target_pairs={{0,2},{2,0},{4,6},{6,4},{1,3},{3,1},{5,7},{7,5},{8,10},{10,8},{12,... | collective-permute-start | bytes 491528 | tf_op jit(solution)/shard_map/ppermute | solution.py:764
  24.5 1.5 %collective-permute-start.13 = (f32[20,16,128]{2,1,0:T(8,128)S(1)}, f32[20,16,128]{2,1,0:T(8,128)S(1)}, u32[]{:S(2)}, u32[]{:S(2)}) collective-permute-start(f32[20,16,128]{2,1,0:T(8,128)S(1)} %get-tuple-element.80), channel_id=1, source_target_pairs={{0,6},{2,4},{4,2},{6,0},{1,7},{3,5},{5,3},{7,1},{8,14},{10,12},{12... | collective-permute-start | bytes 491528 | tf_op jit(solution)/shard_map/ppermute | solution.py:764
  25.9 0.1 shard_map.64.source_ref
  26.0 0.2 shard_map.65
  26.2 0.1 collective-permute-start.10
  26.3 0.9 %collective-permute-start.11 = (f32[25,16,128]{2,1,0:T(8,128)S(1)}, f32[25,16,128]{2,1,0:T(8,128)S(1)}, u32[]{:S(2)}, u32[]{:S(2)}) collective-permute-start(f32[25,16,128]{2,1,0:T(8,128)S(1)} %get-tuple-element.77), channel_id=1, source_target_pairs={{0,24},{8,16},{16,8},{24,0},{1,25},{9,17},{17,9},{25,1},{2,26},{10... | collective-permute-start | bytes 614408 | tf_op jit(solution)/shard_map/ppermute | solution.py:764
  27.2 0.3 shard_map.66.source_ref.order_ref
  27.5 3.2 %collective-permute-done.12.eta_a = f32[20,16,128]{2,1,0:T(8,128)S(1)} collective-permute-done((f32[20,16,128]{2,1,0:T(8,128)S(1)}, f32[20,16,128]{2,1,0:T(8,128)S(1)}, u32[]{:S(2)}, u32[]{:S(2)}) %collective-permute-start.12) | collective-permute-done | bytes 163872 | tf_op jit(solution)/shard_map/ppermute | solution.py:764
  30.7 2.0 %collective-permute-done.13.eta_b = f32[20,16,128]{2,1,0:T(8,128)S(1)} collective-permute-done((f32[20,16,128]{2,1,0:T(8,128)S(1)}, f32[20,16,128]{2,1,0:T(8,128)S(1)}, u32[]{:S(2)}, u32[]{:S(2)}) %collective-permute-start.13) | collective-permute-done | bytes 163872 | tf_op jit(solution)/shard_map/ppermute | solution.py:764
  32.7 0.1 shard_map.70
  32.8 0.1 collective-permute-start.14
  32.9 0.9 %collective-permute-start.15 = (f32[240,128]{1,0:T(8,128)S(1)}, f32[240,128]{1,0:T(8,128)S(1)}, u32[]{:S(2)}, u32[]{:S(2)}) collective-permute-start(f32[240,128]{1,0:T(8,128)S(1)} %get-tuple-element.85), channel_id=1, source_target_pairs={{0,8},{8,0},{16,24},{24,16},{1,9},{9,1},{17,25},{25,17},{2,10},{10... | collective-permute-start | bytes 368648 | tf_op jit(solution)/shard_map/ppermute | solution.py:764
  33.8 0.4 %shard_map.67 = (f32[4,256,128]{2,1,0:T(8,128)S(1)}, f32[128,128]{1,0:T(8,128)S(1)}, f32[5,8,128]{2,1,0:T(8,128)S(1)}, f32[5,8,128]{2,1,0:T(8,128)S(1)}) custom-call(f32[4,256,128]{2,1,0:T(8,128)S(1)} %shard_map.66.source_ref.order_ref, f32[1,256,128]{2,1,0:T(8,128)S(1)} %get-tuple-element.78.mass_ref, f32[20,16,128]{2,1,0:T(8,128)S(1)} %collective-permute-done.12.eta_a, ...), custom_call_target="tpu_custom_call" | custom-call | bytes 3600000 | tf_op jit(solution)/shard_map/pallas_call | solution.py:805
  34.3 1.6 %collective-permute-start.17 = (f32[128,128]{1,0:T(8,128)S(1)}, f32[128,128]{1,0:T(8,128)S(1)}, u32[]{:S(2)}, u32[]{:S(2)}) collective-permute-start(f32[128,128]{1,0:T(8,128)S(1)} %get-tuple-element.87), channel_id=1, source_target_pairs={{0,1},{1,0},{2,3},{3,2},{4,5},{5,4},{6,7},{7,6},{8,9},{9,8},{10,11... | collective-permute-start | bytes 196616 | tf_op jit(solution)/shard_map/ppermute | solution.py:785
  35.9 0.4 %collective-permute-start.16 = (f32[5,8,128]{2,1,0:T(8,128)S(1)}, f32[5,8,128]{2,1,0:T(8,128)S(1)}, u32[]{:S(2)}, u32[]{:S(2)}) collective-permute-start(f32[5,8,128]{2,1,0:T(8,128)S(1)} %get-tuple-element.86), channel_id=1, source_target_pairs={{0,25},{1,24},{8,17},{9,16},{16,9},{17,8},{24,1},{25,0},{2,27},{3,... | collective-permute-start | bytes 61448 | tf_op jit(solution)/shard_map/ppermute | solution.py:776
  36.3 1.9 %collective-permute-start.18 = (f32[5,8,128]{2,1,0:T(8,128)S(1)}, f32[5,8,128]{2,1,0:T(8,128)S(1)}, u32[]{:S(2)}, u32[]{:S(2)}) collective-permute-start(f32[5,8,128]{2,1,0:T(8,128)S(1)} %get-tuple-element.88), channel_id=1, source_target_pairs={{0,9},{1,8},{8,1},{9,0},{16,25},{17,24},{24,17},{25,16},{2,11},{3,... | collective-permute-start | bytes 61448 | tf_op jit(solution)/shard_map/ppermute | solution.py:776
  38.2 0.2 shard_map.68.source_ref
  38.5 0.2 shard_map.69
  38.7 0.6 %shard_map.71.order_ref.state_ref = f32[4,256,128]{2,1,0:T(8,128)S(1)} custom-call(f32[4,256,128]{2,1,0:T(8,128)S(1)} %shard_map.68.source_ref, f32[384,128]{1,0:T(8,128)S(1)} %get-tuple-element.82.first_source, f32[384,128]{1,0:T(8,128)S(1)} %get-tuple-element.83.second_source, f32[240,128]{1,0:T(8,128)S(1)} %collective-permute-done.14.edge_b, ...), custom_call_target="tpu_custom_call" | custom-call | bytes 3600000 | tf_op jit(solution)/shard_map/pallas_call | solution.py:805
  39.3 0.2 shard_map.72.mass_ref
  39.6 0.6 %collective-permute-done.16 = f32[5,8,128]{2,1,0:T(8,128)S(1)} collective-permute-done((f32[5,8,128]{2,1,0:T(8,128)S(1)}, f32[5,8,128]{2,1,0:T(8,128)S(1)}, u32[]{:S(2)}, u32[]{:S(2)}) %collective-permute-start.16) | collective-permute-done | bytes 20512 | tf_op jit(solution)/shard_map/ppermute | solution.py:776
  40.1 1.2 %shard_map.73 = f32[5,256,128]{2,1,0:T(8,128)} custom-call(f32[1,256,128]{2,1,0:T(8,128)S(1)} %shard_map.72.mass_ref, f32[4,256,128]{2,1,0:T(8,128)S(1)} %shard_map.71.order_ref.state_ref, f32[40,128]{1,0:T(8,128)S(1)} %bitcast.12, f32[40,128]{1,0:T(8,128)S(1)} %bitcast.13, f32[128,128]{1,0:T(8,128)S(1)} %collective-permute-done.17.below_ref.above_ref, ...), custom_call_target="tpu_custom_call" | custom-call | bytes 3600000 | tf_op jit(solution)/shard_map/pallas_call | solution.py:805
  (9 shorter events, 0.0 us)
Async XLA Ops:
  2.2 10.3 %collective-permute-start = (f32[10,16,128]{2,1,0:T(8,128)S(1)}, f32[10,16,128]{2,1,0:T(8,128)S(1)}, u32[]{:S(2)}, u32[]{:S(2)}) collective-permute-start(f32[10,16,128]{2,1,0:T(8,128)S(1)} %get-tuple-element.57), channel_id=1, source_target_pairs={{0,2},{2,0},{4,6},{6,4},{1,3},{3,1},{5,7},{7,5},{8,10},{10,8},{12,... | collective-permute-start | bytes 245768 | tf_op jit(solution)/shard_map/ppermute | solution.py:764
  5.3 7.2 %collective-permute-start.1 = (f32[10,16,128]{2,1,0:T(8,128)S(1)}, f32[10,16,128]{2,1,0:T(8,128)S(1)}, u32[]{:S(2)}, u32[]{:S(2)}) collective-permute-start(f32[10,16,128]{2,1,0:T(8,128)S(1)} %get-tuple-element.58), channel_id=1, source_target_pairs={{0,6},{2,4},{4,2},{6,0},{1,7},{3,5},{5,3},{7,1},{8,14},{10,12},{12... | collective-permute-start | bytes 245768 | tf_op jit(solution)/shard_map/ppermute | solution.py:764
  7.8 4.7 %collective-permute-start.2 = (f32[10,16,128]{2,1,0:T(8,128)S(1)}, f32[10,16,128]{2,1,0:T(8,128)S(1)}, u32[]{:S(2)}, u32[]{:S(2)}) collective-permute-start(f32[10,16,128]{2,1,0:T(8,128)S(1)} %get-tuple-element.59), channel_id=1, source_target_pairs={{0,24},{8,16},{16,8},{24,0},{1,25},{9,17},{17,9},{25,1},{2,26},{10... | collective-permute-start | bytes 245768 | tf_op jit(solution)/shard_map/ppermute | solution.py:764
  8.1 4.4 %collective-permute-start.3 = (f32[10,16,128]{2,1,0:T(8,128)S(1)}, f32[10,16,128]{2,1,0:T(8,128)S(1)}, u32[]{:S(2)}, u32[]{:S(2)}) collective-permute-start(f32[10,16,128]{2,1,0:T(8,128)S(1)} %get-tuple-element.60), channel_id=1, source_target_pairs={{0,8},{8,0},{16,24},{24,16},{1,9},{9,1},{17,25},{25,17},{2,10},{10... | collective-permute-start | bytes 245768 | tf_op jit(solution)/shard_map/ppermute | solution.py:764
  9.4 3.8 %collective-permute-start.4 = (f32[5,8,128]{2,1,0:T(8,128)S(1)}, f32[5,8,128]{2,1,0:T(8,128)S(1)}, u32[]{:S(2)}, u32[]{:S(2)}) collective-permute-start(f32[5,8,128]{2,1,0:T(8,128)S(1)} %get-tuple-element.48.refs_2_), channel_id=1, source_target_pairs={{0,1},{1,0},{2,3},{3,2},{4,5},{5,4},{6,7},{7,6},{8,9},{9,8},{10,11... | collective-permute-start | bytes 61448 | tf_op jit(solution)/shard_map/ppermute | solution.py:785
  14.6 7.2 %collective-permute-start.5 = (f32[13,16,128]{2,1,0:T(8,128)S(1)}, f32[13,16,128]{2,1,0:T(8,128)S(1)}, u32[]{:S(2)}, u32[]{:S(2)}) collective-permute-start(f32[13,16,128]{2,1,0:T(8,128)S(1)} %get-tuple-element.67), channel_id=1, source_target_pairs={{0,2},{2,0},{4,6},{6,4},{1,3},{3,1},{5,7},{7,5},{8,10},{10,8},{12,... | collective-permute-start | bytes 319496 | tf_op jit(solution)/shard_map/ppermute | solution.py:764
  15.3 6.7 %collective-permute-start.6 = (f32[13,16,128]{2,1,0:T(8,128)S(1)}, f32[13,16,128]{2,1,0:T(8,128)S(1)}, u32[]{:S(2)}, u32[]{:S(2)}) collective-permute-start(f32[13,16,128]{2,1,0:T(8,128)S(1)} %get-tuple-element.68), channel_id=1, source_target_pairs={{0,6},{2,4},{4,2},{6,0},{1,7},{3,5},{5,3},{7,1},{8,14},{10,12},{12... | collective-permute-start | bytes 319496 | tf_op jit(solution)/shard_map/ppermute | solution.py:764
  17.3 4.4 %collective-permute-start.7 = (f32[8,16,128]{2,1,0:T(8,128)S(1)}, f32[8,16,128]{2,1,0:T(8,128)S(1)}, u32[]{:S(2)}, u32[]{:S(2)}) collective-permute-start(f32[8,16,128]{2,1,0:T(8,128)S(1)} %get-tuple-element.70), channel_id=1, source_target_pairs={{0,24},{8,16},{16,8},{24,0},{1,25},{9,17},{17,9},{25,1},{2,26},{10... | collective-permute-start | bytes 196616 | tf_op jit(solution)/shard_map/ppermute | solution.py:764
  17.4 4.3 %collective-permute-start.8 = (f32[8,16,128]{2,1,0:T(8,128)S(1)}, f32[8,16,128]{2,1,0:T(8,128)S(1)}, u32[]{:S(2)}, u32[]{:S(2)}) collective-permute-start(f32[8,16,128]{2,1,0:T(8,128)S(1)} %get-tuple-element.71), channel_id=1, source_target_pairs={{0,8},{8,0},{16,24},{24,16},{1,9},{9,1},{17,25},{25,17},{2,10},{10... | collective-permute-start | bytes 196616 | tf_op jit(solution)/shard_map/ppermute | solution.py:764
  19.0 3.7 %collective-permute-start.9 = (f32[4,8,128]{2,1,0:T(8,128)S(1)}, f32[4,8,128]{2,1,0:T(8,128)S(1)}, u32[]{:S(2)}, u32[]{:S(2)}) collective-permute-start(f32[4,8,128]{2,1,0:T(8,128)S(1)} %get-tuple-element.72), channel_id=1, source_target_pairs={{0,1},{1,0},{2,3},{3,2},{4,5},{5,4},{6,7},{7,6},{8,9},{9,8},{10,11... | collective-permute-start | bytes 49160 | tf_op jit(solution)/shard_map/ppermute | solution.py:785
  23.2 7.5 %collective-permute-start.12 = (f32[20,16,128]{2,1,0:T(8,128)S(1)}, f32[20,16,128]{2,1,0:T(8,128)S(1)}, u32[]{:S(2)}, u32[]{:S(2)}) collective-permute-start(f32[20,16,128]{2,1,0:T(8,128)S(1)} %get-tuple-element.79), channel_id=1, source_target_pairs={{0,2},{2,0},{4,6},{6,4},{1,3},{3,1},{5,7},{7,5},{8,10},{10,8},{12,... | collective-permute-start | bytes 491528 | tf_op jit(solution)/shard_map/ppermute | solution.py:764
  24.5 8.3 %collective-permute-start.13 = (f32[20,16,128]{2,1,0:T(8,128)S(1)}, f32[20,16,128]{2,1,0:T(8,128)S(1)}, u32[]{:S(2)}, u32[]{:S(2)}) collective-permute-start(f32[20,16,128]{2,1,0:T(8,128)S(1)} %get-tuple-element.80), channel_id=1, source_target_pairs={{0,6},{2,4},{4,2},{6,0},{1,7},{3,5},{5,3},{7,1},{8,14},{10,12},{12... | collective-permute-start | bytes 491528 | tf_op jit(solution)/shard_map/ppermute | solution.py:764
  26.2 9.7 %collective-permute-start.10 = (f32[25,16,128]{2,1,0:T(8,128)S(1)}, f32[25,16,128]{2,1,0:T(8,128)S(1)}, u32[]{:S(2)}, u32[]{:S(2)}) collective-permute-start(f32[25,16,128]{2,1,0:T(8,128)S(1)} %get-tuple-element.76), channel_id=1, source_target_pairs={{0,8},{8,0},{16,24},{24,16},{1,9},{9,1},{17,25},{25,17},{2,10},{10... | collective-permute-start | bytes 614408 | tf_op jit(solution)/shard_map/ppermute | solution.py:764
  26.3 10.0 %collective-permute-start.11 = (f32[25,16,128]{2,1,0:T(8,128)S(1)}, f32[25,16,128]{2,1,0:T(8,128)S(1)}, u32[]{:S(2)}, u32[]{:S(2)}) collective-permute-start(f32[25,16,128]{2,1,0:T(8,128)S(1)} %get-tuple-element.77), channel_id=1, source_target_pairs={{0,24},{8,16},{16,8},{24,0},{1,25},{9,17},{17,9},{25,1},{2,26},{10... | collective-permute-start | bytes 614408 | tf_op jit(solution)/shard_map/ppermute | solution.py:764
  32.8 5.9 %collective-permute-start.14 = (f32[240,128]{1,0:T(8,128)S(1)}, f32[240,128]{1,0:T(8,128)S(1)}, u32[]{:S(2)}, u32[]{:S(2)}) collective-permute-start(f32[240,128]{1,0:T(8,128)S(1)} %get-tuple-element.84), channel_id=1, source_target_pairs={{0,24},{8,16},{16,8},{24,0},{1,25},{9,17},{17,9},{25,1},{2,26},{10... | collective-permute-start | bytes 368648 | tf_op jit(solution)/shard_map/ppermute | solution.py:764
  32.9 5.8 %collective-permute-start.15 = (f32[240,128]{1,0:T(8,128)S(1)}, f32[240,128]{1,0:T(8,128)S(1)}, u32[]{:S(2)}, u32[]{:S(2)}) collective-permute-start(f32[240,128]{1,0:T(8,128)S(1)} %get-tuple-element.85), channel_id=1, source_target_pairs={{0,8},{8,0},{16,24},{24,16},{1,9},{9,1},{17,25},{25,17},{2,10},{10... | collective-permute-start | bytes 368648 | tf_op jit(solution)/shard_map/ppermute | solution.py:764
  34.3 5.9 %collective-permute-start.17 = (f32[128,128]{1,0:T(8,128)S(1)}, f32[128,128]{1,0:T(8,128)S(1)}, u32[]{:S(2)}, u32[]{:S(2)}) collective-permute-start(f32[128,128]{1,0:T(8,128)S(1)} %get-tuple-element.87), channel_id=1, source_target_pairs={{0,1},{1,0},{2,3},{3,2},{4,5},{5,4},{6,7},{7,6},{8,9},{9,8},{10,11... | collective-permute-start | bytes 196616 | tf_op jit(solution)/shard_map/ppermute | solution.py:785
  35.9 4.3 %collective-permute-start.16 = (f32[5,8,128]{2,1,0:T(8,128)S(1)}, f32[5,8,128]{2,1,0:T(8,128)S(1)}, u32[]{:S(2)}, u32[]{:S(2)}) collective-permute-start(f32[5,8,128]{2,1,0:T(8,128)S(1)} %get-tuple-element.86), channel_id=1, source_target_pairs={{0,25},{1,24},{8,17},{9,16},{16,9},{17,8},{24,1},{25,0},{2,27},{3,... | collective-permute-start | bytes 61448 | tf_op jit(solution)/shard_map/ppermute | solution.py:776
  36.3 3.8 %collective-permute-start.18 = (f32[5,8,128]{2,1,0:T(8,128)S(1)}, f32[5,8,128]{2,1,0:T(8,128)S(1)}, u32[]{:S(2)}, u32[]{:S(2)}) collective-permute-start(f32[5,8,128]{2,1,0:T(8,128)S(1)} %get-tuple-element.88), channel_id=1, source_target_pairs={{0,9},{1,8},{8,1},{9,0},{16,25},{17,24},{24,17},{25,16},{2,11},{3,... | collective-permute-start | bytes 61448 | tf_op jit(solution)/shard_map/ppermute | solution.py:776

commit v10 on v8

--- a/solution.py
+++ b/solution.py
@@ -359,20 +359,7 @@
     zeta_ref[4] = pack_sums(mass_ref[2], sums, grid)
 
 
-def fetch_kernel(count, *refs):
-    sources, results, sems = refs[:count], refs[count + 1 : 2 * count + 1], refs[-1]
-    copies = [
-        pltpu.make_async_copy(source, result, sems.at[index])
-        for index, (source, result) in enumerate(zip(sources, results))
-    ]
-    for copy in copies:
-        copy.start()
-    for copy in copies:
-        copy.wait()
-
-
-def derive_sources(grid, xi_value, eta_value, zeta_value, derive, field, xi_ref, eta_ref, zeta_ref):
-    zeta_ref[field] = lane_product(zeta_value[...], derive)
+def derive_sources(grid, xi_value, eta_value, field, xi_ref, eta_ref):
     for group in range(grid.eta_groups):
         cells = [xi_value[grid.xi_tile(i, group), :] for i in range(grid.nx)]
         for i, value in enumerate(derive_source(cells)):
@@ -383,17 +370,32 @@
             eta_ref[field, grid.eta_major(i, group), :] = value
 
 
-def primitive_source_kernel(grid, prim_ref, mass_ref, tables_ref, *results):
+def primitive_source_kernel(
+    grid, prim_ref, mass_ref, tables_hbm, jacobian_hbm,
+    xi_ref, eta_ref, zeta_ref, tables_ref, jacobian_ref, sems,
+):
+    copies = [
+        pltpu.make_async_copy(tables_hbm, tables_ref, sems.at[0]),
+        pltpu.make_async_copy(jacobian_hbm, jacobian_ref, sems.at[1]),
+    ]
+    for copy in copies:
+        copy.start()
+    for field in range(4):
+        derive_sources(grid, prim_ref.at[field], prim_ref.at[field], field, xi_ref, eta_ref)
+    derive_sources(grid, mass_ref.at[0], mass_ref.at[1], 4, xi_ref, eta_ref)
+    copies[0].wait()
     derive = split_weights(tables_ref[DERIVE])
-    for field in range(4):
-        derive_sources(grid, *[prim_ref.at[field]] * 3, derive, field, *results)
-    derive_sources(grid, *[mass_ref.at[k] for k in range(3)], derive, 4, *results)
-
-
-def contra_source_kernel(grid, contra_ref, tables_ref, *results):
+    for field in range(5):
+        values = prim_ref[field] if field < 4 else mass_ref[2]
+        zeta_ref[field] = lane_product(values, derive)
+    copies[1].wait()
+
+
+def contra_source_kernel(grid, contra_ref, tables_ref, xi_ref, eta_ref, zeta_ref):
     derive = split_weights(tables_ref[DERIVE])
     for field in range(4):
-        derive_sources(grid, *[contra_ref.at[k, field] for k in range(3)], derive, field, *results)
+        zeta_ref[field] = lane_product(contra_ref[2, field], derive)
+        derive_sources(grid, contra_ref.at[0, field], contra_ref.at[1, field], field, xi_ref, eta_ref)
 
 
 def xi_derivative(grid, source_ref, xi_a, xi_b, field, group):
@@ -502,14 +504,18 @@
         )
 
 
-def contra_sums_kernel(grid, contra_ref, sums_ref, xi_first, xi_second, zeta_ref):
+def zeta_sums_kernel(grid, contra_ref, sums_ref, zeta_ref):
     sums = split_weights(sums_ref[...])
+    for field in range(4):
+        zeta_ref[field] = pack_sums(contra_ref[2, field], sums, grid)
+
+
+def xi_sums_kernel(grid, contra_ref, order_ref, xi_first, xi_second):
     for field in range(4):
         send_sums(
             lambda position, group: contra_ref[0, field, grid.xi_tile(position, group), :],
             grid.eta_groups, grid.nx, odd("xi"), xi_first, xi_second, field,
         )
-        zeta_ref[field] = pack_sums(contra_ref[2, field], sums, grid)
 
 
 def xi_divergence_kernel(grid, source_ref, own_ref, xi_b, xi_a, total_ref):
@@ -857,16 +863,13 @@
         scratch=[pltpu.SemaphoreType.DMA((chunks,)), pltpu.SemaphoreType.DMA((10,))],
         far=(0, 1, 2),
     )
-    tables, jacobian = call(
-        functools.partial(fetch_kernel, 2),
-        [like(tables), like(jacobian)],
-        tables, jacobian, sends[-1],
+    eta_sides, xi_sides, ends = exchange(*sends)
+    xi_source, eta_source, own, tables, jacobian = call(
+        functools.partial(primitive_source_kernel, grid),
+        [(5, *block)] * 3 + [like(tables), like(jacobian)],
+        prim, mass, tables, jacobian,
         scratch=[pltpu.SemaphoreType.DMA((2,))],
-        far=(0, 1),
-    )
-    eta_sides, xi_sides, ends = exchange(*sends)
-    xi_source, eta_source, own = call(
-        functools.partial(primitive_source_kernel, grid), [(5, *block)] * 3, prim, mass, tables,
+        far=(2, 3),
     )
     eta_slope, mass_total = call(
         functools.partial(eta_slope_kernel, grid), [(4, *block), block], eta_source, own, *eta_sides,
@@ -886,12 +889,13 @@
         [(3, 4, *block), block] + [(2 * 4 + WIDTH, nx, nz)] * 2,
         u, prim, metrics, jacobian, xi_slope, eta_slope, zeta_slope, mass_total,
     )
+    (zeta,) = call(
+        functools.partial(zeta_sums_kernel, grid), [(4, TILE, LANES)], contra, sums, cost=0.3,
+    )
     sends = call(
-        functools.partial(contra_sums_kernel, grid),
-        [(2 * 4, ny, nz)] * 2 + [(4, TILE, LANES)],
-        contra, sums,
-    )
-    eta_sides, xi_sides, ends = exchange(*eta_sends, *sends)
+        functools.partial(xi_sums_kernel, grid), [(2 * 4, ny, nz)] * 2, contra, zeta, cost=0.2,
+    )
+    eta_sides, xi_sides, ends = exchange(*eta_sends, *sends, zeta)
     xi_source, eta_source, own = call(
         functools.partial(contra_source_kernel, grid), [(4, *block)] * 3, contra, tables,
     )

time: 41.5 us -> 41.6 us (level)
  transfers between devices with their start and end apart: 19 -> 19, of which waited for: 5 -> 5; matrix products, arithmetic and copies ran while one was open for 0% -> 0% of each run, Pallas kernels for 14% -> 13%
where the time goes in v10:
time: 41.6 us; the launch traced here: 41.4 us
  starting transfers between devices  22.6 us (54%)
  Pallas kernels  10.8 us (26%)
  waiting for transfers between devices  7.76 us (19%)
    ppermute x14, starting transfers between devices, pair_swap(): return lax.ppermute(value, axis, pairs)  15.8 us
    pallas_call x22, Pallas kernels, call(): pl.pallas_call(kernel, out_shape=shapes, in_specs=[pl.BlockSpec(memory_sp...  10.8 us
    ppermute x14, waiting for transfers between devices, pair_swap(): return lax.ppermute(value, axis, pairs)  5.81 us
    ppermute x3, starting transfers between devices, ring_swap(): other = lax.ppermute(value, axis, [(0, 1), (1, 0)])  4.62 us
    ppermute x2, starting transfers between devices, send(): return lax.ppermute(value, ('xi', 'zeta'), pairs)  2.21 us
    ppermute x3, waiting for transfers between devices, ring_swap(): other = lax.ppermute(value, axis, [(0, 1), (1, 0)])  1.26 us
  transfers between devices with their start and end apart: 19, of which 5 were waited for; matrix products, arithmetic and copies ran while one was open for 0% of the time, Pallas kernels for 13%

profile of v10, /device:TPU:0, one launch (start us, length us, event | category | flops | bytes accessed | tf_op | source)
XLA Modules:
  0.0 41.4 jit_solution(13530561518272905604)
XLA Ops:
  0.0 2.2 %shard_map.55 = (f32[5,256,128]{2,1,0:T(8,128)S(1)}, f32[128,128]{1,0:T(8,128)S(1)}, f32[9,256,128]{2,1,0:T(8,128)S(1)}, f32[4,256,128]{2,1,0:T(8,128)S(1)}, f32...) custom-call(f32[5,256,128]{2,1,0:T(8,128)} %bitcast.17, ...), custom_call_target="tpu_custom_call" | custom-call | bytes 3600000 | tf_op jit(solution)/shard_map/pallas_call | solution.py:818
  2.2 3.1 %collective-permute-start = (f32[10,16,128]{2,1,0:T(8,128)S(1)}, f32[10,16,128]{2,1,0:T(8,128)S(1)}, u32[]{:S(2)}, u32[]{:S(2)}) collective-permute-start(f32[10,16,128]{2,1,0:T(8,128)S(1)} %get-tuple-element.58), channel_id=1, source_target_pairs={{0,2},{2,0},{4,6},{6,4},{1,3},{3,1},{5,7},{7,5},{8,10},{10,8},{12,... | collective-permute-start | bytes 245768 | tf_op jit(solution)/shard_map/ppermute | solution.py:777
  5.3 2.5 %collective-permute-start.1 = (f32[10,16,128]{2,1,0:T(8,128)S(1)}, f32[10,16,128]{2,1,0:T(8,128)S(1)}, u32[]{:S(2)}, u32[]{:S(2)}) collective-permute-start(f32[10,16,128]{2,1,0:T(8,128)S(1)} %get-tuple-element.59), channel_id=1, source_target_pairs={{0,6},{2,4},{4,2},{6,0},{1,7},{3,5},{5,3},{7,1},{8,14},{10,12},{12... | collective-permute-start | bytes 245768 | tf_op jit(solution)/shard_map/ppermute | solution.py:777
  7.8 0.4 collective-permute-start.2
  8.1 1.2 %collective-permute-start.3 = (f32[10,16,128]{2,1,0:T(8,128)S(1)}, f32[10,16,128]{2,1,0:T(8,128)S(1)}, u32[]{:S(2)}, u32[]{:S(2)}) collective-permute-start(f32[10,16,128]{2,1,0:T(8,128)S(1)} %get-tuple-element.62), channel_id=1, source_target_pairs={{0,8},{8,0},{16,24},{24,16},{1,9},{9,1},{17,25},{25,17},{2,10},{10... | collective-permute-start | bytes 245768 | tf_op jit(solution)/shard_map/ppermute | solution.py:777
  9.4 1.5 %collective-permute-start.4 = (f32[5,8,128]{2,1,0:T(8,128)S(1)}, f32[5,8,128]{2,1,0:T(8,128)S(1)}, u32[]{:S(2)}, u32[]{:S(2)}) collective-permute-start(f32[5,8,128]{2,1,0:T(8,128)S(1)} %get-tuple-element.66), channel_id=1, source_target_pairs={{0,1},{1,0},{2,3},{3,2},{4,5},{5,4},{6,7},{7,6},{8,9},{9,8},{10,11... | collective-permute-start | bytes 61448 | tf_op jit(solution)/shard_map/ppermute | solution.py:798
  10.9 1.3 %shard_map.56 = (f32[5,256,128]{2,1,0:T(8,128)S(1)}, f32[5,256,128]{2,1,0:T(8,128)S(1)}, f32[5,256,128]{2,1,0:T(8,128)S(1)}, f32[4,128,128]{2,1,0:T(8,128)S(1)}, f32[256,128]{1,0:T(8,128)S(1)}) custom-call(f32[4,256,128]{2,1,0:T(8,128)S(1)} %get-tuple-element.51.prim_ref, f32[3,256,128]{2,1,0:T(8,128)S(1)} %get-tuple-element.52.mass_ref, ...), custom_call_target="tpu_custom_call" | custom-call | bytes 3600000 | tf_op jit(solution)/shard_map/pallas_call | solution.py:818
  12.2 0.0 collective-permute-done.eta_a
  12.2 0.0 collective-permute-done.1.eta_b
  12.2 0.3 shard_map.57
  12.6 0.2 shard_map.58
  12.7 0.4 collective-permute-done.4.below_ref.above_ref
  13.1 0.4 shard_map.59
  13.5 1.0 %shard_map.60 = (f32[3,4,256,128]{3,2,1,0:T(8,128)S(1)}, f32[256,128]{1,0:T(8,128)S(1)}, f32[13,16,128]{2,1,0:T(8,128)S(1)}, f32[13,16,128]{2,1,0:T(8,128)S(1)}) custom-call(f32[5,256,128]{2,1,0:T(8,128)S(1)} %get-tuple-element.50.u_ref, f32[4,256,128]{2,1,0:T(8,128)S(1)} %get-tuple-element.51.prim_ref, f32[9,256,128]{2,1,0:T(8,128)S(1)} %get-tuple-element.54.metrics_ref, ...), custom_call_target="tpu_custom_call" | custom-call | bytes 3600000 | tf_op jit(solution)/shard_map/pallas_call | solution.py:818
  14.6 0.7 %collective-permute-start.8 = (f32[13,16,128]{2,1,0:T(8,128)S(1)}, f32[13,16,128]{2,1,0:T(8,128)S(1)}, u32[]{:S(2)}, u32[]{:S(2)}) collective-permute-start(f32[13,16,128]{2,1,0:T(8,128)S(1)} %get-tuple-element.77), channel_id=1, source_target_pairs={{0,2},{2,0},{4,6},{6,4},{1,3},{3,1},{5,7},{7,5},{8,10},{10,8},{12,... | collective-permute-start | bytes 319496 | tf_op jit(solution)/shard_map/ppermute | solution.py:777
  15.3 1.7 %collective-permute-start.9 = (f32[13,16,128]{2,1,0:T(8,128)S(1)}, f32[13,16,128]{2,1,0:T(8,128)S(1)}, u32[]{:S(2)}, u32[]{:S(2)}) collective-permute-start(f32[13,16,128]{2,1,0:T(8,128)S(1)} %get-tuple-element.78), channel_id=1, source_target_pairs={{0,6},{2,4},{4,2},{6,0},{1,7},{3,5},{5,3},{7,1},{8,14},{10,12},{12... | collective-permute-start | bytes 319496 | tf_op jit(solution)/shard_map/ppermute | solution.py:777
  17.0 0.4 shard_map.62.order_ref
  17.4 0.1 collective-permute-start.5
  17.5 1.6 %collective-permute-start.6 = (f32[8,16,128]{2,1,0:T(8,128)S(1)}, f32[8,16,128]{2,1,0:T(8,128)S(1)}, u32[]{:S(2)}, u32[]{:S(2)}) collective-permute-start(f32[8,16,128]{2,1,0:T(8,128)S(1)} %get-tuple-element.76), channel_id=1, source_target_pairs={{0,8},{8,0},{16,24},{24,16},{1,9},{9,1},{17,25},{25,17},{2,10},{10... | collective-permute-start | bytes 196616 | tf_op jit(solution)/shard_map/ppermute | solution.py:777
  19.1 1.5 %collective-permute-start.7 = (f32[4,8,128]{2,1,0:T(8,128)S(1)}, f32[4,8,128]{2,1,0:T(8,128)S(1)}, u32[]{:S(2)}, u32[]{:S(2)}) collective-permute-start(f32[4,8,128]{2,1,0:T(8,128)S(1)} %shard_map.62.order_ref), channel_id=1, source_target_pairs={{0,1},{1,0},{2,3},{3,2},{4,5},{5,4},{6,7},{7,6},{8,9},{9,8},{10,11... | collective-permute-start | bytes 49160 | tf_op jit(solution)/shard_map/ppermute | solution.py:798
  20.6 0.5 %shard_map.61 = (f32[4,256,128]{2,1,0:T(8,128)S(1)}, f32[4,256,128]{2,1,0:T(8,128)S(1)}, f32[4,256,128]{2,1,0:T(8,128)S(1)}) custom-call(f32[3,4,256,128]{3,2,1,0:T(8,128)S(1)} %get-tuple-element.70.contra_ref, f32[4,128,128]{2,1,0:T(8,128)S(1)} %get-tuple-element.67.tables_ref), custom_call_target="tpu_custom_call" | custom-call | bytes 3600000 | tf_op jit(solution)/shard_map/pallas_call | solution.py:818
  21.1 0.7 %collective-permute-done.5.xi_b = f32[8,16,128]{2,1,0:T(8,128)S(1)} collective-permute-done((f32[8,16,128]{2,1,0:T(8,128)S(1)}, f32[8,16,128]{2,1,0:T(8,128)S(1)}, u32[]{:S(2)}, u32[]{:S(2)}) %collective-permute-start.5) | collective-permute-done | bytes 65568 | tf_op jit(solution)/shard_map/ppermute | solution.py:777
  21.9 0.0 collective-permute-done.6.xi_a
  21.9 0.1 shard_map.64.part_ref
  22.0 0.9 %collective-permute-done.7.below_ref.above_ref = f32[4,8,128]{2,1,0:T(8,128)S(1)} collective-permute-done((f32[4,8,128]{2,1,0:T(8,128)S(1)}, f32[4,8,128]{2,1,0:T(8,128)S(1)}, u32[]{:S(2)}, u32[]{:S(2)}) %collective-permute-start.7) | collective-permute-done | bytes 16416 | tf_op jit(solution)/shard_map/ppermute | solution.py:798
  22.9 0.4 shard_map.65.total_ref
  23.2 0.4 %shard_map.66 = (f32[4,256,128]{2,1,0:T(8,128)S(1)}, f32[20,16,128]{2,1,0:T(8,128)S(1)}, f32[20,16,128]{2,1,0:T(8,128)S(1)}) custom-call(f32[5,256,128]{2,1,0:T(8,128)S(1)} %get-tuple-element.50.u_ref, f32[256,128]{1,0:T(8,128)S(1)} %get-tuple-element.53.jacobian_ref, f32[4,256,128]{2,1,0:T(8,128)S(1)} %get-tuple-element.71.source_ref, ...), custom_call_target="tpu_custom_call" | custom-call | bytes 3600000 | tf_op jit(solution)/shard_map/pallas_call | solution.py:818
  23.7 0.3 collective-permute-start.12
  24.0 1.7 %collective-permute-start.13 = (f32[20,16,128]{2,1,0:T(8,128)S(1)}, f32[20,16,128]{2,1,0:T(8,128)S(1)}, u32[]{:S(2)}, u32[]{:S(2)}) collective-permute-start(f32[20,16,128]{2,1,0:T(8,128)S(1)} %get-tuple-element.86), channel_id=1, source_target_pairs={{0,6},{2,4},{4,2},{6,0},{1,7},{3,5},{5,3},{7,1},{8,14},{10,12},{12... | collective-permute-start | bytes 491528 | tf_op jit(solution)/shard_map/ppermute | solution.py:777
  25.6 0.1 shard_map.67.source_ref
  25.7 0.2 shard_map.68
  25.9 0.1 collective-permute-start.10
  26.0 1.4 %collective-permute-start.11 = (f32[25,16,128]{2,1,0:T(8,128)S(1)}, f32[25,16,128]{2,1,0:T(8,128)S(1)}, u32[]{:S(2)}, u32[]{:S(2)}) collective-permute-start(f32[25,16,128]{2,1,0:T(8,128)S(1)} %get-tuple-element.83), channel_id=1, source_target_pairs={{0,24},{8,16},{16,8},{24,0},{1,25},{9,17},{17,9},{25,1},{2,26},{10... | collective-permute-start | bytes 614408 | tf_op jit(solution)/shard_map/ppermute | solution.py:777
  27.3 0.3 shard_map.70.source_ref.order_ref
  27.6 5.1 %collective-permute-done.12.eta_a = f32[20,16,128]{2,1,0:T(8,128)S(1)} collective-permute-done((f32[20,16,128]{2,1,0:T(8,128)S(1)}, f32[20,16,128]{2,1,0:T(8,128)S(1)}, u32[]{:S(2)}, u32[]{:S(2)}) %collective-permute-start.12) | collective-permute-done | bytes 163872 | tf_op jit(solution)/shard_map/ppermute | solution.py:777
  32.7 0.1 shard_map.74
  32.8 0.1 collective-permute-start.14
  32.8 1.1 %collective-permute-start.15 = (f32[240,128]{1,0:T(8,128)S(1)}, f32[240,128]{1,0:T(8,128)S(1)}, u32[]{:S(2)}, u32[]{:S(2)}) collective-permute-start(f32[240,128]{1,0:T(8,128)S(1)} %get-tuple-element.91), channel_id=1, source_target_pairs={{0,8},{8,0},{16,24},{24,16},{1,9},{9,1},{17,25},{25,17},{2,10},{10... | collective-permute-start | bytes 368648 | tf_op jit(solution)/shard_map/ppermute | solution.py:777
  33.9 0.4 %shard_map.71 = (f32[4,256,128]{2,1,0:T(8,128)S(1)}, f32[128,128]{1,0:T(8,128)S(1)}, f32[5,8,128]{2,1,0:T(8,128)S(1)}, f32[5,8,128]{2,1,0:T(8,128)S(1)}) custom-call(f32[4,256,128]{2,1,0:T(8,128)S(1)} %shard_map.70.source_ref.order_ref, f32[1,256,128]{2,1,0:T(8,128)S(1)} %get-tuple-element.84.mass_ref, f32[20,16,128]{2,1,0:T(8,128)S(1)} %collective-permute-done.12.eta_a, ...), custom_call_target="tpu_custom_call" | custom-call | bytes 3600000 | tf_op jit(solution)/shard_map/pallas_call | solution.py:818
  34.4 1.6 %collective-permute-start.17 = (f32[128,128]{1,0:T(8,128)S(1)}, f32[128,128]{1,0:T(8,128)S(1)}, u32[]{:S(2)}, u32[]{:S(2)}) collective-permute-start(f32[128,128]{1,0:T(8,128)S(1)} %get-tuple-element.93), channel_id=1, source_target_pairs={{0,1},{1,0},{2,3},{3,2},{4,5},{5,4},{6,7},{7,6},{8,9},{9,8},{10,11... | collective-permute-start | bytes 196616 | tf_op jit(solution)/shard_map/ppermute | solution.py:798
  36.0 0.3 collective-permute-start.16
  36.3 1.9 %collective-permute-start.18 = (f32[5,8,128]{2,1,0:T(8,128)S(1)}, f32[5,8,128]{2,1,0:T(8,128)S(1)}, u32[]{:S(2)}, u32[]{:S(2)}) collective-permute-start(f32[5,8,128]{2,1,0:T(8,128)S(1)} %get-tuple-element.94), channel_id=1, source_target_pairs={{0,9},{1,8},{8,1},{9,0},{16,25},{17,24},{24,17},{25,16},{2,11},{3,... | collective-permute-start | bytes 61448 | tf_op jit(solution)/shard_map/ppermute | solution.py:789
  38.2 0.2 shard_map.72.source_ref
  38.4 0.2 shard_map.73
  38.7 0.2 shard_map.69.mass_ref
  38.9 0.6 %shard_map.75.state_ref = f32[4,256,128]{2,1,0:T(8,128)S(1)} custom-call(f32[4,256,128]{2,1,0:T(8,128)S(1)} %shard_map.72.source_ref, f32[384,128]{1,0:T(8,128)S(1)} %get-tuple-element.88.first_source, f32[384,128]{1,0:T(8,128)S(1)} %get-tuple-element.89.second_source, f32[240,128]{1,0:T(8,128)S(1)} %collective-permute-done.14.edge_b, ...), custom_call_target="tpu_custom_call" | custom-call | bytes 3600000 | tf_op jit(solution)/shard_map/pallas_call | solution.py:818
  39.5 0.7 %collective-permute-done.16 = f32[5,8,128]{2,1,0:T(8,128)S(1)} collective-permute-done((f32[5,8,128]{2,1,0:T(8,128)S(1)}, f32[5,8,128]{2,1,0:T(8,128)S(1)}, u32[]{:S(2)}, u32[]{:S(2)}) %collective-permute-start.16) | collective-permute-done | bytes 20512 | tf_op jit(solution)/shard_map/ppermute | solution.py:789
  40.2 1.2 %shard_map.76 = f32[5,256,128]{2,1,0:T(8,128)} custom-call(f32[1,256,128]{2,1,0:T(8,128)S(1)} %shard_map.69.mass_ref, f32[4,256,128]{2,1,0:T(8,128)S(1)} %shard_map.75.state_ref, f32[40,128]{1,0:T(8,128)S(1)} %bitcast.12, f32[40,128]{1,0:T(8,128)S(1)} %bitcast.13, f32[128,128]{1,0:T(8,128)S(1)} %collective-permute-done.17.below_ref.above_ref, ...), custom_call_target="tpu_custom_call" | custom-call | bytes 3600000 | tf_op jit(solution)/shard_map/pallas_call | solution.py:818
  (12 shorter events, 0.1 us)
Async XLA Ops:
  2.2 10.0 %collective-permute-start = (f32[10,16,128]{2,1,0:T(8,128)S(1)}, f32[10,16,128]{2,1,0:T(8,128)S(1)}, u32[]{:S(2)}, u32[]{:S(2)}) collective-permute-start(f32[10,16,128]{2,1,0:T(8,128)S(1)} %get-tuple-element.58), channel_id=1, source_target_pairs={{0,2},{2,0},{4,6},{6,4},{1,3},{3,1},{5,7},{7,5},{8,10},{10,8},{12,... | collective-permute-start | bytes 245768 | tf_op jit(solution)/shard_map/ppermute | solution.py:777
  5.3 6.9 %collective-permute-start.1 = (f32[10,16,128]{2,1,0:T(8,128)S(1)}, f32[10,16,128]{2,1,0:T(8,128)S(1)}, u32[]{:S(2)}, u32[]{:S(2)}) collective-permute-start(f32[10,16,128]{2,1,0:T(8,128)S(1)} %get-tuple-element.59), channel_id=1, source_target_pairs={{0,6},{2,4},{4,2},{6,0},{1,7},{3,5},{5,3},{7,1},{8,14},{10,12},{12... | collective-permute-start | bytes 245768 | tf_op jit(solution)/shard_map/ppermute | solution.py:777
  7.8 4.8 %collective-permute-start.2 = (f32[10,16,128]{2,1,0:T(8,128)S(1)}, f32[10,16,128]{2,1,0:T(8,128)S(1)}, u32[]{:S(2)}, u32[]{:S(2)}) collective-permute-start(f32[10,16,128]{2,1,0:T(8,128)S(1)} %get-tuple-element.61), channel_id=1, source_target_pairs={{0,24},{8,16},{16,8},{24,0},{1,25},{9,17},{17,9},{25,1},{2,26},{10... | collective-permute-start | bytes 245768 | tf_op jit(solution)/shard_map/ppermute | solution.py:777
  8.1 4.5 %collective-permute-start.3 = (f32[10,16,128]{2,1,0:T(8,128)S(1)}, f32[10,16,128]{2,1,0:T(8,128)S(1)}, u32[]{:S(2)}, u32[]{:S(2)}) collective-permute-start(f32[10,16,128]{2,1,0:T(8,128)S(1)} %get-tuple-element.62), channel_id=1, source_target_pairs={{0,8},{8,0},{16,24},{24,16},{1,9},{9,1},{17,25},{25,17},{2,10},{10... | collective-permute-start | bytes 245768 | tf_op jit(solution)/shard_map/ppermute | solution.py:777
  9.4 3.8 %collective-permute-start.4 = (f32[5,8,128]{2,1,0:T(8,128)S(1)}, f32[5,8,128]{2,1,0:T(8,128)S(1)}, u32[]{:S(2)}, u32[]{:S(2)}) collective-permute-start(f32[5,8,128]{2,1,0:T(8,128)S(1)} %get-tuple-element.66), channel_id=1, source_target_pairs={{0,1},{1,0},{2,3},{3,2},{4,5},{5,4},{6,7},{7,6},{8,9},{9,8},{10,11... | collective-permute-start | bytes 61448 | tf_op jit(solution)/shard_map/ppermute | solution.py:798
  14.6 8.6 %collective-permute-start.8 = (f32[13,16,128]{2,1,0:T(8,128)S(1)}, f32[13,16,128]{2,1,0:T(8,128)S(1)}, u32[]{:S(2)}, u32[]{:S(2)}) collective-permute-start(f32[13,16,128]{2,1,0:T(8,128)S(1)} %get-tuple-element.77), channel_id=1, source_target_pairs={{0,2},{2,0},{4,6},{6,4},{1,3},{3,1},{5,7},{7,5},{8,10},{10,8},{12,... | collective-permute-start | bytes 319496 | tf_op jit(solution)/shard_map/ppermute | solution.py:777
  15.3 7.9 %collective-permute-start.9 = (f32[13,16,128]{2,1,0:T(8,128)S(1)}, f32[13,16,128]{2,1,0:T(8,128)S(1)}, u32[]{:S(2)}, u32[]{:S(2)}) collective-permute-start(f32[13,16,128]{2,1,0:T(8,128)S(1)} %get-tuple-element.78), channel_id=1, source_target_pairs={{0,6},{2,4},{4,2},{6,0},{1,7},{3,5},{5,3},{7,1},{8,14},{10,12},{12... | collective-permute-start | bytes 319496 | tf_op jit(solution)/shard_map/ppermute | solution.py:777
  17.4 4.4 %collective-permute-start.5 = (f32[8,16,128]{2,1,0:T(8,128)S(1)}, f32[8,16,128]{2,1,0:T(8,128)S(1)}, u32[]{:S(2)}, u32[]{:S(2)}) collective-permute-start(f32[8,16,128]{2,1,0:T(8,128)S(1)} %get-tuple-element.75), channel_id=1, source_target_pairs={{0,24},{8,16},{16,8},{24,0},{1,25},{9,17},{17,9},{25,1},{2,26},{10... | collective-permute-start | bytes 196616 | tf_op jit(solution)/shard_map/ppermute | solution.py:777
  17.5 4.3 %collective-permute-start.6 = (f32[8,16,128]{2,1,0:T(8,128)S(1)}, f32[8,16,128]{2,1,0:T(8,128)S(1)}, u32[]{:S(2)}, u32[]{:S(2)}) collective-permute-start(f32[8,16,128]{2,1,0:T(8,128)S(1)} %get-tuple-element.76), channel_id=1, source_target_pairs={{0,8},{8,0},{16,24},{24,16},{1,9},{9,1},{17,25},{25,17},{2,10},{10... | collective-permute-start | bytes 196616 | tf_op jit(solution)/shard_map/ppermute | solution.py:777
  19.1 3.7 %collective-permute-start.7 = (f32[4,8,128]{2,1,0:T(8,128)S(1)}, f32[4,8,128]{2,1,0:T(8,128)S(1)}, u32[]{:S(2)}, u32[]{:S(2)}) collective-permute-start(f32[4,8,128]{2,1,0:T(8,128)S(1)} %shard_map.62.order_ref), channel_id=1, source_target_pairs={{0,1},{1,0},{2,3},{3,2},{4,5},{5,4},{6,7},{7,6},{8,9},{9,8},{10,11... | collective-permute-start | bytes 49160 | tf_op jit(solution)/shard_map/ppermute | solution.py:798
  23.7 9.0 %collective-permute-start.12 = (f32[20,16,128]{2,1,0:T(8,128)S(1)}, f32[20,16,128]{2,1,0:T(8,128)S(1)}, u32[]{:S(2)}, u32[]{:S(2)}) collective-permute-start(f32[20,16,128]{2,1,0:T(8,128)S(1)} %get-tuple-element.85), channel_id=1, source_target_pairs={{0,2},{2,0},{4,6},{6,4},{1,3},{3,1},{5,7},{7,5},{8,10},{10,8},{12,... | collective-permute-start | bytes 491528 | tf_op jit(solution)/shard_map/ppermute | solution.py:777
  24.0 8.7 %collective-permute-start.13 = (f32[20,16,128]{2,1,0:T(8,128)S(1)}, f32[20,16,128]{2,1,0:T(8,128)S(1)}, u32[]{:S(2)}, u32[]{:S(2)}) collective-permute-start(f32[20,16,128]{2,1,0:T(8,128)S(1)} %get-tuple-element.86), channel_id=1, source_target_pairs={{0,6},{2,4},{4,2},{6,0},{1,7},{3,5},{5,3},{7,1},{8,14},{10,12},{12... | collective-permute-start | bytes 491528 | tf_op jit(solution)/shard_map/ppermute | solution.py:777
  25.9 10.1 %collective-permute-start.10 = (f32[25,16,128]{2,1,0:T(8,128)S(1)}, f32[25,16,128]{2,1,0:T(8,128)S(1)}, u32[]{:S(2)}, u32[]{:S(2)}) collective-permute-start(f32[25,16,128]{2,1,0:T(8,128)S(1)} %get-tuple-element.82), channel_id=1, source_target_pairs={{0,8},{8,0},{16,24},{24,16},{1,9},{9,1},{17,25},{25,17},{2,10},{10... | collective-permute-start | bytes 614408 | tf_op jit(solution)/shard_map/ppermute | solution.py:777
  26.0 10.3 %collective-permute-start.11 = (f32[25,16,128]{2,1,0:T(8,128)S(1)}, f32[25,16,128]{2,1,0:T(8,128)S(1)}, u32[]{:S(2)}, u32[]{:S(2)}) collective-permute-start(f32[25,16,128]{2,1,0:T(8,128)S(1)} %get-tuple-element.83), channel_id=1, source_target_pairs={{0,24},{8,16},{16,8},{24,0},{1,25},{9,17},{17,9},{25,1},{2,26},{10... | collective-permute-start | bytes 614408 | tf_op jit(solution)/shard_map/ppermute | solution.py:777
  32.8 6.1 %collective-permute-start.14 = (f32[240,128]{1,0:T(8,128)S(1)}, f32[240,128]{1,0:T(8,128)S(1)}, u32[]{:S(2)}, u32[]{:S(2)}) collective-permute-start(f32[240,128]{1,0:T(8,128)S(1)} %get-tuple-element.90), channel_id=1, source_target_pairs={{0,24},{8,16},{16,8},{24,0},{1,25},{9,17},{17,9},{25,1},{2,26},{10... | collective-permute-start | bytes 368648 | tf_op jit(solution)/shard_map/ppermute | solution.py:777
  32.8 6.1 %collective-permute-start.15 = (f32[240,128]{1,0:T(8,128)S(1)}, f32[240,128]{1,0:T(8,128)S(1)}, u32[]{:S(2)}, u32[]{:S(2)}) collective-permute-start(f32[240,128]{1,0:T(8,128)S(1)} %get-tuple-element.91), channel_id=1, source_target_pairs={{0,8},{8,0},{16,24},{24,16},{1,9},{9,1},{17,25},{25,17},{2,10},{10... | collective-permute-start | bytes 368648 | tf_op jit(solution)/shard_map/ppermute | solution.py:777
  34.4 5.8 %collective-permute-start.17 = (f32[128,128]{1,0:T(8,128)S(1)}, f32[128,128]{1,0:T(8,128)S(1)}, u32[]{:S(2)}, u32[]{:S(2)}) collective-permute-start(f32[128,128]{1,0:T(8,128)S(1)} %get-tuple-element.93), channel_id=1, source_target_pairs={{0,1},{1,0},{2,3},{3,2},{4,5},{5,4},{6,7},{7,6},{8,9},{9,8},{10,11... | collective-permute-start | bytes 196616 | tf_op jit(solution)/shard_map/ppermute | solution.py:798
  36.0 4.2 %collective-permute-start.16 = (f32[5,8,128]{2,1,0:T(8,128)S(1)}, f32[5,8,128]{2,1,0:T(8,128)S(1)}, u32[]{:S(2)}, u32[]{:S(2)}) collective-permute-start(f32[5,8,128]{2,1,0:T(8,128)S(1)} %get-tuple-element.92), channel_id=1, source_target_pairs={{0,25},{1,24},{8,17},{9,16},{16,9},{17,8},{24,1},{25,0},{2,27},{3,... | collective-permute-start | bytes 61448 | tf_op jit(solution)/shard_map/ppermute | solution.py:789
  36.3 3.9 %collective-permute-start.18 = (f32[5,8,128]{2,1,0:T(8,128)S(1)}, f32[5,8,128]{2,1,0:T(8,128)S(1)}, u32[]{:S(2)}, u32[]{:S(2)}) collective-permute-start(f32[5,8,128]{2,1,0:T(8,128)S(1)} %get-tuple-element.94), channel_id=1, source_target_pairs={{0,9},{1,8},{8,1},{9,0},{16,25},{17,24},{24,17},{25,16},{2,11},{3,... | collective-permute-start | bytes 61448 | tf_op jit(solution)/shard_map/ppermute | solution.py:789
